TPU v7x, 512 devices: a whole 4x8x8 slice. The times are simulated.
512 devices in a mesh: dp: 32 (over y, z_hi), seq: 16 (over z_lo, x, core).
Axes of the slice: x: 4, y: 8, z: 8 (z_hi: 4, z_lo: 2; z = z_hi * 2 + z_lo), core: 2. Of those that a mesh axis runs over, the one named last changes fastest.
Arguments:
- clips: bfloat16 [32, 16, 128, 1152], P('dp', 'seq'), may hold values from -6 to 6
- qkv_spatial: bfloat16 [3, 1152, 576], P(None, 'dp'), may hold values from -16 to 16
- out_spatial: bfloat16 [576, 1152], P('dp'), may hold values from -0.25 to 0.25
- qkv_temporal: bfloat16 [3, 1152, 576], P(None, 'dp'), may hold values from -16 to 16
- out_temporal: bfloat16 [576, 1152], P('dp'), may hold values from -0.25 to 0.25
- cotangent: bfloat16 [32, 16, 128, 1152], P('dp', 'seq'), may hold values from -6 to 6
Outputs:
- mixed_out: bfloat16 [32, 16, 128, 1152], P('dp', 'seq')
- input_grad: bfloat16 [32, 16, 128, 1152], P('dp', 'seq')
- out_temporal_grad: float32 [576, 1152], P('dp')
All inputs are finite; a program needn't handle non-finite values.
Results may differ from a plain program's by a relative error of at most 0.034.
Values may be sent and summed in bfloat16 or wider, within the bound.
No kernel may reach another device: no remote copies, remote signals or barrier semaphores. Data moves between devices by JAX's collectives and lax.ppermute only.
A program may use at most 64 MiB of HBM per device.

v0:
```python
import jax
import jax.numpy as jnp
from jax import lax
from jax.sharding import PartitionSpec as P

HEAD_DIM = 72


EPSILON = 1e-06


def normalize(values):
    centred = values - jnp.mean(values, axis=-1, keepdims=True)
    inverse = lax.rsqrt(jnp.mean(centred * centred, axis=-1, keepdims=True) + EPSILON)
    return (centred * inverse, inverse)


def norm_back(grad, normed, inverse):
    return inverse * (
        grad
        - jnp.mean(grad, axis=-1, keepdims=True)
        - normed * jnp.mean(grad * normed, axis=-1, keepdims=True)
    )


def attend(queries, key_rows, value_rows, layout):
    key_layout = layout.replace("l", "m")
    scaling = queries.shape[-1] ** (-0.5)
    scores = (
        jnp.einsum(
            layout + "," + key_layout + "->bhlm",
            queries,
            key_rows,
            preferred_element_type=jnp.float32,
        )
        * scaling
    )
    scores = scores - jnp.max(scores, axis=-1, keepdims=True)
    powers = jnp.exp(scores)
    softmax_out = powers / jnp.sum(powers, axis=-1, keepdims=True)
    context = jnp.einsum(
        "bhlm," + key_layout + "->" + layout,
        softmax_out.astype(jnp.bfloat16),
        value_rows,
        preferred_element_type=jnp.float32,
    )
    return (context.astype(jnp.bfloat16), softmax_out)


def attend_back(queries, key_rows, value_rows, softmax_out, context, context_grad, layout):
    key_layout = layout.replace("l", "m")
    scaling = queries.shape[-1] ** (-0.5)
    rounded = softmax_out.astype(jnp.bfloat16)
    value_grad = jnp.einsum(
        "bhlm," + layout + "->" + key_layout,
        rounded,
        context_grad,
        preferred_element_type=jnp.float32,
    ).astype(jnp.bfloat16)
    prob_grad = jnp.einsum(
        layout + "," + key_layout + "->bhlm",
        context_grad,
        value_rows,
        preferred_element_type=jnp.float32,
    )
    row_dots = jnp.einsum(
        layout + "," + layout + "->bhl", context_grad, context, preferred_element_type=jnp.float32
    )
    score_grad = (softmax_out * (prob_grad - row_dots[..., None]) * scaling).astype(jnp.bfloat16)
    query_grad = jnp.einsum(
        "bhlm," + key_layout + "->" + layout,
        score_grad,
        key_rows,
        preferred_element_type=jnp.float32,
    ).astype(jnp.bfloat16)
    key_grad = jnp.einsum(
        "bhlm," + layout + "->" + key_layout,
        score_grad,
        queries,
        preferred_element_type=jnp.float32,
    ).astype(jnp.bfloat16)
    return jnp.stack([query_grad, key_grad, value_grad])


def project(normed, weight):
    return jnp.einsum("fpd,tdc->tfpc", normed, weight, preferred_element_type=jnp.float32).astype(
        jnp.bfloat16
    )


def back_project(grads, weight):
    return jnp.einsum("tfpc,tdc->fpd", grads, weight, preferred_element_type=jnp.float32)


def per_device(clips, qkv_spatial, out_spatial, qkv_temporal, out_temporal, cotangent):
    inputs = clips[0]
    out_grad = cotangent[0]
    frame_local, patch_count, model_width = inputs.shape
    width = qkv_spatial.shape[2]
    head_size = HEAD_DIM
    head_count = width // head_size
    full_qkv_s, full_out_s, full_qkv_t, full_out_t = (
        lax.all_gather(qkv_spatial, "dp", axis=1, tiled=True),
        lax.all_gather(out_spatial, "dp", axis=0, tiled=True),
        lax.all_gather(qkv_temporal, "dp", axis=1, tiled=True),
        lax.all_gather(out_temporal, "dp", axis=0, tiled=True),
    )
    inputs_f = inputs.astype(jnp.float32)
    normed_s, inverse_s = normalize(inputs_f)
    heads_s = project(normed_s.astype(jnp.bfloat16), full_qkv_s).reshape(
        3, frame_local, patch_count, head_count, head_size
    )
    context_s, probs_s = attend(heads_s[0], heads_s[1], heads_s[2], "blhe")
    flat_s = context_s.reshape(frame_local, patch_count, width)
    hidden = (
        inputs_f + jnp.einsum("fpc,cd->fpd", flat_s, full_out_s, preferred_element_type=jnp.float32)
    ).astype(jnp.bfloat16)
    hidden_f = hidden.astype(jnp.float32)
    normed_t, inverse_t = normalize(hidden_f)
    normed_t_b = normed_t.astype(jnp.bfloat16)
    local_proj = project(normed_t_b, full_qkv_t)
    pixel_proj = lax.all_to_all(local_proj, "seq", split_axis=2, concat_axis=1, tiled=True)
    frame_count = pixel_proj.shape[1]
    patch_local = pixel_proj.shape[2]
    heads_t = pixel_proj.reshape(3, frame_count, patch_local, head_count, head_size)
    context_t, probs_t = attend(heads_t[0], heads_t[1], heads_t[2], "lbhe")
    context_back = lax.all_to_all(
        context_t.reshape(frame_count, patch_local, width),
        "seq",
        split_axis=0,
        concat_axis=1,
        tiled=True,
    )
    mixed = (
        hidden_f
        + jnp.einsum("fpc,cd->fpd", context_back, full_out_t, preferred_element_type=jnp.float32)
    ).astype(jnp.bfloat16)
    context_rows = context_back.reshape(-1, width)
    grad_rows = out_grad.reshape(-1, model_width)
    weight_share = lax.psum_scatter(
        lax.dot_general(
            context_rows, grad_rows, (((0,), (0,)), ((), ())), preferred_element_type=jnp.float32
        ).astype(jnp.bfloat16),
        "dp",
        scatter_dimension=0,
        tiled=True,
    )
    weight_grad = lax.psum(weight_share, "seq").astype(jnp.float32)
    out_grad_f = out_grad.astype(jnp.float32)
    grad_t = jnp.einsum(
        "fpd,cd->fpc", out_grad, full_out_t, preferred_element_type=jnp.float32
    ).astype(jnp.bfloat16)
    pixel_grad = lax.all_to_all(grad_t, "seq", split_axis=1, concat_axis=0, tiled=True)
    grads_t = attend_back(
        heads_t[0],
        heads_t[1],
        heads_t[2],
        probs_t,
        context_t,
        pixel_grad.reshape(frame_count, patch_local, head_count, head_size),
        "lbhe",
    )
    frame_grads = lax.all_to_all(
        grads_t.reshape(3, frame_count, patch_local, width),
        "seq",
        split_axis=1,
        concat_axis=2,
        tiled=True,
    )
    normal_grad_b = back_project(frame_grads, full_qkv_t).astype(jnp.bfloat16)
    normal_grad_t = lax.optimization_barrier(normal_grad_b).astype(jnp.float32)
    hidden_grad = (out_grad_f + norm_back(normal_grad_t, normed_t, inverse_t)).astype(jnp.bfloat16)
    grad_s = jnp.einsum(
        "fpd,cd->fpc", hidden_grad, full_out_s, preferred_element_type=jnp.float32
    ).astype(jnp.bfloat16)
    grads_s = attend_back(
        heads_s[0],
        heads_s[1],
        heads_s[2],
        probs_s,
        context_s,
        grad_s.reshape(frame_local, patch_count, head_count, head_size),
        "blhe",
    )
    normal_grad_s = back_project(grads_s.reshape(3, frame_local, patch_count, width), full_qkv_s)
    input_grad = (
        hidden_grad.astype(jnp.float32) + norm_back(normal_grad_s, normed_s, inverse_s)
    ).astype(jnp.bfloat16)
    return (mixed[None], input_grad[None], weight_grad)


def solution(mesh):
    placed = (
        P("dp", "seq", None, None),
        P(None, "dp", None),
        P("dp", None),
        P(None, "dp", None),
        P("dp", None),
        P("dp", "seq", None, None),
    )
    return jax.shard_map(
        per_device,
        mesh=mesh,
        in_specs=placed,
        out_specs=(P("dp", "seq", None, None), P("dp", "seq", None, None), P("dp", None)),
        check_vma=False,
    )
```

profile of v0, /device:TPU:1, one launch (start us, length us, event | category | flops | bytes accessed | tf_op | source)
XLA Modules:
  0.0 871.4 jit_solution(8592444056042022644)
XLA Ops:
  8.7 1.7 copy.50
  10.4 1.7 copy.53
  13.2 1.2 fusion.70
  14.4 84.2 %all-gather.13.cloned.1.call-done = bf16[32,18,1152]{2,1,0:T(8,128)(2,1)} async-done(((bf16[1,18,1152]{2,1,0:T(8,128)(2,1)}), bf16[32,18,1152]{2,1,0:T(8,128)(2,1)}) %all-gather.13.cloned.1.call-update) | async-done | bytes 1327120 | tf_op jit(solution)/shard_map/all_gather | solution.py:106
  98.7 2.4 reshape.361
  102.4 1.6 reduce.29
  104.9 10.3 %all-to-all-start.2 = ((bf16[16,2,2304]{2,1,0:T(2,128)(2,1)}), bf16[16,2,2304]{2,1,0:T(2,128)(2,1)}, u32[]{:S(2)}, u32[]{:S(2)}) async-start(bf16[16,2,2304]{2,1,0:T(2,128)(2,1)} %reshape.377), calls=%async_computation.2 | async-start | bytes 294912 | tf_op jit(solution)/shard_map/all_to_all | solution.py:153
  115.2 68.9 %all-gather.11.cloned.1.call-done = bf16[32,18,1152]{2,1,0:T(8,128)(2,1)} async-done(((bf16[1,18,1152]{2,1,0:T(8,128)(2,1)}), bf16[32,18,1152]{2,1,0:T(8,128)(2,1)}) %all-gather.11.cloned.1.call-update) | async-done | bytes 1327120 | tf_op jit(solution)/shard_map/all_gather | solution.py:104
  184.1 2.4 reshape.359
  186.5 118.7 %all-gather.7.cloned.1.call-done = bf16[3,1152,576]{2,0,1:T(4,128)(2,1)} async-done(((bf16[3,36,576]{2,0,1:T(4,128)(2,1)}), bf16[3,1152,576]{2,0,1:T(4,128)(2,1)}) %all-gather.7.cloned.1.call-update) | async-done | bytes 3981328 | tf_op jit(solution)/shard_map/all_gather | solution.py:103
  305.2 4.4 fusion.43
  310.9 1.2 convolution_convert_fusion.8
  312.1 1.4 fusion.140
  313.8 108.5 %all-gather.9.cloned.1.call-done = bf16[3,1152,576]{2,0,1:T(4,128)(2,1)} async-done(((bf16[3,36,576]{2,0,1:T(4,128)(2,1)}), bf16[3,1152,576]{2,0,1:T(4,128)(2,1)}) %all-gather.9.cloned.1.call-update) | async-done | bytes 3981328 | tf_op jit(solution)/shard_map/all_gather | solution.py:105
  422.3 5.2 fusion.40
  427.5 2.1 copy.55
  429.6 6.0 all-to-all-start
  435.7 2.2 reshape.378
  437.9 2.6 bitcast_reduce_fusion
  440.4 1.9 reshape.351
  442.3 1.8 bitcast_convert_fusion
  444.2 2.8 all-to-all-done
  447.0 4.8 slice_reduce_fusion.1
  451.8 1.9 squeeze.8
  453.7 1.9 squeeze.7
  455.6 1.9 squeeze.6
  457.5 2.9 fusion.141
  460.5 2.5 fusion.50
  463.0 3.5 multiply_reduce_fusion.1
  466.5 1.7 copy.60
  468.2 1.9 reshape.348
  470.1 5.1 all-to-all-start.1
  475.2 1.7 copy.71
  476.9 1.9 stack.26
  478.8 1.7 fusion.47
  482.2 1.9 stack.25
  484.0 1.3 fusion.48
  486.2 1.9 stack.24
  490.0 5.8 all-to-all-start.3
  496.1 1.3 dynamic-slice
  498.0 2.7 convolution_convert_fusion
  500.7 2.0 fusion.22
  502.7 2.6 all-to-all-done.3
  505.4 4.2 fusion.23
  510.9 1.4 convolution_convert_fusion.5
  513.2 4.2 fusion.137
  518.4 275.0 %all-reduce.3.cloned.1.call-done = bf16[576,1152]{1,0:T(8,128)(2,1)} async-done(((bf16[576,1152]{1,0:T(8,128)(2,1)}), bf16[576,1152]{1,0:T(8,128)(2,1)}) %all-reduce.3.cloned.1.call-update) | async-done | bytes 1327120
  794.4 69.8 %psum.7 = bf16[18,1152]{1,0:T(8,128)(2,1)S(1)} all-reduce(bf16[18,1152]{1,0:T(8,128)(2,1)S(1)} %constant_dynamic-slice_fusion), channel_id=1, replica_groups=mesh['dp'=32,'seq'=16] {'seq'}, use_global_device_ids=true, to_apply=%region_13.0 | all-reduce | flops 20736 | bytes 82944 | tf_op jit(solution)/shard_map/psum | solution.py:148
  (72 shorter events, 15.7 us)
Async XLA Ops:
  7.2 91.5 %all-gather.13.cloned.1.call-start = ((), (), s32[]{:S(2)}) async-start(), calls=%async_computation.7 | async-start | bytes 1824768 | tf_op jit(solution)/shard_map/all_gather | solution.py:106
  7.9 176.2 %all-gather.11.cloned.1.call-start = ((), (), s32[]{:S(2)}) async-start(), calls=%async_computation.6 | async-start | bytes 1824768 | tf_op jit(solution)/shard_map/all_gather | solution.py:104
  8.6 296.6 %all-gather.7.cloned.1.call-start = ((), (), s32[]{:S(2)}) async-start(), calls=%async_computation.4 | async-start | bytes 6082560 | tf_op jit(solution)/shard_map/all_gather | solution.py:103
  10.4 411.9 %all-gather.9.cloned.1.call-start = ((), (), s32[]{:S(2)}) async-start(), calls=%async_computation.5 | async-start | bytes 6082560 | tf_op jit(solution)/shard_map/all_gather | solution.py:105
  13.2 87.9 %copy-start.1 = (bf16[1,1,128,1152]{3,2,1,0:T(8,128)(2,1)S(1)}, bf16[1,1,128,1152]{3,2,1,0:T(8,128)(2,1)}, u32[]{:S(2)}) copy-start(bf16[1,1,128,1152]{3,2,1,0:T(8,128)(2,1)} %param.11) | copy-start | bytes 884740
  104.9 200.4 %copy-start = (bf16[1,1,128,1152]{3,2,1,0:T(8,128)(2,1)S(1)}, bf16[1,1,128,1152]{3,2,1,0:T(8,128)(2,1)}, u32[]{:S(2)}) copy-start(bf16[1,1,128,1152]{3,2,1,0:T(8,128)(2,1)} %param.6) | copy-start | bytes 884740
  104.9 324.8 %all-to-all-start.2 = ((bf16[16,2,2304]{2,1,0:T(2,128)(2,1)}), bf16[16,2,2304]{2,1,0:T(2,128)(2,1)}, u32[]{:S(2)}, u32[]{:S(2)}) async-start(bf16[16,2,2304]{2,1,0:T(2,128)(2,1)} %reshape.377), calls=%async_computation.2 | async-start | bytes 294912 | tf_op jit(solution)/shard_map/all_to_all | solution.py:153
  309.7 2.4 copy-start.6
  309.7 2.4 copy-start.8
  309.7 2.4 copy-start.10
  310.9 1.2 copy-start.13
  429.6 17.4 %all-to-all-start = ((bf16[3,1,128,576]{3,0,1,2:T(4,128)(2,1)}), bf16[3,1,128,576]{3,0,1,2:T(4,128)(2,1)}, u32[]{:S(2)}, u32[]{:S(2)}) async-start(bf16[3,1,128,576]{3,0,1,2:T(4,128)(2,1)} %copy.55), calls=%async_computation | async-start | bytes 1310720 | tf_op jit(solution)/shard_map/all_to_all | solution.py:122
  470.1 19.9 %all-to-all-start.1 = ((bf16[16,8,576]{2,1,0:T(8,128)(2,1)}), bf16[16,8,576]{2,1,0:T(8,128)(2,1)}, u32[]{:S(2)}, u32[]{:S(2)}) async-start(bf16[16,8,576]{2,1,0:T(8,128)(2,1)} %reshape.348), calls=%async_computation.1 | async-start | bytes 327680 | tf_op jit(solution)/shard_map/all_to_all | solution.py:127
  478.8 2.4 copy-start.4
  480.4 0.7 copy-start.3
  490.0 15.3 %all-to-all-start.3 = ((bf16[3,16,8,576]{3,2,0,1:T(8,128)(2,1)}), bf16[3,16,8,576]{3,2,0,1:T(8,128)(2,1)}, u32[]{:S(2)}, u32[]{:S(2)}) async-start(bf16[3,16,8,576]{3,2,0,1:T(8,128)(2,1)} %copy.72), calls=%async_computation.3 | async-start | bytes 983040 | tf_op jit(solution)/shard_map/all_to_all | solution.py:163
  495.8 297.6 %all-reduce.3.cloned.1.call-start = ((), (), s32[]{:S(2)}) async-start(), calls=%async_computation.8 | async-start | bytes 2654208
  502.7 7.1 copy-start.2
  509.9 0.9 copy-start.7
  509.9 1.0 copy-start.9
  510.7 1.5 copy-start.5
  510.7 1.6 copy-start.11
  510.7 1.6 copy-start.12
  510.7 1.6 copy-start.14
Sparse Core Ops, SparseCore 0:
  11.3 87.3 all-gather.12
  101.9 82.1 all-gather.10
  187.9 117.3 all-gather.6
  308.8 113.4 all-gather.8
  500.8 292.5 all-reduce.2
where the time goes:
time: 876 us; the launch traced here: 871 us
  waiting for transfers between devices  662 us (76%)
  blocking collectives  69.8 us (8%)
  local copies, waits for them, and re-layouts  45.4 us (5%)
  matrix products  42 us (5%)
  starting transfers between devices  27.6 us (3%)
  between operations  14.8 us (2%)
  other arithmetic  9.46 us (1%)
    unnamed x6, waiting for transfers between devices  276 us
    all_gather x1, waiting for transfers between devices, per_device(): lax.all_gather(qkv_spatial, 'dp', axis=1, tiled=True)  119 us
    all_gather x1, waiting for transfers between devices, per_device(): lax.all_gather(qkv_temporal, 'dp', axis=1, tiled=True)  109 us
    all_gather x1, waiting for transfers between devices, per_device(): lax.all_gather(out_temporal, 'dp', axis=0, tiled=True)  84.2 us
    psum x1, blocking collectives, per_device(): weight_grad = lax.psum(weight_share, 'seq').astype(jnp.float32)  69.8 us
    all_gather x1, waiting for transfers between devices, per_device(): lax.all_gather(out_spatial, 'dp', axis=0, tiled=True)  68.9 us
  transfers between devices with their start and end apart: 9, of which 7 were waited for; matrix products, arithmetic and copies ran while one was open for 8% of the time, Pallas kernels for 0%

commit v1 on v0

v1 whole, which is shorter than its diff:
```python
import functools

import jax
import jax.numpy as jnp
from jax import lax
from jax.experimental import pallas as pl
from jax.experimental.pallas import tpu as pltpu
from jax.sharding import PartitionSpec as P

BF = jnp.bfloat16
F32 = jnp.float32
EPSILON = 1e-06
D = 1152
WIDTH = 576
PAD = 640
HEADS = 8
HEAD = 72
TOKENS = 128
PATCH_BLOCK = 8
SCALING = HEAD ** (-0.5)
SHARE = 288
QK, V_ROWS, O_ROWS, ALL_ROWS = 0, 1152, 1728, 2304
VMEM_LIMIT = 48 * 1024 * 1024


def nn(a, b):
    return lax.dot_general(a, b, (((1,), (0,)), ((), ())), preferred_element_type=F32)


def nt(a, b):
    return lax.dot_general(a, b, (((1,), (1,)), ((), ())), preferred_element_type=F32)


def tn(a, b):
    return lax.dot_general(a, b, (((0,), (0,)), ((), ())), preferred_element_type=F32)


def lanes(shape):
    return lax.broadcasted_iota(jnp.int32, shape, len(shape) - 1)


def normalize(values):
    centred = values - jnp.mean(values, axis=-1, keepdims=True)
    inverse = lax.rsqrt(jnp.mean(centred * centred, axis=-1, keepdims=True) + EPSILON)
    return centred * inverse, inverse


def norm_back(grad, normed, inverse):
    return inverse * (
        grad
        - jnp.mean(grad, axis=-1, keepdims=True)
        - normed * jnp.mean(grad * normed, axis=-1, keepdims=True)
    )


def keep_width(a):
    return jnp.where(lanes(a.shape) < WIDTH, a, 0.0)


def window(h):
    low = h * HEAD // 128 * 128
    high = -(-(h * HEAD + HEAD) // 128) * 128
    return low, high


def head_mask(h):
    low, high = window(h)
    at = lanes((TOKENS, high - low)) + low
    return (at >= h * HEAD) & (at < h * HEAD + HEAD)


def add_window(tiles, h, part):
    low, high = window(h)
    part = jnp.where(head_mask(h), part, 0.0)
    for t in range(low // 128, high // 128):
        piece = part[:, t * 128 - low : t * 128 - low + 128]
        tiles[t] = piece if tiles[t] is None else tiles[t] + piece


def join(tiles):
    return jnp.concatenate(tiles, axis=1)


def project(normed, weights):
    normed_b = normed.astype(BF)
    qk = nn(normed_b, weights[QK:V_ROWS, :])
    swapped = pltpu.roll(normed, WIDTH, 1)
    first = keep_width(normed[:, :PAD]).astype(BF)
    second = keep_width(swapped[:, :PAD]).astype(BF)
    v = nn(first, weights[V_ROWS : V_ROWS + PAD, :PAD])
    v = v + pltpu.roll(nn(second, weights[V_ROWS : V_ROWS + PAD, D - PAD :]), WIDTH, 1)
    k = pltpu.roll(qk, WIDTH, 1)
    return qk[:, :PAD].astype(BF), k[:, :PAD].astype(BF), keep_width(v).astype(BF)


def back_project(dq, dk, dv, weights):
    zeros = jnp.zeros((TOKENS, D - PAD), F32)
    dqk = jnp.concatenate([dq, zeros], axis=1) + pltpu.roll(
        jnp.concatenate([dk, zeros], axis=1), WIDTH, 1
    )
    grad = nt(dqk.astype(BF), weights[QK:V_ROWS, :])
    first = nt(dv.astype(BF), weights[V_ROWS : V_ROWS + PAD, :PAD])
    second = nt(pltpu.roll(dv, PAD - WIDTH, 1).astype(BF), weights[V_ROWS : V_ROWS + PAD, D - PAD :])
    first = jnp.concatenate([keep_width(first), zeros], axis=1)
    second = jnp.concatenate([keep_width(second), zeros], axis=1)
    return grad + first + pltpu.roll(second, WIDTH, 1)


def rounded(a):
    return a.astype(BF).astype(F32)


def attend(q, k, v, allowed, probs_ref):
    tiles = [None] * (PAD // 128)
    for h in range(HEADS):
        low, high = window(h)
        masked = jnp.where(head_mask(h), q[:, low:high].astype(F32), 0.0).astype(BF)
        scores = nt(masked, k[:, low:high]) * SCALING
        if allowed is not None:
            scores = jnp.where(allowed, scores, -1e38)
        powers = jnp.exp(scores - jnp.max(scores, axis=-1, keepdims=True))
        probs = powers / jnp.sum(powers, axis=-1, keepdims=True)
        probs_ref[h] = probs
        add_window(tiles, h, nn(probs.astype(BF), v[:, low:high]))
    return join(tiles).astype(BF)


def attend_back(q, k, v, context, context_grad, probs_ref):
    dq, dk, dv = ([None] * (PAD // 128) for _ in range(3))
    for h in range(HEADS):
        low, high = window(h)
        grad = context_grad[:, low:high]
        masked = jnp.where(head_mask(h), grad.astype(F32), 0.0)
        probs = probs_ref[h]
        prob_grad = nt(masked.astype(BF), v[:, low:high])
        row = jnp.sum(masked * context[:, low:high].astype(F32), axis=-1, keepdims=True)
        score_grad = (probs * (prob_grad - row) * SCALING).astype(BF)
        add_window(dv, h, tn(probs.astype(BF), grad))
        add_window(dq, h, nn(score_grad, k[:, low:high]))
        add_window(dk, h, tn(score_grad, q[:, low:high]))
    return rounded(join(dq)), rounded(join(dk)), rounded(join(dv))


def load_weights(core_ref, own_ref, other_ref, weights, sems):
    core = core_ref[0]
    copies = []
    for half, ref in ((core, own_ref), (1 - core, other_ref)):
        for i in range(8):
            at = pl.multiple_of(i * SHARE + half * (SHARE // 2), SHARE // 2)
            copies.append(
                pltpu.make_async_copy(
                    ref.at[i], weights.at[pl.ds(at, SHARE // 2), :], sems.at[len(copies)]
                )
            )
    for copy in copies:
        copy.start()
    for copy in copies:
        copy.wait()


def prepare_kernel(x_ref, cot_ref, order_ref, x_out, cot_out, normed_out):
    order = order_ref[...]
    x = nn(x_ref[...], order)
    x_out[...] = x.astype(BF)
    cot_out[...] = nn(cot_ref[...], order).astype(BF)
    normed_out[...] = normalize(x)[0]


def forward_kernel(
    core_ref, x_ref, normed_ref, own_ref, other_ref, order_ref, hidden_ref, qkv_ref, probs_ref,
    context_ref, weights, sems,
):
    load_weights(core_ref, own_ref, other_ref, weights, sems)
    q, k, v = project(normed_ref[...], weights)
    qkv_ref[0], qkv_ref[1], qkv_ref[2] = q, k, v
    context = attend(q, k, v, None, probs_ref)
    context_ref[...] = context
    ordered = nn(context, order_ref[...]).astype(BF)
    out = nn(ordered, weights[ALL_ROWS - PAD :, :])
    hidden_ref[...] = (x_ref[...].astype(F32) + out).astype(BF)


def temporal_kernel(
    core_ref, hidden_ref, cot_ref, own_ref, other_ref, order_ref, mixed_ref, grad_ref, share_ref,
    weights, probs, sems,
):
    load_weights(core_ref, own_ref, other_ref, weights, sems)
    hidden = hidden_ref[...].astype(F32)
    normed, inverse = normalize(hidden)
    q, k, v = project(rounded(normed), weights)
    rows = lax.broadcasted_iota(jnp.int32, (TOKENS, TOKENS), 0)
    cols = lax.broadcasted_iota(jnp.int32, (TOKENS, TOKENS), 1)
    allowed = (rows & (PATCH_BLOCK - 1)) == (cols & (PATCH_BLOCK - 1))
    context = attend(q, k, v, allowed, probs)
    order = order_ref[...]
    ordered = nn(context, order).astype(BF)
    out_weights = weights[ALL_ROWS - PAD :, :]
    mixed_ref[...] = (hidden + nn(ordered, out_weights)).astype(BF)
    cot = cot_ref[...]
    share_ref[...] = tn(ordered, cot)[PAD - WIDTH :, :].astype(BF)
    context_grad = nt(nt(cot, out_weights).astype(BF), order).astype(BF)
    dq, dk, dv = attend_back(q, k, v, context, context_grad, probs)
    normed_grad = rounded(back_project(dq, dk, dv, weights))
    grad_ref[...] = (cot.astype(F32) + norm_back(normed_grad, normed, inverse)).astype(BF)


def backward_kernel(
    core_ref, x_ref, grad_ref, mixed_ref, qkv_ref, probs_ref, context_ref, own_ref, other_ref,
    order_ref, full_ref, input_grad_ref, mixed_out, weights, sems,
):
    load_weights(core_ref, own_ref, other_ref, weights, sems)
    full = full_ref[...]
    mixed_out[...] = nt(mixed_ref[...], full).astype(BF)
    grad = grad_ref[...]
    context_grad = nt(nt(grad, weights[ALL_ROWS - PAD :, :]).astype(BF), order_ref[...]).astype(BF)
    dq, dk, dv = attend_back(
        qkv_ref[0], qkv_ref[1], qkv_ref[2], context_ref[...], context_grad, probs_ref
    )
    normed_grad = back_project(dq, dk, dv, weights)
    normed, inverse = normalize(x_ref[...].astype(F32))
    total = grad.astype(F32) + norm_back(normed_grad, normed, inverse)
    input_grad_ref[...] = nt(total.astype(BF), full).astype(BF)


def call(kernel, outs, scratch, flops, *args, smem=True, hbm=()):
    in_specs = []
    for at in range(len(args)):
        space = pltpu.VMEM
        if smem and at == 0:
            space = pltpu.SMEM
        elif at in hbm:
            space = pl.ANY
        in_specs.append(pl.BlockSpec(memory_space=space))
    return pl.pallas_call(
        kernel,
        out_shape=[jax.ShapeDtypeStruct(s, t) for s, t in outs],
        in_specs=in_specs,
        out_specs=[pl.BlockSpec(memory_space=pltpu.VMEM) for _ in outs],
        scratch_shapes=scratch,
        compiler_params=pltpu.CompilerParams(vmem_limit_bytes=VMEM_LIMIT),
        cost_estimate=pl.CostEstimate(flops=flops, bytes_accessed=10_000_000, transcendentals=0),
    )(*args)


def place_in_share(dp, row):
    y, z = dp // 4, dp % 4
    return (z // 2) * 144 + y * 18 + (z % 2) * 9 + row


def model_order():
    n = jnp.arange(D)
    dp, row = n // 36, n % 36
    at = (row // 9) * SHARE + place_in_share(dp, row % 9)
    return (at[:, None] == jnp.arange(D)[None, :]).astype(BF)


def context_order():
    f = jnp.arange(PAD)
    dp, row = f // 18, f % 18
    at = PAD - WIDTH + (row // 9) * SHARE + place_in_share(dp, row % 9)
    at = jnp.where(f < WIDTH, at, -1)
    return (at[:, None] == jnp.arange(PAD)[None, :]).astype(BF)


def order_columns(a):
    rows = a.shape[0]
    a = a.reshape(rows, 8, 2, 2, 4, 9)
    return a.transpose(0, 4, 2, 1, 3, 5).reshape(rows, D)


def restore_columns(a):
    rows = a.shape[0]
    a = a.reshape(rows, 4, 2, 8, 2, 9)
    return a.transpose(0, 3, 2, 4, 1, 5).reshape(rows, D)


GROUPS_Z = [[y * 4 + z for z in range(4)] for y in range(8)]
GROUPS_Y = [[y * 4 + z for y in range(8)] for z in range(4)]
GROUPS_CHIP = [[2 * i + c for i in range(8)] for c in range(2)]
SWAP = [(s, s ^ 1) for s in range(16)]


def spread(block, axis, groups):
    count = len(groups[0])
    return lax.all_to_all(
        jnp.broadcast_to(block[None], (count,) + block.shape), axis, 0, 0,
        axis_index_groups=groups, tiled=True,
    )


def local_rows(qkv, out):
    q, k, v = qkv[0], qkv[1], qkv[2]
    return jnp.concatenate(
        [
            jnp.concatenate([q, k], axis=1),
            jnp.concatenate([v[:18], v[18:]], axis=1),
            order_columns(out),
        ],
        axis=0,
    )


def per_device(clips, qkv_spatial, out_spatial, qkv_temporal, out_temporal, cotangent):
    x = clips.reshape(TOKENS, D)
    out_grad = cotangent.reshape(TOKENS, D)
    seq = lax.axis_index("seq")
    chip, core = seq // 2, seq % 2
    core_arg = core.reshape(1).astype(jnp.int32)

    rows = jnp.stack([local_rows(qkv_spatial, out_spatial), local_rows(qkv_temporal, out_temporal)])
    mine = lax.dynamic_slice_in_dim(rows, chip * 9, 9, axis=1)
    four = spread(mine, "dp", GROUPS_Z).reshape(4, 2, 9, D)
    half = lax.dynamic_slice_in_dim(four, core * 2, 2, axis=0)
    half = half.transpose(1, 0, 2, 3).reshape(36, D)
    column = spread(half, "dp", GROUPS_Y).reshape(8, 2, 18, D)
    blocks = column.transpose(1, 0, 2, 3).reshape(2, 144, D)
    own_s = spread(blocks[0], "seq", GROUPS_CHIP).reshape(8, 144, D)
    other_s = lax.ppermute(own_s, "seq", SWAP)
    own_t = spread(blocks[1], "seq", GROUPS_CHIP).reshape(8, 144, D)
    other_t = lax.ppermute(own_t, "seq", SWAP)

    full_order = model_order()
    small_order = context_order()
    tokens_b = ((TOKENS, D), BF)
    tokens_f = ((TOKENS, D), F32)
    weights = pltpu.VMEM((ALL_ROWS, D), BF)
    sems = pltpu.SemaphoreType.DMA((16,))
    probs = (HEADS, TOKENS, TOKENS)

    x_o, cot_o, normed = call(
        prepare_kernel, [tokens_b, tokens_b, tokens_f], [], 700_000_000, x, out_grad, full_order, smem=False
    )

    def to_patches(a):
        return lax.all_to_all(a.reshape(16, PATCH_BLOCK, D), "seq", 0, 0, tiled=True).reshape(
            TOKENS, D
        )

    cot_p = to_patches(cot_o)
    hidden, qkv, probs_s, context_s = call(
        forward_kernel,
        [tokens_b, ((3, TOKENS, PAD), BF), (probs, F32), ((TOKENS, PAD), BF)],
        [weights, sems],
        700_000_000,
        core_arg, x_o, normed, own_s, other_s, small_order,
        hbm=(3, 4),
    )
    hidden_p = to_patches(hidden)
    mixed_p, grad_p, share = call(
        temporal_kernel,
        [tokens_b, tokens_b, ((WIDTH, D), BF)],
        [weights, pltpu.VMEM(probs, F32), sems],
        1_600_000_000,
        core_arg, hidden_p, cot_p, own_t, other_t, small_order,
        hbm=(3, 4),
    )
    back = lax.all_to_all(
        jnp.concatenate([grad_p, mixed_p], axis=1).reshape(16, PATCH_BLOCK, 2 * D),
        "seq", 0, 0, tiled=True,
    ).reshape(TOKENS, 2 * D)
    input_grad, mixed = call(
        backward_kernel,
        [tokens_b, tokens_b],
        [weights, sems],
        800_000_000,
        core_arg, x_o, back[:, :D], back[:, D:], qkv, probs_s, context_s, own_s, other_s,
        small_order, full_order,
        hbm=(7, 8),
    )

    share = share.reshape(2, SHARE, D)
    keep = lax.dynamic_index_in_dim(share, core, 0, keepdims=False)
    send = lax.dynamic_index_in_dim(share, 1 - core, 0, keepdims=False)
    both = (keep.astype(F32) + lax.ppermute(send, "seq", SWAP).astype(F32)).astype(BF)
    both = both.reshape(2, 8, 2, 9, D).transpose(1, 0, 2, 3, 4).reshape(8, 36, D)
    over_y = lax.all_to_all(both, "dp", 0, 0, axis_index_groups=GROUPS_Y, tiled=True)
    over_y = jnp.sum(over_y.astype(F32), axis=0).astype(BF).reshape(4, 9, D)
    over_z = lax.all_to_all(over_y, "dp", 0, 0, axis_index_groups=GROUPS_Z, tiled=True)
    over_z = jnp.sum(over_z.astype(F32), axis=0).astype(BF)
    over_seq = spread(over_z, "seq", [list(range(16))]).reshape(8, 2, 9, D)
    out_temporal_grad = restore_columns(jnp.sum(over_seq.astype(F32), axis=0).reshape(18, D))

    return mixed[None, None], input_grad[None, None], out_temporal_grad


def solution(mesh):
    tokens = P("dp", "seq", None, None)
    placed = (tokens, P(None, "dp", None), P("dp", None), P(None, "dp", None), P("dp", None), tokens)
    return jax.shard_map(
        per_device,
        mesh=mesh,
        in_specs=placed,
        out_specs=(tokens, tokens, P("dp", None)),
        check_vma=False,
    )
```

time: 876 us -> 260 us (0.30)
  waiting for transfers between devices: 662 us -> 94 us
  matrix products: 42 us -> 0 us
  Pallas kernels: 0 us -> 28.2 us
  starting transfers between devices: 27.6 us -> 55.4 us
  blocking collectives: 69.8 us -> 49.7 us
  local copies, waits for them, and re-layouts: 45.4 us -> 25.4 us
  between operations: 14.8 us -> 1.06 us
    all_gather x4 -> x0, waiting for transfers between devices: 380 us -> none  [the longest x1 119 us: per_device(): lax.all_gather(qkv_spatial, 'dp', axis=1, tiled=True)]
    unnamed x6 -> x0, waiting for transfers between devices: 276 us -> none
    all_to_all x4 -> x8, waiting for transfers between devices: 5.49 us -> 92 us  [the longest x4 67.6 us: spread(): lax.all_to_all(jnp.broadcast_to(block[None], (count,) + block.shape), axi...]
    psum x1 -> x0, blocking collectives: 69.8 us -> none  [per_device(): weight_grad = lax.psum(weight_share, 'seq').astype(jnp.float32)]
    all_to_all x0 -> x2, blocking collectives: none -> 49.7 us  [the longest x1 25.4 us: per_device(): lax.all_to_all(both, 'dp', 0, 0, axis_index_groups=GROUPS_Y, tiled=True)]
    dot_general x19 -> x0, matrix products: 37.9 us -> none  [the longest x2 9.65 us: project(): jnp.einsum('fpd,tdc->tfpc', normed, weight, preferred_element_type=jnp.fl...]
    pallas_call x0 -> x4, Pallas kernels: none -> 28.2 us  [call(): pl.pallas_call(kernel, out_shape=[jax.ShapeDtypeStruct(s, t) for s, t in...]
    all_to_all x4 -> x8, starting transfers between devices: 27.2 us -> 46.1 us  [the longest x4 26.5 us: spread(): lax.all_to_all(jnp.broadcast_to(block[None], (count,) + block.shape), axi...]
  transfers between devices with their start and end apart: 9 -> 11, of which waited for: 7 -> 7; matrix products, arithmetic and copies ran while one was open for 8% -> 1% of each run, Pallas kernels for 0% -> 7%
where the time goes in v1:
time: 260 us; the launch traced here: 258 us
  waiting for transfers between devices  94 us (36%)
  starting transfers between devices  55.4 us (21%)
  blocking collectives  49.7 us (19%)
  Pallas kernels  28.2 us (11%)
  local copies, waits for them, and re-layouts  25.4 us (10%)
  other arithmetic  4.49 us (2%)
    all_to_all x4, waiting for transfers between devices, spread(): lax.all_to_all(jnp.broadcast_to(block[None], (count,) + block.shape), axi...  67.6 us
    pallas_call x4, Pallas kernels, call(): pl.pallas_call(kernel, out_shape=[jax.ShapeDtypeStruct(s, t) for s, t in...  28.2 us
    all_to_all x4, starting transfers between devices, spread(): lax.all_to_all(jnp.broadcast_to(block[None], (count,) + block.shape), axi...  26.5 us
    all_to_all x1, blocking collectives, per_device(): lax.all_to_all(both, 'dp', 0, 0, axis_index_groups=GROUPS_Y, tiled=True)  25.4 us
    all_to_all x1, blocking collectives, spread(): lax.all_to_all(jnp.broadcast_to(block[None], (count,) + block.shape), axi...  24.3 us
    all_to_all x1, waiting for transfers between devices, per_device(): lax.all_to_all(jnp.concatenate([grad_p, mixed_p], axis=1).reshape(16, PAT...  10.6 us
    all_to_all x2, starting transfers between devices, to_patches(): lax.all_to_all(a.reshape(16, PATCH_BLOCK, D), 'seq', 0, 0, tiled=True)  9.49 us
    all_to_all x2, waiting for transfers between devices, to_patches(): lax.all_to_all(a.reshape(16, PATCH_BLOCK, D), 'seq', 0, 0, tiled=True)  7.39 us
  transfers between devices with their start and end apart: 11, of which 7 were waited for; matrix products, arithmetic and copies ran while one was open for 1% of the time, Pallas kernels for 7%

profile of v1, /device:TPU:1, one launch (start us, length us, event | category | flops | bytes accessed | tf_op | source)
XLA Modules:
  0.0 258.2 jit_solution(6978471562824498540)
XLA Ops:
  0.6 0.8 slice_bitcast_fusion.1
  1.5 0.8 slice_bitcast_fusion.5
  2.3 0.8 slice_bitcast_fusion.3
  3.2 0.8 slice_bitcast_fusion.7
  4.0 1.9 reshape.265
  6.5 0.7 reshape.266
  7.2 1.2 reshape.267
  8.4 0.5 copy.61
  8.9 0.7 reshape.268
  9.8 0.8 broadcast_in_dim.22
  10.6 10.8 %all-to-all-start = ((bf16[4,2,9,1152]{3,1,2,0:T(2,128)(2,1)}), bf16[4,2,9,1152]{3,1,2,0:T(2,128)(2,1)S(1)}, u32[]{:S(2)}, u32[]{:S(2)}) async-start(bf16[4,2,9,1152]{3,1,2,0:T(2,128)(2,1)} %broadcast_in_dim.22), calls=%async_computation | async-start | bytes 331776 | tf_op jit(solution)/shard_map/all_to_all | solution.py:285
  21.4 7.6 %all-to-all-done = bf16[4,2,9,1152]{3,1,2,0:T(2,128)(2,1)S(1)} async-done(((bf16[4,2,9,1152]{3,1,2,0:T(2,128)(2,1)}), bf16[4,2,9,1152]{3,1,2,0:T(2,128)(2,1)S(1)}, u32[]{:S(2)}, u32[]{:S(2)}) %all-to-all-start) | async-done | bytes 165920 | tf_op jit(solution)/shard_map/all_to_all | solution.py:285
  29.3 24.3 %all_to_all.50 = bf16[8,36,1152]{2,1,0:T(8,128)(2,1)S(1)} all-to-all(bf16[8,36,1152]{2,1,0:T(8,128)(2,1)S(1)} %broadcast_in_dim.24), channel_id=1, replica_groups={{0,64,128,192,256,320,384,448},{16,80,144,208,272,336,400,464},{32,96,1..., dimensions={0} | all-to-all | bytes 1327104 | tf_op jit(solution)/shard_map/all_to_all | solution.py:285
  53.9 1.8 broadcast_in_dim.49
  55.6 6.5 %all-to-all-start.2 = ((bf16[8,144,1152]{2,1,0:T(8,128)(2,1)}), bf16[8,144,1152]{2,1,0:T(8,128)(2,1)}, u32[]{:S(2)}, u32[]{:S(2)}) async-start(bf16[8,144,1152]{2,1,0:T(8,128)(2,1)} %broadcast_in_dim.49), calls=%async_computation.2 | async-start | bytes 5308416 | tf_op jit(solution)/shard_map/all_to_all | solution.py:285
  62.2 31.3 %all-to-all-done.2.own_ref = bf16[8,144,1152]{2,1,0:T(8,128)(2,1)} async-done(((bf16[8,144,1152]{2,1,0:T(8,128)(2,1)}), bf16[8,144,1152]{2,1,0:T(8,128)(2,1)}, u32[]{:S(2)}, u32[]{:S(2)}) %all-to-all-start.2) | async-done | bytes 2654240 | tf_op jit(solution)/shard_map/all_to_all | solution.py:285
  93.5 1.7 broadcast_in_dim.51
  95.2 4.5 %all-to-all-start.5 = ((bf16[8,144,1152]{2,1,0:T(8,128)(2,1)}), bf16[8,144,1152]{2,1,0:T(8,128)(2,1)}, u32[]{:S(2)}, u32[]{:S(2)}) async-start(bf16[8,144,1152]{2,1,0:T(8,128)(2,1)} %broadcast_in_dim.51), calls=%async_computation.5 | async-start | bytes 5308416 | tf_op jit(solution)/shard_map/all_to_all | solution.py:285
  99.7 3.5 %collective-permute-start = (bf16[8,144,1152]{2,1,0:T(8,128)(2,1)}, bf16[8,144,1152]{2,1,0:T(8,128)(2,1)}, u32[]{:S(2)}, u32[]{:S(2)}) collective-permute-start(bf16[8,144,1152]{2,1,0:T(8,128)(2,1)} %all-to-all-done.2.own_ref), channel_id=1, source_target_pairs={{0,1},{1,0},{2,3},{3,2},{4,5},{5,4},{6,7},{7,6},{8,9},{9,8},{10,11... | collective-permute-start | bytes 7962632 | tf_op jit(solution)/shard_map/ppermute | solution.py:318
  103.2 28.7 %all-to-all-done.5.own_ref = bf16[8,144,1152]{2,1,0:T(8,128)(2,1)} async-done(((bf16[8,144,1152]{2,1,0:T(8,128)(2,1)}), bf16[8,144,1152]{2,1,0:T(8,128)(2,1)}, u32[]{:S(2)}, u32[]{:S(2)}) %all-to-all-start.5) | async-done | bytes 2654240 | tf_op jit(solution)/shard_map/all_to_all | solution.py:285
  131.9 2.8 %collective-permute-start.1 = (bf16[8,144,1152]{2,1,0:T(8,128)(2,1)}, bf16[8,144,1152]{2,1,0:T(8,128)(2,1)}, u32[]{:S(2)}, u32[]{:S(2)}) collective-permute-start(bf16[8,144,1152]{2,1,0:T(8,128)(2,1)} %all-to-all-done.5.own_ref), channel_id=1, source_target_pairs={{0,1},{1,0},{2,3},{3,2},{4,5},{5,4},{6,7},{7,6},{8,9},{9,8},{10,11... | collective-permute-start | bytes 7962632 | tf_op jit(solution)/shard_map/ppermute | solution.py:320
  135.8 1.8 shard_map.85
  137.6 3.8 %all-to-all-start.4 = ((bf16[16,8,1152]{2,1,0:T(8,128)(2,1)}), bf16[16,8,1152]{2,1,0:T(8,128)(2,1)S(1)}, u32[]{:S(2)}, u32[]{:S(2)}) async-start(bf16[16,8,1152]{2,1,0:T(8,128)(2,1)} %bitcast.20), calls=%async_computation.4 | async-start | bytes 589824 | tf_op jit(solution)/shard_map/all_to_all | solution.py:335
  141.6 6.3 %shard_map.86 = (bf16[128,1152]{1,0:T(8,128)(2,1)}, bf16[3,128,640]{2,1,0:T(8,128)(2,1)S(1)}, f32[8,128,128]{2,1,0:T(8,128)S(1)}, bf16[128,640]{1,0:T(8,128)(2,1)S(1)}) custom-call(s32[1]{0:T(128)} %bitcast.core_ref, bf16[128,1152]{1,0:T(8,128)(2,1)S(1)} %get-tuple-element.15.x_ref, f32[128,1152]{1,0:T(8,128)S(1)} %get-tuple-element.16.normed_ref, ...), custom_call_target="tpu_custom_call" | custom-call | flops 700000000 | bytes 10000000 | tf_op jit(solution)/shard_map/pallas_call | solution.py:234
  147.9 0.8 copy-done.1
  148.7 0.8 copy-done.3
  149.5 5.7 %all-to-all-start.3 = ((bf16[16,8,1152]{2,1,0:T(8,128)(2,1)}), bf16[16,8,1152]{2,1,0:T(8,128)(2,1)S(1)}, u32[]{:S(2)}, u32[]{:S(2)}) async-start(bf16[16,8,1152]{2,1,0:T(8,128)(2,1)} %bitcast.18), calls=%async_computation.3 | async-start | bytes 589824 | tf_op jit(solution)/shard_map/all_to_all | solution.py:335
  155.2 7.4 %all-to-all-done.3 = bf16[16,8,1152]{2,1,0:T(8,128)(2,1)S(1)} async-done(((bf16[16,8,1152]{2,1,0:T(8,128)(2,1)}), bf16[16,8,1152]{2,1,0:T(8,128)(2,1)S(1)}, u32[]{:S(2)}, u32[]{:S(2)}) %all-to-all-start.3) | async-done | bytes 294944 | tf_op jit(solution)/shard_map/all_to_all | solution.py:335
  162.6 9.6 %shard_map.87 = (bf16[128,1152]{1,0:T(8,128)(2,1)S(1)}, bf16[128,1152]{1,0:T(8,128)(2,1)S(1)}, bf16[576,1152]{1,0:T(8,128)(2,1)S(1)}) custom-call(s32[1]{0:T(128)} %bitcast.core_ref, bf16[128,1152]{1,0:T(8,128)(2,1)S(1)} %bitcast.53, bf16[128,1152]{1,0:T(8,128)(2,1)S(1)} %bitcast.52, bf16[8,144,1152]{2,1,0:T(8,128)(2,1)} %all-to-all-done.5.own_ref, ...), custom_call_target="tpu_custom_call" | custom-call | flops 1600000000 | bytes 10000000 | tf_op jit(solution)/shard_map/pallas_call | solution.py:234
  172.2 0.7 copy-done.7
  172.9 0.9 dynamic-slice_bitcast_fusion
  173.8 3.0 %collective-permute-start.2 = (bf16[288,1152]{1,0:T(8,128)(2,1)}, bf16[288,1152]{1,0:T(8,128)(2,1)}, u32[]{:S(2)}, u32[]{:S(2)}) collective-permute-start(bf16[288,1152]{1,0:T(8,128)(2,1)} %dynamic-slice_bitcast_fusion), channel_id=1, source_target_pairs={{0,1},{1,0},{2,3},{3,2},{4,5},{5,4},{6,7},{7,6},{8,9},{9,8},{10,11... | collective-permute-start | bytes 1990664 | tf_op jit(solution)/shard_map/ppermute | solution.py:374
  176.8 2.0 collective-permute-done.2
  178.9 2.1 fusion.2
  181.0 1.4 reshape.277
  182.7 25.4 %all_to_all.51 = bf16[8,36,1152]{2,1,0:T(8,128)(2,1)S(1)} all-to-all(bf16[8,36,1152]{2,1,0:T(8,128)(2,1)S(1)} %copy.68), channel_id=1, replica_groups={{0,64,128,192,256,320,384,448},{16,80,144,208,272,336,400,464},{32,96,1..., dimensions={0} | all-to-all | bytes 1327104 | tf_op jit(solution)/shard_map/all_to_all | solution.py:376
  208.2 0.7 reshape.279
  208.9 3.3 %all-to-all-start.8 = ((bf16[4,9,1152]{2,1,0:T(8,128)(2,1)}), bf16[4,9,1152]{2,1,0:T(8,128)(2,1)S(1)}, u32[]{:S(2)}, u32[]{:S(2)}) async-start(bf16[4,9,1152]{2,1,0:T(8,128)(2,1)} %reshape.279), calls=%async_computation.8 | async-start | bytes 294912 | tf_op jit(solution)/shard_map/all_to_all | solution.py:378
  212.2 0.9 maximum_bitcast_fusion
  213.1 6.4 %all-to-all-done.8 = bf16[4,9,1152]{2,1,0:T(8,128)(2,1)S(1)} async-done(((bf16[4,9,1152]{2,1,0:T(8,128)(2,1)}), bf16[4,9,1152]{2,1,0:T(8,128)(2,1)S(1)}, u32[]{:S(2)}, u32[]{:S(2)}) %all-to-all-start.8) | async-done | bytes 82976 | tf_op jit(solution)/shard_map/all_to_all | solution.py:378
  219.5 6.8 %all-to-all-start.6 = ((bf16[16,8,2304]{2,1,0:T(8,128)(2,1)}), bf16[16,8,2304]{2,1,0:T(8,128)(2,1)S(1)}, u32[]{:S(2)}, u32[]{:S(2)}) async-start(bf16[16,8,2304]{2,1,0:T(8,128)(2,1)} %maximum_bitcast_fusion), calls=%async_computation.6 | async-start | bytes 1179648 | tf_op jit(solution)/shard_map/all_to_all | solution.py:357
  226.4 10.6 %all-to-all-done.6 = bf16[16,8,2304]{2,1,0:T(8,128)(2,1)S(1)} async-done(((bf16[16,8,2304]{2,1,0:T(8,128)(2,1)}), bf16[16,8,2304]{2,1,0:T(8,128)(2,1)S(1)}, u32[]{:S(2)}, u32[]{:S(2)}) %all-to-all-start.6) | async-done | bytes 589856 | tf_op jit(solution)/shard_map/all_to_all | solution.py:357
  236.9 0.9 broadcast_in_dim.54
  237.9 4.7 %all-to-all-start.9 = ((bf16[16,9,1152]{2,1,0:T(8,128)(2,1)}), bf16[16,9,1152]{2,1,0:T(8,128)(2,1)S(1)}, u32[]{:S(2)}, u32[]{:S(2)}) async-start(bf16[16,9,1152]{2,1,0:T(8,128)(2,1)} %broadcast_in_dim.54), calls=%async_computation.9 | async-start | bytes 1179648 | tf_op jit(solution)/shard_map/all_to_all | solution.py:285
  242.6 10.5 %shard_map.88 = (bf16[128,1152]{1,0:T(8,128)(2,1)}, bf16[128,1152]{1,0:T(8,128)(2,1)}) custom-call(s32[1]{0:T(128)} %bitcast.core_ref, bf16[128,1152]{1,0:T(8,128)(2,1)S(1)} %get-tuple-element.15.x_ref, bf16[128,1152]{1,0:T(8,128)(2,1)S(1)} %get-tuple-element.30.grad_ref, bf16[128,1152]{1,0:T(8,128)(2,1)S(1)} %get-tuple-element.29.mixed_ref, ...), custom_call_target="tpu_custom_call" | custom-call | flops 800000000 | bytes 10000000 | tf_op jit(solution)/shard_map/pallas_call | solution.py:234
  253.9 1.8 reshape_reshape.3
  255.7 0.8 copy.71
  256.6 1.6 reshape.280
  (48 shorter events, 3.9 us)
Async XLA Ops:
  3.2 4.0 %copy-start.9 = (bf16[18,1152]{1,0:T(8,128)(2,1)S(1)}, bf16[18,1152]{1,0:T(8,128)(2,1)}, u32[]{:S(2)}) copy-start(bf16[18,1152]{1,0:T(8,128)(2,1)} %param.10) | copy-start | bytes 124420
  10.6 18.5 %all-to-all-start = ((bf16[4,2,9,1152]{3,1,2,0:T(2,128)(2,1)}), bf16[4,2,9,1152]{3,1,2,0:T(2,128)(2,1)S(1)}, u32[]{:S(2)}, u32[]{:S(2)}) async-start(bf16[4,2,9,1152]{3,1,2,0:T(2,128)(2,1)} %broadcast_in_dim.22), calls=%async_computation | async-start | bytes 331776 | tf_op jit(solution)/shard_map/all_to_all | solution.py:285
  55.6 37.9 %all-to-all-start.2 = ((bf16[8,144,1152]{2,1,0:T(8,128)(2,1)}), bf16[8,144,1152]{2,1,0:T(8,128)(2,1)}, u32[]{:S(2)}, u32[]{:S(2)}) async-start(bf16[8,144,1152]{2,1,0:T(8,128)(2,1)} %broadcast_in_dim.49), calls=%async_computation.2 | async-start | bytes 5308416 | tf_op jit(solution)/shard_map/all_to_all | solution.py:285
  95.2 36.7 %all-to-all-start.5 = ((bf16[8,144,1152]{2,1,0:T(8,128)(2,1)}), bf16[8,144,1152]{2,1,0:T(8,128)(2,1)}, u32[]{:S(2)}, u32[]{:S(2)}) async-start(bf16[8,144,1152]{2,1,0:T(8,128)(2,1)} %broadcast_in_dim.51), calls=%async_computation.5 | async-start | bytes 5308416 | tf_op jit(solution)/shard_map/all_to_all | solution.py:285
  99.7 41.9 %collective-permute-start = (bf16[8,144,1152]{2,1,0:T(8,128)(2,1)}, bf16[8,144,1152]{2,1,0:T(8,128)(2,1)}, u32[]{:S(2)}, u32[]{:S(2)}) collective-permute-start(bf16[8,144,1152]{2,1,0:T(8,128)(2,1)} %all-to-all-done.2.own_ref), channel_id=1, source_target_pairs={{0,1},{1,0},{2,3},{3,2},{4,5},{5,4},{6,7},{7,6},{8,9},{9,8},{10,11... | collective-permute-start | bytes 7962632 | tf_op jit(solution)/shard_map/ppermute | solution.py:318
  131.9 23.3 %collective-permute-start.1 = (bf16[8,144,1152]{2,1,0:T(8,128)(2,1)}, bf16[8,144,1152]{2,1,0:T(8,128)(2,1)}, u32[]{:S(2)}, u32[]{:S(2)}) collective-permute-start(bf16[8,144,1152]{2,1,0:T(8,128)(2,1)} %all-to-all-done.5.own_ref), channel_id=1, source_target_pairs={{0,1},{1,0},{2,3},{3,2},{4,5},{5,4},{6,7},{7,6},{8,9},{9,8},{10,11... | collective-permute-start | bytes 7962632 | tf_op jit(solution)/shard_map/ppermute | solution.py:320
  134.7 1.0 copy-start.5
  134.7 1.0 copy-start.6
  135.2 2.3 copy-start
  137.6 11.9 %all-to-all-start.4 = ((bf16[16,8,1152]{2,1,0:T(8,128)(2,1)}), bf16[16,8,1152]{2,1,0:T(8,128)(2,1)S(1)}, u32[]{:S(2)}, u32[]{:S(2)}) async-start(bf16[16,8,1152]{2,1,0:T(8,128)(2,1)} %bitcast.20), calls=%async_computation.4 | async-start | bytes 589824 | tf_op jit(solution)/shard_map/all_to_all | solution.py:335
  147.9 0.8 copy-start.1
  148.7 0.8 copy-start.3
  149.5 13.1 %all-to-all-start.3 = ((bf16[16,8,1152]{2,1,0:T(8,128)(2,1)}), bf16[16,8,1152]{2,1,0:T(8,128)(2,1)S(1)}, u32[]{:S(2)}, u32[]{:S(2)}) async-start(bf16[16,8,1152]{2,1,0:T(8,128)(2,1)} %bitcast.18), calls=%async_computation.3 | async-start | bytes 589824 | tf_op jit(solution)/shard_map/all_to_all | solution.py:335
  172.2 0.7 copy-start.7
  173.8 5.1 %collective-permute-start.2 = (bf16[288,1152]{1,0:T(8,128)(2,1)}, bf16[288,1152]{1,0:T(8,128)(2,1)}, u32[]{:S(2)}, u32[]{:S(2)}) collective-permute-start(bf16[288,1152]{1,0:T(8,128)(2,1)} %dynamic-slice_bitcast_fusion), channel_id=1, source_target_pairs={{0,1},{1,0},{2,3},{3,2},{4,5},{5,4},{6,7},{7,6},{8,9},{9,8},{10,11... | collective-permute-start | bytes 1990664 | tf_op jit(solution)/shard_map/ppermute | solution.py:374
  182.7 29.5 %copy-start.8 = (bf16[128,1152]{1,0:T(8,128)(2,1)S(1)}, bf16[128,1152]{1,0:T(8,128)(2,1)}, u32[]{:S(2)}) copy-start(bf16[128,1152]{1,0:T(8,128)(2,1)} %copy-done.7) | copy-start | bytes 884740
  208.9 10.6 %all-to-all-start.8 = ((bf16[4,9,1152]{2,1,0:T(8,128)(2,1)}), bf16[4,9,1152]{2,1,0:T(8,128)(2,1)S(1)}, u32[]{:S(2)}, u32[]{:S(2)}) async-start(bf16[4,9,1152]{2,1,0:T(8,128)(2,1)} %reshape.279), calls=%async_computation.8 | async-start | bytes 294912 | tf_op jit(solution)/shard_map/all_to_all | solution.py:378
  219.5 17.4 %all-to-all-start.6 = ((bf16[16,8,2304]{2,1,0:T(8,128)(2,1)}), bf16[16,8,2304]{2,1,0:T(8,128)(2,1)S(1)}, u32[]{:S(2)}, u32[]{:S(2)}) async-start(bf16[16,8,2304]{2,1,0:T(8,128)(2,1)} %maximum_bitcast_fusion), calls=%async_computation.6 | async-start | bytes 1179648 | tf_op jit(solution)/shard_map/all_to_all | solution.py:357
  237.9 4.7 %copy-start.2 = (f32[8,128,128]{2,1,0:T(8,128)S(1)}, f32[8,128,128]{2,1,0:T(8,128)}, u32[]{:S(2)}) copy-start(f32[8,128,128]{2,1,0:T(8,128)} %copy-done.1) | copy-start | bytes 1572868
  237.9 4.7 %copy-start.4 = (bf16[3,128,640]{2,1,0:T(8,128)(2,1)S(1)}, bf16[3,128,640]{2,1,0:T(8,128)(2,1)}, u32[]{:S(2)}) copy-start(bf16[3,128,640]{2,1,0:T(8,128)(2,1)} %copy-done.3) | copy-start | bytes 1474564
  237.9 15.3 %all-to-all-start.9 = ((bf16[16,9,1152]{2,1,0:T(8,128)(2,1)}), bf16[16,9,1152]{2,1,0:T(8,128)(2,1)S(1)}, u32[]{:S(2)}, u32[]{:S(2)}) async-start(bf16[16,9,1152]{2,1,0:T(8,128)(2,1)} %broadcast_in_dim.54), calls=%async_computation.9 | async-start | bytes 1179648 | tf_op jit(solution)/shard_map/all_to_all | solution.py:285

commit v2 on v1

--- a/solution.py
+++ b/solution.py
@@ -21,6 +21,7 @@
 SHARE = 288
 QK, V_ROWS, O_ROWS, ALL_ROWS = 0, 1152, 1728, 2304
 VMEM_LIMIT = 48 * 1024 * 1024
+RING = (0, 1, -1, 2, -2, 3, -3, 4)
 
 
 def nn(a, b):
@@ -141,8 +142,32 @@
     return rounded(join(dq)), rounded(join(dk)), rounded(join(dv))
 
 
-def load_weights(core_ref, own_ref, other_ref, weights, sems):
-    core = core_ref[0]
+def start_all(copies):
+    for copy in copies:
+        copy.start()
+    for copy in copies:
+        copy.wait()
+
+
+def load_spatial(at_ref, blocks, swapped, weights, sems):
+    y, core = at_ref[0], at_ref[1]
+    copies = []
+    for half, mine in ((core, True), (1 - core, False)):
+        sign = 1 - 2 * half
+        for n, step in enumerate(RING):
+            source = blocks[n] if mine else swapped[n // 4].at[n % 4]
+            place = lax.rem(y - sign * step + 16, 8)
+            at = pl.multiple_of(half * D + place * 144, 144)
+            copies.append(
+                pltpu.make_async_copy(
+                    source, weights.at[pl.ds(at, 144), :], sems.at[len(copies)]
+                )
+            )
+    start_all(copies)
+
+
+def load_temporal(at_ref, own_ref, other_ref, weights, sems):
+    core = at_ref[1]
     copies = []
     for half, ref in ((core, own_ref), (1 - core, other_ref)):
         for i in range(8):
@@ -152,42 +177,118 @@
                     ref.at[i], weights.at[pl.ds(at, SHARE // 2), :], sems.at[len(copies)]
                 )
             )
-    for copy in copies:
-        copy.start()
-    for copy in copies:
-        copy.wait()
-
-
-def prepare_kernel(x_ref, cot_ref, order_ref, x_out, cot_out, normed_out):
-    order = order_ref[...]
-    x = nn(x_ref[...], order)
-    x_out[...] = x.astype(BF)
-    cot_out[...] = nn(cot_ref[...], order).astype(BF)
-    normed_out[...] = normalize(x)[0]
-
-
-def forward_kernel(
-    core_ref, x_ref, normed_ref, own_ref, other_ref, order_ref, hidden_ref, qkv_ref, probs_ref,
-    context_ref, weights, sems,
-):
-    load_weights(core_ref, own_ref, other_ref, weights, sems)
-    q, k, v = project(normed_ref[...], weights)
+    start_all(copies)
+
+
+def project_spatial(normed, weights):
+    normed_b = normed.astype(BF)
+    qk = nn(normed_b, weights[:D, :])
+    v = keep_width(nn(normed_b, weights[D:, :PAD]))
+    k = pltpu.roll(qk, WIDTH, 1)
+    return qk[:, :PAD].astype(BF), k[:, :PAD].astype(BF), v.astype(BF)
+
+
+def pair_lanes(dq, dk):
+    zeros = jnp.zeros((TOKENS, D - PAD), F32)
+    return jnp.concatenate([dq, zeros], axis=1) + pltpu.roll(
+        jnp.concatenate([dk, zeros], axis=1), WIDTH, 1
+    )
+
+
+def back_project_spatial(dq, dk, dv, weights):
+    return nt(pair_lanes(dq, dk).astype(BF), weights[:D, :]) + nt(
+        dv.astype(BF), weights[D:, :PAD]
+    )
+
+
+def late(a):
+    return jnp.where(lanes(a.shape) >= PAD - WIDTH, a, 0.0)
+
+
+def out_spatial_of(context, expand, weights):
+    zeros = jnp.zeros((TOKENS, D - PAD), F32)
+    spread_out = nn(context, expand)
+    first = late(nn(spread_out.astype(BF), weights[D:, D - PAD :]))
+    second = late(nn(pltpu.roll(spread_out, 18, 1).astype(BF), weights[D:, D - PAD :]))
+    return pltpu.roll(
+        jnp.concatenate([first, zeros], axis=1), D - (PAD - WIDTH), 1
+    ) + jnp.concatenate([zeros, second], axis=1)
+
+
+def context_grad_spatial(grad, expand, weights):
+    first = late(pltpu.roll(grad, PAD - WIDTH, 1)[:, :PAD])
+    second = late(grad[:, D - PAD :])
+    total = nt(first.astype(BF), weights[D:, D - PAD :]) + pltpu.roll(
+        nt(second.astype(BF), weights[D:, D - PAD :]), D - 18, 1
+    )
+    return nt(total.astype(BF), expand).astype(BF)
+
+
+def selection(rows, columns, shift):
+    r = lax.broadcasted_iota(jnp.int32, (rows, columns), 0)
+    c = lax.broadcasted_iota(jnp.int32, (rows, columns), 1)
+    return r + shift == c
+
+
+def pack_kernel(at_ref, qkv_s, out_s, qkv_t, out_t, block_ref):
+    chip, core = at_ref[2], at_ref[1]
+
+    def pick(which, a):
+        return nn(which.astype(F32).astype(BF), a)
+
+    def side(a, b):
+        return jnp.concatenate([a, b], axis=1)
+
+    def rows(count, at, size):
+        return selection(count, size, at)
+
+    q, k, v, out = qkv_s[0], qkv_s[1], qkv_s[2], out_s[...]
+    lead = selection(36, 18, 0)
+    tail = selection(36, 18, -18)
+    halves = pick(lead, out[:, :WIDTH]) + pick(tail, out[:, WIDTH:])
+    first = side(q.astype(F32), k.astype(F32))
+    second = side(v.astype(F32), halves)
+    spatial = jnp.where(core == 0, first, second)
+
+    q, k, v, out = qkv_t[0], qkv_t[1], qkv_t[2], out_t[...]
+    nine = lax.broadcasted_iota(jnp.int32, (12, 1), 0) < 9
+
+    def inside(low, high):
+        return nine & (chip >= low) & (chip < high)
+
+    here = rows(12, chip * 9, 36) & inside(0, 4)
+    upper = rows(12, (chip - 4) * 9, 36) & inside(4, 6)
+    lower = rows(12, (chip - 4) * 9 + 18, 36) & inside(4, 6)
+    last = rows(12, (chip - 6) * 9, 18) & inside(6, 8)
+    temporal = side(pick(here, q) + pick(upper, v), pick(here, k) + pick(lower, v))
+    temporal = temporal + pick(last, out)
+    block = jnp.concatenate([spatial, temporal], axis=0).astype(BF)
+    for z in range(4):
+        block_ref[z] = block
+
+
+def forward_kernel(*refs):
+    (at_ref, x_ref, expand_ref), refs = refs[:3], refs[3:]
+    blocks, swapped, refs = refs[:8], refs[8:10], refs[10:]
+    hidden_ref, qkv_ref, probs_ref, context_ref, weights, sems = refs
+    load_spatial(at_ref, blocks, swapped, weights, sems)
+    x = x_ref[...].astype(F32)
+    q, k, v = project_spatial(normalize(x)[0], weights)
     qkv_ref[0], qkv_ref[1], qkv_ref[2] = q, k, v
     context = attend(q, k, v, None, probs_ref)
     context_ref[...] = context
-    ordered = nn(context, order_ref[...]).astype(BF)
-    out = nn(ordered, weights[ALL_ROWS - PAD :, :])
-    hidden_ref[...] = (x_ref[...].astype(F32) + out).astype(BF)
+    hidden_ref[...] = (x + out_spatial_of(context, expand_ref[...], weights)).astype(BF)
 
 
 def temporal_kernel(
-    core_ref, hidden_ref, cot_ref, own_ref, other_ref, order_ref, mixed_ref, grad_ref, share_ref,
-    weights, probs, sems,
+    at_ref, hidden_ref, cot_ref, own_ref, other_ref, order_ref, full_ref, mixed_ref, grad_ref,
+    share_ref, weights, probs, sems,
 ):
-    load_weights(core_ref, own_ref, other_ref, weights, sems)
+    load_temporal(at_ref, own_ref, other_ref, weights, sems)
     hidden = hidden_ref[...].astype(F32)
+    full = full_ref[...]
     normed, inverse = normalize(hidden)
-    q, k, v = project(rounded(normed), weights)
+    q, k, v = project(nn(normed.astype(BF), full), weights)
     rows = lax.broadcasted_iota(jnp.int32, (TOKENS, TOKENS), 0)
     cols = lax.broadcasted_iota(jnp.int32, (TOKENS, TOKENS), 1)
     allowed = (rows & (PATCH_BLOCK - 1)) == (cols & (PATCH_BLOCK - 1))
@@ -200,26 +301,23 @@
     share_ref[...] = tn(ordered, cot)[PAD - WIDTH :, :].astype(BF)
     context_grad = nt(nt(cot, out_weights).astype(BF), order).astype(BF)
     dq, dk, dv = attend_back(q, k, v, context, context_grad, probs)
-    normed_grad = rounded(back_project(dq, dk, dv, weights))
+    normed_grad = nt(back_project(dq, dk, dv, weights).astype(BF), full)
     grad_ref[...] = (cot.astype(F32) + norm_back(normed_grad, normed, inverse)).astype(BF)
 
 
-def backward_kernel(
-    core_ref, x_ref, grad_ref, mixed_ref, qkv_ref, probs_ref, context_ref, own_ref, other_ref,
-    order_ref, full_ref, input_grad_ref, mixed_out, weights, sems,
-):
-    load_weights(core_ref, own_ref, other_ref, weights, sems)
-    full = full_ref[...]
-    mixed_out[...] = nt(mixed_ref[...], full).astype(BF)
-    grad = grad_ref[...]
-    context_grad = nt(nt(grad, weights[ALL_ROWS - PAD :, :]).astype(BF), order_ref[...]).astype(BF)
+def backward_kernel(*refs):
+    (at_ref, x_ref, grad_ref, qkv_ref, probs_ref, context_ref, expand_ref), refs = refs[:7], refs[7:]
+    blocks, swapped, refs = refs[:8], refs[8:10], refs[10:]
+    input_grad_ref, weights, sems = refs
+    load_spatial(at_ref, blocks, swapped, weights, sems)
+    grad = grad_ref[...].astype(F32)
+    context_grad = context_grad_spatial(grad, expand_ref[...], weights)
     dq, dk, dv = attend_back(
         qkv_ref[0], qkv_ref[1], qkv_ref[2], context_ref[...], context_grad, probs_ref
     )
-    normed_grad = back_project(dq, dk, dv, weights)
+    normed_grad = back_project_spatial(dq, dk, dv, weights)
     normed, inverse = normalize(x_ref[...].astype(F32))
-    total = grad.astype(F32) + norm_back(normed_grad, normed, inverse)
-    input_grad_ref[...] = nt(total.astype(BF), full).astype(BF)
+    input_grad_ref[...] = (grad + norm_back(normed_grad, normed, inverse)).astype(BF)
 
 
 def call(kernel, outs, scratch, flops, *args, smem=True, hbm=()):
@@ -262,16 +360,10 @@
     return (at[:, None] == jnp.arange(PAD)[None, :]).astype(BF)
 
 
-def order_columns(a):
-    rows = a.shape[0]
-    a = a.reshape(rows, 8, 2, 2, 4, 9)
-    return a.transpose(0, 4, 2, 1, 3, 5).reshape(rows, D)
-
-
-def restore_columns(a):
-    rows = a.shape[0]
-    a = a.reshape(rows, 4, 2, 8, 2, 9)
-    return a.transpose(0, 3, 2, 4, 1, 5).reshape(rows, D)
+def expand_order():
+    f = jnp.arange(PAD)
+    at = jnp.where(f < WIDTH, 36 * (f // 18) + f % 18, -1)
+    return (at[:, None] == jnp.arange(D)[None, :]).astype(BF)
 
 
 GROUPS_Z = [[y * 4 + z for z in range(4)] for y in range(8)]
@@ -288,85 +380,100 @@
     )
 
 
-def local_rows(qkv, out):
-    q, k, v = qkv[0], qkv[1], qkv[2]
-    return jnp.concatenate(
-        [
-            jnp.concatenate([q, k], axis=1),
-            jnp.concatenate([v[:18], v[18:]], axis=1),
-            order_columns(out),
-        ],
-        axis=0,
-    )
+def along_y(distance):
+    pairs = []
+    for y in range(8):
+        for z in range(4):
+            for s in range(16):
+                to = (y + (distance if s % 2 == 0 else -distance)) % 8
+                pairs.append(((y * 4 + z) * 16 + s, (to * 4 + z) * 16 + s))
+    return pairs
+
+
+UP, DOWN = along_y(1), along_y(-1)
+
+
+def move(a, pairs):
+    return lax.ppermute(a, ("dp", "seq"), pairs)
 
 
 def per_device(clips, qkv_spatial, out_spatial, qkv_temporal, out_temporal, cotangent):
     x = clips.reshape(TOKENS, D)
     out_grad = cotangent.reshape(TOKENS, D)
-    seq = lax.axis_index("seq")
-    chip, core = seq // 2, seq % 2
-    core_arg = core.reshape(1).astype(jnp.int32)
-
-    rows = jnp.stack([local_rows(qkv_spatial, out_spatial), local_rows(qkv_temporal, out_temporal)])
-    mine = lax.dynamic_slice_in_dim(rows, chip * 9, 9, axis=1)
-    four = spread(mine, "dp", GROUPS_Z).reshape(4, 2, 9, D)
-    half = lax.dynamic_slice_in_dim(four, core * 2, 2, axis=0)
-    half = half.transpose(1, 0, 2, 3).reshape(36, D)
-    column = spread(half, "dp", GROUPS_Y).reshape(8, 2, 18, D)
-    blocks = column.transpose(1, 0, 2, 3).reshape(2, 144, D)
-    own_s = spread(blocks[0], "seq", GROUPS_CHIP).reshape(8, 144, D)
-    other_s = lax.ppermute(own_s, "seq", SWAP)
-    own_t = spread(blocks[1], "seq", GROUPS_CHIP).reshape(8, 144, D)
-    other_t = lax.ppermute(own_t, "seq", SWAP)
-
-    full_order = model_order()
-    small_order = context_order()
+    seq, dp = lax.axis_index("seq"), lax.axis_index("dp")
+    y, chip, core = dp // 4, seq // 2, seq % 2
+    at = jnp.stack([y, core, chip]).astype(jnp.int32)
+
     tokens_b = ((TOKENS, D), BF)
-    tokens_f = ((TOKENS, D), F32)
-    weights = pltpu.VMEM((ALL_ROWS, D), BF)
+    probs = (HEADS, TOKENS, TOKENS)
     sems = pltpu.SemaphoreType.DMA((16,))
-    probs = (HEADS, TOKENS, TOKENS)
-
-    x_o, cot_o, normed = call(
-        prepare_kernel, [tokens_b, tokens_b, tokens_f], [], 700_000_000, x, out_grad, full_order, smem=False
-    )
 
     def to_patches(a):
         return lax.all_to_all(a.reshape(16, PATCH_BLOCK, D), "seq", 0, 0, tiled=True).reshape(
             TOKENS, D
         )
 
-    cot_p = to_patches(cot_o)
+    (packed,) = call(
+        pack_kernel, [((4, 48, D), BF)], [], 100_000_000, at, qkv_spatial, out_spatial,
+        qkv_temporal, out_temporal,
+    )
+    four = lax.all_to_all(packed, "dp", 0, 0, axis_index_groups=GROUPS_Z, tiled=True)
+    block = four[:, :36].reshape(144, D)
+    column = lax.dynamic_slice_in_dim(four, core * 2, 2, axis=0)[:, 36:45].reshape(1, 18, D)
+
+    up, down = [block], [block]
+    up.append(move(block, UP))
+    down.append(move(block, DOWN))
+    column = jnp.concatenate([column, move(column, along_y(4))])
+    up.append(move(up[-1], UP))
+    down.append(move(down[-1], DOWN))
+    column = jnp.concatenate([column, move(column, along_y(-2))])
+    up.append(move(up[-1], UP))
+    down.append(move(down[-1], DOWN))
+    column = jnp.concatenate([column, move(column, along_y(-1))])
+    up.append(move(up[-1], UP))
+    blocks = [block, up[1], down[1], up[2], down[2], up[3], down[3], up[4]]
+    swapped = [lax.ppermute(jnp.stack(blocks[n : n + 4]), "seq", SWAP) for n in (0, 4)]
+
+    places = jnp.arange(8)
+    offset = jnp.where(core == 0, places - y, y - places) % 8
+    at_offset = jnp.array([0, 4, 2, 6, 1, 5, 3, 7])[offset]
+    column = jnp.take(column, at_offset, axis=0).reshape(144, D)
+    own_t = spread(column, "seq", GROUPS_CHIP).reshape(8, 144, D)
+    other_t = lax.ppermute(own_t, "seq", SWAP)
+
+    full_order = model_order()
+    small_order = context_order()
+    expand = expand_order()
+    cot_p = to_patches(out_grad)
+
     hidden, qkv, probs_s, context_s = call(
         forward_kernel,
         [tokens_b, ((3, TOKENS, PAD), BF), (probs, F32), ((TOKENS, PAD), BF)],
-        [weights, sems],
+        [pltpu.VMEM((2 * D, D), BF), sems],
         700_000_000,
-        core_arg, x_o, normed, own_s, other_s, small_order,
-        hbm=(3, 4),
+        at, x, expand, *blocks, *swapped,
+        hbm=range(3, 13),
     )
     hidden_p = to_patches(hidden)
     mixed_p, grad_p, share = call(
         temporal_kernel,
         [tokens_b, tokens_b, ((WIDTH, D), BF)],
-        [weights, pltpu.VMEM(probs, F32), sems],
+        [pltpu.VMEM((ALL_ROWS, D), BF), pltpu.VMEM(probs, F32), sems],
         1_600_000_000,
-        core_arg, hidden_p, cot_p, own_t, other_t, small_order,
+        at, hidden_p, cot_p, own_t, other_t, small_order, full_order,
         hbm=(3, 4),
     )
-    back = lax.all_to_all(
-        jnp.concatenate([grad_p, mixed_p], axis=1).reshape(16, PATCH_BLOCK, 2 * D),
-        "seq", 0, 0, tiled=True,
-    ).reshape(TOKENS, 2 * D)
-    input_grad, mixed = call(
+    grad = to_patches(grad_p)
+    (input_grad,) = call(
         backward_kernel,
-        [tokens_b, tokens_b],
-        [weights, sems],
+        [tokens_b],
+        [pltpu.VMEM((2 * D, D), BF), sems],
         800_000_000,
-        core_arg, x_o, back[:, :D], back[:, D:], qkv, probs_s, context_s, own_s, other_s,
-        small_order, full_order,
-        hbm=(7, 8),
-    )
+        at, x, grad, qkv, probs_s, context_s, expand, *blocks, *swapped,
+        hbm=range(7, 17),
+    )
+    mixed = to_patches(mixed_p)
 
     share = share.reshape(2, SHARE, D)
     keep = lax.dynamic_index_in_dim(share, core, 0, keepdims=False)
@@ -378,7 +485,7 @@
     over_z = lax.all_to_all(over_y, "dp", 0, 0, axis_index_groups=GROUPS_Z, tiled=True)
     over_z = jnp.sum(over_z.astype(F32), axis=0).astype(BF)
     over_seq = spread(over_z, "seq", [list(range(16))]).reshape(8, 2, 9, D)
-    out_temporal_grad = restore_columns(jnp.sum(over_seq.astype(F32), axis=0).reshape(18, D))
+    out_temporal_grad = jnp.sum(over_seq.astype(F32), axis=0).reshape(18, D)
 
     return mixed[None, None], input_grad[None, None], out_temporal_grad
 

time: 260 us -> 260 us (level)
  starting transfers between devices: 55.4 us -> 101 us
  waiting for transfers between devices: 94 us -> 54.8 us
  blocking collectives: 49.7 us -> 37.7 us
  other arithmetic: 4.49 us -> 12.9 us
  local copies, waits for them, and re-layouts: 25.4 us -> 17.8 us
  Pallas kernels: 28.2 us -> 32.3 us
    all_to_all x4 -> x2, waiting for transfers between devices: 67.6 us -> 1.64 us  [spread(): lax.all_to_all(jnp.broadcast_to(block[None], (count,) + block.shape), axi...]
    ppermute x1 -> x12, starting transfers between devices: 3.5 us -> 49.2 us  [the longest x10 40.1 us: move(): return lax.ppermute(a, ('dp', 'seq'), pairs)]
    ppermute x1 -> x12, waiting for transfers between devices: 0.01 us -> 21.9 us  [the longest x10 21.9 us: move(): return lax.ppermute(a, ('dp', 'seq'), pairs)]
    all_to_all x1, blocking collectives: 24.3 us -> 11.1 us  [per_device(): lax.all_to_all(over_y, 'dp', 0, 0, axis_index_groups=GROUPS_Z, tiled=True)]
    all_to_all x2 -> x4, starting transfers between devices: 9.49 us -> 22.6 us  [to_patches(): lax.all_to_all(a.reshape(16, PATCH_BLOCK, D), 'seq', 0, 0, tiled=True)]
    all_to_all x4 -> x2, starting transfers between devices: 26.5 us -> 13.9 us  [spread(): lax.all_to_all(jnp.broadcast_to(block[None], (count,) + block.shape), axi...]
    all_to_all x2 -> x4, waiting for transfers between devices: 7.39 us -> 19 us  [to_patches(): lax.all_to_all(a.reshape(16, PATCH_BLOCK, D), 'seq', 0, 0, tiled=True)]
    all_to_all x2 -> x1, waiting for transfers between devices: 17 us -> 10.5 us  [per_device(): lax.all_to_all(packed, 'dp', 0, 0, axis_index_groups=GROUPS_Z, tiled=True)]
  transfers between devices with their start and end apart: 11 -> 21, of which waited for: 7 -> 13; matrix products, arithmetic and copies ran while one was open for 1% -> 5% of each run, Pallas kernels for 7% -> 7%
where the time goes in v2:
time: 260 us; the launch traced here: 258 us
  starting transfers between devices  101 us (39%)
  waiting for transfers between devices  54.8 us (21%)
  blocking collectives  37.7 us (15%)
  Pallas kernels  32.3 us (12%)
  local copies, waits for them, and re-layouts  17.8 us (7%)
  other arithmetic  12.9 us (5%)
    ppermute x10, starting transfers between devices, move(): return lax.ppermute(a, ('dp', 'seq'), pairs)  40.1 us
    pallas_call x4, Pallas kernels, call(): pl.pallas_call(kernel, out_shape=[jax.ShapeDtypeStruct(s, t) for s, t in...  32.3 us
    all_to_all x1, blocking collectives, per_device(): lax.all_to_all(both, 'dp', 0, 0, axis_index_groups=GROUPS_Y, tiled=True)  26.5 us
    all_to_all x4, starting transfers between devices, to_patches(): lax.all_to_all(a.reshape(16, PATCH_BLOCK, D), 'seq', 0, 0, tiled=True)  22.6 us
    ppermute x10, waiting for transfers between devices, move(): return lax.ppermute(a, ('dp', 'seq'), pairs)  21.9 us
    all_to_all x4, waiting for transfers between devices, to_patches(): lax.all_to_all(a.reshape(16, PATCH_BLOCK, D), 'seq', 0, 0, tiled=True)  19 us
    all_to_all x2, starting transfers between devices, spread(): lax.all_to_all(jnp.broadcast_to(block[None], (count,) + block.shape), axi...  13.9 us
    all_to_all x1, blocking collectives, per_device(): lax.all_to_all(over_y, 'dp', 0, 0, axis_index_groups=GROUPS_Z, tiled=True)  11.1 us
  transfers between devices with their start and end apart: 21, of which 13 were waited for; matrix products, arithmetic and copies ran while one was open for 5% of the time, Pallas kernels for 7%

profile of v2, /device:TPU:1, one launch (start us, length us, event | category | flops | bytes accessed | tf_op | source)
XLA Modules:
  0.0 258.2 jit_solution(9511302693947188995)
XLA Ops:
  4.2 1.7 shard_map.94
  5.9 10.8 %all-to-all-start = ((bf16[4,48,1152]{2,1,0:T(8,128)(2,1)}), bf16[4,48,1152]{2,1,0:T(8,128)(2,1)S(1)}, u32[]{:S(2)}, u32[]{:S(2)}) async-start(bf16[4,48,1152]{2,1,0:T(8,128)(2,1)} %shard_map.94), calls=%async_computation | async-start | bytes 884736 | tf_op jit(solution)/shard_map/all_to_all | solution.py:420
  16.7 10.5 %all-to-all-done = bf16[4,48,1152]{2,1,0:T(8,128)(2,1)S(1)} async-done(((bf16[4,48,1152]{2,1,0:T(8,128)(2,1)}), bf16[4,48,1152]{2,1,0:T(8,128)(2,1)S(1)}, u32[]{:S(2)}, u32[]{:S(2)}) %all-to-all-start) | async-done | bytes 442400 | tf_op jit(solution)/shard_map/all_to_all | solution.py:420
  27.3 7.5 %collective-permute-start.9 = (bf16[1,18,1152]{2,1,0:T(8,128)(2,1)S(1)}, bf16[1,18,1152]{2,1,0:T(8,128)(2,1)S(1)}, u32[]{:S(2)}, u32[]{:S(2)}) collective-permute-start(bf16[1,18,1152]{2,1,0:T(8,128)(2,1)S(1)} %reshape.334), channel_id=1, source_target_pairs={{0,256},{1,257},{2,258},{3,259},{4,260},{5,261},{6,262},{7,263},{8... | collective-permute-start | bytes 124424 | tf_op jit(solution)/shard_map/ppermute | solution.py:397
  36.4 4.6 %collective-permute-start.10 = (bf16[2,18,1152]{2,1,0:T(8,128)(2,1)S(1)}, bf16[2,18,1152]{2,1,0:T(8,128)(2,1)S(1)}, u32[]{:S(2)}, u32[]{:S(2)}) collective-permute-start(bf16[2,18,1152]{2,1,0:T(8,128)(2,1)S(1)} %pad_maximum_fusion.4), channel_id=1, source_target_pairs={{0,384},{1,129},{2,386},{3,131},{4,388},{5,133},{6,390},{7,135},{8... | collective-permute-start | bytes 248840 | tf_op jit(solution)/shard_map/ppermute | solution.py:397
  41.0 3.2 %collective-permute-done.10 = bf16[2,18,1152]{2,1,0:T(8,128)(2,1)S(1)} collective-permute-done((bf16[2,18,1152]{2,1,0:T(8,128)(2,1)S(1)}, bf16[2,18,1152]{2,1,0:T(8,128)(2,1)S(1)}, u32[]{:S(2)}, u32[]{:S(2)}) %collective-permute-start.10) | collective-permute-done | bytes 82976 | tf_op jit(solution)/shard_map/ppermute | solution.py:397
  44.3 4.0 %collective-permute-start.11 = (bf16[4,18,1152]{2,1,0:T(8,128)(2,1)S(1)}, bf16[4,18,1152]{2,1,0:T(8,128)(2,1)S(1)}, u32[]{:S(2)}, u32[]{:S(2)}) collective-permute-start(bf16[4,18,1152]{2,1,0:T(8,128)(2,1)S(1)} %pad_maximum_fusion.3), channel_id=1, source_target_pairs={{0,448},{1,65},{2,450},{3,67},{4,452},{5,69},{6,454},{7,71},{8,456... | collective-permute-start | bytes 497672 | tf_op jit(solution)/shard_map/ppermute | solution.py:397
  48.5 4.3 %collective-permute-done.11 = bf16[4,18,1152]{2,1,0:T(8,128)(2,1)S(1)} collective-permute-done((bf16[4,18,1152]{2,1,0:T(8,128)(2,1)S(1)}, bf16[4,18,1152]{2,1,0:T(8,128)(2,1)S(1)}, u32[]{:S(2)}, u32[]{:S(2)}) %collective-permute-start.11) | collective-permute-done | bytes 165920 | tf_op jit(solution)/shard_map/ppermute | solution.py:397
  53.7 1.7 broadcast_in_dim.42
  55.4 8.8 %all-to-all-start.3 = ((bf16[8,144,1152]{2,1,0:T(8,128)(2,1)}), bf16[8,144,1152]{2,1,0:T(8,128)(2,1)S(1)}, u32[]{:S(2)}, u32[]{:S(2)}) async-start(bf16[8,144,1152]{2,1,0:T(8,128)(2,1)} %broadcast_in_dim.42), calls=%async_computation.3 | async-start | bytes 5308416 | tf_op jit(solution)/shard_map/all_to_all | solution.py:377
  66.0 3.4 %collective-permute-start = (bf16[144,1152]{1,0:T(8,128)(2,1)S(1)}, bf16[144,1152]{1,0:T(8,128)(2,1)S(1)}, u32[]{:S(2)}, u32[]{:S(2)}) collective-permute-start(bf16[144,1152]{1,0:T(8,128)(2,1)S(1)} %reshape.330.refs_3_.refs_7_), channel_id=1, source_target_pairs={{0,64},{1,449},{2,66},{3,451},{4,68},{5,453},{6,70},{7,455},{8,72}... | collective-permute-start | bytes 995336 | tf_op jit(solution)/shard_map/ppermute | solution.py:397
  69.4 1.9 collective-permute-start.1
  71.3 2.9 %collective-permute-done.refs_4_.refs_8_ = bf16[144,1152]{1,0:T(8,128)(2,1)S(1)} collective-permute-done((bf16[144,1152]{1,0:T(8,128)(2,1)S(1)}, bf16[144,1152]{1,0:T(8,128)(2,1)S(1)}, u32[]{:S(2)}, u32[]{:S(2)}) %collective-permute-start) | collective-permute-done | bytes 331808 | tf_op jit(solution)/shard_map/ppermute | solution.py:397
  74.2 4.4 %collective-permute-start.2 = (bf16[144,1152]{1,0:T(8,128)(2,1)S(1)}, bf16[144,1152]{1,0:T(8,128)(2,1)S(1)}, u32[]{:S(2)}, u32[]{:S(2)}) collective-permute-start(bf16[144,1152]{1,0:T(8,128)(2,1)S(1)} %collective-permute-done.refs_4_.refs_8_), channel_id=1, source_target_pairs={{0,64},{1,449},{2,66},{3,451},{4,68},{5,453},{6,70},{7,455},{8,72}... | collective-permute-start | bytes 995336 | tf_op jit(solution)/shard_map/ppermute | solution.py:397
  78.6 1.9 collective-permute-done.1.refs_5_.refs_9_
  80.5 1.9 collective-permute-start.3
  82.4 3.3 %collective-permute-done.2.refs_6_.refs_10_ = bf16[144,1152]{1,0:T(8,128)(2,1)S(1)} collective-permute-done((bf16[144,1152]{1,0:T(8,128)(2,1)S(1)}, bf16[144,1152]{1,0:T(8,128)(2,1)S(1)}, u32[]{:S(2)}, u32[]{:S(2)}) %collective-permute-start.2) | collective-permute-done | bytes 331808 | tf_op jit(solution)/shard_map/ppermute | solution.py:397
  85.7 5.1 %collective-permute-start.4 = (bf16[144,1152]{1,0:T(8,128)(2,1)S(1)}, bf16[144,1152]{1,0:T(8,128)(2,1)}, u32[]{:S(2)}, u32[]{:S(2)}) collective-permute-start(bf16[144,1152]{1,0:T(8,128)(2,1)S(1)} %collective-permute-done.2.refs_6_.refs_10_), channel_id=1, source_target_pairs={{0,64},{1,449},{2,66},{3,451},{4,68},{5,453},{6,70},{7,455},{8,72}... | collective-permute-start | bytes 995336 | tf_op jit(solution)/shard_map/ppermute | solution.py:397
  90.9 1.9 collective-permute-start.5
  92.8 5.4 %collective-permute-done.4.refs_8_.refs_12_ = bf16[144,1152]{1,0:T(8,128)(2,1)} collective-permute-done((bf16[144,1152]{1,0:T(8,128)(2,1)S(1)}, bf16[144,1152]{1,0:T(8,128)(2,1)}, u32[]{:S(2)}, u32[]{:S(2)}) %collective-permute-start.4) | collective-permute-done | bytes 331808 | tf_op jit(solution)/shard_map/ppermute | solution.py:397
  98.2 5.4 %collective-permute-start.6 = (bf16[144,1152]{1,0:T(8,128)(2,1)}, bf16[144,1152]{1,0:T(8,128)(2,1)}, u32[]{:S(2)}, u32[]{:S(2)}) collective-permute-start(bf16[144,1152]{1,0:T(8,128)(2,1)} %collective-permute-done.4.refs_8_.refs_12_), channel_id=1, source_target_pairs={{0,64},{1,449},{2,66},{3,451},{4,68},{5,453},{6,70},{7,455},{8,72}... | collective-permute-start | bytes 995336 | tf_op jit(solution)/shard_map/ppermute | solution.py:397
  103.6 1.8 stack_reshape.3
  105.4 2.4 pad_maximum_fusion
  107.9 4.8 %collective-permute-start.7 = (bf16[4,144,1152]{2,1,0:T(8,128)(2,1)}, bf16[4,144,1152]{2,1,0:T(8,128)(2,1)}, u32[]{:S(2)}, u32[]{:S(2)}) collective-permute-start(bf16[4,144,1152]{2,1,0:T(8,128)(2,1)} %pad_maximum_fusion), channel_id=1, source_target_pairs={{0,1},{1,0},{2,3},{3,2},{4,5},{5,4},{6,7},{7,6},{8,9},{9,8},{10,11... | collective-permute-start | bytes 3981320 | tf_op jit(solution)/shard_map/ppermute | solution.py:436
  112.6 2.6 %pad_maximum_fusion.1 = bf16[4,144,1152]{2,1,0:T(8,128)(2,1)} fusion(bf16[1,144,1152]{2,1,0:T(8,128)(2,1)} %bitcast.10, bf16[1,144,1152]{2,1,0:T(8,128)(2,1)} %bitcast.9, bf16[1,144,1152]{2,1,0:T(8,128)(2,1)} %bitcast.8, bf16[1,144,1152]{2,1,0:T(8,128)(2,1)} %bitcast.7), kind=kLoop, calls=%fused_computation.9 | loop fusion | flops 1990656 | bytes 2654208 | tf_op jit(solution)/shard_map/stack | solution.py:436
  115.2 4.3 %collective-permute-start.8 = (bf16[4,144,1152]{2,1,0:T(8,128)(2,1)}, bf16[4,144,1152]{2,1,0:T(8,128)(2,1)}, u32[]{:S(2)}, u32[]{:S(2)}) collective-permute-start(bf16[4,144,1152]{2,1,0:T(8,128)(2,1)} %pad_maximum_fusion.1), channel_id=1, source_target_pairs={{0,1},{1,0},{2,3},{3,2},{4,5},{5,4},{6,7},{7,6},{8,9},{9,8},{10,11... | collective-permute-start | bytes 3981320 | tf_op jit(solution)/shard_map/ppermute | solution.py:436
  119.6 1.9 collective-permute-start.12
  121.5 6.1 %all-to-all-start.2 = ((bf16[16,8,1152]{2,1,0:T(8,128)(2,1)}), bf16[16,8,1152]{2,1,0:T(8,128)(2,1)}, u32[]{:S(2)}, u32[]{:S(2)}) async-start(bf16[16,8,1152]{2,1,0:T(8,128)(2,1)} %bitcast.49), calls=%async_computation.2 | async-start | bytes 589824 | tf_op jit(solution)/shard_map/all_to_all | solution.py:412
  127.7 1.5 fusion.1.refs_2_.refs_6_
  129.2 7.8 %shard_map.95 = (bf16[128,1152]{1,0:T(8,128)(2,1)S(1)}, bf16[3,128,640]{2,1,0:T(8,128)(2,1)S(1)}, f32[8,128,128]{2,1,0:T(8,128)S(1)}, bf16[128,640]{1,0:T(8,128)(2,1)S(1)}) custom-call(s32[3]{0:T(128)S(1)} %pad_add_fusion.at_ref.refs_0_, bf16[128,1152]{1,0:T(8,128)(2,1)S(1)} %bitcast.41, bf16[640,1152]{1,0:T(8,128)(2,1)} %fusion.1.refs_2_.refs_6_, ...), custom_call_target="tpu_custom_call" | custom-call | flops 700000000 | bytes 10000000 | tf_op jit(solution)/shard_map/pallas_call | solution.py:332
  140.0 5.7 %all-to-all-start.1 = ((bf16[16,8,1152]{2,1,0:T(8,128)(2,1)}), bf16[16,8,1152]{2,1,0:T(8,128)(2,1)}, u32[]{:S(2)}, u32[]{:S(2)}) async-start(bf16[16,8,1152]{2,1,0:T(8,128)(2,1)} %bitcast.44), calls=%async_computation.1 | async-start | bytes 589824 | tf_op jit(solution)/shard_map/all_to_all | solution.py:412
  145.7 2.0 fusion.full_ref
  148.0 5.2 %all-to-all-done.1 = bf16[16,8,1152]{2,1,0:T(8,128)(2,1)} async-done(((bf16[16,8,1152]{2,1,0:T(8,128)(2,1)}), bf16[16,8,1152]{2,1,0:T(8,128)(2,1)}, u32[]{:S(2)}, u32[]{:S(2)}) %all-to-all-start.1) | async-done | bytes 294944 | tf_op jit(solution)/shard_map/all_to_all | solution.py:412
  153.2 13.8 %shard_map.96 = (bf16[128,1152]{1,0:T(8,128)(2,1)}, bf16[128,1152]{1,0:T(8,128)(2,1)}, bf16[576,1152]{1,0:T(8,128)(2,1)S(1)}) custom-call(s32[3]{0:T(128)S(1)} %pad_add_fusion.at_ref.refs_0_, bf16[128,1152]{1,0:T(8,128)(2,1)} %bitcast.12.hidden_ref, bf16[128,1152]{1,0:T(8,128)(2,1)} %bitcast.14.cot_ref, bf16[8,144,1152]{2,1,0:T(8,128)(2,1)S(1)} %all-to-all-done.3.own_ref, ...), custom_call_target="tpu_custom_call" | custom-call | flops 1600000000 | bytes 10000000 | tf_op jit(solution)/shard_map/pallas_call | solution.py:332
  167.0 1.1 copy-done.10
  168.2 3.0 %collective-permute-start.13 = (bf16[288,1152]{1,0:T(8,128)(2,1)S(1)}, bf16[288,1152]{1,0:T(8,128)(2,1)S(1)}, u32[]{:S(2)}, u32[]{:S(2)}) collective-permute-start(bf16[288,1152]{1,0:T(8,128)(2,1)S(1)} %dynamic-slice_bitcast_fusion), channel_id=1, source_target_pairs={{0,1},{1,0},{2,3},{3,2},{4,5},{5,4},{6,7},{7,6},{8,9},{9,8},{10,11... | collective-permute-start | bytes 1990664 | tf_op jit(solution)/shard_map/ppermute | solution.py:481
  171.2 1.7 collective-permute-done.13
  172.9 1.3 fusion.3
  174.8 26.5 %all_to_all.45 = bf16[8,36,1152]{2,1,0:T(8,128)(2,1)S(1)} all-to-all(bf16[8,36,1152]{2,1,0:T(8,128)(2,1)S(1)} %copy.23), channel_id=1, replica_groups={{0,64,128,192,256,320,384,448},{16,80,144,208,272,336,400,464},{32,96,1..., dimensions={0} | all-to-all | bytes 1327104 | tf_op jit(solution)/shard_map/all_to_all | solution.py:483
  201.3 5.1 %all-to-all-start.5 = ((bf16[16,8,1152]{2,1,0:T(8,128)(2,1)}), bf16[16,8,1152]{2,1,0:T(8,128)(2,1)S(1)}, u32[]{:S(2)}, u32[]{:S(2)}) async-start(bf16[16,8,1152]{2,1,0:T(8,128)(2,1)} %bitcast.20), calls=%async_computation.5 | async-start | bytes 589824 | tf_op jit(solution)/shard_map/all_to_all | solution.py:412
  206.7 7.3 %all-to-all-done.5 = bf16[16,8,1152]{2,1,0:T(8,128)(2,1)S(1)} async-done(((bf16[16,8,1152]{2,1,0:T(8,128)(2,1)}), bf16[16,8,1152]{2,1,0:T(8,128)(2,1)S(1)}, u32[]{:S(2)}, u32[]{:S(2)}) %all-to-all-start.5) | async-done | bytes 294944 | tf_op jit(solution)/shard_map/all_to_all | solution.py:412
  214.0 11.1 %all_to_all.46 = bf16[4,9,1152]{2,1,0:T(8,128)(2,1)} all-to-all(bf16[4,9,1152]{2,1,0:T(8,128)(2,1)S(1)} %reshape.341), channel_id=1, replica_groups={{0,16,32,48},{64,80,96,112},{128,144,160,176},{192,208,224,240},{256,27..., dimensions={0} | all-to-all | bytes 165888 | tf_op jit(solution)/shard_map/all_to_all | solution.py:485
  225.1 5.7 %all-to-all-start.4 = ((bf16[16,8,1152]{2,1,0:T(8,128)(2,1)}), bf16[16,8,1152]{2,1,0:T(8,128)(2,1)S(1)}, u32[]{:S(2)}, u32[]{:S(2)}) async-start(bf16[16,8,1152]{2,1,0:T(8,128)(2,1)} %bitcast.18), calls=%async_computation.4 | async-start | bytes 589824 | tf_op jit(solution)/shard_map/all_to_all | solution.py:412
  231.8 6.5 %all-to-all-done.4 = bf16[16,8,1152]{2,1,0:T(8,128)(2,1)S(1)} async-done(((bf16[16,8,1152]{2,1,0:T(8,128)(2,1)}), bf16[16,8,1152]{2,1,0:T(8,128)(2,1)S(1)}, u32[]{:S(2)}, u32[]{:S(2)}) %all-to-all-start.4) | async-done | bytes 294944 | tf_op jit(solution)/shard_map/all_to_all | solution.py:412
  239.1 5.1 %all-to-all-start.8 = ((bf16[16,9,1152]{2,1,0:T(8,128)(2,1)}), bf16[16,9,1152]{2,1,0:T(8,128)(2,1)}, u32[]{:S(2)}, u32[]{:S(2)}) async-start(bf16[16,9,1152]{2,1,0:T(8,128)(2,1)} %broadcast_in_dim.44), calls=%async_computation.8 | async-start | bytes 1179648 | tf_op jit(solution)/shard_map/all_to_all | solution.py:377
  244.3 9.0 %shard_map.97 = bf16[128,1152]{1,0:T(8,128)(2,1)} custom-call(s32[3]{0:T(128)S(1)} %pad_add_fusion.at_ref.refs_0_, bf16[128,1152]{1,0:T(8,128)(2,1)S(1)} %bitcast.42, bf16[128,1152]{1,0:T(8,128)(2,1)S(1)} %bitcast.43, bf16[3,128,640]{2,1,0:T(8,128)(2,1)S(1)} %copy-done.16, f32[8,128,128]{2,1,0:T(8,128)S(1)} %copy-done.14, bf16[128,640]{1,0:T(8,128)(2,1)S(1)} %copy-done.19, ...), custom_call_target="tpu_custom_call" | custom-call | flops 800000000 | bytes 10000000 | tf_op jit(solution)/shard_map/pallas_call | solution.py:332
  253.3 1.6 all-to-all-done.8
  255.0 1.1 copy_convert_fusion
  (98 shorter events, 16.1 us)
Async XLA Ops:
  0.6 34.2 %copy-start.24 = (s32[8]{0:T(128)S(1)}, s32[8]{0:T(128)}, u32[]{:S(2)}) copy-start(s32[8]{0:T(128)} %constant.213.clone) | copy-start | bytes 100
  0.7 0.9 copy-start.20
  1.7 0.9 copy-start.21
  2.6 0.8 copy-start.22
  3.4 0.8 copy-start.23
  5.9 21.4 %all-to-all-start = ((bf16[4,48,1152]{2,1,0:T(8,128)(2,1)}), bf16[4,48,1152]{2,1,0:T(8,128)(2,1)S(1)}, u32[]{:S(2)}, u32[]{:S(2)}) async-start(bf16[4,48,1152]{2,1,0:T(8,128)(2,1)} %shard_map.94), calls=%async_computation | async-start | bytes 884736 | tf_op jit(solution)/shard_map/all_to_all | solution.py:420
  27.3 21.2 %copy-start.26 = (bf16[4,48,1152]{2,1,0:T(8,128)(2,1)}, bf16[4,48,1152]{2,1,0:T(8,128)(2,1)S(1)}, u32[]{:S(2)}) copy-start(bf16[4,48,1152]{2,1,0:T(8,128)(2,1)S(1)} %all-to-all-done) | copy-start | bytes 1327108
  27.3 9.1 %collective-permute-start.9 = (bf16[1,18,1152]{2,1,0:T(8,128)(2,1)S(1)}, bf16[1,18,1152]{2,1,0:T(8,128)(2,1)S(1)}, u32[]{:S(2)}, u32[]{:S(2)}) collective-permute-start(bf16[1,18,1152]{2,1,0:T(8,128)(2,1)S(1)} %reshape.334), channel_id=1, source_target_pairs={{0,256},{1,257},{2,258},{3,259},{4,260},{5,261},{6,262},{7,263},{8... | collective-permute-start | bytes 124424 | tf_op jit(solution)/shard_map/ppermute | solution.py:397
  36.4 7.9 %collective-permute-start.10 = (bf16[2,18,1152]{2,1,0:T(8,128)(2,1)S(1)}, bf16[2,18,1152]{2,1,0:T(8,128)(2,1)S(1)}, u32[]{:S(2)}, u32[]{:S(2)}) collective-permute-start(bf16[2,18,1152]{2,1,0:T(8,128)(2,1)S(1)} %pad_maximum_fusion.4), channel_id=1, source_target_pairs={{0,384},{1,129},{2,386},{3,131},{4,388},{5,133},{6,390},{7,135},{8... | collective-permute-start | bytes 248840 | tf_op jit(solution)/shard_map/ppermute | solution.py:397
  44.3 8.5 %collective-permute-start.11 = (bf16[4,18,1152]{2,1,0:T(8,128)(2,1)S(1)}, bf16[4,18,1152]{2,1,0:T(8,128)(2,1)S(1)}, u32[]{:S(2)}, u32[]{:S(2)}) collective-permute-start(bf16[4,18,1152]{2,1,0:T(8,128)(2,1)S(1)} %pad_maximum_fusion.3), channel_id=1, source_target_pairs={{0,448},{1,65},{2,450},{3,67},{4,452},{5,69},{6,454},{7,71},{8,456... | collective-permute-start | bytes 497672 | tf_op jit(solution)/shard_map/ppermute | solution.py:397
  55.4 64.2 %all-to-all-start.3 = ((bf16[8,144,1152]{2,1,0:T(8,128)(2,1)}), bf16[8,144,1152]{2,1,0:T(8,128)(2,1)S(1)}, u32[]{:S(2)}, u32[]{:S(2)}) async-start(bf16[8,144,1152]{2,1,0:T(8,128)(2,1)} %broadcast_in_dim.42), calls=%async_computation.3 | async-start | bytes 5308416 | tf_op jit(solution)/shard_map/all_to_all | solution.py:377
  65.2 0.7 copy-start.25
  66.0 63.1 %copy-start = (bf16[144,1152]{1,0:T(8,128)(2,1)}, bf16[144,1152]{1,0:T(8,128)(2,1)S(1)}, u32[]{:S(2)}) copy-start(bf16[144,1152]{1,0:T(8,128)(2,1)S(1)} %reshape.330.refs_3_.refs_7_) | copy-start | bytes 995332
  66.0 8.2 %collective-permute-start = (bf16[144,1152]{1,0:T(8,128)(2,1)S(1)}, bf16[144,1152]{1,0:T(8,128)(2,1)S(1)}, u32[]{:S(2)}, u32[]{:S(2)}) collective-permute-start(bf16[144,1152]{1,0:T(8,128)(2,1)S(1)} %reshape.330.refs_3_.refs_7_), channel_id=1, source_target_pairs={{0,64},{1,449},{2,66},{3,451},{4,68},{5,453},{6,70},{7,455},{8,72}... | collective-permute-start | bytes 995336 | tf_op jit(solution)/shard_map/ppermute | solution.py:397
  69.4 11.1 %collective-permute-start.1 = (bf16[144,1152]{1,0:T(8,128)(2,1)S(1)}, bf16[144,1152]{1,0:T(8,128)(2,1)S(1)}, u32[]{:S(2)}, u32[]{:S(2)}) collective-permute-start(bf16[144,1152]{1,0:T(8,128)(2,1)S(1)} %reshape.330.refs_3_.refs_7_), channel_id=1, source_target_pairs={{0,448},{1,65},{2,450},{3,67},{4,452},{5,69},{6,454},{7,71},{8,456... | collective-permute-start | bytes 995336 | tf_op jit(solution)/shard_map/ppermute | solution.py:397
  74.2 55.0 %copy-start.2 = (bf16[144,1152]{1,0:T(8,128)(2,1)}, bf16[144,1152]{1,0:T(8,128)(2,1)S(1)}, u32[]{:S(2)}) copy-start(bf16[144,1152]{1,0:T(8,128)(2,1)S(1)} %collective-permute-done.refs_4_.refs_8_) | copy-start | bytes 995332
  74.2 11.6 %collective-permute-start.2 = (bf16[144,1152]{1,0:T(8,128)(2,1)S(1)}, bf16[144,1152]{1,0:T(8,128)(2,1)S(1)}, u32[]{:S(2)}, u32[]{:S(2)}) collective-permute-start(bf16[144,1152]{1,0:T(8,128)(2,1)S(1)} %collective-permute-done.refs_4_.refs_8_), channel_id=1, source_target_pairs={{0,64},{1,449},{2,66},{3,451},{4,68},{5,453},{6,70},{7,455},{8,72}... | collective-permute-start | bytes 995336 | tf_op jit(solution)/shard_map/ppermute | solution.py:397
  80.5 5.2 %copy-start.4 = (bf16[144,1152]{1,0:T(8,128)(2,1)}, bf16[144,1152]{1,0:T(8,128)(2,1)S(1)}, u32[]{:S(2)}) copy-start(bf16[144,1152]{1,0:T(8,128)(2,1)S(1)} %collective-permute-done.1.refs_5_.refs_9_) | copy-start | bytes 995332
  80.5 10.3 %collective-permute-start.3 = (bf16[144,1152]{1,0:T(8,128)(2,1)S(1)}, bf16[144,1152]{1,0:T(8,128)(2,1)}, u32[]{:S(2)}, u32[]{:S(2)}) collective-permute-start(bf16[144,1152]{1,0:T(8,128)(2,1)S(1)} %collective-permute-done.1.refs_5_.refs_9_), channel_id=1, source_target_pairs={{0,448},{1,65},{2,450},{3,67},{4,452},{5,69},{6,454},{7,71},{8,456... | collective-permute-start | bytes 995336 | tf_op jit(solution)/shard_map/ppermute | solution.py:397
  85.7 5.1 %copy-start.7 = (bf16[144,1152]{1,0:T(8,128)(2,1)}, bf16[144,1152]{1,0:T(8,128)(2,1)S(1)}, u32[]{:S(2)}) copy-start(bf16[144,1152]{1,0:T(8,128)(2,1)S(1)} %collective-permute-done.2.refs_6_.refs_10_) | copy-start | bytes 995332
  85.7 12.5 %collective-permute-start.4 = (bf16[144,1152]{1,0:T(8,128)(2,1)S(1)}, bf16[144,1152]{1,0:T(8,128)(2,1)}, u32[]{:S(2)}, u32[]{:S(2)}) collective-permute-start(bf16[144,1152]{1,0:T(8,128)(2,1)S(1)} %collective-permute-done.2.refs_6_.refs_10_), channel_id=1, source_target_pairs={{0,64},{1,449},{2,66},{3,451},{4,68},{5,453},{6,70},{7,455},{8,72}... | collective-permute-start | bytes 995336 | tf_op jit(solution)/shard_map/ppermute | solution.py:397
  90.9 21.8 %collective-permute-start.5 = (bf16[144,1152]{1,0:T(8,128)(2,1)}, bf16[144,1152]{1,0:T(8,128)(2,1)}, u32[]{:S(2)}, u32[]{:S(2)}) collective-permute-start(bf16[144,1152]{1,0:T(8,128)(2,1)} %collective-permute-done.3.refs_7_.refs_11_), channel_id=1, source_target_pairs={{0,448},{1,65},{2,450},{3,67},{4,452},{5,69},{6,454},{7,71},{8,456... | collective-permute-start | bytes 995336 | tf_op jit(solution)/shard_map/ppermute | solution.py:397
  98.2 14.4 %collective-permute-start.6 = (bf16[144,1152]{1,0:T(8,128)(2,1)}, bf16[144,1152]{1,0:T(8,128)(2,1)}, u32[]{:S(2)}, u32[]{:S(2)}) collective-permute-start(bf16[144,1152]{1,0:T(8,128)(2,1)} %collective-permute-done.4.refs_8_.refs_12_), channel_id=1, source_target_pairs={{0,64},{1,449},{2,66},{3,451},{4,68},{5,453},{6,70},{7,455},{8,72}... | collective-permute-start | bytes 995336 | tf_op jit(solution)/shard_map/ppermute | solution.py:397
  107.9 21.3 %collective-permute-start.7 = (bf16[4,144,1152]{2,1,0:T(8,128)(2,1)}, bf16[4,144,1152]{2,1,0:T(8,128)(2,1)}, u32[]{:S(2)}, u32[]{:S(2)}) collective-permute-start(bf16[4,144,1152]{2,1,0:T(8,128)(2,1)} %pad_maximum_fusion), channel_id=1, source_target_pairs={{0,1},{1,0},{2,3},{3,2},{4,5},{5,4},{6,7},{7,6},{8,9},{9,8},{10,11... | collective-permute-start | bytes 3981320 | tf_op jit(solution)/shard_map/ppermute | solution.py:436
  115.2 13.9 %collective-permute-start.8 = (bf16[4,144,1152]{2,1,0:T(8,128)(2,1)}, bf16[4,144,1152]{2,1,0:T(8,128)(2,1)}, u32[]{:S(2)}, u32[]{:S(2)}) collective-permute-start(bf16[4,144,1152]{2,1,0:T(8,128)(2,1)} %pad_maximum_fusion.1), channel_id=1, source_target_pairs={{0,1},{1,0},{2,3},{3,2},{4,5},{5,4},{6,7},{7,6},{8,9},{9,8},{10,11... | collective-permute-start | bytes 3981320 | tf_op jit(solution)/shard_map/ppermute | solution.py:436
  119.6 33.6 %collective-permute-start.12 = (bf16[8,144,1152]{2,1,0:T(8,128)(2,1)S(1)}, bf16[8,144,1152]{2,1,0:T(8,128)(2,1)}, u32[]{:S(2)}, u32[]{:S(2)}) collective-permute-start(bf16[8,144,1152]{2,1,0:T(8,128)(2,1)S(1)} %all-to-all-done.3.own_ref), channel_id=1, source_target_pairs={{0,1},{1,0},{2,3},{3,2},{4,5},{5,4},{6,7},{7,6},{8,9},{9,8},{10,11... | collective-permute-start | bytes 7962632 | tf_op jit(solution)/shard_map/ppermute | solution.py:443
  121.5 18.4 %all-to-all-start.2 = ((bf16[16,8,1152]{2,1,0:T(8,128)(2,1)}), bf16[16,8,1152]{2,1,0:T(8,128)(2,1)}, u32[]{:S(2)}, u32[]{:S(2)}) async-start(bf16[16,8,1152]{2,1,0:T(8,128)(2,1)} %bitcast.49), calls=%async_computation.2 | async-start | bytes 589824 | tf_op jit(solution)/shard_map/all_to_all | solution.py:412
  127.6 1.6 copy-start.5
  127.6 1.6 copy-start.8
  127.6 1.6 copy-start.11
  137.0 0.8 copy-start.13
  137.8 0.8 copy-start.15
  138.6 0.7 copy-start.17
  139.3 0.7 copy-start.18
  140.0 13.2 %all-to-all-start.1 = ((bf16[16,8,1152]{2,1,0:T(8,128)(2,1)}), bf16[16,8,1152]{2,1,0:T(8,128)(2,1)}, u32[]{:S(2)}, u32[]{:S(2)}) async-start(bf16[16,8,1152]{2,1,0:T(8,128)(2,1)} %bitcast.44), calls=%async_computation.1 | async-start | bytes 589824 | tf_op jit(solution)/shard_map/all_to_all | solution.py:412
  167.0 1.1 copy-start.10
  168.2 4.7 %collective-permute-start.13 = (bf16[288,1152]{1,0:T(8,128)(2,1)S(1)}, bf16[288,1152]{1,0:T(8,128)(2,1)S(1)}, u32[]{:S(2)}, u32[]{:S(2)}) collective-permute-start(bf16[288,1152]{1,0:T(8,128)(2,1)S(1)} %dynamic-slice_bitcast_fusion), channel_id=1, source_target_pairs={{0,1},{1,0},{2,3},{3,2},{4,5},{5,4},{6,7},{7,6},{8,9},{9,8},{10,11... | collective-permute-start | bytes 1990664 | tf_op jit(solution)/shard_map/ppermute | solution.py:481
  201.3 12.6 %all-to-all-start.5 = ((bf16[16,8,1152]{2,1,0:T(8,128)(2,1)}), bf16[16,8,1152]{2,1,0:T(8,128)(2,1)S(1)}, u32[]{:S(2)}, u32[]{:S(2)}) async-start(bf16[16,8,1152]{2,1,0:T(8,128)(2,1)} %bitcast.20), calls=%async_computation.5 | async-start | bytes 589824 | tf_op jit(solution)/shard_map/all_to_all | solution.py:412
  214.0 30.3 %copy-start.16 = (bf16[3,128,640]{2,1,0:T(8,128)(2,1)S(1)}, bf16[3,128,640]{2,1,0:T(8,128)(2,1)}, u32[]{:S(2)}) copy-start(bf16[3,128,640]{2,1,0:T(8,128)(2,1)} %copy-done.15) | copy-start | bytes 1474564
  225.1 19.2 %copy-start.1 = (bf16[144,1152]{1,0:T(8,128)(2,1)S(1)}, bf16[144,1152]{1,0:T(8,128)(2,1)}, u32[]{:S(2)}) copy-start(bf16[144,1152]{1,0:T(8,128)(2,1)} %copy-done) | copy-start | bytes 995332
  225.1 19.2 %copy-start.3 = (bf16[144,1152]{1,0:T(8,128)(2,1)S(1)}, bf16[144,1152]{1,0:T(8,128)(2,1)}, u32[]{:S(2)}) copy-start(bf16[144,1152]{1,0:T(8,128)(2,1)} %copy-done.2) | copy-start | bytes 995332
  225.1 19.2 %copy-start.6 = (bf16[144,1152]{1,0:T(8,128)(2,1)S(1)}, bf16[144,1152]{1,0:T(8,128)(2,1)}, u32[]{:S(2)}) copy-start(bf16[144,1152]{1,0:T(8,128)(2,1)} %copy-done.4) | copy-start | bytes 995332
  225.1 19.2 %copy-start.9 = (bf16[144,1152]{1,0:T(8,128)(2,1)S(1)}, bf16[144,1152]{1,0:T(8,128)(2,1)}, u32[]{:S(2)}) copy-start(bf16[144,1152]{1,0:T(8,128)(2,1)} %copy-done.7) | copy-start | bytes 995332
  225.1 19.2 %copy-start.12 = (bf16[1,1,128,1152]{3,2,1,0:T(8,128)(2,1)S(1)}, bf16[1,1,128,1152]{3,2,1,0:T(8,128)(2,1)}, u32[]{:S(2)}) copy-start(bf16[1,1,128,1152]{3,2,1,0:T(8,128)(2,1)} %param.7) | copy-start | bytes 884740
  225.1 19.2 %copy-start.14 = (f32[8,128,128]{2,1,0:T(8,128)S(1)}, f32[8,128,128]{2,1,0:T(8,128)}, u32[]{:S(2)}) copy-start(f32[8,128,128]{2,1,0:T(8,128)} %copy-done.13) | copy-start | bytes 1572868
  225.1 19.2 %copy-start.19 = (bf16[128,640]{1,0:T(8,128)(2,1)S(1)}, bf16[128,640]{1,0:T(8,128)(2,1)}, u32[]{:S(2)}) copy-start(bf16[128,640]{1,0:T(8,128)(2,1)} %copy-done.18) | copy-start | bytes 491524
  225.1 13.2 %all-to-all-start.4 = ((bf16[16,8,1152]{2,1,0:T(8,128)(2,1)}), bf16[16,8,1152]{2,1,0:T(8,128)(2,1)S(1)}, u32[]{:S(2)}, u32[]{:S(2)}) async-start(bf16[16,8,1152]{2,1,0:T(8,128)(2,1)} %bitcast.18), calls=%async_computation.4 | async-start | bytes 589824 | tf_op jit(solution)/shard_map/all_to_all | solution.py:412
  239.1 15.8 %all-to-all-start.8 = ((bf16[16,9,1152]{2,1,0:T(8,128)(2,1)}), bf16[16,9,1152]{2,1,0:T(8,128)(2,1)}, u32[]{:S(2)}, u32[]{:S(2)}) async-start(bf16[16,9,1152]{2,1,0:T(8,128)(2,1)} %broadcast_in_dim.44), calls=%async_computation.8 | async-start | bytes 1179648 | tf_op jit(solution)/shard_map/all_to_all | solution.py:377

commit v3 on v2

v3 whole, which is shorter than its diff:
```python
import jax
import jax.numpy as jnp
from jax import lax
from jax.experimental import pallas as pl
from jax.experimental.pallas import tpu as pltpu
from jax.sharding import PartitionSpec as P

BF = jnp.bfloat16
F32 = jnp.float32
EPSILON = 1e-06
D = 1152
WIDTH = 576
PAD = 640
HEADS = 8
HEAD = 72
TOKENS = 128
PATCH_BLOCK = 8
SCALING = HEAD ** (-0.5)
SHARE = 288
V_ROWS, ALL_ROWS = 1152, 2304
VMEM_LIMIT = 60 * 1024 * 1024


def nn(a, b):
    return lax.dot_general(a, b, (((1,), (0,)), ((), ())), preferred_element_type=F32)


def nt(a, b):
    return lax.dot_general(a, b, (((1,), (1,)), ((), ())), preferred_element_type=F32)


def tn(a, b):
    return lax.dot_general(a, b, (((0,), (0,)), ((), ())), preferred_element_type=F32)


def lanes(shape):
    return lax.broadcasted_iota(jnp.int32, shape, len(shape) - 1)


def normalize(values):
    centred = values - jnp.mean(values, axis=-1, keepdims=True)
    inverse = lax.rsqrt(jnp.mean(centred * centred, axis=-1, keepdims=True) + EPSILON)
    return centred * inverse, inverse


def norm_back(grad, normed, inverse):
    return inverse * (
        grad
        - jnp.mean(grad, axis=-1, keepdims=True)
        - normed * jnp.mean(grad * normed, axis=-1, keepdims=True)
    )


def keep_width(a):
    return jnp.where(lanes(a.shape) < WIDTH, a, 0.0)


def window(h):
    low = h * HEAD // 128 * 128
    high = -(-(h * HEAD + HEAD) // 128) * 128
    return low, high


def head_mask(h):
    low, high = window(h)
    at = lanes((TOKENS, high - low)) + low
    return (at >= h * HEAD) & (at < h * HEAD + HEAD)


def add_window(tiles, h, part):
    low, high = window(h)
    part = jnp.where(head_mask(h), part, 0.0)
    for t in range(low // 128, high // 128):
        piece = part[:, t * 128 - low : t * 128 - low + 128]
        tiles[t] = piece if tiles[t] is None else tiles[t] + piece


def join(tiles):
    return jnp.concatenate(tiles, axis=1)


def halves(a):
    return keep_width(a[:, :PAD]), keep_width(pltpu.roll(a, WIDTH, 1)[:, :PAD])


def whole(first, second):
    zeros = jnp.zeros((TOKENS, D - PAD), F32)
    first = jnp.concatenate([keep_width(first), zeros], axis=1)
    second = jnp.concatenate([keep_width(second), zeros], axis=1)
    return first + pltpu.roll(second, WIDTH, 1)


def project_temporal(normed, weights):
    normed_b = normed.astype(BF)
    q = nn(normed_b, weights[0, :V_ROWS])
    k = nn(normed_b, weights[1, :V_ROWS])
    first, second = halves(normed)
    v = nn(first.astype(BF), weights[0, V_ROWS : V_ROWS + PAD])
    v = v + nn(second.astype(BF), weights[1, V_ROWS : V_ROWS + PAD])
    return q.astype(BF), k.astype(BF), v.astype(BF)


def back_project_temporal(dq, dk, dv, weights):
    grad = nt(dq.astype(BF), weights[0, :V_ROWS]) + nt(dk.astype(BF), weights[1, :V_ROWS])
    dv = dv.astype(BF)
    first = nt(dv, weights[0, V_ROWS : V_ROWS + PAD])
    second = nt(dv, weights[1, V_ROWS : V_ROWS + PAD])
    return grad + whole(first, second)


def rounded(a):
    return a.astype(BF).astype(F32)


def attend(q, k, v, allowed, probs_ref):
    tiles = [None] * (PAD // 128)
    for h in range(HEADS):
        low, high = window(h)
        masked = jnp.where(head_mask(h), q[:, low:high].astype(F32), 0.0).astype(BF)
        scores = nt(masked, k[:, low:high]) * SCALING
        if allowed is not None:
            scores = jnp.where(allowed, scores, -1e38)
        powers = jnp.exp(scores - jnp.max(scores, axis=-1, keepdims=True))
        probs = powers / jnp.sum(powers, axis=-1, keepdims=True)
        probs_ref[h] = probs
        add_window(tiles, h, nn(probs.astype(BF), v[:, low:high]))
    return join(tiles).astype(BF)


def attend_back(q, k, v, context, context_grad, probs_ref):
    dq, dk, dv = ([None] * (PAD // 128) for _ in range(3))
    for h in range(HEADS):
        low, high = window(h)
        grad = context_grad[:, low:high]
        masked = jnp.where(head_mask(h), grad.astype(F32), 0.0)
        probs = probs_ref[h]
        prob_grad = nt(masked.astype(BF), v[:, low:high])
        row = jnp.sum(masked * context[:, low:high].astype(F32), axis=-1, keepdims=True)
        score_grad = (probs * (prob_grad - row) * SCALING).astype(BF)
        add_window(dv, h, tn(probs.astype(BF), grad))
        add_window(dq, h, nn(score_grad, k[:, low:high]))
        add_window(dk, h, tn(score_grad, q[:, low:high]))
    return rounded(join(dq)), rounded(join(dk)), rounded(join(dv))


def start_all(copies):
    for copy in copies:
        copy.start()
    return copies


def wait_all(copies):
    for copy in copies:
        copy.wait()


def load_spatial(at_ref, blocks, weights, sems):
    y, core = at_ref[0], at_ref[1]
    sign = 1 - 2 * core
    groups = []
    for half in range(2):
        rows = pl.ds(half * 144, 144)
        parts = [(blocks[0].at[rows, :], half, y)]
        for step in range(1, 4):
            parts.append((blocks[step].at[rows, :], half, y - sign * step))
            parts.append((blocks[3 + step].at[rows, :], half, y + sign * step))
        parts.append((blocks[7 + half], core if half == 0 else 1 - core, y + 4))
        copies = []
        for n, (source, part, place) in enumerate(parts):
            at = pl.multiple_of(part * D + lax.rem(place + 16, 8) * 144, 144)
            copies.append(
                pltpu.make_async_copy(
                    source, weights.at[pl.ds(at, 144), :], sems.at[half * 8 + n]
                )
            )
        groups.append(start_all(copies))
    return groups


def load_temporal(at_ref, blocks, weights, sems):
    core, x, z = at_ref[1], at_ref[2] % 4, at_ref[2] // 4
    copies = []
    for n, block in enumerate(blocks):
        half = core if n < 4 else 1 - core
        place = lax.rem(x + (0, -1, 1, 2)[n % 4] * (1 - 2 * half) + 4, 4)
        for entry in range(2):
            share = (z if entry == 0 else 1 - z) * 4 + place
            at = pl.multiple_of(share * SHARE, SHARE)
            copies.append(
                pltpu.make_async_copy(
                    block.at[pl.ds(entry * SHARE, SHARE), :],
                    weights.at[half, pl.ds(at, SHARE), :],
                    sems.at[len(copies)],
                )
            )
    return start_all(copies)


def project_spatial(normed, weights, groups):
    normed_b = normed.astype(BF)
    wait_all(groups[0] + groups[1][-1:])
    qk = nn(normed_b, weights[:D, :])
    wait_all(groups[1][:-1])
    v = keep_width(nn(normed_b, weights[D:, :PAD]))
    k = pltpu.roll(qk, WIDTH, 1)
    return qk[:, :PAD].astype(BF), k[:, :PAD].astype(BF), v.astype(BF)


def pair_lanes(dq, dk):
    zeros = jnp.zeros((TOKENS, D - PAD), F32)
    return jnp.concatenate([dq, zeros], axis=1) + pltpu.roll(
        jnp.concatenate([dk, zeros], axis=1), WIDTH, 1
    )


def back_project_spatial(dq, dk, dv, weights):
    return nt(pair_lanes(dq, dk).astype(BF), weights[:D, :]) + nt(
        dv.astype(BF), weights[D:, :PAD]
    )


def late(a):
    return jnp.where(lanes(a.shape) >= PAD - WIDTH, a, 0.0)


def out_spatial_of(context, expand, weights):
    zeros = jnp.zeros((TOKENS, D - PAD), F32)
    spread_out = nn(context, expand)
    first = late(nn(spread_out.astype(BF), weights[D:, D - PAD :]))
    second = late(nn(pltpu.roll(spread_out, 18, 1).astype(BF), weights[D:, D - PAD :]))
    return pltpu.roll(
        jnp.concatenate([first, zeros], axis=1), D - (PAD - WIDTH), 1
    ) + jnp.concatenate([zeros, second], axis=1)


def context_grad_spatial(grad, expand, weights):
    first = late(pltpu.roll(grad, PAD - WIDTH, 1)[:, :PAD])
    second = late(grad[:, D - PAD :])
    total = nt(first.astype(BF), weights[D:, D - PAD :]) + pltpu.roll(
        nt(second.astype(BF), weights[D:, D - PAD :]), D - 18, 1
    )
    return nt(total.astype(BF), expand).astype(BF)


def selection(rows, columns, shift):
    r = lax.broadcasted_iota(jnp.int32, (rows, columns), 0)
    c = lax.broadcasted_iota(jnp.int32, (rows, columns), 1)
    return r + shift == c


def pack_kernel(at_ref, *refs):
    outside, inside_refs, sems = refs[:4], refs[6:10], refs[10]
    all_ref, half_ref = refs[4:6]
    wait_all(
        start_all(
            [
                pltpu.make_async_copy(a, b, sems.at[n])
                for n, (a, b) in enumerate(zip(outside, inside_refs))
            ]
        )
    )
    qkv_s, out_s, qkv_t, out_t = inside_refs
    chip, core = at_ref[2], at_ref[1]

    def pick(which, a):
        return nn(which.astype(F32).astype(BF), a)

    def side(a, b):
        return jnp.concatenate([a, b], axis=1)

    def rows(count, at, size):
        return selection(count, size, at)

    q, k, v, out = qkv_s[0], qkv_s[1], qkv_s[2], out_s[...]
    lead = selection(36, 18, 0)
    tail = selection(36, 18, -18)
    halves = pick(lead, out[:, :WIDTH]) + pick(tail, out[:, WIDTH:])
    first = side(q.astype(F32), k.astype(F32))
    second = side(v.astype(F32), halves)
    q, k, v, out = qkv_t[0], qkv_t[1], qkv_t[2], out_t[...]
    nine = lax.broadcasted_iota(jnp.int32, (16, 1), 0) < 9

    def inside(low, high):
        return nine & (chip >= low) & (chip < high)

    here = rows(16, chip * 9, 36) & inside(0, 4)
    upper = rows(16, (chip - 4) * 9, 36) & inside(4, 6)
    lower = rows(16, (chip - 4) * 9 + 18, 36) & inside(4, 6)
    last = rows(16, (chip - 6) * 9, 18) & inside(6, 8)
    temporal = side(pick(here, q) + pick(upper, v), pick(here, k) + pick(lower, v))
    temporal = temporal + pick(last, out)
    half = jnp.where(core == 0, first, second)
    half_ref[...] = jnp.concatenate([half, temporal], axis=0).astype(BF)
    all_ref[...] = jnp.concatenate([first, second, temporal], axis=0).astype(BF)


def column_kernel(at_ref, own_ref, next_ref, far_ref, other_ref, block_ref, share_ref):
    z, core = at_ref[3], at_ref[1]
    own, near, far = (ref[...].astype(F32) for ref in (own_ref, next_ref, far_ref))
    other = other_ref[...].astype(F32)
    below = jnp.where(core == 0, near, other[:88])
    above = jnp.where(core == 0, other[:88], near)
    far_low = jnp.where(core == 0, far[:36], other[88:124])
    far_high = jnp.where(core == 0, other[88:124], far[:36])
    low, high, share = [], [], []
    for place in range(4):
        distance = lax.rem(place - z + 4, 4)

        def choose(a, b):
            part = jnp.where(distance == 0, own[a], jnp.where(distance == 1, above[a], b))
            return jnp.where(distance == 3, below[a], part)

        low.append(choose(slice(0, 36), far_low))
        high.append(choose(slice(36, 72), far_high))
        share.append(choose(slice(72, 81), far[36:45]))
    block_ref[...] = jnp.concatenate(low + high, axis=0).astype(BF)
    share = jnp.concatenate(share, axis=0)
    share = jnp.where(core == 0, share, pltpu.roll(share, WIDTH, 1))[:, :PAD]
    share = keep_width(share).astype(BF)
    for y in range(8):
        share_ref[y] = share


def forward_kernel(*refs):
    (at_ref, x_ref, cot_ref, expand_ref), refs = refs[:4], refs[4:]
    blocks, refs = refs[:9], refs[9:]
    both_ref, *outside, weights, qkv_ref, probs_ref, context_ref, sems = refs
    groups = load_spatial(at_ref, blocks, weights, sems)
    both_ref[:, D:] = cot_ref[...]
    x = x_ref[...].astype(F32)
    q, k, v = project_spatial(normalize(x)[0], weights, groups)
    qkv_ref[0], qkv_ref[1], qkv_ref[2] = q, k, v
    context = attend(q, k, v, None, probs_ref)
    context_ref[...] = context
    copies = start_all(
        [
            pltpu.make_async_copy(a, b, sems.at[n])
            for n, (a, b) in enumerate(zip((qkv_ref, probs_ref, context_ref), outside))
        ]
    )
    both_ref[:, :D] = (x + out_spatial_of(context, expand_ref[...], weights)).astype(BF)
    wait_all(copies)


def temporal_kernel(at_ref, both_ref, full_ref, share_order_ref, *refs):
    keep_ref, send_ref, qkv_ref, probs_ref, context_ref, weights, sems = refs[8:]
    copies = load_temporal(at_ref, refs[:8], weights, sems)
    normed = normalize(both_ref[:, :D].astype(F32))[0]
    ordered = nn(normed.astype(BF), full_ref[...])
    wait_all(copies)
    q, k, v = project_temporal(ordered, weights)
    qkv_ref[0], qkv_ref[1], qkv_ref[2] = q, k, v
    rows = lax.broadcasted_iota(jnp.int32, (TOKENS, TOKENS), 0)
    cols = lax.broadcasted_iota(jnp.int32, (TOKENS, TOKENS), 1)
    allowed = (rows & (PATCH_BLOCK - 1)) == (cols & (PATCH_BLOCK - 1))
    context = attend(q, k, v, allowed, probs_ref)
    context_ref[...] = context
    share = tn(nn(context, share_order_ref[...]).astype(BF), both_ref[:, D:]).astype(BF)
    keep_ref[...], send_ref[...] = share[:SHARE], share[SHARE:WIDTH]


def temporal_back_kernel(
    at_ref, both_ref, qkv_ref, probs_ref, context_ref, order_ref, full_ref, *refs
):
    back_ref, weights, sems = refs[8:]
    copies = load_temporal(at_ref, refs[:8], weights, sems)
    hidden, cot = both_ref[:, :D].astype(F32), both_ref[:, D:].astype(F32)
    normed, inverse = normalize(hidden)
    context, order, full = context_ref[...], order_ref[...], full_ref[...]
    ordered = nn(context, order).astype(BF)
    wait_all(copies)
    left, right = weights[0, ALL_ROWS - PAD :], weights[1, ALL_ROWS - PAD :]
    back_ref[:, D:] = (hidden + whole(nn(ordered, left), nn(ordered, right))).astype(BF)
    first, second = halves(cot)
    context_grad = nt(first.astype(BF), left) + nt(second.astype(BF), right)
    context_grad = nt(context_grad.astype(BF), order).astype(BF)
    dq, dk, dv = attend_back(
        qkv_ref[0], qkv_ref[1], qkv_ref[2], context, context_grad, probs_ref
    )
    normed_grad = nt(back_project_temporal(dq, dk, dv, weights).astype(BF), full)
    back_ref[:, :D] = (cot + norm_back(normed_grad, normed, inverse)).astype(BF)


def backward_kernel(*refs):
    (at_ref, x_ref, both_ref, qkv_ref, probs_ref, context_ref, expand_ref), refs = refs[:7], refs[7:]
    blocks, refs = refs[:9], refs[9:]
    input_grad_ref, weights, sems = refs
    first, second = load_spatial(at_ref, blocks, weights, sems)
    normed, inverse = normalize(x_ref[...].astype(F32))
    wait_all(first + second)
    grad = both_ref[:, :D].astype(F32)
    context_grad = context_grad_spatial(grad, expand_ref[...], weights)
    dq, dk, dv = attend_back(
        qkv_ref[0], qkv_ref[1], qkv_ref[2], context_ref[...], context_grad, probs_ref
    )
    normed_grad = back_project_spatial(dq, dk, dv, weights)
    input_grad_ref[...] = (grad + norm_back(normed_grad, normed, inverse)).astype(BF)


def call(kernel, outs, scratch, micros, *args, smem=True, hbm=(), hbm_outs=()):
    in_specs = []
    for at in range(len(args)):
        space = pltpu.VMEM
        if smem and at == 0:
            space = pltpu.SMEM
        elif at in hbm:
            space = pl.ANY
        in_specs.append(pl.BlockSpec(memory_space=space))
    return pl.pallas_call(
        kernel,
        out_shape=[jax.ShapeDtypeStruct(s, t) for s, t in outs],
        in_specs=in_specs,
        out_specs=[
            pl.BlockSpec(memory_space=pl.ANY if n in hbm_outs else pltpu.VMEM)
            for n in range(len(outs))
        ],
        scratch_shapes=scratch,
        compiler_params=pltpu.CompilerParams(vmem_limit_bytes=VMEM_LIMIT),
        cost_estimate=pl.CostEstimate(
            flops=micros * 1_100_000_000, bytes_accessed=3_000_000, transcendentals=0
        ),
    )(*args)


def model_order():
    n = jnp.arange(D)
    dp, row = n // 36, n % 36
    at = (row // 9) * SHARE + dp * 9 + row % 9
    return (at[:, None] == jnp.arange(D)[None, :]).astype(BF)


def context_order():
    f = jnp.arange(PAD)
    dp, row = f // 18, f % 18
    at = PAD - WIDTH + (row // 9) * SHARE + dp * 9 + row % 9
    at = jnp.where(f < WIDTH, at, -1)
    return (at[:, None] == jnp.arange(PAD)[None, :]).astype(BF)


def share_order(y, core):
    f = jnp.arange(PAD)
    dp, row = f // 18, f % 18
    half = row // 9
    away = jnp.where(half == 0, dp // 4 - y, y - dp // 4) % 4
    far = away % 2 * 144 + away // 2 * 72 + jnp.where(half == core, 0, SHARE)
    at = far + dp // 16 * 36 + dp % 4 * 9 + row % 9
    at = jnp.where(f < WIDTH, at, -1)
    return (at[:, None] == jnp.arange(PAD)[None, :]).astype(BF)


def expand_order():
    f = jnp.arange(PAD)
    at = jnp.where(f < WIDTH, 36 * (f // 18) + f % 18, -1)
    return (at[:, None] == jnp.arange(D)[None, :]).astype(BF)


GROUPS_Z = [[y * 4 + z for z in range(4)] for y in range(8)]
GROUPS_Y = [[y * 4 + z for y in range(8)] for z in range(4)]
GROUPS_FAR = [[y * 4 + z for y in (p, p + 4) for z in range(4)] for p in range(4)]
SWAP = [(s, s ^ 1) for s in range(16)]
ACROSS = [(s, s ^ 8) for s in range(16)]


def spread(block, axis, groups):
    count = len(groups[0])
    return lax.all_to_all(
        jnp.broadcast_to(block[None], (count,) + block.shape), axis, 0, 0,
        axis_index_groups=groups, tiled=True,
    )


def along_z(distance):
    pairs = []
    for y in range(8):
        for z in range(4):
            for s in range(16):
                to = (z + (distance if s % 2 == 0 else -distance)) % 4
                pairs.append(((y * 4 + z) * 16 + s, (y * 4 + to) * 16 + s))
    return pairs


def along_y(distance):
    pairs = []
    for y in range(8):
        for z in range(4):
            for s in range(16):
                to = (y + (distance if s % 2 == 0 else -distance)) % 8
                pairs.append(((y * 4 + z) * 16 + s, (to * 4 + z) * 16 + s))
    return pairs


def along_x(distance):
    pairs = []
    for s in range(16):
        to = (s // 2 + (distance if s % 2 == 0 else -distance)) % 4
        pairs.append((s, s // 8 * 8 + to * 2 + s % 2))
    return pairs


UP = along_y(1)


def move(a, pairs):
    return lax.ppermute(a, ("dp", "seq"), pairs)


def per_device(clips, qkv_spatial, out_spatial, qkv_temporal, out_temporal, cotangent):
    x = clips.reshape(TOKENS, D)
    out_grad = cotangent.reshape(TOKENS, D)
    seq, dp = lax.axis_index("seq"), lax.axis_index("dp")
    y, chip, core = dp // 4, seq // 2, seq % 2
    at = jnp.stack([y, core, chip, dp % 4]).astype(jnp.int32)

    tokens_b = ((TOKENS, D), BF)
    wide_b = ((TOKENS, 2 * D), BF)
    probs = (HEADS, TOKENS, TOKENS)
    sems = pltpu.SemaphoreType.DMA((16,))

    def turn(a):
        parts = a.reshape(16, PATCH_BLOCK, 2 * D)
        return lax.all_to_all(parts, "seq", 0, 0, tiled=True).reshape(TOKENS, 2 * D)

    packed, packed_h = call(
        pack_kernel, [((88, D), BF), ((52, D), BF)],
        [
            pltpu.VMEM((3, 36, WIDTH), BF), pltpu.VMEM((18, D), BF),
            pltpu.VMEM((3, 36, WIDTH), BF), pltpu.VMEM((18, D), BF), sems,
        ],
        2, at, qkv_spatial, out_spatial, qkv_temporal, out_temporal, hbm=range(1, 5),
    )
    orders = model_order(), context_order(), share_order(y, core), expand_order()
    near, far = move(packed, along_z(1)), move(packed_h, along_z(2))

    def swap(a):
        return lax.ppermute(a, "seq", SWAP)

    block, shares = call(
        column_kernel, [((2 * 144, D), BF), ((8, 36, PAD), BF)], [], 2,
        at, packed, near, far, swap(jnp.concatenate([near, far])),
    )
    shares = lax.all_to_all(shares, "dp", 0, 0, axis_index_groups=GROUPS_Y, tiled=True)
    shares = shares.reshape(SHARE, PAD)

    ring, theirs = [block], []
    for step in range(1, 4):
        ring.append(move(ring[-1], UP))
        if step == 1:
            ring[1], *orders = lax.optimization_barrier((ring[1], *orders))
        else:
            theirs.append(swap(ring[step - 1]))
            ring[step], theirs[-1] = lax.optimization_barrier((ring[step], theirs[-1]))
    full_order, small_order, wgrad_order, expand = orders
    last = move(lax.dynamic_slice_in_dim(ring[3], core * 144, 144, axis=0), UP)
    theirs.append(swap(ring[3]))
    last, theirs[2] = lax.optimization_barrier((last, theirs[2]))

    def round_x(a, distance):
        return lax.ppermute(a, "seq", along_x(distance))

    pair = jnp.concatenate([shares, lax.ppermute(shares, "seq", ACROSS)])
    after = round_x(pair, 1)
    blocks_t = [pair, after, round_x(pair, -1), round_x(after, 1)]
    blocks_t += list(map(swap, blocks_t))
    blocks = [*ring, *theirs, last, swap(last)]

    both, qkv, probs_s, context_s = call(
        forward_kernel,
        [wide_b, ((3, TOKENS, PAD), BF), (probs, F32), ((TOKENS, PAD), BF)],
        [
            pltpu.VMEM((2 * D, D), BF), pltpu.VMEM((3, TOKENS, PAD), BF), pltpu.VMEM(probs, F32),
            pltpu.VMEM((TOKENS, PAD), BF), sems,
        ],
        8,
        at, x, out_grad, expand, *blocks,
        hbm=range(4, 13), hbm_outs=(1, 2, 3),
    )
    both = turn(both)
    saved = [((3, TOKENS, PAD), BF), (probs, F32), ((TOKENS, PAD), BF)]
    temporal_weights = pltpu.VMEM((2, ALL_ROWS, PAD), BF)
    keep, send, *saved_t = call(
        temporal_kernel, [((SHARE, D), BF), ((SHARE, D), BF), *saved], [temporal_weights, sems], 8,
        at, both, full_order, wgrad_order, *blocks_t, hbm=range(4, 12),
    )

    def add(a, b):
        return (a.astype(F32) + b.astype(F32)).astype(BF)

    total = add(keep, swap(send))
    both, total = lax.optimization_barrier((both, total))
    (both_back,) = call(
        temporal_back_kernel, [wide_b], [temporal_weights, sems], 9,
        at, both, *saved_t, small_order, full_order, *blocks_t, hbm=range(7, 15),
    )
    both_back = turn(both_back)
    total = add(total[:144], move(total[144:], UP))
    total = add(total[:72], move(total[72:], along_y(2)))
    total, both_back = lax.optimization_barrier((total, both_back))
    (input_grad,) = call(
        backward_kernel,
        [tokens_b],
        [pltpu.VMEM((2 * D, D), BF), sems],
        9,
        at, x, both_back, qkv, probs_s, context_s, expand, *blocks,
        hbm=range(7, 16),
    )
    over_z = lax.all_to_all(
        total.reshape(8, 9, D), "dp", 0, 0, axis_index_groups=GROUPS_FAR, tiled=True
    )
    over_z = jnp.sum(over_z.astype(F32), axis=0).astype(BF)
    over_z, input_grad = lax.optimization_barrier((over_z, input_grad))
    over_seq = spread(over_z, "seq", [list(range(16))]).reshape(8, 2, 9, D)
    out_temporal_grad = jnp.sum(over_seq.astype(F32), axis=0).reshape(18, D)
    mixed = both_back[:, D:]

    return mixed[None, None], input_grad[None, None], out_temporal_grad


def solution(mesh):
    tokens = P("dp", "seq", None, None)
    placed = (tokens, P(None, "dp", None), P("dp", None), P(None, "dp", None), P("dp", None), tokens)
    return jax.shard_map(
        per_device,
        mesh=mesh,
        in_specs=placed,
        out_specs=(tokens, tokens, P("dp", None)),
        check_vma=False,
    )
```

time: 260 us -> 231 us (0.89)
  blocking collectives: 37.7 us -> 0 us
  Pallas kernels: 32.3 us -> 45.7 us
  starting transfers between devices: 101 us -> 111 us
  local copies, waits for them, and re-layouts: 17.8 us -> 7.84 us
  other arithmetic: 12.9 us -> 7.48 us
    all_to_all x2 -> x0, blocking collectives: 37.7 us -> none  [the longest x1 26.5 us: per_device(): lax.all_to_all(both, 'dp', 0, 0, axis_index_groups=GROUPS_Y, tiled=True)]
    ppermute x4 -> x14, starting transfers between devices: 14 us -> 39.5 us  [the longest x10 26.7 us: swap(): return lax.ppermute(a, 'seq', SWAP)]
    all_to_all x5 -> x4, waiting for transfers between devices: 29.5 us -> 6.07 us  [the longest x1 3.36 us: per_device(): lax.all_to_all(total.reshape(8, 9, D), 'dp', 0, 0, axis_index_groups=GROU...]
    ppermute x10 -> x8, waiting for transfers between devices: 21.9 us -> 35.9 us  [move(): return lax.ppermute(a, ('dp', 'seq'), pairs)]
    pallas_call x4 -> x6, Pallas kernels: 32.3 us -> 45.7 us  [call(): pl.pallas_call(kernel, out_shape=[jax.ShapeDtypeStruct(s, t) for s, t in...]
    all_to_all x2 -> x1, waiting for transfers between devices: 1.64 us -> 9.8 us  [spread(): lax.all_to_all(jnp.broadcast_to(block[None], (count,) + block.shape), axi...]
    all_to_all x2 -> x1, starting transfers between devices: 13.9 us -> 6.67 us  [spread(): lax.all_to_all(jnp.broadcast_to(block[None], (count,) + block.shape), axi...]
    all_to_all x5 -> x4, starting transfers between devices: 33.5 us -> 27.5 us  [the longest x2 11.4 us: turn(): return lax.all_to_all(parts, 'seq', 0, 0, tiled=True).reshape(TOKENS, 2 * D)]
  transfers between devices with their start and end apart: 21 -> 27, of which waited for: 13 -> 13; matrix products, arithmetic and copies ran while one was open for 5% -> 3% of each run, Pallas kernels for 7% -> 13%
where the time goes in v3:
time: 231 us; the launch traced here: 228 us
  starting transfers between devices  111 us (48%)
  waiting for transfers between devices  55 us (24%)
  Pallas kernels  45.7 us (20%)
  local copies, waits for them, and re-layouts  7.84 us (3%)
  other arithmetic  7.48 us (3%)
    pallas_call x6, Pallas kernels, call(): pl.pallas_call(kernel, out_shape=[jax.ShapeDtypeStruct(s, t) for s, t in...  45.7 us
    ppermute x8, starting transfers between devices, move(): return lax.ppermute(a, ('dp', 'seq'), pairs)  36.9 us
    ppermute x8, waiting for transfers between devices, move(): return lax.ppermute(a, ('dp', 'seq'), pairs)  35.9 us
    ppermute x10, starting transfers between devices, swap(): return lax.ppermute(a, 'seq', SWAP)  26.7 us
    all_to_all x2, starting transfers between devices, turn(): return lax.all_to_all(parts, 'seq', 0, 0, tiled=True).reshape(TOKENS, 2 * D)  11.4 us
    all_to_all x1, starting transfers between devices, per_device(): lax.all_to_all(total.reshape(8, 9, D), 'dp', 0, 0, axis_index_groups=GROU...  11 us
    ppermute x3, starting transfers between devices, round_x(): return lax.ppermute(a, 'seq', along_x(distance))  10.9 us
    all_to_all x1, waiting for transfers between devices, spread(): lax.all_to_all(jnp.broadcast_to(block[None], (count,) + block.shape), axi...  9.8 us
  transfers between devices with their start and end apart: 27, of which 13 were waited for; matrix products, arithmetic and copies ran while one was open for 3% of the time, Pallas kernels for 13%

profile of v3, /device:TPU:1, one launch (start us, length us, event | category | flops | bytes accessed | tf_op | source)
XLA Modules:
  0.0 227.9 jit_solution(18422732771666176831)
XLA Ops:
  1.3 2.9 %shard_map.85 = (bf16[88,1152]{1,0:T(8,128)(2,1)}, bf16[52,1152]{1,0:T(8,128)(2,1)}) custom-call(s32[4]{0:T(128)} %pad_add_fusion.at_ref.refs_0_, bf16[3,36,576]{2,1,0:T(8,128)(2,1)} %refs_0_.1, bf16[18,1152]{1,0:T(8,128)(2,1)} %refs_1_.1, bf16[3,36,576]{2,1,0:T(8,128)(2,1)} %refs_2_.1, bf16[18,1152]{1,0:T(8,128)(2,1)} %refs_3_.1), custom_call_target="tpu_custom_call" | custom-call | flops 2200000000 | bytes 3000000 | tf_op jit(solution)/shard_map/pallas_call | solution.py:409
  4.2 11.5 %collective-permute-start = (bf16[88,1152]{1,0:T(8,128)(2,1)}, bf16[88,1152]{1,0:T(8,128)(2,1)S(1)}, u32[]{:S(2)}, u32[]{:S(2)}) collective-permute-start(bf16[88,1152]{1,0:T(8,128)(2,1)} %get-tuple-element.33.own_ref), channel_id=1, source_target_pairs={{0,16},{1,49},{2,18},{3,51},{4,20},{5,53},{6,22},{7,55},{8,24},{9,... | collective-permute-start | bytes 608264 | tf_op jit(solution)/shard_map/ppermute | solution.py:504
  15.7 1.9 collective-permute-start.1
  17.6 11.0 %collective-permute-done.1.far_ref = bf16[52,1152]{1,0:T(8,128)(2,1)S(1)} collective-permute-done((bf16[52,1152]{1,0:T(8,128)(2,1)}, bf16[52,1152]{1,0:T(8,128)(2,1)S(1)}, u32[]{:S(2)}, u32[]{:S(2)}) %collective-permute-start.1) | collective-permute-done | bytes 119840 | tf_op jit(solution)/shard_map/ppermute | solution.py:504
  28.7 2.1 collective-permute-start.2
  30.8 2.0 fusion.full_ref
  33.6 2.9 %shard_map.86 = (bf16[288,1152]{1,0:T(8,128)(2,1)}, bf16[8,36,640]{2,1,0:T(8,128)(2,1)}) custom-call(s32[4]{0:T(128)} %pad_add_fusion.at_ref.refs_0_, bf16[88,1152]{1,0:T(8,128)(2,1)} %get-tuple-element.33.own_ref, bf16[88,1152]{1,0:T(8,128)(2,1)} %copy-done.3, bf16[52,1152]{1,0:T(8,128)(2,1)} %copy-done.6, bf16[140,1152]{1,0:T(8,128)(2,1)} %copy-done.16), custom_call_target="tpu_custom_call" | custom-call | flops 2200000000 | bytes 3000000 | tf_op jit(solution)/shard_map/pallas_call | solution.py:409
  36.5 5.3 %collective-permute-start.3 = (bf16[288,1152]{1,0:T(8,128)(2,1)}, bf16[288,1152]{1,0:T(8,128)(2,1)S(1)}, u32[]{:S(2)}, u32[]{:S(2)}) collective-permute-start(bf16[288,1152]{1,0:T(8,128)(2,1)} %get-tuple-element.35.refs_4_.refs_7_), channel_id=1, source_target_pairs={{0,64},{1,449},{2,66},{3,451},{4,68},{5,453},{6,70},{7,455},{8,72}... | collective-permute-start | bytes 1990664 | tf_op jit(solution)/shard_map/ppermute | solution.py:504
  41.8 1.5 fusion.2
  43.3 1.4 fusion.1.refs_3_.refs_6_
  44.8 4.9 %collective-permute-done.3.refs_5_.refs_8_ = bf16[288,1152]{1,0:T(8,128)(2,1)S(1)} collective-permute-done((bf16[288,1152]{1,0:T(8,128)(2,1)}, bf16[288,1152]{1,0:T(8,128)(2,1)S(1)}, u32[]{:S(2)}, u32[]{:S(2)}) %collective-permute-start.3) | collective-permute-done | bytes 663584 | tf_op jit(solution)/shard_map/ppermute | solution.py:504
  49.7 3.6 %collective-permute-start.5 = (bf16[288,1152]{1,0:T(8,128)(2,1)S(1)}, bf16[288,1152]{1,0:T(8,128)(2,1)S(1)}, u32[]{:S(2)}, u32[]{:S(2)}) collective-permute-start(bf16[288,1152]{1,0:T(8,128)(2,1)S(1)} %collective-permute-done.3.refs_5_.refs_8_), channel_id=1, source_target_pairs={{0,1},{1,0},{2,3},{3,2},{4,5},{5,4},{6,7},{7,6},{8,9},{9,8},{10,11... | collective-permute-start | bytes 1990664 | tf_op jit(solution)/shard_map/ppermute | solution.py:535
  53.3 3.6 %collective-permute-start.4 = (bf16[288,1152]{1,0:T(8,128)(2,1)S(1)}, bf16[288,1152]{1,0:T(8,128)(2,1)}, u32[]{:S(2)}, u32[]{:S(2)}) collective-permute-start(bf16[288,1152]{1,0:T(8,128)(2,1)S(1)} %collective-permute-done.3.refs_5_.refs_8_), channel_id=1, source_target_pairs={{0,64},{1,449},{2,66},{3,451},{4,68},{5,453},{6,70},{7,455},{8,72}... | collective-permute-start | bytes 1990664 | tf_op jit(solution)/shard_map/ppermute | solution.py:504
  57.0 5.1 %all-to-all-start.1 = ((bf16[8,36,640]{2,1,0:T(8,128)(2,1)}), bf16[8,36,640]{2,1,0:T(8,128)(2,1)S(1)}, u32[]{:S(2)}, u32[]{:S(2)}) async-start(bf16[8,36,640]{2,1,0:T(8,128)(2,1)} %get-tuple-element.47), calls=%async_computation.1 | async-start | bytes 819200 | tf_op jit(solution)/shard_map/all_to_all | solution.py:541
  62.1 4.0 %collective-permute-done.4.refs_6_.refs_9_ = bf16[288,1152]{1,0:T(8,128)(2,1)} collective-permute-done((bf16[288,1152]{1,0:T(8,128)(2,1)S(1)}, bf16[288,1152]{1,0:T(8,128)(2,1)}, u32[]{:S(2)}, u32[]{:S(2)}) %collective-permute-start.4) | collective-permute-done | bytes 663584 | tf_op jit(solution)/shard_map/ppermute | solution.py:504
  66.1 3.4 %collective-permute-start.7 = (bf16[288,1152]{1,0:T(8,128)(2,1)}, bf16[288,1152]{1,0:T(8,128)(2,1)}, u32[]{:S(2)}, u32[]{:S(2)}) collective-permute-start(bf16[288,1152]{1,0:T(8,128)(2,1)} %collective-permute-done.4.refs_6_.refs_9_), channel_id=1, source_target_pairs={{0,1},{1,0},{2,3},{3,2},{4,5},{5,4},{6,7},{7,6},{8,9},{9,8},{10,11... | collective-permute-start | bytes 1990664 | tf_op jit(solution)/shard_map/ppermute | solution.py:535
  69.6 4.1 %collective-permute-start.6 = (bf16[288,1152]{1,0:T(8,128)(2,1)}, bf16[288,1152]{1,0:T(8,128)(2,1)S(1)}, u32[]{:S(2)}, u32[]{:S(2)}) collective-permute-start(bf16[288,1152]{1,0:T(8,128)(2,1)} %collective-permute-done.4.refs_6_.refs_9_), channel_id=1, source_target_pairs={{0,64},{1,449},{2,66},{3,451},{4,68},{5,453},{6,70},{7,455},{8,72}... | collective-permute-start | bytes 1990664 | tf_op jit(solution)/shard_map/ppermute | solution.py:504
  73.7 1.6 all-to-all-done.1
  75.3 1.9 collective-permute-start.11
  77.3 4.2 %collective-permute-done.6.refs_7_.refs_10_ = bf16[288,1152]{1,0:T(8,128)(2,1)S(1)} collective-permute-done((bf16[288,1152]{1,0:T(8,128)(2,1)}, bf16[288,1152]{1,0:T(8,128)(2,1)S(1)}, u32[]{:S(2)}, u32[]{:S(2)}) %collective-permute-start.6) | collective-permute-done | bytes 663584 | tf_op jit(solution)/shard_map/ppermute | solution.py:504
  81.6 3.9 %collective-permute-start.9 = (bf16[288,1152]{1,0:T(8,128)(2,1)S(1)}, bf16[288,1152]{1,0:T(8,128)(2,1)S(1)}, u32[]{:S(2)}, u32[]{:S(2)}) collective-permute-start(bf16[288,1152]{1,0:T(8,128)(2,1)S(1)} %collective-permute-done.6.refs_7_.refs_10_), channel_id=1, source_target_pairs={{0,1},{1,0},{2,3},{3,2},{4,5},{5,4},{6,7},{7,6},{8,9},{9,8},{10,11... | collective-permute-start | bytes 1990664 | tf_op jit(solution)/shard_map/ppermute | solution.py:535
  86.5 4.4 %collective-permute-start.12 = (bf16[576,640]{1,0:T(8,128)(2,1)S(1)}, bf16[576,640]{1,0:T(8,128)(2,1)S(1)}, u32[]{:S(2)}, u32[]{:S(2)}) collective-permute-start(bf16[576,640]{1,0:T(8,128)(2,1)S(1)} %constant_dynamic-update-slice_fusion.refs_0_), channel_id=1, source_target_pairs={{0,2},{1,7},{2,4},{3,1},{4,6},{5,3},{6,0},{7,5},{8,10},{9,15},{10,... | collective-permute-start | bytes 2211848 | tf_op jit(solution)/shard_map/ppermute | solution.py:558
  91.0 2.4 %collective-permute-start.8 = (bf16[144,1152]{1,0:T(8,128)(2,1)S(1)}, bf16[144,1152]{1,0:T(8,128)(2,1)S(1)}, u32[]{:S(2)}, u32[]{:S(2)}) collective-permute-start(bf16[144,1152]{1,0:T(8,128)(2,1)S(1)} %constant_dynamic-slice_fusion), channel_id=1, source_target_pairs={{0,64},{1,449},{2,66},{3,451},{4,68},{5,453},{6,70},{7,455},{8,72}... | collective-permute-start | bytes 995336 | tf_op jit(solution)/shard_map/ppermute | solution.py:504
  93.4 8.5 %collective-permute-done.8.refs_11_.refs_14_ = bf16[144,1152]{1,0:T(8,128)(2,1)S(1)} collective-permute-done((bf16[144,1152]{1,0:T(8,128)(2,1)S(1)}, bf16[144,1152]{1,0:T(8,128)(2,1)S(1)}, u32[]{:S(2)}, u32[]{:S(2)}) %collective-permute-start.8) | collective-permute-done | bytes 331808 | tf_op jit(solution)/shard_map/ppermute | solution.py:504
  101.8 2.3 %collective-permute-start.10 = (bf16[144,1152]{1,0:T(8,128)(2,1)S(1)}, bf16[144,1152]{1,0:T(8,128)(2,1)S(1)}, u32[]{:S(2)}, u32[]{:S(2)}) collective-permute-start(bf16[144,1152]{1,0:T(8,128)(2,1)S(1)} %collective-permute-done.8.refs_11_.refs_14_), channel_id=1, source_target_pairs={{0,1},{1,0},{2,3},{3,2},{4,5},{5,4},{6,7},{7,6},{8,9},{9,8},{10,11... | collective-permute-start | bytes 995336 | tf_op jit(solution)/shard_map/ppermute | solution.py:535
  104.1 3.1 %collective-permute-start.13 = (bf16[576,640]{1,0:T(8,128)(2,1)S(1)}, bf16[576,640]{1,0:T(8,128)(2,1)}, u32[]{:S(2)}, u32[]{:S(2)}) collective-permute-start(bf16[576,640]{1,0:T(8,128)(2,1)S(1)} %constant_dynamic-update-slice_fusion.refs_0_), channel_id=1, source_target_pairs={{0,6},{1,3},{2,0},{3,5},{4,2},{5,7},{6,4},{7,1},{8,14},{9,11},{10,... | collective-permute-start | bytes 2211848 | tf_op jit(solution)/shard_map/ppermute | solution.py:558
  107.3 3.4 %collective-permute-start.14 = (bf16[576,640]{1,0:T(8,128)(2,1)S(1)}, bf16[576,640]{1,0:T(8,128)(2,1)}, u32[]{:S(2)}, u32[]{:S(2)}) collective-permute-start(bf16[576,640]{1,0:T(8,128)(2,1)S(1)} %collective-permute-done.12.refs_1_), channel_id=1, source_target_pairs={{0,2},{1,7},{2,4},{3,1},{4,6},{5,3},{6,0},{7,5},{8,10},{9,15},{10,... | collective-permute-start | bytes 2211848 | tf_op jit(solution)/shard_map/ppermute | solution.py:558
  111.4 9.7 %shard_map.87 = (bf16[128,2304]{1,0:T(8,128)(2,1)}, bf16[3,128,640]{2,1,0:T(8,128)(2,1)}, f32[8,128,128]{2,1,0:T(8,128)}, bf16[128,640]{1,0:T(8,128)(2,1)}) custom-call(s32[4]{0:T(128)} %pad_add_fusion.at_ref.refs_0_, bf16[128,1152]{1,0:T(8,128)(2,1)} %bitcast.22, bf16[128,1152]{1,0:T(8,128)(2,1)} %bitcast.21, bf16[640,1152]{1,0:T(8,128)(2,1)} %fusion.1.refs_3_.refs_6_, ...), custom_call_target="tpu_custom_call" | custom-call | flops 8800000000 | bytes 3000000 | tf_op jit(solution)/shard_map/pallas_call | solution.py:409
  121.1 3.6 %all-to-all-start = ((bf16[16,8,2304]{2,1,0:T(8,128)(2,1)}), bf16[16,8,2304]{2,1,0:T(8,128)(2,1)S(1)}, u32[]{:S(2)}, u32[]{:S(2)}) async-start(bf16[16,8,2304]{2,1,0:T(8,128)(2,1)} %bitcast.19), calls=%async_computation | async-start | bytes 1179648 | tf_op jit(solution)/shard_map/all_to_all | solution.py:521
  124.7 2.0 collective-permute-start.15
  126.8 2.3 %collective-permute-start.16 = (bf16[576,640]{1,0:T(8,128)(2,1)S(1)}, bf16[576,640]{1,0:T(8,128)(2,1)S(1)}, u32[]{:S(2)}, u32[]{:S(2)}) collective-permute-start(bf16[576,640]{1,0:T(8,128)(2,1)S(1)} %collective-permute-done.12.refs_1_), channel_id=1, source_target_pairs={{0,1},{1,0},{2,3},{3,2},{4,5},{5,4},{6,7},{7,6},{8,9},{9,8},{10,11... | collective-permute-start | bytes 2211848 | tf_op jit(solution)/shard_map/ppermute | solution.py:535
  129.1 2.0 collective-permute-start.17
  131.1 2.3 %collective-permute-start.18 = (bf16[576,640]{1,0:T(8,128)(2,1)}, bf16[576,640]{1,0:T(8,128)(2,1)}, u32[]{:S(2)}, u32[]{:S(2)}) collective-permute-start(bf16[576,640]{1,0:T(8,128)(2,1)} %collective-permute-done.14.refs_3_), channel_id=1, source_target_pairs={{0,1},{1,0},{2,3},{3,2},{4,5},{5,4},{6,7},{7,6},{8,9},{9,8},{10,11... | collective-permute-start | bytes 2211848 | tf_op jit(solution)/shard_map/ppermute | solution.py:535
  136.4 9.3 %shard_map.88 = (bf16[288,1152]{1,0:T(8,128)(2,1)}, bf16[288,1152]{1,0:T(8,128)(2,1)}, bf16[3,128,640]{2,1,0:T(8,128)(2,1)}, f32[8,128,128]{2,1,0:T(8,128)}, bf16[128,640]{1,0:T(8,128)(2,1)}) custom-call(s32[4]{0:T(128)} %pad_add_fusion.at_ref.refs_0_, bf16[128,2304]{1,0:T(8,128)(2,1)} %bitcast.17, bf16[1152,1152]{1,0:T(8,128)(2,1)} %fusion.full_ref, ...), custom_call_target="tpu_custom_call" | custom-call | flops 8800000000 | bytes 3000000 | tf_op jit(solution)/shard_map/pallas_call | solution.py:409
  145.8 2.7 %collective-permute-start.19 = (bf16[288,1152]{1,0:T(8,128)(2,1)}, bf16[288,1152]{1,0:T(8,128)(2,1)S(1)}, u32[]{:S(2)}, u32[]{:S(2)}) collective-permute-start(bf16[288,1152]{1,0:T(8,128)(2,1)} %get-tuple-element.49), channel_id=1, source_target_pairs={{0,1},{1,0},{2,3},{3,2},{4,5},{5,4},{6,7},{7,6},{8,9},{9,8},{10,11... | collective-permute-start | bytes 1990664 | tf_op jit(solution)/shard_map/ppermute | solution.py:535
  148.5 1.9 collective-permute-done.19
  150.4 1.2 add_convert_fusion
  151.7 2.1 collective-permute-start.20
  153.8 11.4 %shard_map.89 = bf16[128,2304]{1,0:T(8,128)(2,1)} custom-call(s32[4]{0:T(128)} %pad_add_fusion.at_ref.refs_0_, bf16[128,2304]{1,0:T(8,128)(2,1)} %bitcast.18, bf16[3,128,640]{2,1,0:T(8,128)(2,1)} %get-tuple-element.52.qkv_ref, f32[8,128,128]{2,1,0:T(8,128)} %get-tuple-element.53.probs_ref, bf16[128,640]{1,0:T(8,128)(2,1)} %get-tuple-element.54.context_ref, ...), custom_call_target="tpu_custom_call" | custom-call | flops 9900000256 | bytes 3000000 | tf_op jit(solution)/shard_map/pallas_call | solution.py:409
  165.2 7.8 %all-to-all-start.2 = ((bf16[16,8,2304]{2,1,0:T(8,128)(2,1)}), bf16[16,8,2304]{2,1,0:T(8,128)(2,1)S(1)}, u32[]{:S(2)}, u32[]{:S(2)}) async-start(bf16[16,8,2304]{2,1,0:T(8,128)(2,1)} %bitcast.20), calls=%async_computation.2 | async-start | bytes 1179648 | tf_op jit(solution)/shard_map/all_to_all | solution.py:521
  173.1 6.0 %collective-permute-start.21 = (bf16[72,1152]{1,0:T(8,128)(2,1)S(1)}, bf16[72,1152]{1,0:T(8,128)(2,1)S(1)}, u32[]{:S(2)}, u32[]{:S(2)}) collective-permute-start(bf16[72,1152]{1,0:T(8,128)(2,1)S(1)} %slice.21), channel_id=1, source_target_pairs={{0,128},{1,385},{2,130},{3,387},{4,132},{5,389},{6,134},{7,391},{8... | collective-permute-start | bytes 497672 | tf_op jit(solution)/shard_map/ppermute | solution.py:504
  179.2 3.2 %collective-permute-done.21 = bf16[72,1152]{1,0:T(8,128)(2,1)S(1)} collective-permute-done((bf16[72,1152]{1,0:T(8,128)(2,1)S(1)}, bf16[72,1152]{1,0:T(8,128)(2,1)S(1)}, u32[]{:S(2)}, u32[]{:S(2)}) %collective-permute-start.21) | collective-permute-done | bytes 165920 | tf_op jit(solution)/shard_map/ppermute | solution.py:504
  182.4 1.1 all-to-all-done.2
  184.4 11.0 %all-to-all-start.3 = ((bf16[8,9,1152]{2,1,0:T(8,128)(2,1)}), bf16[8,9,1152]{2,1,0:T(8,128)(2,1)S(1)}, u32[]{:S(2)}, u32[]{:S(2)}) async-start(bf16[8,9,1152]{2,1,0:T(8,128)(2,1)} %reshape.210), calls=%async_computation.3 | async-start | bytes 589824 | tf_op jit(solution)/shard_map/all_to_all | solution.py:606
  195.5 9.5 %shard_map.90 = bf16[128,1152]{1,0:T(8,128)(2,1)} custom-call(s32[4]{0:T(128)} %pad_add_fusion.at_ref.refs_0_, bf16[128,1152]{1,0:T(8,128)(2,1)} %bitcast.23, bf16[128,2304]{1,0:T(8,128)(2,1)} %bitcast.15, bf16[3,128,640]{2,1,0:T(8,128)(2,1)} %get-tuple-element.58.refs_3_, f32[8,128,128]{2,1,0:T(8,128)} %get-tuple-element.59.refs_4_, ...), custom_call_target="tpu_custom_call" | custom-call | flops 9900000256 | bytes 3000000 | tf_op jit(solution)/shard_map/pallas_call | solution.py:409
  205.0 3.4 %all-to-all-done.3 = bf16[8,9,1152]{2,1,0:T(8,128)(2,1)S(1)} async-done(((bf16[8,9,1152]{2,1,0:T(8,128)(2,1)}), bf16[8,9,1152]{2,1,0:T(8,128)(2,1)S(1)}, u32[]{:S(2)}, u32[]{:S(2)}) %all-to-all-start.3) | async-done | bytes 165920 | tf_op jit(solution)/shard_map/all_to_all | solution.py:606
  209.3 6.7 %all-to-all-start.4 = ((bf16[16,9,1152]{2,1,0:T(8,128)(2,1)}), bf16[16,9,1152]{2,1,0:T(8,128)(2,1)S(1)}, u32[]{:S(2)}, u32[]{:S(2)}) async-start(bf16[16,9,1152]{2,1,0:T(8,128)(2,1)} %broadcast_in_dim.16), calls=%async_computation.4 | async-start | bytes 1179648 | tf_op jit(solution)/shard_map/all_to_all | solution.py:466
  216.7 9.8 %all-to-all-done.4 = bf16[16,9,1152]{2,1,0:T(8,128)(2,1)S(1)} async-done(((bf16[16,9,1152]{2,1,0:T(8,128)(2,1)}), bf16[16,9,1152]{2,1,0:T(8,128)(2,1)S(1)}, u32[]{:S(2)}, u32[]{:S(2)}) %all-to-all-start.4) | async-done | bytes 331808 | tf_op jit(solution)/shard_map/all_to_all | solution.py:466
  (73 shorter events, 10.5 us)
Async XLA Ops:
  4.2 24.5 %collective-permute-start = (bf16[88,1152]{1,0:T(8,128)(2,1)}, bf16[88,1152]{1,0:T(8,128)(2,1)S(1)}, u32[]{:S(2)}, u32[]{:S(2)}) collective-permute-start(bf16[88,1152]{1,0:T(8,128)(2,1)} %get-tuple-element.33.own_ref), channel_id=1, source_target_pairs={{0,16},{1,49},{2,18},{3,51},{4,20},{5,53},{6,22},{7,55},{8,24},{9,... | collective-permute-start | bytes 608264 | tf_op jit(solution)/shard_map/ppermute | solution.py:504
  15.7 13.0 %collective-permute-start.1 = (bf16[52,1152]{1,0:T(8,128)(2,1)}, bf16[52,1152]{1,0:T(8,128)(2,1)S(1)}, u32[]{:S(2)}, u32[]{:S(2)}) collective-permute-start(bf16[52,1152]{1,0:T(8,128)(2,1)} %get-tuple-element.34), channel_id=1, source_target_pairs={{0,32},{1,33},{2,34},{3,35},{4,36},{5,37},{6,38},{7,39},{8,40},{9,... | collective-permute-start | bytes 359432 | tf_op jit(solution)/shard_map/ppermute | solution.py:504
  28.7 4.1 %copy-start.6 = (bf16[52,1152]{1,0:T(8,128)(2,1)}, bf16[52,1152]{1,0:T(8,128)(2,1)S(1)}, u32[]{:S(2)}) copy-start(bf16[52,1152]{1,0:T(8,128)(2,1)S(1)} %collective-permute-done.1.far_ref) | copy-start | bytes 359428
  28.7 4.1 %copy-start.3 = (bf16[88,1152]{1,0:T(8,128)(2,1)}, bf16[88,1152]{1,0:T(8,128)(2,1)S(1)}, u32[]{:S(2)}) copy-start(bf16[88,1152]{1,0:T(8,128)(2,1)S(1)} %collective-permute-done.next_ref) | copy-start | bytes 608260
  28.7 4.2 %collective-permute-start.2 = (bf16[140,1152]{1,0:T(8,128)(2,1)S(1)}, bf16[140,1152]{1,0:T(8,128)(2,1)S(1)}, u32[]{:S(2)}, u32[]{:S(2)}) collective-permute-start(bf16[140,1152]{1,0:T(8,128)(2,1)S(1)} %pad_maximum_fusion), channel_id=1, source_target_pairs={{0,1},{1,0},{2,3},{3,2},{4,5},{5,4},{6,7},{7,6},{8,9},{9,8},{10,11... | collective-permute-start | bytes 967688 | tf_op jit(solution)/shard_map/ppermute | solution.py:535
  32.9 0.7 copy-start.16
  36.5 13.2 %collective-permute-start.3 = (bf16[288,1152]{1,0:T(8,128)(2,1)}, bf16[288,1152]{1,0:T(8,128)(2,1)S(1)}, u32[]{:S(2)}, u32[]{:S(2)}) collective-permute-start(bf16[288,1152]{1,0:T(8,128)(2,1)} %get-tuple-element.35.refs_4_.refs_7_), channel_id=1, source_target_pairs={{0,64},{1,449},{2,66},{3,451},{4,68},{5,453},{6,70},{7,455},{8,72}... | collective-permute-start | bytes 1990664 | tf_op jit(solution)/shard_map/ppermute | solution.py:504
  49.7 36.8 %copy-start.11 = (bf16[288,1152]{1,0:T(8,128)(2,1)}, bf16[288,1152]{1,0:T(8,128)(2,1)S(1)}, u32[]{:S(2)}) copy-start(bf16[288,1152]{1,0:T(8,128)(2,1)S(1)} %collective-permute-done.3.refs_5_.refs_8_) | copy-start | bytes 1990660
  49.7 12.4 %collective-permute-start.5 = (bf16[288,1152]{1,0:T(8,128)(2,1)S(1)}, bf16[288,1152]{1,0:T(8,128)(2,1)S(1)}, u32[]{:S(2)}, u32[]{:S(2)}) collective-permute-start(bf16[288,1152]{1,0:T(8,128)(2,1)S(1)} %collective-permute-done.3.refs_5_.refs_8_), channel_id=1, source_target_pairs={{0,1},{1,0},{2,3},{3,2},{4,5},{5,4},{6,7},{7,6},{8,9},{9,8},{10,11... | collective-permute-start | bytes 1990664 | tf_op jit(solution)/shard_map/ppermute | solution.py:535
  53.3 12.8 %collective-permute-start.4 = (bf16[288,1152]{1,0:T(8,128)(2,1)S(1)}, bf16[288,1152]{1,0:T(8,128)(2,1)}, u32[]{:S(2)}, u32[]{:S(2)}) collective-permute-start(bf16[288,1152]{1,0:T(8,128)(2,1)S(1)} %collective-permute-done.3.refs_5_.refs_8_), channel_id=1, source_target_pairs={{0,64},{1,449},{2,66},{3,451},{4,68},{5,453},{6,70},{7,455},{8,72}... | collective-permute-start | bytes 1990664 | tf_op jit(solution)/shard_map/ppermute | solution.py:504
  57.0 18.3 %all-to-all-start.1 = ((bf16[8,36,640]{2,1,0:T(8,128)(2,1)}), bf16[8,36,640]{2,1,0:T(8,128)(2,1)S(1)}, u32[]{:S(2)}, u32[]{:S(2)}) async-start(bf16[8,36,640]{2,1,0:T(8,128)(2,1)} %get-tuple-element.47), calls=%async_computation.1 | async-start | bytes 819200 | tf_op jit(solution)/shard_map/all_to_all | solution.py:541
  62.1 15.2 %copy-start.12 = (bf16[288,1152]{1,0:T(8,128)(2,1)}, bf16[288,1152]{1,0:T(8,128)(2,1)S(1)}, u32[]{:S(2)}) copy-start(bf16[288,1152]{1,0:T(8,128)(2,1)S(1)} %collective-permute-done.5.refs_8_.refs_11_) | copy-start | bytes 1990660
  66.1 11.2 %collective-permute-start.7 = (bf16[288,1152]{1,0:T(8,128)(2,1)}, bf16[288,1152]{1,0:T(8,128)(2,1)}, u32[]{:S(2)}, u32[]{:S(2)}) collective-permute-start(bf16[288,1152]{1,0:T(8,128)(2,1)} %collective-permute-done.4.refs_6_.refs_9_), channel_id=1, source_target_pairs={{0,1},{1,0},{2,3},{3,2},{4,5},{5,4},{6,7},{7,6},{8,9},{9,8},{10,11... | collective-permute-start | bytes 1990664 | tf_op jit(solution)/shard_map/ppermute | solution.py:535
  69.6 12.0 %collective-permute-start.6 = (bf16[288,1152]{1,0:T(8,128)(2,1)}, bf16[288,1152]{1,0:T(8,128)(2,1)S(1)}, u32[]{:S(2)}, u32[]{:S(2)}) collective-permute-start(bf16[288,1152]{1,0:T(8,128)(2,1)} %collective-permute-done.4.refs_6_.refs_9_), channel_id=1, source_target_pairs={{0,64},{1,449},{2,66},{3,451},{4,68},{5,453},{6,70},{7,455},{8,72}... | collective-permute-start | bytes 1990664 | tf_op jit(solution)/shard_map/ppermute | solution.py:504
  75.3 11.2 %collective-permute-start.11 = (bf16[288,640]{1,0:T(8,128)(2,1)S(1)}, bf16[288,640]{1,0:T(8,128)(2,1)S(1)}, u32[]{:S(2)}, u32[]{:S(2)}) collective-permute-start(bf16[288,640]{1,0:T(8,128)(2,1)S(1)} %reshape.207), channel_id=1, source_target_pairs={{0,8},{1,9},{2,10},{3,11},{4,12},{5,13},{6,14},{7,15},{8,0},{9,1},... | collective-permute-start | bytes 1105928 | tf_op jit(solution)/shard_map/ppermute | solution.py:560
  81.6 29.1 %copy-start.5 = (bf16[288,1152]{1,0:T(8,128)(2,1)}, bf16[288,1152]{1,0:T(8,128)(2,1)S(1)}, u32[]{:S(2)}) copy-start(bf16[288,1152]{1,0:T(8,128)(2,1)S(1)} %collective-permute-done.6.refs_7_.refs_10_) | copy-start | bytes 1990660
  81.6 20.3 %collective-permute-start.9 = (bf16[288,1152]{1,0:T(8,128)(2,1)S(1)}, bf16[288,1152]{1,0:T(8,128)(2,1)S(1)}, u32[]{:S(2)}, u32[]{:S(2)}) collective-permute-start(bf16[288,1152]{1,0:T(8,128)(2,1)S(1)} %collective-permute-done.6.refs_7_.refs_10_), channel_id=1, source_target_pairs={{0,1},{1,0},{2,3},{3,2},{4,5},{5,4},{6,7},{7,6},{8,9},{9,8},{10,11... | collective-permute-start | bytes 1990664 | tf_op jit(solution)/shard_map/ppermute | solution.py:535
  86.5 38.2 %copy-start.4 = (bf16[576,640]{1,0:T(8,128)(2,1)}, bf16[576,640]{1,0:T(8,128)(2,1)S(1)}, u32[]{:S(2)}) copy-start(bf16[576,640]{1,0:T(8,128)(2,1)S(1)} %constant_dynamic-update-slice_fusion.refs_0_) | copy-start | bytes 2211844
  86.5 20.7 %collective-permute-start.12 = (bf16[576,640]{1,0:T(8,128)(2,1)S(1)}, bf16[576,640]{1,0:T(8,128)(2,1)S(1)}, u32[]{:S(2)}, u32[]{:S(2)}) collective-permute-start(bf16[576,640]{1,0:T(8,128)(2,1)S(1)} %constant_dynamic-update-slice_fusion.refs_0_), channel_id=1, source_target_pairs={{0,2},{1,7},{2,4},{3,1},{4,6},{5,3},{6,0},{7,5},{8,10},{9,15},{10,... | collective-permute-start | bytes 2211848 | tf_op jit(solution)/shard_map/ppermute | solution.py:558
  91.0 10.8 %collective-permute-start.8 = (bf16[144,1152]{1,0:T(8,128)(2,1)S(1)}, bf16[144,1152]{1,0:T(8,128)(2,1)S(1)}, u32[]{:S(2)}, u32[]{:S(2)}) collective-permute-start(bf16[144,1152]{1,0:T(8,128)(2,1)S(1)} %constant_dynamic-slice_fusion), channel_id=1, source_target_pairs={{0,64},{1,449},{2,66},{3,451},{4,68},{5,453},{6,70},{7,455},{8,72}... | collective-permute-start | bytes 995336 | tf_op jit(solution)/shard_map/ppermute | solution.py:504
  101.8 8.9 %copy-start.14 = (bf16[144,1152]{1,0:T(8,128)(2,1)}, bf16[144,1152]{1,0:T(8,128)(2,1)S(1)}, u32[]{:S(2)}) copy-start(bf16[144,1152]{1,0:T(8,128)(2,1)S(1)} %collective-permute-done.8.refs_11_.refs_14_) | copy-start | bytes 995332
  101.8 5.5 %copy-start.13 = (bf16[288,1152]{1,0:T(8,128)(2,1)}, bf16[288,1152]{1,0:T(8,128)(2,1)S(1)}, u32[]{:S(2)}) copy-start(bf16[288,1152]{1,0:T(8,128)(2,1)S(1)} %collective-permute-done.9.refs_10_.refs_13_) | copy-start | bytes 1990660
  101.8 8.9 %collective-permute-start.10 = (bf16[144,1152]{1,0:T(8,128)(2,1)S(1)}, bf16[144,1152]{1,0:T(8,128)(2,1)S(1)}, u32[]{:S(2)}, u32[]{:S(2)}) collective-permute-start(bf16[144,1152]{1,0:T(8,128)(2,1)S(1)} %collective-permute-done.8.refs_11_.refs_14_), channel_id=1, source_target_pairs={{0,1},{1,0},{2,3},{3,2},{4,5},{5,4},{6,7},{7,6},{8,9},{9,8},{10,11... | collective-permute-start | bytes 995336 | tf_op jit(solution)/shard_map/ppermute | solution.py:535
  104.1 25.0 %collective-permute-start.13 = (bf16[576,640]{1,0:T(8,128)(2,1)S(1)}, bf16[576,640]{1,0:T(8,128)(2,1)}, u32[]{:S(2)}, u32[]{:S(2)}) collective-permute-start(bf16[576,640]{1,0:T(8,128)(2,1)S(1)} %constant_dynamic-update-slice_fusion.refs_0_), channel_id=1, source_target_pairs={{0,6},{1,3},{2,0},{3,5},{4,2},{5,7},{6,4},{7,1},{8,14},{9,11},{10,... | collective-permute-start | bytes 2211848 | tf_op jit(solution)/shard_map/ppermute | solution.py:558
  107.3 19.5 %copy-start.7 = (bf16[576,640]{1,0:T(8,128)(2,1)}, bf16[576,640]{1,0:T(8,128)(2,1)S(1)}, u32[]{:S(2)}) copy-start(bf16[576,640]{1,0:T(8,128)(2,1)S(1)} %collective-permute-done.12.refs_1_) | copy-start | bytes 2211844
  107.3 23.8 %collective-permute-start.14 = (bf16[576,640]{1,0:T(8,128)(2,1)S(1)}, bf16[576,640]{1,0:T(8,128)(2,1)}, u32[]{:S(2)}, u32[]{:S(2)}) collective-permute-start(bf16[576,640]{1,0:T(8,128)(2,1)S(1)} %collective-permute-done.12.refs_1_), channel_id=1, source_target_pairs={{0,2},{1,7},{2,4},{3,1},{4,6},{5,3},{6,0},{7,5},{8,10},{9,15},{10,... | collective-permute-start | bytes 2211848 | tf_op jit(solution)/shard_map/ppermute | solution.py:558
  110.7 0.7 copy-start.15
  121.1 14.5 %all-to-all-start = ((bf16[16,8,2304]{2,1,0:T(8,128)(2,1)}), bf16[16,8,2304]{2,1,0:T(8,128)(2,1)S(1)}, u32[]{:S(2)}, u32[]{:S(2)}) async-start(bf16[16,8,2304]{2,1,0:T(8,128)(2,1)} %bitcast.19), calls=%async_computation | async-start | bytes 1179648 | tf_op jit(solution)/shard_map/all_to_all | solution.py:521
  124.7 8.7 %collective-permute-start.15 = (bf16[576,640]{1,0:T(8,128)(2,1)S(1)}, bf16[576,640]{1,0:T(8,128)(2,1)S(1)}, u32[]{:S(2)}, u32[]{:S(2)}) collective-permute-start(bf16[576,640]{1,0:T(8,128)(2,1)S(1)} %constant_dynamic-update-slice_fusion.refs_0_), channel_id=1, source_target_pairs={{0,1},{1,0},{2,3},{3,2},{4,5},{5,4},{6,7},{7,6},{8,9},{9,8},{10,11... | collective-permute-start | bytes 2211848 | tf_op jit(solution)/shard_map/ppermute | solution.py:535
  126.8 6.7 %collective-permute-start.16 = (bf16[576,640]{1,0:T(8,128)(2,1)S(1)}, bf16[576,640]{1,0:T(8,128)(2,1)S(1)}, u32[]{:S(2)}, u32[]{:S(2)}) collective-permute-start(bf16[576,640]{1,0:T(8,128)(2,1)S(1)} %collective-permute-done.12.refs_1_), channel_id=1, source_target_pairs={{0,1},{1,0},{2,3},{3,2},{4,5},{5,4},{6,7},{7,6},{8,9},{9,8},{10,11... | collective-permute-start | bytes 2211848 | tf_op jit(solution)/shard_map/ppermute | solution.py:535
  129.1 4.4 %collective-permute-start.17 = (bf16[576,640]{1,0:T(8,128)(2,1)}, bf16[576,640]{1,0:T(8,128)(2,1)S(1)}, u32[]{:S(2)}, u32[]{:S(2)}) collective-permute-start(bf16[576,640]{1,0:T(8,128)(2,1)} %collective-permute-done.13.refs_2_), channel_id=1, source_target_pairs={{0,1},{1,0},{2,3},{3,2},{4,5},{5,4},{6,7},{7,6},{8,9},{9,8},{10,11... | collective-permute-start | bytes 2211848 | tf_op jit(solution)/shard_map/ppermute | solution.py:535
  131.1 4.5 %collective-permute-start.18 = (bf16[576,640]{1,0:T(8,128)(2,1)}, bf16[576,640]{1,0:T(8,128)(2,1)}, u32[]{:S(2)}, u32[]{:S(2)}) collective-permute-start(bf16[576,640]{1,0:T(8,128)(2,1)} %collective-permute-done.14.refs_3_), channel_id=1, source_target_pairs={{0,1},{1,0},{2,3},{3,2},{4,5},{5,4},{6,7},{7,6},{8,9},{9,8},{10,11... | collective-permute-start | bytes 2211848 | tf_op jit(solution)/shard_map/ppermute | solution.py:535
  133.5 2.2 copy-start.8
  133.5 0.9 copy-start.10
  134.4 0.9 copy-start.9
  135.6 0.8 copy-start.2
  145.8 4.7 %collective-permute-start.19 = (bf16[288,1152]{1,0:T(8,128)(2,1)}, bf16[288,1152]{1,0:T(8,128)(2,1)S(1)}, u32[]{:S(2)}, u32[]{:S(2)}) collective-permute-start(bf16[288,1152]{1,0:T(8,128)(2,1)} %get-tuple-element.49), channel_id=1, source_target_pairs={{0,1},{1,0},{2,3},{3,2},{4,5},{5,4},{6,7},{7,6},{8,9},{9,8},{10,11... | collective-permute-start | bytes 1990664 | tf_op jit(solution)/shard_map/ppermute | solution.py:535
  151.7 21.3 %collective-permute-start.20 = (bf16[144,1152]{1,0:T(8,128)(2,1)S(1)}, bf16[144,1152]{1,0:T(8,128)(2,1)S(1)}, u32[]{:S(2)}, u32[]{:S(2)}) collective-permute-start(bf16[144,1152]{1,0:T(8,128)(2,1)S(1)} %slice.16), channel_id=1, source_target_pairs={{0,64},{1,449},{2,66},{3,451},{4,68},{5,453},{6,70},{7,455},{8,72}... | collective-permute-start | bytes 995336 | tf_op jit(solution)/shard_map/ppermute | solution.py:504
  165.2 18.3 %all-to-all-start.2 = ((bf16[16,8,2304]{2,1,0:T(8,128)(2,1)}), bf16[16,8,2304]{2,1,0:T(8,128)(2,1)S(1)}, u32[]{:S(2)}, u32[]{:S(2)}) async-start(bf16[16,8,2304]{2,1,0:T(8,128)(2,1)} %bitcast.20), calls=%async_computation.2 | async-start | bytes 1179648 | tf_op jit(solution)/shard_map/all_to_all | solution.py:521
  173.1 9.3 %collective-permute-start.21 = (bf16[72,1152]{1,0:T(8,128)(2,1)S(1)}, bf16[72,1152]{1,0:T(8,128)(2,1)S(1)}, u32[]{:S(2)}, u32[]{:S(2)}) collective-permute-start(bf16[72,1152]{1,0:T(8,128)(2,1)S(1)} %slice.21), channel_id=1, source_target_pairs={{0,128},{1,385},{2,130},{3,387},{4,132},{5,389},{6,134},{7,391},{8... | collective-permute-start | bytes 497672 | tf_op jit(solution)/shard_map/ppermute | solution.py:504
  183.5 11.9 %copy-start = (bf16[16,8,2304]{2,1,0:T(8,128)(2,1)}, bf16[16,8,2304]{2,1,0:T(8,128)(2,1)S(1)}, u32[]{:S(2)}) copy-start(bf16[16,8,2304]{2,1,0:T(8,128)(2,1)S(1)} %all-to-all-done.2) | copy-start | bytes 1769476
  184.4 23.9 %all-to-all-start.3 = ((bf16[8,9,1152]{2,1,0:T(8,128)(2,1)}), bf16[8,9,1152]{2,1,0:T(8,128)(2,1)S(1)}, u32[]{:S(2)}, u32[]{:S(2)}) async-start(bf16[8,9,1152]{2,1,0:T(8,128)(2,1)} %reshape.210), calls=%async_computation.3 | async-start | bytes 589824 | tf_op jit(solution)/shard_map/all_to_all | solution.py:606
  205.0 11.0 %copy-start.1 = (bf16[16,8,2304]{2,1,0:T(8,128)(2,1)S(1)}, bf16[16,8,2304]{2,1,0:T(8,128)(2,1)}, u32[]{:S(2)}) copy-start(bf16[16,8,2304]{2,1,0:T(8,128)(2,1)} %copy-done) | copy-start | bytes 1769476
  209.3 17.2 %all-to-all-start.4 = ((bf16[16,9,1152]{2,1,0:T(8,128)(2,1)}), bf16[16,9,1152]{2,1,0:T(8,128)(2,1)S(1)}, u32[]{:S(2)}, u32[]{:S(2)}) async-start(bf16[16,9,1152]{2,1,0:T(8,128)(2,1)} %broadcast_in_dim.16), calls=%async_computation.4 | async-start | bytes 1179648 | tf_op jit(solution)/shard_map/all_to_all | solution.py:466

commit v4 on v3

v4 whole, which is shorter than its diff:
```python
import jax
import jax.numpy as jnp
from jax import lax
from jax.experimental import pallas as pl
from jax.experimental.pallas import tpu as pltpu
from jax.sharding import PartitionSpec as P

BF = jnp.bfloat16
F32 = jnp.float32
EPSILON = 1e-06
D = 1152
WIDTH = 576
PAD = 640
HEADS = 8
HEAD = 72
TOKENS = 128
PATCH_BLOCK = 8
SCALING = HEAD ** (-0.5)
SHARE = 288
BLOCK = 144
VMEM_LIMIT = 62 * 1024 * 1024


def nn(a, b):
    return lax.dot_general(a, b, (((1,), (0,)), ((), ())), preferred_element_type=F32)


def nt(a, b):
    return lax.dot_general(a, b, (((1,), (1,)), ((), ())), preferred_element_type=F32)


def tn(a, b):
    return lax.dot_general(a, b, (((0,), (0,)), ((), ())), preferred_element_type=F32)


def lanes(shape):
    return lax.broadcasted_iota(jnp.int32, shape, len(shape) - 1)


def normalize(values):
    centred = values - jnp.mean(values, axis=-1, keepdims=True)
    inverse = lax.rsqrt(jnp.mean(centred * centred, axis=-1, keepdims=True) + EPSILON)
    return centred * inverse, inverse


def norm_back(grad, normed, inverse):
    return inverse * (
        grad
        - jnp.mean(grad, axis=-1, keepdims=True)
        - normed * jnp.mean(grad * normed, axis=-1, keepdims=True)
    )


def keep_width(a):
    return jnp.where(lanes(a.shape) < WIDTH, a, 0.0)


def window(h):
    low = h * HEAD // 128 * 128
    high = -(-(h * HEAD + HEAD) // 128) * 128
    return low, high


def head_mask(h):
    low, high = window(h)
    at = lanes((TOKENS, high - low)) + low
    return (at >= h * HEAD) & (at < h * HEAD + HEAD)


def add_window(tiles, h, part):
    low, high = window(h)
    part = jnp.where(head_mask(h), part, 0.0)
    for t in range(low // 128, high // 128):
        piece = part[:, t * 128 - low : t * 128 - low + 128]
        tiles[t] = piece if tiles[t] is None else tiles[t] + piece


def join(tiles):
    return jnp.concatenate(tiles, axis=1)


def rounded(a):
    return a.astype(BF).astype(F32)


def attend(q, k, v, allowed, probs_ref):
    tiles = [None] * (PAD // 128)
    for h in range(HEADS):
        low, high = window(h)
        masked = jnp.where(head_mask(h), q[:, low:high].astype(F32), 0.0).astype(BF)
        scores = nt(masked, k[:, low:high]) * SCALING
        if allowed is not None:
            scores = jnp.where(allowed, scores, -1e38)
        powers = jnp.exp(scores - jnp.max(scores, axis=-1, keepdims=True))
        probs = powers / jnp.sum(powers, axis=-1, keepdims=True)
        probs_ref[h] = probs
        add_window(tiles, h, nn(probs.astype(BF), v[:, low:high]))
    return join(tiles).astype(BF)


def attend_back(q, k, v, context, context_grad, probs_ref):
    dq, dk, dv = ([None] * (PAD // 128) for _ in range(3))
    for h in range(HEADS):
        low, high = window(h)
        grad = context_grad[:, low:high]
        masked = jnp.where(head_mask(h), grad.astype(F32), 0.0)
        probs = probs_ref[h]
        prob_grad = nt(masked.astype(BF), v[:, low:high])
        row = jnp.sum(masked * context[:, low:high].astype(F32), axis=-1, keepdims=True)
        score_grad = (probs * (prob_grad - row) * SCALING).astype(BF)
        add_window(dv, h, tn(probs.astype(BF), grad))
        add_window(dq, h, nn(score_grad, k[:, low:high]))
        add_window(dk, h, tn(score_grad, q[:, low:high]))
    return rounded(join(dq)), rounded(join(dk)), rounded(join(dv))


def start_all(copies):
    for copy in copies:
        copy.start()
    return copies


def wait_all(copies):
    for copy in copies:
        copy.wait()


def load_weights(at_ref, blocks, weights, sems, order):
    y, core = at_ref[0], at_ref[1]
    sign = 1 - 2 * core

    def copy(source, half, place, sem):
        at = pl.multiple_of(half * D + lax.rem(place + 16, 8) * BLOCK, BLOCK)
        return pltpu.make_async_copy(source, weights.at[pl.ds(at, BLOCK), :], sems.at[sem])

    last = start_all([copy(blocks[7], core, y + 4, 0), copy(blocks[8], 1 - core, y + 4, 8)])
    groups = {}
    for half in order:
        rows = pl.ds(half * BLOCK, BLOCK)
        copies = [copy(blocks[0].at[rows, :], half, y, half * 8 + 1)]
        for step in range(1, 4):
            below, above = blocks[step].at[rows, :], blocks[3 + step].at[rows, :]
            copies.append(copy(below, half, y - sign * step, half * 8 + 2 * step))
            copies.append(copy(above, half, y + sign * step, half * 8 + 2 * step + 1))
        groups[half] = start_all(copies)
    groups[order[0]] = last + groups[order[0]]
    return groups


def project(normed, weights, wait_first, wait_second):
    normed_b = normed.astype(BF)
    wait_first()
    qk = nn(normed_b, weights[:D, :])
    wait_second()
    v = keep_width(nn(normed_b, weights[D:, :PAD]))
    k = pltpu.roll(qk, WIDTH, 1)
    return qk[:, :PAD].astype(BF), k[:, :PAD].astype(BF), v.astype(BF)


def pair_lanes(dq, dk):
    zeros = jnp.zeros((TOKENS, D - PAD), F32)
    return jnp.concatenate([dq, zeros], axis=1) + pltpu.roll(
        jnp.concatenate([dk, zeros], axis=1), WIDTH, 1
    )


def back_project(dq, dk, dv, weights):
    return nt(pair_lanes(dq, dk).astype(BF), weights[:D, :]) + nt(dv.astype(BF), weights[D:, :PAD])


def late(a):
    return jnp.where(lanes(a.shape) >= PAD - WIDTH, a, 0.0)


def out_weights(weights, side):
    starts = [D + y * BLOCK + side * 72 for y in range(8)]
    return jnp.concatenate([weights[at : at + 72, D - PAD :] for at in starts], axis=0)


def project_out(context, left, right):
    zeros = jnp.zeros((TOKENS, D - PAD), F32)
    context = context[:, :WIDTH]
    first, second = late(nn(context, left)), late(nn(context, right))
    return pltpu.roll(
        jnp.concatenate([first, zeros], axis=1), D - (PAD - WIDTH), 1
    ) + jnp.concatenate([zeros, second], axis=1)


def back_project_out(grad, left, right):
    first = late(pltpu.roll(grad, PAD - WIDTH, 1)[:, :PAD])
    second = late(grad[:, D - PAD :])
    context_grad = nt(first.astype(BF), left) + nt(second.astype(BF), right)
    return jnp.concatenate([context_grad, jnp.zeros((TOKENS, PAD - WIDTH), F32)], axis=1).astype(BF)


def selection(rows, columns, shift):
    r = lax.broadcasted_iota(jnp.int32, (rows, columns), 0)
    c = lax.broadcasted_iota(jnp.int32, (rows, columns), 1)
    return r + shift == c


def pack_kernel(at_ref, *refs):
    outside, inside_refs, sems = refs[:4], refs[8:12], refs[12]
    wait_all(
        start_all(
            [
                pltpu.make_async_copy(a, b, sems.at[n])
                for n, (a, b) in enumerate(zip(outside, inside_refs))
            ]
        )
    )
    qkv_s, out_s, qkv_t, out_t = inside_refs
    core = at_ref[1]

    def pick(which, a):
        return nn(which.astype(F32).astype(BF), a)

    def side(a, b):
        return jnp.concatenate([a, b], axis=1)

    lead = selection(36, 18, 0)
    tail = selection(36, 18, -18)

    def blocks(qkv, out_ref):
        q, k, v, out = qkv[0], qkv[1], qkv[2], out_ref[...]
        halves = pick(lead, out[:, :WIDTH]) + pick(tail, out[:, WIDTH:])
        return side(q.astype(F32), k.astype(F32)), side(v.astype(F32), halves)

    for n, (qkv, out_ref) in enumerate(((qkv_s, out_s), (qkv_t, out_t))):
        all_ref, half_ref = refs[4 + 2 * n : 6 + 2 * n]
        first, second = blocks(qkv, out_ref)
        half_ref[...] = jnp.where(core == 0, first, second).astype(BF)
        all_ref[...] = jnp.concatenate([first, second], axis=0).astype(BF)


def in_sides(parts):
    plain = jnp.concatenate(parts, axis=0)
    by_side = jnp.concatenate([p[:18] for p in parts] + [p[18:] for p in parts], axis=0)
    return jnp.where(lanes(plain.shape) < WIDTH, plain, by_side)


def in_order(z, own, below, above, far):
    parts = []
    for place in range(4):
        distance = lax.rem(place - z + 4, 4)
        part = jnp.where(distance == 0, own, jnp.where(distance == 1, above, far))
        parts.append(jnp.where(distance == 3, below, part))
    return parts


def column_kernel(at_ref, own_ref, next_ref, far_ref, other_ref, block_ref):
    z, core = at_ref[3], at_ref[1]
    own, near, far = (ref[...].astype(F32) for ref in (own_ref, next_ref, far_ref))
    other = other_ref[...].astype(F32)
    below = jnp.where(core == 0, near, other[:72])
    above = jnp.where(core == 0, other[:72], near)
    low = jnp.where(core == 0, far, other[72:])
    high = jnp.where(core == 0, other[72:], far)
    first = in_order(z, own[:36], below[:36], above[:36], low)
    second = in_order(z, own[36:], below[36:], above[36:], high)
    block_ref[:BLOCK] = jnp.concatenate(first, axis=0).astype(BF)
    block_ref[BLOCK:] = in_sides(second).astype(BF)


def fetch(pairs, sems):
    return start_all(
        [pltpu.make_async_copy(a, b, sems.at[n]) for n, (a, b) in enumerate(pairs)]
    )


def forward_kernel(at_ref, x_hbm, cot_hbm, *refs):
    blocks, refs = refs[:9], refs[9:]
    both_ref, *outside, weights, x_ref, qkv_ref, probs_ref, context_ref, sems, more = refs
    tokens = fetch([(x_hbm, x_ref)], more)
    groups = load_weights(at_ref, blocks, weights, sems, (0, 1))
    cotangent = pltpu.make_async_copy(cot_hbm, both_ref.at[:, pl.ds(D, D)], more.at[1])
    cotangent.start()
    wait_all(tokens)
    x = x_ref[...].astype(F32)
    q, k, v = project(
        normalize(x)[0], weights, lambda: wait_all(groups[0]), lambda: wait_all(groups[1])
    )
    qkv_ref[0], qkv_ref[1], qkv_ref[2] = q, k, v
    left, right = out_weights(weights, 0), out_weights(weights, 1)
    context = attend(q, k, v, None, probs_ref)
    context_ref[...] = context
    copies = fetch(zip((qkv_ref, probs_ref, context_ref), outside), sems)
    both_ref[:, :D] = (x + project_out(context, left, right)).astype(BF)
    cotangent.wait()
    wait_all(copies)


def temporal_kernel(at_ref, both_hbm, order_hbm, *refs):
    back_ref, keep_ref, send_ref, weights, both_ref, order_ref, probs, sems, more = refs[9:]
    tokens, order = fetch([(both_hbm, both_ref), (order_hbm, order_ref)], more)
    groups = load_weights(at_ref, refs[:9], weights, sems, (0, 1))
    tokens.wait()
    hidden = both_ref[:, :D].astype(F32)
    normed, inverse = normalize(hidden)
    q, k, v = project(
        normed, weights, lambda: wait_all(groups[0]), lambda: wait_all(groups[1])
    )
    left, right = out_weights(weights, 0), out_weights(weights, 1)
    rows = lax.broadcasted_iota(jnp.int32, (TOKENS, TOKENS), 0)
    cols = lax.broadcasted_iota(jnp.int32, (TOKENS, TOKENS), 1)
    allowed = (rows & (PATCH_BLOCK - 1)) == (cols & (PATCH_BLOCK - 1))
    context = attend(q, k, v, allowed, probs)
    cot = both_ref[:, D:]
    order.wait()
    share = tn(nn(context, order_ref[...]).astype(BF), cot).astype(BF)
    keep_ref[...], send_ref[...] = share[:SHARE], share[SHARE:WIDTH]
    back_ref[:, D:] = (hidden + project_out(context, left, right)).astype(BF)
    cot = cot.astype(F32)
    context_grad = back_project_out(cot, left, right)
    dq, dk, dv = attend_back(q, k, v, context, context_grad, probs)
    normed_grad = rounded(back_project(dq, dk, dv, weights))
    back_ref[:, :D] = (cot + norm_back(normed_grad, normed, inverse)).astype(BF)


def backward_kernel(at_ref, x_hbm, both_hbm, qkv_hbm, probs_hbm, context_hbm, *refs):
    blocks, refs = refs[:9], refs[9:]
    input_grad_ref, weights, x_ref, grad_ref, qkv_ref, probs_ref, context_ref, sems, more = refs
    copies = fetch([(both_hbm.at[:, pl.ds(0, D)], grad_ref), (x_hbm, x_ref)], more)
    groups = load_weights(at_ref, blocks, weights, sems, (1, 0))
    kept = (qkv_hbm, qkv_ref), (probs_hbm, probs_ref), (context_hbm, context_ref)
    copies += [pltpu.make_async_copy(a, b, more.at[2 + n]) for n, (a, b) in enumerate(kept)]
    start_all(copies[2:])
    wait_all(copies[:2])
    grad = grad_ref[...].astype(F32)
    normed, inverse = normalize(x_ref[...].astype(F32))
    wait_all(groups[1])
    context_grad = back_project_out(grad, out_weights(weights, 0), out_weights(weights, 1))
    wait_all(copies[2:])
    dq, dk, dv = attend_back(
        qkv_ref[0], qkv_ref[1], qkv_ref[2], context_ref[...], context_grad, probs_ref
    )
    wait_all(groups[0])
    normed_grad = back_project(dq, dk, dv, weights)
    input_grad_ref[...] = (grad + norm_back(normed_grad, normed, inverse)).astype(BF)


def call(kernel, outs, scratch, micros, *args, smem=True, hbm=(), hbm_outs=()):
    in_specs = []
    for at in range(len(args)):
        space = pltpu.VMEM
        if smem and at == 0:
            space = pltpu.SMEM
        elif at in hbm:
            space = pl.ANY
        in_specs.append(pl.BlockSpec(memory_space=space))
    return pl.pallas_call(
        kernel,
        out_shape=[jax.ShapeDtypeStruct(s, t) for s, t in outs],
        in_specs=in_specs,
        out_specs=[
            pl.BlockSpec(memory_space=pl.ANY if n in hbm_outs else pltpu.VMEM)
            for n in range(len(outs))
        ],
        scratch_shapes=scratch,
        compiler_params=pltpu.CompilerParams(vmem_limit_bytes=VMEM_LIMIT),
        cost_estimate=pl.CostEstimate(
            flops=micros * 1_100_000_000, bytes_accessed=3_000_000, transcendentals=0
        ),
    )(*args)


def share_order(y, core):
    f = jnp.arange(PAD)
    dp, row = f // 18, f % 18
    half = row // 9
    far = jnp.where((dp // 4 - y) % 2 == 0, 0, 144) + jnp.where(half == core, 0, SHARE)
    at = far + dp // 8 * 36 + dp % 4 * 9 + row % 9
    at = jnp.where(f < WIDTH, at, -1)
    return (at[:, None] == jnp.arange(PAD)[None, :]).astype(BF)


GROUPS_FAR = [[y * 4 + z for y in range(p, 8, 2) for z in range(4)] for p in range(2)]
SWAP = [(s, s ^ 1) for s in range(16)]


def spread(block, axis, groups):
    count = len(groups[0])
    return lax.all_to_all(
        jnp.broadcast_to(block[None], (count,) + block.shape), axis, 0, 0,
        axis_index_groups=groups, tiled=True,
    )


def along_z(distance):
    pairs = []
    for y in range(8):
        for z in range(4):
            for s in range(16):
                to = (z + (distance if s % 2 == 0 else -distance)) % 4
                pairs.append(((y * 4 + z) * 16 + s, (y * 4 + to) * 16 + s))
    return pairs


def along_y(distance):
    pairs = []
    for y in range(8):
        for z in range(4):
            for s in range(16):
                to = (y + (distance if s % 2 == 0 else -distance)) % 8
                pairs.append(((y * 4 + z) * 16 + s, (to * 4 + z) * 16 + s))
    return pairs


UP = along_y(1)


def move(a, pairs):
    return lax.ppermute(a, ("dp", "seq"), pairs)


def per_device(clips, qkv_spatial, out_spatial, qkv_temporal, out_temporal, cotangent):
    x = clips.reshape(TOKENS, D)
    out_grad = cotangent.reshape(TOKENS, D)
    seq, dp = lax.axis_index("seq"), lax.axis_index("dp")
    y, chip, core = dp // 4, seq // 2, seq % 2
    at = jnp.stack([y, core, chip, dp % 4]).astype(jnp.int32)

    tokens_b = ((TOKENS, D), BF)
    wide_b = ((TOKENS, 2 * D), BF)
    probs = (HEADS, TOKENS, TOKENS)
    sems = pltpu.SemaphoreType.DMA((16,))

    def turn(a):
        parts = a.reshape(16, PATCH_BLOCK, 2 * D)
        return lax.all_to_all(parts, "seq", 0, 0, tiled=True).reshape(TOKENS, 2 * D)

    packed, packed_h, packed_t, packed_th = call(
        pack_kernel, [((72, D), BF), ((36, D), BF)] * 2,
        [
            pltpu.VMEM((3, 36, WIDTH), BF), pltpu.VMEM((18, D), BF),
            pltpu.VMEM((3, 36, WIDTH), BF), pltpu.VMEM((18, D), BF), sems,
        ],
        2, at, qkv_spatial, out_spatial, qkv_temporal, out_temporal, hbm=range(1, 5),
    )

    def swap(a):
        return lax.ppermute(a, "seq", SWAP)

    def column(rows, near, far):
        return call(
            column_kernel, [((2 * BLOCK, D), BF)], [], 2,
            at, rows, near, far, swap(jnp.concatenate([near, far])),
        )[0]

    def onward(ring):
        ring.append(move(ring[-1], UP))
        theirs = swap(ring[-2])
        ring[-1], theirs = lax.optimization_barrier((ring[-1], theirs))
        return theirs

    def final(ring):
        theirs = swap(ring[3])
        last = move(lax.dynamic_slice_in_dim(ring[3], core * BLOCK, BLOCK, axis=0), UP)
        return lax.optimization_barrier((last, theirs))

    near, far = move(packed, along_z(1)), move(packed_h, along_z(2))
    near, far, packed_t, packed_th = lax.optimization_barrier((near, far, packed_t, packed_th))
    near_t, far_t = move(packed_t, along_z(1)), move(packed_th, along_z(2))
    wgrad_order = share_order(y, core)

    block = column(packed, near, far)
    ring = [block, move(block, UP)]
    ring[1], near_t, far_t, wgrad_order = lax.optimization_barrier(
        (ring[1], near_t, far_t, wgrad_order)
    )
    block_t = column(packed_t, near_t, far_t)
    theirs = [onward(ring)]
    ring[2], block_t = lax.optimization_barrier((ring[2], block_t))
    ring_t = [block_t, move(block_t, UP)]
    theirs.append(onward(ring))
    last, other = final(ring)
    theirs_t = [onward(ring_t)]
    last_other, ring_t[2] = lax.optimization_barrier((swap(last), ring_t[2]))
    blocks = [*ring, *theirs, other, last, last_other]
    theirs_t.append(onward(ring_t))
    last_t, other = final(ring_t)
    blocks_t = [*ring_t, *theirs_t, other, last_t, swap(last_t)]

    more = pltpu.SemaphoreType.DMA((5,))
    weights = pltpu.VMEM((2 * D, D), BF)
    tokens, wide = pltpu.VMEM((TOKENS, D), BF), pltpu.VMEM((TOKENS, 2 * D), BF)
    kept = pltpu.VMEM((3, TOKENS, PAD), BF), pltpu.VMEM(probs, F32), pltpu.VMEM((TOKENS, PAD), BF)
    both, qkv, probs_s, context_s = call(
        forward_kernel,
        [wide_b, ((3, TOKENS, PAD), BF), (probs, F32), ((TOKENS, PAD), BF)],
        [weights, tokens, *kept, sems, more],
        8,
        at, x, out_grad, *blocks,
        hbm=range(1, 12), hbm_outs=(1, 2, 3),
    )
    both = turn(both)
    both_back, keep, send = call(
        temporal_kernel,
        [wide_b, ((SHARE, D), BF), ((SHARE, D), BF)],
        [weights, wide, pltpu.VMEM((PAD, PAD), BF), pltpu.VMEM(probs, F32), sems, more],
        12,
        at, both, wgrad_order, *blocks_t,
        hbm=range(1, 12),
    )
    both_back = turn(both_back)

    def add(a, b):
        return (a.astype(F32) + b.astype(F32)).astype(BF)

    total = add(keep, swap(send))
    total = add(total[:144], move(total[144:], UP))
    (input_grad,) = call(
        backward_kernel,
        [tokens_b],
        [weights, tokens, tokens, *kept, sems, more],
        9,
        at, x, both_back, qkv, probs_s, context_s, *blocks,
        hbm=range(1, 15),
    )
    over_z = lax.all_to_all(
        total.reshape(16, 9, D), "dp", 0, 0, axis_index_groups=GROUPS_FAR, tiled=True
    )
    over_z = jnp.sum(over_z.astype(F32), axis=0).astype(BF)
    over_z, input_grad = lax.optimization_barrier((over_z, input_grad))
    over_seq = spread(over_z, "seq", [list(range(16))]).reshape(8, 2, 9, D)
    out_temporal_grad = jnp.sum(over_seq.astype(F32), axis=0).reshape(18, D)
    mixed = both_back[:, D:]

    return mixed[None, None], input_grad[None, None], out_temporal_grad


def solution(mesh):
    tokens = P("dp", "seq", None, None)
    placed = (tokens, P(None, "dp", None), P("dp", None), P(None, "dp", None), P("dp", None), tokens)
    return jax.shard_map(
        per_device,
        mesh=mesh,
        in_specs=placed,
        out_specs=(tokens, tokens, P("dp", None)),
        check_vma=False,
    )
```

time: 231 us -> 225 us (0.974)
  Pallas kernels: 45.7 us -> 36.2 us
  waiting for transfers between devices: 55 us -> 63.9 us
  other arithmetic: 7.48 us -> 2.48 us
    ppermute x8 -> x13, starting transfers between devices: 36.9 us -> 51.4 us  [move(): return lax.ppermute(a, ('dp', 'seq'), pairs)]
    ppermute x4 -> x0, starting transfers between devices: 12.8 us -> none  [the longest x3 10.9 us: round_x(): return lax.ppermute(a, 'seq', along_x(distance))]
    ppermute x10 -> x11, starting transfers between devices: 26.7 us -> 36.8 us  [swap(): return lax.ppermute(a, 'seq', SWAP)]
    all_to_all x2 -> x1, waiting for transfers between devices: 4.95 us -> 14.7 us  [per_device(): lax.all_to_all(total.reshape(16, 9, D), 'dp', 0, 0, axis_index_groups=GRO...]
    pallas_call x6, Pallas kernels: 45.7 us -> 36.2 us  [call(): pl.pallas_call(kernel, out_shape=[jax.ShapeDtypeStruct(s, t) for s, t in...]
    all_to_all x2 -> x1, starting transfers between devices: 16.2 us -> 7.94 us  [per_device(): lax.all_to_all(total.reshape(16, 9, D), 'dp', 0, 0, axis_index_groups=GRO...]
    convert_element_type x3 -> x1, other arithmetic: 4.97 us -> 1.12 us  [share_order(): return (at[:, None] == jnp.arange(PAD)[None, :]).astype(BF)]
    ppermute x8 -> x13, waiting for transfers between devices: 35.9 us -> 34.2 us  [move(): return lax.ppermute(a, ('dp', 'seq'), pairs)]
  transfers between devices with their start and end apart: 27 -> 28, of which waited for: 13 -> 15; matrix products, arithmetic and copies ran while one was open for 3% -> 2% of each run, Pallas kernels for 13% -> 8%
where the time goes in v4:
time: 225 us; the launch traced here: 223 us
  starting transfers between devices  112 us (50%)
  waiting for transfers between devices  63.9 us (28%)
  Pallas kernels  36.2 us (16%)
  local copies, waits for them, and re-layouts  7.81 us (3%)
  other arithmetic  2.48 us (1%)
    ppermute x13, starting transfers between devices, move(): return lax.ppermute(a, ('dp', 'seq'), pairs)  51.4 us
    ppermute x11, starting transfers between devices, swap(): return lax.ppermute(a, 'seq', SWAP)  36.8 us
    pallas_call x6, Pallas kernels, call(): pl.pallas_call(kernel, out_shape=[jax.ShapeDtypeStruct(s, t) for s, t in...  36.2 us
    ppermute x13, waiting for transfers between devices, move(): return lax.ppermute(a, ('dp', 'seq'), pairs)  34.2 us
    all_to_all x1, waiting for transfers between devices, per_device(): lax.all_to_all(total.reshape(16, 9, D), 'dp', 0, 0, axis_index_groups=GRO...  14.7 us
    all_to_all x2, starting transfers between devices, turn(): return lax.all_to_all(parts, 'seq', 0, 0, tiled=True).reshape(TOKENS, 2 * D)  9.96 us
    all_to_all x1, waiting for transfers between devices, spread(): lax.all_to_all(jnp.broadcast_to(block[None], (count,) + block.shape), axi...  9.88 us
    all_to_all x1, starting transfers between devices, per_device(): lax.all_to_all(total.reshape(16, 9, D), 'dp', 0, 0, axis_index_groups=GRO...  7.94 us
  transfers between devices with their start and end apart: 28, of which 15 were waited for; matrix products, arithmetic and copies ran while one was open for 2% of the time, Pallas kernels for 8%

profile of v4, /device:TPU:1, one launch (start us, length us, event | category | flops | bytes accessed | tf_op | source)
XLA Modules:
  0.0 223.2 jit_solution(5786304566807818150)
XLA Ops:
  1.2 2.9 %shard_map.85 = (bf16[72,1152]{1,0:T(8,128)(2,1)}, bf16[36,1152]{1,0:T(8,128)(2,1)}, bf16[72,1152]{1,0:T(8,128)(2,1)}, bf16[36,1152]{1,0:T(8,128)(2,1)}) custom-call(s32[4]{0:T(128)} %pad_add_fusion.at_ref, bf16[3,36,576]{2,1,0:T(8,128)(2,1)} %refs_0_.1, bf16[18,1152]{1,0:T(8,128)(2,1)} %refs_1_.1, bf16[3,36,576]{2,1,0:T(8,128)(2,1)} %refs_2_.1, ...), custom_call_target="tpu_custom_call" | custom-call | flops 2200000000 | bytes 3000000 | tf_op jit(solution)/shard_map/pallas_call | solution.py:351
  4.2 11.5 %collective-permute-start = (bf16[72,1152]{1,0:T(8,128)(2,1)}, bf16[72,1152]{1,0:T(8,128)(2,1)S(1)}, u32[]{:S(2)}, u32[]{:S(2)}) collective-permute-start(bf16[72,1152]{1,0:T(8,128)(2,1)} %get-tuple-element.40.own_ref), channel_id=1, source_target_pairs={{0,16},{1,49},{2,18},{3,51},{4,20},{5,53},{6,22},{7,55},{8,24},{9,... | collective-permute-start | bytes 497672 | tf_op jit(solution)/shard_map/ppermute | solution.py:413
  15.7 1.9 collective-permute-start.1
  17.6 8.0 %collective-permute-done.1.far_ref = bf16[36,1152]{1,0:T(8,128)(2,1)S(1)} collective-permute-done((bf16[36,1152]{1,0:T(8,128)(2,1)}, bf16[36,1152]{1,0:T(8,128)(2,1)S(1)}, u32[]{:S(2)}, u32[]{:S(2)}) %collective-permute-start.1) | collective-permute-done | bytes 82976 | tf_op jit(solution)/shard_map/ppermute | solution.py:413
  25.6 2.1 collective-permute-start.2
  27.7 1.5 collective-permute-done.2.other_ref
  29.9 2.4 %shard_map.86.refs_0_ = bf16[288,1152]{1,0:T(8,128)(2,1)} custom-call(s32[4]{0:T(128)} %pad_add_fusion.at_ref, bf16[72,1152]{1,0:T(8,128)(2,1)} %get-tuple-element.40.own_ref, bf16[72,1152]{1,0:T(8,128)(2,1)} %copy-done.6, bf16[36,1152]{1,0:T(8,128)(2,1)} %copy-done.8, bf16[108,1152]{1,0:T(8,128)(2,1)} %copy-done.20), custom_call_target="tpu_custom_call" | custom-call | flops 2200000000 | bytes 3000000 | tf_op jit(solution)/shard_map/pallas_call | solution.py:351
  32.3 7.2 %collective-permute-start.3 = (bf16[288,1152]{1,0:T(8,128)(2,1)}, bf16[288,1152]{1,0:T(8,128)(2,1)S(1)}, u32[]{:S(2)}, u32[]{:S(2)}) collective-permute-start(bf16[288,1152]{1,0:T(8,128)(2,1)} %shard_map.86.refs_0_), channel_id=1, source_target_pairs={{0,64},{1,449},{2,66},{3,451},{4,68},{5,453},{6,70},{7,455},{8,72}... | collective-permute-start | bytes 1990664 | tf_op jit(solution)/shard_map/ppermute | solution.py:413
  39.5 3.3 %collective-permute-start.5 = (bf16[36,1152]{1,0:T(8,128)(2,1)S(1)}, bf16[36,1152]{1,0:T(8,128)(2,1)S(1)}, u32[]{:S(2)}, u32[]{:S(2)}) collective-permute-start(bf16[36,1152]{1,0:T(8,128)(2,1)S(1)} %copy-done.23), channel_id=1, source_target_pairs={{0,32},{1,33},{2,34},{3,35},{4,36},{5,37},{6,38},{7,39},{8,40},{9,... | collective-permute-start | bytes 248840 | tf_op jit(solution)/shard_map/ppermute | solution.py:413
  42.8 4.1 %collective-permute-start.4 = (bf16[72,1152]{1,0:T(8,128)(2,1)S(1)}, bf16[72,1152]{1,0:T(8,128)(2,1)S(1)}, u32[]{:S(2)}, u32[]{:S(2)}) collective-permute-start(bf16[72,1152]{1,0:T(8,128)(2,1)S(1)} %copy-done.22), channel_id=1, source_target_pairs={{0,16},{1,49},{2,18},{3,51},{4,20},{5,53},{6,22},{7,55},{8,24},{9,... | collective-permute-start | bytes 497672 | tf_op jit(solution)/shard_map/ppermute | solution.py:413
  47.0 1.1 fusion.order_hbm
  48.1 2.4 %collective-permute-done.5.far_ref = bf16[36,1152]{1,0:T(8,128)(2,1)S(1)} collective-permute-done((bf16[36,1152]{1,0:T(8,128)(2,1)S(1)}, bf16[36,1152]{1,0:T(8,128)(2,1)S(1)}, u32[]{:S(2)}, u32[]{:S(2)}) %collective-permute-start.5) | collective-permute-done | bytes 82976 | tf_op jit(solution)/shard_map/ppermute | solution.py:413
  50.8 5.5 %collective-permute-start.7 = (bf16[288,1152]{1,0:T(8,128)(2,1)S(1)}, bf16[288,1152]{1,0:T(8,128)(2,1)S(1)}, u32[]{:S(2)}, u32[]{:S(2)}) collective-permute-start(bf16[288,1152]{1,0:T(8,128)(2,1)S(1)} %collective-permute-done.3.refs_1_), channel_id=1, source_target_pairs={{0,1},{1,0},{2,3},{3,2},{4,5},{5,4},{6,7},{7,6},{8,9},{9,8},{10,11... | collective-permute-start | bytes 1990664 | tf_op jit(solution)/shard_map/ppermute | solution.py:442
  56.3 3.5 %collective-permute-start.6 = (bf16[288,1152]{1,0:T(8,128)(2,1)S(1)}, bf16[288,1152]{1,0:T(8,128)(2,1)}, u32[]{:S(2)}, u32[]{:S(2)}) collective-permute-start(bf16[288,1152]{1,0:T(8,128)(2,1)S(1)} %collective-permute-done.3.refs_1_), channel_id=1, source_target_pairs={{0,64},{1,449},{2,66},{3,451},{4,68},{5,453},{6,70},{7,455},{8,72}... | collective-permute-start | bytes 1990664 | tf_op jit(solution)/shard_map/ppermute | solution.py:413
  59.9 1.9 collective-permute-start.8
  61.9 1.5 collective-permute-done.8.other_ref
  64.1 2.4 %shard_map.87.refs_0_ = bf16[288,1152]{1,0:T(8,128)(2,1)} custom-call(s32[4]{0:T(128)} %pad_add_fusion.at_ref, bf16[72,1152]{1,0:T(8,128)(2,1)} %get-tuple-element.46.own_ref, bf16[72,1152]{1,0:T(8,128)(2,1)} %copy-done.5, bf16[36,1152]{1,0:T(8,128)(2,1)} %copy-done.7, bf16[108,1152]{1,0:T(8,128)(2,1)} %copy-done.21), custom_call_target="tpu_custom_call" | custom-call | flops 2200000000 | bytes 3000000 | tf_op jit(solution)/shard_map/pallas_call | solution.py:351
  66.4 1.7 collective-permute-done.6.refs_2_
  68.2 4.0 %collective-permute-start.10 = (bf16[288,1152]{1,0:T(8,128)(2,1)}, bf16[288,1152]{1,0:T(8,128)(2,1)S(1)}, u32[]{:S(2)}, u32[]{:S(2)}) collective-permute-start(bf16[288,1152]{1,0:T(8,128)(2,1)} %collective-permute-done.6.refs_2_), channel_id=1, source_target_pairs={{0,1},{1,0},{2,3},{3,2},{4,5},{5,4},{6,7},{7,6},{8,9},{9,8},{10,11... | collective-permute-start | bytes 1990664 | tf_op jit(solution)/shard_map/ppermute | solution.py:442
  72.2 2.4 %collective-permute-start.9 = (bf16[288,1152]{1,0:T(8,128)(2,1)}, bf16[288,1152]{1,0:T(8,128)(2,1)S(1)}, u32[]{:S(2)}, u32[]{:S(2)}) collective-permute-start(bf16[288,1152]{1,0:T(8,128)(2,1)} %collective-permute-done.6.refs_2_), channel_id=1, source_target_pairs={{0,64},{1,449},{2,66},{3,451},{4,68},{5,453},{6,70},{7,455},{8,72}... | collective-permute-start | bytes 1990664 | tf_op jit(solution)/shard_map/ppermute | solution.py:413
  74.5 3.1 %collective-permute-start.14 = (bf16[288,1152]{1,0:T(8,128)(2,1)}, bf16[288,1152]{1,0:T(8,128)(2,1)S(1)}, u32[]{:S(2)}, u32[]{:S(2)}) collective-permute-start(bf16[288,1152]{1,0:T(8,128)(2,1)} %shard_map.87.refs_0_), channel_id=1, source_target_pairs={{0,64},{1,449},{2,66},{3,451},{4,68},{5,453},{6,70},{7,455},{8,72}... | collective-permute-start | bytes 1990664 | tf_op jit(solution)/shard_map/ppermute | solution.py:413
  77.7 6.4 %collective-permute-done.9.refs_3_ = bf16[288,1152]{1,0:T(8,128)(2,1)S(1)} collective-permute-done((bf16[288,1152]{1,0:T(8,128)(2,1)}, bf16[288,1152]{1,0:T(8,128)(2,1)S(1)}, u32[]{:S(2)}, u32[]{:S(2)}) %collective-permute-start.9) | collective-permute-done | bytes 663584 | tf_op jit(solution)/shard_map/ppermute | solution.py:413
  84.1 4.0 %collective-permute-start.12 = (bf16[288,1152]{1,0:T(8,128)(2,1)S(1)}, bf16[288,1152]{1,0:T(8,128)(2,1)S(1)}, u32[]{:S(2)}, u32[]{:S(2)}) collective-permute-start(bf16[288,1152]{1,0:T(8,128)(2,1)S(1)} %collective-permute-done.9.refs_3_), channel_id=1, source_target_pairs={{0,1},{1,0},{2,3},{3,2},{4,5},{5,4},{6,7},{7,6},{8,9},{9,8},{10,11... | collective-permute-start | bytes 1990664 | tf_op jit(solution)/shard_map/ppermute | solution.py:442
  88.1 1.9 collective-permute-start.11
  90.0 1.1 collective-permute-done.14.refs_1_
  91.2 4.0 %collective-permute-start.16 = (bf16[288,1152]{1,0:T(8,128)(2,1)S(1)}, bf16[288,1152]{1,0:T(8,128)(2,1)S(1)}, u32[]{:S(2)}, u32[]{:S(2)}) collective-permute-start(bf16[288,1152]{1,0:T(8,128)(2,1)S(1)} %collective-permute-done.14.refs_1_), channel_id=1, source_target_pairs={{0,1},{1,0},{2,3},{3,2},{4,5},{5,4},{6,7},{7,6},{8,9},{9,8},{10,11... | collective-permute-start | bytes 1990664 | tf_op jit(solution)/shard_map/ppermute | solution.py:442
  95.2 1.9 collective-permute-start.15
  98.0 3.1 %collective-permute-start.13 = (bf16[144,1152]{1,0:T(8,128)(2,1)S(1)}, bf16[144,1152]{1,0:T(8,128)(2,1)S(1)}, u32[]{:S(2)}, u32[]{:S(2)}) collective-permute-start(bf16[144,1152]{1,0:T(8,128)(2,1)S(1)} %collective-permute-done.11.refs_7_), channel_id=1, source_target_pairs={{0,1},{1,0},{2,3},{3,2},{4,5},{5,4},{6,7},{7,6},{8,9},{9,8},{10,11... | collective-permute-start | bytes 995336 | tf_op jit(solution)/shard_map/ppermute | solution.py:442
  101.2 5.8 %collective-permute-done.15.refs_2_ = bf16[288,1152]{1,0:T(8,128)(2,1)} collective-permute-done((bf16[288,1152]{1,0:T(8,128)(2,1)S(1)}, bf16[288,1152]{1,0:T(8,128)(2,1)}, u32[]{:S(2)}, u32[]{:S(2)}) %collective-permute-start.15) | collective-permute-done | bytes 663584 | tf_op jit(solution)/shard_map/ppermute | solution.py:413
  107.0 4.0 %collective-permute-start.18 = (bf16[288,1152]{1,0:T(8,128)(2,1)}, bf16[288,1152]{1,0:T(8,128)(2,1)}, u32[]{:S(2)}, u32[]{:S(2)}) collective-permute-start(bf16[288,1152]{1,0:T(8,128)(2,1)} %collective-permute-done.15.refs_2_), channel_id=1, source_target_pairs={{0,1},{1,0},{2,3},{3,2},{4,5},{5,4},{6,7},{7,6},{8,9},{9,8},{10,11... | collective-permute-start | bytes 1990664 | tf_op jit(solution)/shard_map/ppermute | solution.py:442
  111.0 1.9 collective-permute-start.17
  113.0 8.6 %shard_map.88 = (bf16[128,2304]{1,0:T(8,128)(2,1)}, bf16[3,128,640]{2,1,0:T(8,128)(2,1)}, f32[8,128,128]{2,1,0:T(8,128)}, bf16[128,640]{1,0:T(8,128)(2,1)}) custom-call(s32[4]{0:T(128)} %pad_add_fusion.at_ref, bf16[128,1152]{1,0:T(8,128)(2,1)} %bitcast.21, bf16[128,1152]{1,0:T(8,128)(2,1)} %bitcast.20, bf16[288,1152]{1,0:T(8,128)(2,1)} %shard_map.86.refs_0_, ...), custom_call_target="tpu_custom_call" | custom-call | flops 8800000000 | bytes 3000000 | tf_op jit(solution)/shard_map/pallas_call | solution.py:351
  121.5 4.4 %all-to-all-start = ((bf16[16,8,2304]{2,1,0:T(8,128)(2,1)}), bf16[16,8,2304]{2,1,0:T(8,128)(2,1)S(1)}, u32[]{:S(2)}, u32[]{:S(2)}) async-start(bf16[16,8,2304]{2,1,0:T(8,128)(2,1)} %bitcast.19), calls=%async_computation | async-start | bytes 1179648 | tf_op jit(solution)/shard_map/all_to_all | solution.py:430
  126.0 2.0 collective-permute-start.20
  129.0 4.7 %collective-permute-start.19 = (bf16[144,1152]{1,0:T(8,128)(2,1)S(1)}, bf16[144,1152]{1,0:T(8,128)(2,1)S(1)}, u32[]{:S(2)}, u32[]{:S(2)}) collective-permute-start(bf16[144,1152]{1,0:T(8,128)(2,1)S(1)} %constant_dynamic-slice_fusion), channel_id=1, source_target_pairs={{0,64},{1,449},{2,66},{3,451},{4,68},{5,453},{6,70},{7,455},{8,72}... | collective-permute-start | bytes 995336 | tf_op jit(solution)/shard_map/ppermute | solution.py:413
  133.8 4.0 %collective-permute-done.19.refs_7_ = bf16[144,1152]{1,0:T(8,128)(2,1)S(1)} collective-permute-done((bf16[144,1152]{1,0:T(8,128)(2,1)S(1)}, bf16[144,1152]{1,0:T(8,128)(2,1)S(1)}, u32[]{:S(2)}, u32[]{:S(2)}) %collective-permute-start.19) | collective-permute-done | bytes 331808 | tf_op jit(solution)/shard_map/ppermute | solution.py:413
  137.8 3.9 %collective-permute-start.21 = (bf16[144,1152]{1,0:T(8,128)(2,1)S(1)}, bf16[144,1152]{1,0:T(8,128)(2,1)S(1)}, u32[]{:S(2)}, u32[]{:S(2)}) collective-permute-start(bf16[144,1152]{1,0:T(8,128)(2,1)S(1)} %collective-permute-done.19.refs_7_), channel_id=1, source_target_pairs={{0,1},{1,0},{2,3},{3,2},{4,5},{5,4},{6,7},{7,6},{8,9},{9,8},{10,11... | collective-permute-start | bytes 995336 | tf_op jit(solution)/shard_map/ppermute | solution.py:442
  143.6 12.2 %shard_map.89 = (bf16[128,2304]{1,0:T(8,128)(2,1)}, bf16[288,1152]{1,0:T(8,128)(2,1)}, bf16[288,1152]{1,0:T(8,128)(2,1)}) custom-call(s32[4]{0:T(128)} %pad_add_fusion.at_ref, bf16[128,2304]{1,0:T(8,128)(2,1)} %bitcast.17, bf16[640,640]{1,0:T(8,128)(2,1)} %fusion.order_hbm, bf16[288,1152]{1,0:T(8,128)(2,1)} %shard_map.87.refs_0_, ...), custom_call_target="tpu_custom_call" | custom-call | flops 13200000000 | bytes 3000000 | tf_op jit(solution)/shard_map/pallas_call | solution.py:351
  155.8 2.4 %collective-permute-start.22 = (bf16[288,1152]{1,0:T(8,128)(2,1)}, bf16[288,1152]{1,0:T(8,128)(2,1)S(1)}, u32[]{:S(2)}, u32[]{:S(2)}) collective-permute-start(bf16[288,1152]{1,0:T(8,128)(2,1)} %get-tuple-element.71), channel_id=1, source_target_pairs={{0,1},{1,0},{2,3},{3,2},{4,5},{5,4},{6,7},{7,6},{8,9},{9,8},{10,11... | collective-permute-start | bytes 1990664 | tf_op jit(solution)/shard_map/ppermute | solution.py:442
  158.2 5.5 %all-to-all-start.1 = ((bf16[16,8,2304]{2,1,0:T(8,128)(2,1)}), bf16[16,8,2304]{2,1,0:T(8,128)(2,1)S(1)}, u32[]{:S(2)}, u32[]{:S(2)}) async-start(bf16[16,8,2304]{2,1,0:T(8,128)(2,1)} %bitcast.18), calls=%async_computation.1 | async-start | bytes 1179648 | tf_op jit(solution)/shard_map/all_to_all | solution.py:430
  163.9 3.8 %collective-permute-start.23 = (bf16[144,1152]{1,0:T(8,128)(2,1)S(1)}, bf16[144,1152]{1,0:T(8,128)(2,1)S(1)}, u32[]{:S(2)}, u32[]{:S(2)}) collective-permute-start(bf16[144,1152]{1,0:T(8,128)(2,1)S(1)} %slice.14), channel_id=1, source_target_pairs={{0,64},{1,449},{2,66},{3,451},{4,68},{5,453},{6,70},{7,455},{8,72}... | collective-permute-start | bytes 995336 | tf_op jit(solution)/shard_map/ppermute | solution.py:413
  167.7 4.3 %collective-permute-done.23 = bf16[144,1152]{1,0:T(8,128)(2,1)S(1)} collective-permute-done((bf16[144,1152]{1,0:T(8,128)(2,1)S(1)}, bf16[144,1152]{1,0:T(8,128)(2,1)S(1)}, u32[]{:S(2)}, u32[]{:S(2)}) %collective-permute-start.23) | collective-permute-done | bytes 331808 | tf_op jit(solution)/shard_map/ppermute | solution.py:413
  173.1 1.1 all-to-all-done.1
  174.2 7.9 %all-to-all-start.2 = ((bf16[16,9,1152]{2,1,0:T(8,128)(2,1)}), bf16[16,9,1152]{2,1,0:T(8,128)(2,1)S(1)}, u32[]{:S(2)}, u32[]{:S(2)}) async-start(bf16[16,9,1152]{2,1,0:T(8,128)(2,1)} %reshape.130), calls=%async_computation.2 | async-start | bytes 1179648 | tf_op jit(solution)/shard_map/all_to_all | solution.py:520
  182.2 7.8 %shard_map.90 = bf16[128,1152]{1,0:T(8,128)(2,1)} custom-call(s32[4]{0:T(128)} %pad_add_fusion.at_ref, bf16[128,1152]{1,0:T(8,128)(2,1)} %bitcast.22, bf16[128,2304]{1,0:T(8,128)(2,1)} %bitcast.15, bf16[3,128,640]{2,1,0:T(8,128)(2,1)} %get-tuple-element.72.qkv_hbm, f32[8,128,128]{2,1,0:T(8,128)} %get-tuple-element.73.probs_hbm, ...), custom_call_target="tpu_custom_call" | custom-call | flops 9900000256 | bytes 3000000 | tf_op jit(solution)/shard_map/pallas_call | solution.py:351
  190.0 14.7 %all-to-all-done.2 = bf16[16,9,1152]{2,1,0:T(8,128)(2,1)S(1)} async-done(((bf16[16,9,1152]{2,1,0:T(8,128)(2,1)}), bf16[16,9,1152]{2,1,0:T(8,128)(2,1)S(1)}, u32[]{:S(2)}, u32[]{:S(2)}) %all-to-all-start.2) | async-done | bytes 331808 | tf_op jit(solution)/shard_map/all_to_all | solution.py:520
  205.6 5.5 %all-to-all-start.3 = ((bf16[16,9,1152]{2,1,0:T(8,128)(2,1)}), bf16[16,9,1152]{2,1,0:T(8,128)(2,1)S(1)}, u32[]{:S(2)}, u32[]{:S(2)}) async-start(bf16[16,9,1152]{2,1,0:T(8,128)(2,1)} %broadcast_in_dim.30), calls=%async_computation.3 | async-start | bytes 1179648 | tf_op jit(solution)/shard_map/all_to_all | solution.py:383
  211.9 9.9 %all-to-all-done.3 = bf16[16,9,1152]{2,1,0:T(8,128)(2,1)S(1)} async-done(((bf16[16,9,1152]{2,1,0:T(8,128)(2,1)}), bf16[16,9,1152]{2,1,0:T(8,128)(2,1)S(1)}, u32[]{:S(2)}, u32[]{:S(2)}) %all-to-all-start.3) | async-done | bytes 331808 | tf_op jit(solution)/shard_map/all_to_all | solution.py:383
  (81 shorter events, 10.6 us)
Async XLA Ops:
  4.2 21.4 %collective-permute-start = (bf16[72,1152]{1,0:T(8,128)(2,1)}, bf16[72,1152]{1,0:T(8,128)(2,1)S(1)}, u32[]{:S(2)}, u32[]{:S(2)}) collective-permute-start(bf16[72,1152]{1,0:T(8,128)(2,1)} %get-tuple-element.40.own_ref), channel_id=1, source_target_pairs={{0,16},{1,49},{2,18},{3,51},{4,20},{5,53},{6,22},{7,55},{8,24},{9,... | collective-permute-start | bytes 497672 | tf_op jit(solution)/shard_map/ppermute | solution.py:413
  15.7 9.9 %collective-permute-start.1 = (bf16[36,1152]{1,0:T(8,128)(2,1)}, bf16[36,1152]{1,0:T(8,128)(2,1)S(1)}, u32[]{:S(2)}, u32[]{:S(2)}) collective-permute-start(bf16[36,1152]{1,0:T(8,128)(2,1)} %get-tuple-element.41), channel_id=1, source_target_pairs={{0,32},{1,33},{2,34},{3,35},{4,36},{5,37},{6,38},{7,39},{8,40},{9,... | collective-permute-start | bytes 248840 | tf_op jit(solution)/shard_map/ppermute | solution.py:413
  25.6 3.6 %copy-start.8 = (bf16[36,1152]{1,0:T(8,128)(2,1)}, bf16[36,1152]{1,0:T(8,128)(2,1)S(1)}, u32[]{:S(2)}) copy-start(bf16[36,1152]{1,0:T(8,128)(2,1)S(1)} %collective-permute-done.1.far_ref) | copy-start | bytes 248836
  25.6 3.6 %copy-start.6 = (bf16[72,1152]{1,0:T(8,128)(2,1)}, bf16[72,1152]{1,0:T(8,128)(2,1)S(1)}, u32[]{:S(2)}) copy-start(bf16[72,1152]{1,0:T(8,128)(2,1)S(1)} %collective-permute-done.next_ref) | copy-start | bytes 497668
  25.6 13.9 %copy-start.23 = (bf16[36,1152]{1,0:T(8,128)(2,1)S(1)}, bf16[36,1152]{1,0:T(8,128)(2,1)}, u32[]{:S(2)}) copy-start(bf16[36,1152]{1,0:T(8,128)(2,1)} %get-tuple-element.47) | copy-start | bytes 248836
  25.6 17.2 %copy-start.22 = (bf16[72,1152]{1,0:T(8,128)(2,1)S(1)}, bf16[72,1152]{1,0:T(8,128)(2,1)}, u32[]{:S(2)}) copy-start(bf16[72,1152]{1,0:T(8,128)(2,1)} %get-tuple-element.46.own_ref) | copy-start | bytes 497668
  25.6 3.6 %collective-permute-start.2 = (bf16[108,1152]{1,0:T(8,128)(2,1)S(1)}, bf16[108,1152]{1,0:T(8,128)(2,1)S(1)}, u32[]{:S(2)}, u32[]{:S(2)}) collective-permute-start(bf16[108,1152]{1,0:T(8,128)(2,1)S(1)} %pad_maximum_fusion), channel_id=1, source_target_pairs={{0,1},{1,0},{2,3},{3,2},{4,5},{5,4},{6,7},{7,6},{8,9},{9,8},{10,11... | collective-permute-start | bytes 746504 | tf_op jit(solution)/shard_map/ppermute | solution.py:442
  32.3 18.6 %collective-permute-start.3 = (bf16[288,1152]{1,0:T(8,128)(2,1)}, bf16[288,1152]{1,0:T(8,128)(2,1)S(1)}, u32[]{:S(2)}, u32[]{:S(2)}) collective-permute-start(bf16[288,1152]{1,0:T(8,128)(2,1)} %shard_map.86.refs_0_), channel_id=1, source_target_pairs={{0,64},{1,449},{2,66},{3,451},{4,68},{5,453},{6,70},{7,455},{8,72}... | collective-permute-start | bytes 1990664 | tf_op jit(solution)/shard_map/ppermute | solution.py:413
  39.5 10.9 %collective-permute-start.5 = (bf16[36,1152]{1,0:T(8,128)(2,1)S(1)}, bf16[36,1152]{1,0:T(8,128)(2,1)S(1)}, u32[]{:S(2)}, u32[]{:S(2)}) collective-permute-start(bf16[36,1152]{1,0:T(8,128)(2,1)S(1)} %copy-done.23), channel_id=1, source_target_pairs={{0,32},{1,33},{2,34},{3,35},{4,36},{5,37},{6,38},{7,39},{8,40},{9,... | collective-permute-start | bytes 248840 | tf_op jit(solution)/shard_map/ppermute | solution.py:413
  42.8 8.0 %collective-permute-start.4 = (bf16[72,1152]{1,0:T(8,128)(2,1)S(1)}, bf16[72,1152]{1,0:T(8,128)(2,1)S(1)}, u32[]{:S(2)}, u32[]{:S(2)}) collective-permute-start(bf16[72,1152]{1,0:T(8,128)(2,1)S(1)} %copy-done.22), channel_id=1, source_target_pairs={{0,16},{1,49},{2,18},{3,51},{4,20},{5,53},{6,22},{7,55},{8,24},{9,... | collective-permute-start | bytes 497672 | tf_op jit(solution)/shard_map/ppermute | solution.py:413
  50.4 12.9 %copy-start.7 = (bf16[36,1152]{1,0:T(8,128)(2,1)}, bf16[36,1152]{1,0:T(8,128)(2,1)S(1)}, u32[]{:S(2)}) copy-start(bf16[36,1152]{1,0:T(8,128)(2,1)S(1)} %collective-permute-done.5.far_ref) | copy-start | bytes 248836
  50.8 12.5 %copy-start.5 = (bf16[72,1152]{1,0:T(8,128)(2,1)}, bf16[72,1152]{1,0:T(8,128)(2,1)S(1)}, u32[]{:S(2)}) copy-start(bf16[72,1152]{1,0:T(8,128)(2,1)S(1)} %collective-permute-done.4.next_ref) | copy-start | bytes 497668
  50.8 15.6 %copy-start.9 = (bf16[288,1152]{1,0:T(8,128)(2,1)}, bf16[288,1152]{1,0:T(8,128)(2,1)S(1)}, u32[]{:S(2)}) copy-start(bf16[288,1152]{1,0:T(8,128)(2,1)S(1)} %collective-permute-done.3.refs_1_) | copy-start | bytes 1990660
  50.8 15.6 %collective-permute-start.7 = (bf16[288,1152]{1,0:T(8,128)(2,1)S(1)}, bf16[288,1152]{1,0:T(8,128)(2,1)S(1)}, u32[]{:S(2)}, u32[]{:S(2)}) collective-permute-start(bf16[288,1152]{1,0:T(8,128)(2,1)S(1)} %collective-permute-done.3.refs_1_), channel_id=1, source_target_pairs={{0,1},{1,0},{2,3},{3,2},{4,5},{5,4},{6,7},{7,6},{8,9},{9,8},{10,11... | collective-permute-start | bytes 1990664 | tf_op jit(solution)/shard_map/ppermute | solution.py:442
  56.3 11.8 %collective-permute-start.6 = (bf16[288,1152]{1,0:T(8,128)(2,1)S(1)}, bf16[288,1152]{1,0:T(8,128)(2,1)}, u32[]{:S(2)}, u32[]{:S(2)}) collective-permute-start(bf16[288,1152]{1,0:T(8,128)(2,1)S(1)} %collective-permute-done.3.refs_1_), channel_id=1, source_target_pairs={{0,64},{1,449},{2,66},{3,451},{4,68},{5,453},{6,70},{7,455},{8,72}... | collective-permute-start | bytes 1990664 | tf_op jit(solution)/shard_map/ppermute | solution.py:413
  59.9 3.4 %collective-permute-start.8 = (bf16[108,1152]{1,0:T(8,128)(2,1)S(1)}, bf16[108,1152]{1,0:T(8,128)(2,1)S(1)}, u32[]{:S(2)}, u32[]{:S(2)}) collective-permute-start(bf16[108,1152]{1,0:T(8,128)(2,1)S(1)} %pad_maximum_fusion.1), channel_id=1, source_target_pairs={{0,1},{1,0},{2,3},{3,2},{4,5},{5,4},{6,7},{7,6},{8,9},{9,8},{10,11... | collective-permute-start | bytes 746504 | tf_op jit(solution)/shard_map/ppermute | solution.py:442
  66.4 1.7 copy-start.10
  68.2 9.5 %collective-permute-start.10 = (bf16[288,1152]{1,0:T(8,128)(2,1)}, bf16[288,1152]{1,0:T(8,128)(2,1)S(1)}, u32[]{:S(2)}, u32[]{:S(2)}) collective-permute-start(bf16[288,1152]{1,0:T(8,128)(2,1)} %collective-permute-done.6.refs_2_), channel_id=1, source_target_pairs={{0,1},{1,0},{2,3},{3,2},{4,5},{5,4},{6,7},{7,6},{8,9},{9,8},{10,11... | collective-permute-start | bytes 1990664 | tf_op jit(solution)/shard_map/ppermute | solution.py:442
  72.2 11.9 %collective-permute-start.9 = (bf16[288,1152]{1,0:T(8,128)(2,1)}, bf16[288,1152]{1,0:T(8,128)(2,1)S(1)}, u32[]{:S(2)}, u32[]{:S(2)}) collective-permute-start(bf16[288,1152]{1,0:T(8,128)(2,1)} %collective-permute-done.6.refs_2_), channel_id=1, source_target_pairs={{0,64},{1,449},{2,66},{3,451},{4,68},{5,453},{6,70},{7,455},{8,72}... | collective-permute-start | bytes 1990664 | tf_op jit(solution)/shard_map/ppermute | solution.py:413
  74.5 16.6 %collective-permute-start.14 = (bf16[288,1152]{1,0:T(8,128)(2,1)}, bf16[288,1152]{1,0:T(8,128)(2,1)S(1)}, u32[]{:S(2)}, u32[]{:S(2)}) collective-permute-start(bf16[288,1152]{1,0:T(8,128)(2,1)} %shard_map.87.refs_0_), channel_id=1, source_target_pairs={{0,64},{1,449},{2,66},{3,451},{4,68},{5,453},{6,70},{7,455},{8,72}... | collective-permute-start | bytes 1990664 | tf_op jit(solution)/shard_map/ppermute | solution.py:413
  77.7 35.2 %copy-start.11 = (bf16[288,1152]{1,0:T(8,128)(2,1)}, bf16[288,1152]{1,0:T(8,128)(2,1)S(1)}, u32[]{:S(2)}) copy-start(bf16[288,1152]{1,0:T(8,128)(2,1)S(1)} %collective-permute-done.10.refs_5_) | copy-start | bytes 1990660
  84.1 28.9 %copy-start.4 = (bf16[288,1152]{1,0:T(8,128)(2,1)}, bf16[288,1152]{1,0:T(8,128)(2,1)S(1)}, u32[]{:S(2)}) copy-start(bf16[288,1152]{1,0:T(8,128)(2,1)S(1)} %collective-permute-done.9.refs_3_) | copy-start | bytes 1990660
  84.1 13.0 %collective-permute-start.12 = (bf16[288,1152]{1,0:T(8,128)(2,1)S(1)}, bf16[288,1152]{1,0:T(8,128)(2,1)S(1)}, u32[]{:S(2)}, u32[]{:S(2)}) collective-permute-start(bf16[288,1152]{1,0:T(8,128)(2,1)S(1)} %collective-permute-done.9.refs_3_), channel_id=1, source_target_pairs={{0,1},{1,0},{2,3},{3,2},{4,5},{5,4},{6,7},{7,6},{8,9},{9,8},{10,11... | collective-permute-start | bytes 1990664 | tf_op jit(solution)/shard_map/ppermute | solution.py:442
  88.1 9.0 %collective-permute-start.11 = (bf16[144,1152]{1,0:T(8,128)(2,1)S(1)}, bf16[144,1152]{1,0:T(8,128)(2,1)S(1)}, u32[]{:S(2)}, u32[]{:S(2)}) collective-permute-start(bf16[144,1152]{1,0:T(8,128)(2,1)S(1)} %constant_dynamic-slice_fusion.1), channel_id=1, source_target_pairs={{0,64},{1,449},{2,66},{3,451},{4,68},{5,453},{6,70},{7,455},{8,72}... | collective-permute-start | bytes 995336 | tf_op jit(solution)/shard_map/ppermute | solution.py:413
  91.2 30.4 %copy-start.13 = (bf16[288,1152]{1,0:T(8,128)(2,1)}, bf16[288,1152]{1,0:T(8,128)(2,1)S(1)}, u32[]{:S(2)}) copy-start(bf16[288,1152]{1,0:T(8,128)(2,1)S(1)} %collective-permute-done.14.refs_1_) | copy-start | bytes 1990660
  91.2 9.9 %collective-permute-start.16 = (bf16[288,1152]{1,0:T(8,128)(2,1)S(1)}, bf16[288,1152]{1,0:T(8,128)(2,1)S(1)}, u32[]{:S(2)}, u32[]{:S(2)}) collective-permute-start(bf16[288,1152]{1,0:T(8,128)(2,1)S(1)} %collective-permute-done.14.refs_1_), channel_id=1, source_target_pairs={{0,1},{1,0},{2,3},{3,2},{4,5},{5,4},{6,7},{7,6},{8,9},{9,8},{10,11... | collective-permute-start | bytes 1990664 | tf_op jit(solution)/shard_map/ppermute | solution.py:442
  95.2 11.8 %collective-permute-start.15 = (bf16[288,1152]{1,0:T(8,128)(2,1)S(1)}, bf16[288,1152]{1,0:T(8,128)(2,1)}, u32[]{:S(2)}, u32[]{:S(2)}) collective-permute-start(bf16[288,1152]{1,0:T(8,128)(2,1)S(1)} %collective-permute-done.14.refs_1_), channel_id=1, source_target_pairs={{0,64},{1,449},{2,66},{3,451},{4,68},{5,453},{6,70},{7,455},{8,72}... | collective-permute-start | bytes 1990664 | tf_op jit(solution)/shard_map/ppermute | solution.py:413
  97.1 9.9 %copy-start.16 = (bf16[144,1152]{1,0:T(8,128)(2,1)}, bf16[144,1152]{1,0:T(8,128)(2,1)S(1)}, u32[]{:S(2)}) copy-start(bf16[144,1152]{1,0:T(8,128)(2,1)S(1)} %collective-permute-done.11.refs_7_) | copy-start | bytes 995332
  98.0 9.0 %collective-permute-start.13 = (bf16[144,1152]{1,0:T(8,128)(2,1)S(1)}, bf16[144,1152]{1,0:T(8,128)(2,1)S(1)}, u32[]{:S(2)}, u32[]{:S(2)}) collective-permute-start(bf16[144,1152]{1,0:T(8,128)(2,1)S(1)} %collective-permute-done.11.refs_7_), channel_id=1, source_target_pairs={{0,1},{1,0},{2,3},{3,2},{4,5},{5,4},{6,7},{7,6},{8,9},{9,8},{10,11... | collective-permute-start | bytes 995336 | tf_op jit(solution)/shard_map/ppermute | solution.py:442
  101.1 5.8 %copy-start.14 = (bf16[288,1152]{1,0:T(8,128)(2,1)}, bf16[288,1152]{1,0:T(8,128)(2,1)S(1)}, u32[]{:S(2)}) copy-start(bf16[288,1152]{1,0:T(8,128)(2,1)S(1)} %collective-permute-done.16.refs_4_) | copy-start | bytes 1990660
  107.0 4.0 %copy-start.17 = (bf16[144,1152]{1,0:T(8,128)(2,1)}, bf16[144,1152]{1,0:T(8,128)(2,1)S(1)}, u32[]{:S(2)}) copy-start(bf16[144,1152]{1,0:T(8,128)(2,1)S(1)} %collective-permute-done.13.refs_8_) | copy-start | bytes 995332
  107.0 19.0 %collective-permute-start.18 = (bf16[288,1152]{1,0:T(8,128)(2,1)}, bf16[288,1152]{1,0:T(8,128)(2,1)}, u32[]{:S(2)}, u32[]{:S(2)}) collective-permute-start(bf16[288,1152]{1,0:T(8,128)(2,1)} %collective-permute-done.15.refs_2_), channel_id=1, source_target_pairs={{0,1},{1,0},{2,3},{3,2},{4,5},{5,4},{6,7},{7,6},{8,9},{9,8},{10,11... | collective-permute-start | bytes 1990664 | tf_op jit(solution)/shard_map/ppermute | solution.py:442
  111.0 15.0 %collective-permute-start.17 = (bf16[288,1152]{1,0:T(8,128)(2,1)}, bf16[288,1152]{1,0:T(8,128)(2,1)}, u32[]{:S(2)}, u32[]{:S(2)}) collective-permute-start(bf16[288,1152]{1,0:T(8,128)(2,1)} %collective-permute-done.15.refs_2_), channel_id=1, source_target_pairs={{0,64},{1,449},{2,66},{3,451},{4,68},{5,453},{6,70},{7,455},{8,72}... | collective-permute-start | bytes 1990664 | tf_op jit(solution)/shard_map/ppermute | solution.py:413
  121.5 20.2 %all-to-all-start = ((bf16[16,8,2304]{2,1,0:T(8,128)(2,1)}), bf16[16,8,2304]{2,1,0:T(8,128)(2,1)S(1)}, u32[]{:S(2)}, u32[]{:S(2)}) async-start(bf16[16,8,2304]{2,1,0:T(8,128)(2,1)} %bitcast.19), calls=%async_computation | async-start | bytes 1179648 | tf_op jit(solution)/shard_map/all_to_all | solution.py:430
  126.0 11.8 %collective-permute-start.20 = (bf16[288,1152]{1,0:T(8,128)(2,1)}, bf16[288,1152]{1,0:T(8,128)(2,1)S(1)}, u32[]{:S(2)}, u32[]{:S(2)}) collective-permute-start(bf16[288,1152]{1,0:T(8,128)(2,1)} %collective-permute-done.17.refs_3_), channel_id=1, source_target_pairs={{0,1},{1,0},{2,3},{3,2},{4,5},{5,4},{6,7},{7,6},{8,9},{9,8},{10,11... | collective-permute-start | bytes 1990664 | tf_op jit(solution)/shard_map/ppermute | solution.py:442
  129.0 8.8 %collective-permute-start.19 = (bf16[144,1152]{1,0:T(8,128)(2,1)S(1)}, bf16[144,1152]{1,0:T(8,128)(2,1)S(1)}, u32[]{:S(2)}, u32[]{:S(2)}) collective-permute-start(bf16[144,1152]{1,0:T(8,128)(2,1)S(1)} %constant_dynamic-slice_fusion), channel_id=1, source_target_pairs={{0,64},{1,449},{2,66},{3,451},{4,68},{5,453},{6,70},{7,455},{8,72}... | collective-permute-start | bytes 995336 | tf_op jit(solution)/shard_map/ppermute | solution.py:413
  137.8 5.0 %copy-start.18 = (bf16[144,1152]{1,0:T(8,128)(2,1)}, bf16[144,1152]{1,0:T(8,128)(2,1)S(1)}, u32[]{:S(2)}) copy-start(bf16[144,1152]{1,0:T(8,128)(2,1)S(1)} %collective-permute-done.19.refs_7_) | copy-start | bytes 995332
  137.8 5.0 %copy-start.15 = (bf16[288,1152]{1,0:T(8,128)(2,1)}, bf16[288,1152]{1,0:T(8,128)(2,1)S(1)}, u32[]{:S(2)}) copy-start(bf16[288,1152]{1,0:T(8,128)(2,1)S(1)} %collective-permute-done.20.refs_6_) | copy-start | bytes 1990660
  137.8 5.0 %collective-permute-start.21 = (bf16[144,1152]{1,0:T(8,128)(2,1)S(1)}, bf16[144,1152]{1,0:T(8,128)(2,1)S(1)}, u32[]{:S(2)}, u32[]{:S(2)}) collective-permute-start(bf16[144,1152]{1,0:T(8,128)(2,1)S(1)} %collective-permute-done.19.refs_7_), channel_id=1, source_target_pairs={{0,1},{1,0},{2,3},{3,2},{4,5},{5,4},{6,7},{7,6},{8,9},{9,8},{10,11... | collective-permute-start | bytes 995336 | tf_op jit(solution)/shard_map/ppermute | solution.py:442
  141.8 1.1 copy-start.3
  155.7 8.0 %copy-start.2 = (bf16[288,1152]{1,0:T(8,128)(2,1)S(1)}, bf16[288,1152]{1,0:T(8,128)(2,1)}, u32[]{:S(2)}) copy-start(bf16[288,1152]{1,0:T(8,128)(2,1)} %get-tuple-element.70) | copy-start | bytes 1990660
  155.8 7.9 %collective-permute-start.22 = (bf16[288,1152]{1,0:T(8,128)(2,1)}, bf16[288,1152]{1,0:T(8,128)(2,1)S(1)}, u32[]{:S(2)}, u32[]{:S(2)}) collective-permute-start(bf16[288,1152]{1,0:T(8,128)(2,1)} %get-tuple-element.71), channel_id=1, source_target_pairs={{0,1},{1,0},{2,3},{3,2},{4,5},{5,4},{6,7},{7,6},{8,9},{9,8},{10,11... | collective-permute-start | bytes 1990664 | tf_op jit(solution)/shard_map/ppermute | solution.py:442
  158.2 16.1 %all-to-all-start.1 = ((bf16[16,8,2304]{2,1,0:T(8,128)(2,1)}), bf16[16,8,2304]{2,1,0:T(8,128)(2,1)S(1)}, u32[]{:S(2)}, u32[]{:S(2)}) async-start(bf16[16,8,2304]{2,1,0:T(8,128)(2,1)} %bitcast.18), calls=%async_computation.1 | async-start | bytes 1179648 | tf_op jit(solution)/shard_map/all_to_all | solution.py:430
  163.9 8.2 %collective-permute-start.23 = (bf16[144,1152]{1,0:T(8,128)(2,1)S(1)}, bf16[144,1152]{1,0:T(8,128)(2,1)S(1)}, u32[]{:S(2)}, u32[]{:S(2)}) collective-permute-start(bf16[144,1152]{1,0:T(8,128)(2,1)S(1)} %slice.14), channel_id=1, source_target_pairs={{0,64},{1,449},{2,66},{3,451},{4,68},{5,453},{6,70},{7,455},{8,72}... | collective-permute-start | bytes 995336 | tf_op jit(solution)/shard_map/ppermute | solution.py:413
  174.2 7.9 %copy-start = (bf16[16,8,2304]{2,1,0:T(8,128)(2,1)}, bf16[16,8,2304]{2,1,0:T(8,128)(2,1)S(1)}, u32[]{:S(2)}) copy-start(bf16[16,8,2304]{2,1,0:T(8,128)(2,1)S(1)} %all-to-all-done.1) | copy-start | bytes 1769476
  174.2 30.4 %all-to-all-start.2 = ((bf16[16,9,1152]{2,1,0:T(8,128)(2,1)}), bf16[16,9,1152]{2,1,0:T(8,128)(2,1)S(1)}, u32[]{:S(2)}, u32[]{:S(2)}) async-start(bf16[16,9,1152]{2,1,0:T(8,128)(2,1)} %reshape.130), calls=%async_computation.2 | async-start | bytes 1179648 | tf_op jit(solution)/shard_map/all_to_all | solution.py:520
  204.8 6.4 %copy-start.1 = (bf16[16,8,2304]{2,1,0:T(8,128)(2,1)S(1)}, bf16[16,8,2304]{2,1,0:T(8,128)(2,1)}, u32[]{:S(2)}) copy-start(bf16[16,8,2304]{2,1,0:T(8,128)(2,1)} %copy-done) | copy-start | bytes 1769476
  205.6 16.1 %all-to-all-start.3 = ((bf16[16,9,1152]{2,1,0:T(8,128)(2,1)}), bf16[16,9,1152]{2,1,0:T(8,128)(2,1)S(1)}, u32[]{:S(2)}, u32[]{:S(2)}) async-start(bf16[16,9,1152]{2,1,0:T(8,128)(2,1)} %broadcast_in_dim.30), calls=%async_computation.3 | async-start | bytes 1179648 | tf_op jit(solution)/shard_map/all_to_all | solution.py:383
  (4 other events, 3.0 us)

commit v5 on v4

--- a/solution.py
+++ b/solution.py
@@ -465,9 +465,7 @@
 
     block = column(packed, near, far)
     ring = [block, move(block, UP)]
-    ring[1], near_t, far_t, wgrad_order = lax.optimization_barrier(
-        (ring[1], near_t, far_t, wgrad_order)
-    )
+    ring[1], wgrad_order = lax.optimization_barrier((ring[1], wgrad_order))
     block_t = column(packed_t, near_t, far_t)
     theirs = [onward(ring)]
     ring[2], block_t = lax.optimization_barrier((ring[2], block_t))

time: 225 us -> 221 us (0.982)
  waiting for transfers between devices: 63.9 us -> 60.8 us
    ppermute x13, waiting for transfers between devices: 34.2 us -> 31.1 us  [move(): return lax.ppermute(a, ('dp', 'seq'), pairs)]
    ppermute x11, starting transfers between devices: 36.8 us -> 33.8 us  [swap(): return lax.ppermute(a, 'seq', SWAP)]
  transfers between devices with their start and end apart: 28 -> 28, of which waited for: 15 -> 13; matrix products, arithmetic and copies ran while one was open for 2% -> 2% of each run, Pallas kernels for 8% -> 9%
where the time goes in v5:
time: 221 us; the launch traced here: 219 us
  starting transfers between devices  111 us (50%)
  waiting for transfers between devices  60.8 us (28%)
  Pallas kernels  36.2 us (16%)
  local copies, waits for them, and re-layouts  7.82 us (4%)
  other arithmetic  2.48 us (1%)
    ppermute x13, starting transfers between devices, move(): return lax.ppermute(a, ('dp', 'seq'), pairs)  51.7 us
    pallas_call x6, Pallas kernels, call(): pl.pallas_call(kernel, out_shape=[jax.ShapeDtypeStruct(s, t) for s, t in...  36.2 us
    ppermute x11, starting transfers between devices, swap(): return lax.ppermute(a, 'seq', SWAP)  33.8 us
    ppermute x13, waiting for transfers between devices, move(): return lax.ppermute(a, ('dp', 'seq'), pairs)  31.1 us
    all_to_all x1, waiting for transfers between devices, per_device(): lax.all_to_all(total.reshape(16, 9, D), 'dp', 0, 0, axis_index_groups=GRO...  14.7 us
    all_to_all x2, starting transfers between devices, turn(): return lax.all_to_all(parts, 'seq', 0, 0, tiled=True).reshape(TOKENS, 2 * D)  9.98 us
    all_to_all x1, waiting for transfers between devices, spread(): lax.all_to_all(jnp.broadcast_to(block[None], (count,) + block.shape), axi...  9.88 us
    all_to_all x1, starting transfers between devices, per_device(): lax.all_to_all(total.reshape(16, 9, D), 'dp', 0, 0, axis_index_groups=GRO...  9.53 us
  transfers between devices with their start and end apart: 28, of which 13 were waited for; matrix products, arithmetic and copies ran while one was open for 2% of the time, Pallas kernels for 9%

profile of v5, /device:TPU:1, one launch (start us, length us, event | category | flops | bytes accessed | tf_op | source)
XLA Modules:
  0.0 219.1 jit_solution(13713492585641054247)
XLA Ops:
  1.2 2.9 %shard_map.85 = (bf16[72,1152]{1,0:T(8,128)(2,1)}, bf16[36,1152]{1,0:T(8,128)(2,1)}, bf16[72,1152]{1,0:T(8,128)(2,1)}, bf16[36,1152]{1,0:T(8,128)(2,1)}) custom-call(s32[4]{0:T(128)} %pad_add_fusion.at_ref, bf16[3,36,576]{2,1,0:T(8,128)(2,1)} %refs_0_.1, bf16[18,1152]{1,0:T(8,128)(2,1)} %refs_1_.1, bf16[3,36,576]{2,1,0:T(8,128)(2,1)} %refs_2_.1, ...), custom_call_target="tpu_custom_call" | custom-call | flops 2200000000 | bytes 3000000 | tf_op jit(solution)/shard_map/pallas_call | solution.py:351
  4.2 11.5 %collective-permute-start = (bf16[72,1152]{1,0:T(8,128)(2,1)}, bf16[72,1152]{1,0:T(8,128)(2,1)S(1)}, u32[]{:S(2)}, u32[]{:S(2)}) collective-permute-start(bf16[72,1152]{1,0:T(8,128)(2,1)} %get-tuple-element.38.own_ref), channel_id=1, source_target_pairs={{0,16},{1,49},{2,18},{3,51},{4,20},{5,53},{6,22},{7,55},{8,24},{9,... | collective-permute-start | bytes 497672 | tf_op jit(solution)/shard_map/ppermute | solution.py:413
  15.7 1.9 collective-permute-start.1
  17.6 8.0 %collective-permute-done.1.far_ref = bf16[36,1152]{1,0:T(8,128)(2,1)S(1)} collective-permute-done((bf16[36,1152]{1,0:T(8,128)(2,1)}, bf16[36,1152]{1,0:T(8,128)(2,1)S(1)}, u32[]{:S(2)}, u32[]{:S(2)}) %collective-permute-start.1) | collective-permute-done | bytes 82976 | tf_op jit(solution)/shard_map/ppermute | solution.py:413
  25.6 2.1 collective-permute-start.2
  27.7 1.5 collective-permute-done.2.other_ref
  29.9 2.4 %shard_map.86.refs_0_ = bf16[288,1152]{1,0:T(8,128)(2,1)} custom-call(s32[4]{0:T(128)} %pad_add_fusion.at_ref, bf16[72,1152]{1,0:T(8,128)(2,1)} %get-tuple-element.38.own_ref, bf16[72,1152]{1,0:T(8,128)(2,1)} %copy-done.6, bf16[36,1152]{1,0:T(8,128)(2,1)} %copy-done.8, bf16[108,1152]{1,0:T(8,128)(2,1)} %copy-done.20), custom_call_target="tpu_custom_call" | custom-call | flops 2200000000 | bytes 3000000 | tf_op jit(solution)/shard_map/pallas_call | solution.py:351
  32.3 7.2 %collective-permute-start.3 = (bf16[288,1152]{1,0:T(8,128)(2,1)}, bf16[288,1152]{1,0:T(8,128)(2,1)S(1)}, u32[]{:S(2)}, u32[]{:S(2)}) collective-permute-start(bf16[288,1152]{1,0:T(8,128)(2,1)} %shard_map.86.refs_0_), channel_id=1, source_target_pairs={{0,64},{1,449},{2,66},{3,451},{4,68},{5,453},{6,70},{7,455},{8,72}... | collective-permute-start | bytes 1990664 | tf_op jit(solution)/shard_map/ppermute | solution.py:413
  39.5 3.3 %collective-permute-start.7 = (bf16[36,1152]{1,0:T(8,128)(2,1)S(1)}, bf16[36,1152]{1,0:T(8,128)(2,1)S(1)}, u32[]{:S(2)}, u32[]{:S(2)}) collective-permute-start(bf16[36,1152]{1,0:T(8,128)(2,1)S(1)} %copy-done.23), channel_id=1, source_target_pairs={{0,32},{1,33},{2,34},{3,35},{4,36},{5,37},{6,38},{7,39},{8,40},{9,... | collective-permute-start | bytes 248840 | tf_op jit(solution)/shard_map/ppermute | solution.py:413
  42.8 4.1 %collective-permute-start.6 = (bf16[72,1152]{1,0:T(8,128)(2,1)S(1)}, bf16[72,1152]{1,0:T(8,128)(2,1)S(1)}, u32[]{:S(2)}, u32[]{:S(2)}) collective-permute-start(bf16[72,1152]{1,0:T(8,128)(2,1)S(1)} %copy-done.22), channel_id=1, source_target_pairs={{0,16},{1,49},{2,18},{3,51},{4,20},{5,53},{6,22},{7,55},{8,24},{9,... | collective-permute-start | bytes 497672 | tf_op jit(solution)/shard_map/ppermute | solution.py:413
  47.0 1.1 fusion.order_hbm
  48.1 2.5 %collective-permute-start.5 = (bf16[288,1152]{1,0:T(8,128)(2,1)S(1)}, bf16[288,1152]{1,0:T(8,128)(2,1)S(1)}, u32[]{:S(2)}, u32[]{:S(2)}) collective-permute-start(bf16[288,1152]{1,0:T(8,128)(2,1)S(1)} %collective-permute-done.3.refs_1_), channel_id=1, source_target_pairs={{0,1},{1,0},{2,3},{3,2},{4,5},{5,4},{6,7},{7,6},{8,9},{9,8},{10,11... | collective-permute-start | bytes 1990664 | tf_op jit(solution)/shard_map/ppermute | solution.py:442
  50.6 3.9 %collective-permute-start.4 = (bf16[288,1152]{1,0:T(8,128)(2,1)S(1)}, bf16[288,1152]{1,0:T(8,128)(2,1)}, u32[]{:S(2)}, u32[]{:S(2)}) collective-permute-start(bf16[288,1152]{1,0:T(8,128)(2,1)S(1)} %collective-permute-done.3.refs_1_), channel_id=1, source_target_pairs={{0,64},{1,449},{2,66},{3,451},{4,68},{5,453},{6,70},{7,455},{8,72}... | collective-permute-start | bytes 1990664 | tf_op jit(solution)/shard_map/ppermute | solution.py:413
  54.6 1.9 collective-permute-start.8
  56.5 1.5 collective-permute-done.8.other_ref
  58.7 2.4 %shard_map.87.refs_0_ = bf16[288,1152]{1,0:T(8,128)(2,1)} custom-call(s32[4]{0:T(128)} %pad_add_fusion.at_ref, bf16[72,1152]{1,0:T(8,128)(2,1)} %get-tuple-element.46.own_ref, bf16[72,1152]{1,0:T(8,128)(2,1)} %copy-done.5, bf16[36,1152]{1,0:T(8,128)(2,1)} %copy-done.7, bf16[108,1152]{1,0:T(8,128)(2,1)} %copy-done.21), custom_call_target="tpu_custom_call" | custom-call | flops 2200000000 | bytes 3000000 | tf_op jit(solution)/shard_map/pallas_call | solution.py:351
  61.1 1.3 collective-permute-done.4.refs_2_
  62.4 4.0 %collective-permute-start.10 = (bf16[288,1152]{1,0:T(8,128)(2,1)}, bf16[288,1152]{1,0:T(8,128)(2,1)S(1)}, u32[]{:S(2)}, u32[]{:S(2)}) collective-permute-start(bf16[288,1152]{1,0:T(8,128)(2,1)} %collective-permute-done.4.refs_2_), channel_id=1, source_target_pairs={{0,1},{1,0},{2,3},{3,2},{4,5},{5,4},{6,7},{7,6},{8,9},{9,8},{10,11... | collective-permute-start | bytes 1990664 | tf_op jit(solution)/shard_map/ppermute | solution.py:442
  66.4 3.1 %collective-permute-start.9 = (bf16[288,1152]{1,0:T(8,128)(2,1)}, bf16[288,1152]{1,0:T(8,128)(2,1)S(1)}, u32[]{:S(2)}, u32[]{:S(2)}) collective-permute-start(bf16[288,1152]{1,0:T(8,128)(2,1)} %collective-permute-done.4.refs_2_), channel_id=1, source_target_pairs={{0,64},{1,449},{2,66},{3,451},{4,68},{5,453},{6,70},{7,455},{8,72}... | collective-permute-start | bytes 1990664 | tf_op jit(solution)/shard_map/ppermute | solution.py:413
  69.6 2.3 %collective-permute-start.14 = (bf16[288,1152]{1,0:T(8,128)(2,1)}, bf16[288,1152]{1,0:T(8,128)(2,1)S(1)}, u32[]{:S(2)}, u32[]{:S(2)}) collective-permute-start(bf16[288,1152]{1,0:T(8,128)(2,1)} %shard_map.87.refs_0_), channel_id=1, source_target_pairs={{0,64},{1,449},{2,66},{3,451},{4,68},{5,453},{6,70},{7,455},{8,72}... | collective-permute-start | bytes 1990664 | tf_op jit(solution)/shard_map/ppermute | solution.py:413
  71.9 6.5 %collective-permute-done.9.refs_3_ = bf16[288,1152]{1,0:T(8,128)(2,1)S(1)} collective-permute-done((bf16[288,1152]{1,0:T(8,128)(2,1)}, bf16[288,1152]{1,0:T(8,128)(2,1)S(1)}, u32[]{:S(2)}, u32[]{:S(2)}) %collective-permute-start.9) | collective-permute-done | bytes 663584 | tf_op jit(solution)/shard_map/ppermute | solution.py:413
  78.4 4.0 %collective-permute-start.12 = (bf16[288,1152]{1,0:T(8,128)(2,1)S(1)}, bf16[288,1152]{1,0:T(8,128)(2,1)S(1)}, u32[]{:S(2)}, u32[]{:S(2)}) collective-permute-start(bf16[288,1152]{1,0:T(8,128)(2,1)S(1)} %collective-permute-done.9.refs_3_), channel_id=1, source_target_pairs={{0,1},{1,0},{2,3},{3,2},{4,5},{5,4},{6,7},{7,6},{8,9},{9,8},{10,11... | collective-permute-start | bytes 1990664 | tf_op jit(solution)/shard_map/ppermute | solution.py:442
  82.4 2.0 collective-permute-start.11
  84.4 1.1 collective-permute-done.14.refs_1_
  85.5 4.0 %collective-permute-start.16 = (bf16[288,1152]{1,0:T(8,128)(2,1)S(1)}, bf16[288,1152]{1,0:T(8,128)(2,1)S(1)}, u32[]{:S(2)}, u32[]{:S(2)}) collective-permute-start(bf16[288,1152]{1,0:T(8,128)(2,1)S(1)} %collective-permute-done.14.refs_1_), channel_id=1, source_target_pairs={{0,1},{1,0},{2,3},{3,2},{4,5},{5,4},{6,7},{7,6},{8,9},{9,8},{10,11... | collective-permute-start | bytes 1990664 | tf_op jit(solution)/shard_map/ppermute | solution.py:442
  89.4 2.0 collective-permute-start.15
  92.4 3.0 %collective-permute-start.13 = (bf16[144,1152]{1,0:T(8,128)(2,1)S(1)}, bf16[144,1152]{1,0:T(8,128)(2,1)S(1)}, u32[]{:S(2)}, u32[]{:S(2)}) collective-permute-start(bf16[144,1152]{1,0:T(8,128)(2,1)S(1)} %collective-permute-done.11.refs_7_), channel_id=1, source_target_pairs={{0,1},{1,0},{2,3},{3,2},{4,5},{5,4},{6,7},{7,6},{8,9},{9,8},{10,11... | collective-permute-start | bytes 995336 | tf_op jit(solution)/shard_map/ppermute | solution.py:442
  95.4 5.8 %collective-permute-done.15.refs_2_ = bf16[288,1152]{1,0:T(8,128)(2,1)} collective-permute-done((bf16[288,1152]{1,0:T(8,128)(2,1)S(1)}, bf16[288,1152]{1,0:T(8,128)(2,1)}, u32[]{:S(2)}, u32[]{:S(2)}) %collective-permute-start.15) | collective-permute-done | bytes 663584 | tf_op jit(solution)/shard_map/ppermute | solution.py:413
  101.3 4.0 %collective-permute-start.18 = (bf16[288,1152]{1,0:T(8,128)(2,1)}, bf16[288,1152]{1,0:T(8,128)(2,1)}, u32[]{:S(2)}, u32[]{:S(2)}) collective-permute-start(bf16[288,1152]{1,0:T(8,128)(2,1)} %collective-permute-done.15.refs_2_), channel_id=1, source_target_pairs={{0,1},{1,0},{2,3},{3,2},{4,5},{5,4},{6,7},{7,6},{8,9},{9,8},{10,11... | collective-permute-start | bytes 1990664 | tf_op jit(solution)/shard_map/ppermute | solution.py:442
  105.3 1.9 collective-permute-start.17
  107.2 8.6 %shard_map.88 = (bf16[128,2304]{1,0:T(8,128)(2,1)}, bf16[3,128,640]{2,1,0:T(8,128)(2,1)}, f32[8,128,128]{2,1,0:T(8,128)}, bf16[128,640]{1,0:T(8,128)(2,1)}) custom-call(s32[4]{0:T(128)} %pad_add_fusion.at_ref, bf16[128,1152]{1,0:T(8,128)(2,1)} %bitcast.21, bf16[128,1152]{1,0:T(8,128)(2,1)} %bitcast.20, bf16[288,1152]{1,0:T(8,128)(2,1)} %shard_map.86.refs_0_, ...), custom_call_target="tpu_custom_call" | custom-call | flops 8800000000 | bytes 3000000 | tf_op jit(solution)/shard_map/pallas_call | solution.py:351
  115.8 4.5 %all-to-all-start = ((bf16[16,8,2304]{2,1,0:T(8,128)(2,1)}), bf16[16,8,2304]{2,1,0:T(8,128)(2,1)S(1)}, u32[]{:S(2)}, u32[]{:S(2)}) async-start(bf16[16,8,2304]{2,1,0:T(8,128)(2,1)} %bitcast.19), calls=%async_computation | async-start | bytes 1179648 | tf_op jit(solution)/shard_map/all_to_all | solution.py:430
  120.3 2.0 collective-permute-start.20
  123.3 4.7 %collective-permute-start.19 = (bf16[144,1152]{1,0:T(8,128)(2,1)S(1)}, bf16[144,1152]{1,0:T(8,128)(2,1)S(1)}, u32[]{:S(2)}, u32[]{:S(2)}) collective-permute-start(bf16[144,1152]{1,0:T(8,128)(2,1)S(1)} %constant_dynamic-slice_fusion), channel_id=1, source_target_pairs={{0,64},{1,449},{2,66},{3,451},{4,68},{5,453},{6,70},{7,455},{8,72}... | collective-permute-start | bytes 995336 | tf_op jit(solution)/shard_map/ppermute | solution.py:413
  128.1 4.0 %collective-permute-done.19.refs_7_ = bf16[144,1152]{1,0:T(8,128)(2,1)S(1)} collective-permute-done((bf16[144,1152]{1,0:T(8,128)(2,1)S(1)}, bf16[144,1152]{1,0:T(8,128)(2,1)S(1)}, u32[]{:S(2)}, u32[]{:S(2)}) %collective-permute-start.19) | collective-permute-done | bytes 331808 | tf_op jit(solution)/shard_map/ppermute | solution.py:413
  132.1 3.9 %collective-permute-start.21 = (bf16[144,1152]{1,0:T(8,128)(2,1)S(1)}, bf16[144,1152]{1,0:T(8,128)(2,1)S(1)}, u32[]{:S(2)}, u32[]{:S(2)}) collective-permute-start(bf16[144,1152]{1,0:T(8,128)(2,1)S(1)} %collective-permute-done.19.refs_7_), channel_id=1, source_target_pairs={{0,1},{1,0},{2,3},{3,2},{4,5},{5,4},{6,7},{7,6},{8,9},{9,8},{10,11... | collective-permute-start | bytes 995336 | tf_op jit(solution)/shard_map/ppermute | solution.py:442
  136.1 1.0 collective-permute-done.21.refs_8_
  137.9 12.2 %shard_map.89 = (bf16[128,2304]{1,0:T(8,128)(2,1)}, bf16[288,1152]{1,0:T(8,128)(2,1)}, bf16[288,1152]{1,0:T(8,128)(2,1)}) custom-call(s32[4]{0:T(128)} %pad_add_fusion.at_ref, bf16[128,2304]{1,0:T(8,128)(2,1)} %bitcast.17, bf16[640,640]{1,0:T(8,128)(2,1)} %fusion.order_hbm, bf16[288,1152]{1,0:T(8,128)(2,1)} %shard_map.87.refs_0_, ...), custom_call_target="tpu_custom_call" | custom-call | flops 13200000000 | bytes 3000000 | tf_op jit(solution)/shard_map/pallas_call | solution.py:351
  150.1 2.4 %collective-permute-start.22 = (bf16[288,1152]{1,0:T(8,128)(2,1)}, bf16[288,1152]{1,0:T(8,128)(2,1)S(1)}, u32[]{:S(2)}, u32[]{:S(2)}) collective-permute-start(bf16[288,1152]{1,0:T(8,128)(2,1)} %get-tuple-element.67), channel_id=1, source_target_pairs={{0,1},{1,0},{2,3},{3,2},{4,5},{5,4},{6,7},{7,6},{8,9},{9,8},{10,11... | collective-permute-start | bytes 1990664 | tf_op jit(solution)/shard_map/ppermute | solution.py:442
  152.5 5.5 %all-to-all-start.1 = ((bf16[16,8,2304]{2,1,0:T(8,128)(2,1)}), bf16[16,8,2304]{2,1,0:T(8,128)(2,1)S(1)}, u32[]{:S(2)}, u32[]{:S(2)}) async-start(bf16[16,8,2304]{2,1,0:T(8,128)(2,1)} %bitcast.18), calls=%async_computation.1 | async-start | bytes 1179648 | tf_op jit(solution)/shard_map/all_to_all | solution.py:430
  158.2 3.8 %collective-permute-start.23 = (bf16[144,1152]{1,0:T(8,128)(2,1)S(1)}, bf16[144,1152]{1,0:T(8,128)(2,1)S(1)}, u32[]{:S(2)}, u32[]{:S(2)}) collective-permute-start(bf16[144,1152]{1,0:T(8,128)(2,1)S(1)} %slice.14), channel_id=1, source_target_pairs={{0,64},{1,449},{2,66},{3,451},{4,68},{5,453},{6,70},{7,455},{8,72}... | collective-permute-start | bytes 995336 | tf_op jit(solution)/shard_map/ppermute | solution.py:413
  162.0 4.4 %collective-permute-done.23 = bf16[144,1152]{1,0:T(8,128)(2,1)S(1)} collective-permute-done((bf16[144,1152]{1,0:T(8,128)(2,1)S(1)}, bf16[144,1152]{1,0:T(8,128)(2,1)S(1)}, u32[]{:S(2)}, u32[]{:S(2)}) %collective-permute-start.23) | collective-permute-done | bytes 331808 | tf_op jit(solution)/shard_map/ppermute | solution.py:413
  167.5 1.1 all-to-all-done.1
  168.5 9.5 %all-to-all-start.2 = ((bf16[16,9,1152]{2,1,0:T(8,128)(2,1)}), bf16[16,9,1152]{2,1,0:T(8,128)(2,1)S(1)}, u32[]{:S(2)}, u32[]{:S(2)}) async-start(bf16[16,9,1152]{2,1,0:T(8,128)(2,1)} %reshape.130), calls=%async_computation.2 | async-start | bytes 1179648 | tf_op jit(solution)/shard_map/all_to_all | solution.py:518
  178.1 7.8 %shard_map.90 = bf16[128,1152]{1,0:T(8,128)(2,1)} custom-call(s32[4]{0:T(128)} %pad_add_fusion.at_ref, bf16[128,1152]{1,0:T(8,128)(2,1)} %bitcast.22, bf16[128,2304]{1,0:T(8,128)(2,1)} %bitcast.15, bf16[3,128,640]{2,1,0:T(8,128)(2,1)} %get-tuple-element.68.qkv_hbm, f32[8,128,128]{2,1,0:T(8,128)} %get-tuple-element.69.probs_hbm, ...), custom_call_target="tpu_custom_call" | custom-call | flops 9900000256 | bytes 3000000 | tf_op jit(solution)/shard_map/pallas_call | solution.py:351
  185.9 14.7 %all-to-all-done.2 = bf16[16,9,1152]{2,1,0:T(8,128)(2,1)S(1)} async-done(((bf16[16,9,1152]{2,1,0:T(8,128)(2,1)}), bf16[16,9,1152]{2,1,0:T(8,128)(2,1)S(1)}, u32[]{:S(2)}, u32[]{:S(2)}) %all-to-all-start.2) | async-done | bytes 331808 | tf_op jit(solution)/shard_map/all_to_all | solution.py:518
  201.6 5.5 %all-to-all-start.3 = ((bf16[16,9,1152]{2,1,0:T(8,128)(2,1)}), bf16[16,9,1152]{2,1,0:T(8,128)(2,1)S(1)}, u32[]{:S(2)}, u32[]{:S(2)}) async-start(bf16[16,9,1152]{2,1,0:T(8,128)(2,1)} %broadcast_in_dim.30), calls=%async_computation.3 | async-start | bytes 1179648 | tf_op jit(solution)/shard_map/all_to_all | solution.py:383
  207.8 9.9 %all-to-all-done.3 = bf16[16,9,1152]{2,1,0:T(8,128)(2,1)S(1)} async-done(((bf16[16,9,1152]{2,1,0:T(8,128)(2,1)}), bf16[16,9,1152]{2,1,0:T(8,128)(2,1)S(1)}, u32[]{:S(2)}, u32[]{:S(2)}) %all-to-all-start.3) | async-done | bytes 331808 | tf_op jit(solution)/shard_map/all_to_all | solution.py:383
  (81 shorter events, 9.2 us)
Async XLA Ops:
  4.2 21.4 %collective-permute-start = (bf16[72,1152]{1,0:T(8,128)(2,1)}, bf16[72,1152]{1,0:T(8,128)(2,1)S(1)}, u32[]{:S(2)}, u32[]{:S(2)}) collective-permute-start(bf16[72,1152]{1,0:T(8,128)(2,1)} %get-tuple-element.38.own_ref), channel_id=1, source_target_pairs={{0,16},{1,49},{2,18},{3,51},{4,20},{5,53},{6,22},{7,55},{8,24},{9,... | collective-permute-start | bytes 497672 | tf_op jit(solution)/shard_map/ppermute | solution.py:413
  15.7 9.9 %collective-permute-start.1 = (bf16[36,1152]{1,0:T(8,128)(2,1)}, bf16[36,1152]{1,0:T(8,128)(2,1)S(1)}, u32[]{:S(2)}, u32[]{:S(2)}) collective-permute-start(bf16[36,1152]{1,0:T(8,128)(2,1)} %get-tuple-element.39), channel_id=1, source_target_pairs={{0,32},{1,33},{2,34},{3,35},{4,36},{5,37},{6,38},{7,39},{8,40},{9,... | collective-permute-start | bytes 248840 | tf_op jit(solution)/shard_map/ppermute | solution.py:413
  25.6 3.6 %copy-start.8 = (bf16[36,1152]{1,0:T(8,128)(2,1)}, bf16[36,1152]{1,0:T(8,128)(2,1)S(1)}, u32[]{:S(2)}) copy-start(bf16[36,1152]{1,0:T(8,128)(2,1)S(1)} %collective-permute-done.1.far_ref) | copy-start | bytes 248836
  25.6 3.6 %copy-start.6 = (bf16[72,1152]{1,0:T(8,128)(2,1)}, bf16[72,1152]{1,0:T(8,128)(2,1)S(1)}, u32[]{:S(2)}) copy-start(bf16[72,1152]{1,0:T(8,128)(2,1)S(1)} %collective-permute-done.next_ref) | copy-start | bytes 497668
  25.6 13.9 %copy-start.23 = (bf16[36,1152]{1,0:T(8,128)(2,1)S(1)}, bf16[36,1152]{1,0:T(8,128)(2,1)}, u32[]{:S(2)}) copy-start(bf16[36,1152]{1,0:T(8,128)(2,1)} %get-tuple-element.47) | copy-start | bytes 248836
  25.6 17.2 %copy-start.22 = (bf16[72,1152]{1,0:T(8,128)(2,1)S(1)}, bf16[72,1152]{1,0:T(8,128)(2,1)}, u32[]{:S(2)}) copy-start(bf16[72,1152]{1,0:T(8,128)(2,1)} %get-tuple-element.46.own_ref) | copy-start | bytes 497668
  25.6 3.6 %collective-permute-start.2 = (bf16[108,1152]{1,0:T(8,128)(2,1)S(1)}, bf16[108,1152]{1,0:T(8,128)(2,1)S(1)}, u32[]{:S(2)}, u32[]{:S(2)}) collective-permute-start(bf16[108,1152]{1,0:T(8,128)(2,1)S(1)} %pad_maximum_fusion), channel_id=1, source_target_pairs={{0,1},{1,0},{2,3},{3,2},{4,5},{5,4},{6,7},{7,6},{8,9},{9,8},{10,11... | collective-permute-start | bytes 746504 | tf_op jit(solution)/shard_map/ppermute | solution.py:442
  32.3 15.8 %collective-permute-start.3 = (bf16[288,1152]{1,0:T(8,128)(2,1)}, bf16[288,1152]{1,0:T(8,128)(2,1)S(1)}, u32[]{:S(2)}, u32[]{:S(2)}) collective-permute-start(bf16[288,1152]{1,0:T(8,128)(2,1)} %shard_map.86.refs_0_), channel_id=1, source_target_pairs={{0,64},{1,449},{2,66},{3,451},{4,68},{5,453},{6,70},{7,455},{8,72}... | collective-permute-start | bytes 1990664 | tf_op jit(solution)/shard_map/ppermute | solution.py:413
  39.5 15.0 %collective-permute-start.7 = (bf16[36,1152]{1,0:T(8,128)(2,1)S(1)}, bf16[36,1152]{1,0:T(8,128)(2,1)S(1)}, u32[]{:S(2)}, u32[]{:S(2)}) collective-permute-start(bf16[36,1152]{1,0:T(8,128)(2,1)S(1)} %copy-done.23), channel_id=1, source_target_pairs={{0,32},{1,33},{2,34},{3,35},{4,36},{5,37},{6,38},{7,39},{8,40},{9,... | collective-permute-start | bytes 248840 | tf_op jit(solution)/shard_map/ppermute | solution.py:413
  42.8 11.7 %collective-permute-start.6 = (bf16[72,1152]{1,0:T(8,128)(2,1)S(1)}, bf16[72,1152]{1,0:T(8,128)(2,1)S(1)}, u32[]{:S(2)}, u32[]{:S(2)}) collective-permute-start(bf16[72,1152]{1,0:T(8,128)(2,1)S(1)} %copy-done.22), channel_id=1, source_target_pairs={{0,16},{1,49},{2,18},{3,51},{4,20},{5,53},{6,22},{7,55},{8,24},{9,... | collective-permute-start | bytes 497672 | tf_op jit(solution)/shard_map/ppermute | solution.py:413
  48.1 13.0 %copy-start.9 = (bf16[288,1152]{1,0:T(8,128)(2,1)}, bf16[288,1152]{1,0:T(8,128)(2,1)S(1)}, u32[]{:S(2)}) copy-start(bf16[288,1152]{1,0:T(8,128)(2,1)S(1)} %collective-permute-done.3.refs_1_) | copy-start | bytes 1990660
  48.1 13.0 %collective-permute-start.5 = (bf16[288,1152]{1,0:T(8,128)(2,1)S(1)}, bf16[288,1152]{1,0:T(8,128)(2,1)S(1)}, u32[]{:S(2)}, u32[]{:S(2)}) collective-permute-start(bf16[288,1152]{1,0:T(8,128)(2,1)S(1)} %collective-permute-done.3.refs_1_), channel_id=1, source_target_pairs={{0,1},{1,0},{2,3},{3,2},{4,5},{5,4},{6,7},{7,6},{8,9},{9,8},{10,11... | collective-permute-start | bytes 1990664 | tf_op jit(solution)/shard_map/ppermute | solution.py:442
  50.6 11.8 %collective-permute-start.4 = (bf16[288,1152]{1,0:T(8,128)(2,1)S(1)}, bf16[288,1152]{1,0:T(8,128)(2,1)}, u32[]{:S(2)}, u32[]{:S(2)}) collective-permute-start(bf16[288,1152]{1,0:T(8,128)(2,1)S(1)} %collective-permute-done.3.refs_1_), channel_id=1, source_target_pairs={{0,64},{1,449},{2,66},{3,451},{4,68},{5,453},{6,70},{7,455},{8,72}... | collective-permute-start | bytes 1990664 | tf_op jit(solution)/shard_map/ppermute | solution.py:413
  54.5 3.5 %copy-start.7 = (bf16[36,1152]{1,0:T(8,128)(2,1)}, bf16[36,1152]{1,0:T(8,128)(2,1)S(1)}, u32[]{:S(2)}) copy-start(bf16[36,1152]{1,0:T(8,128)(2,1)S(1)} %collective-permute-done.7.far_ref) | copy-start | bytes 248836
  54.5 3.5 %copy-start.5 = (bf16[72,1152]{1,0:T(8,128)(2,1)}, bf16[72,1152]{1,0:T(8,128)(2,1)S(1)}, u32[]{:S(2)}) copy-start(bf16[72,1152]{1,0:T(8,128)(2,1)S(1)} %collective-permute-done.6.next_ref) | copy-start | bytes 497668
  54.6 3.4 %collective-permute-start.8 = (bf16[108,1152]{1,0:T(8,128)(2,1)S(1)}, bf16[108,1152]{1,0:T(8,128)(2,1)S(1)}, u32[]{:S(2)}, u32[]{:S(2)}) collective-permute-start(bf16[108,1152]{1,0:T(8,128)(2,1)S(1)} %pad_maximum_fusion.1), channel_id=1, source_target_pairs={{0,1},{1,0},{2,3},{3,2},{4,5},{5,4},{6,7},{7,6},{8,9},{9,8},{10,11... | collective-permute-start | bytes 746504 | tf_op jit(solution)/shard_map/ppermute | solution.py:442
  61.1 1.4 copy-start.10
  62.4 9.4 %collective-permute-start.10 = (bf16[288,1152]{1,0:T(8,128)(2,1)}, bf16[288,1152]{1,0:T(8,128)(2,1)S(1)}, u32[]{:S(2)}, u32[]{:S(2)}) collective-permute-start(bf16[288,1152]{1,0:T(8,128)(2,1)} %collective-permute-done.4.refs_2_), channel_id=1, source_target_pairs={{0,1},{1,0},{2,3},{3,2},{4,5},{5,4},{6,7},{7,6},{8,9},{9,8},{10,11... | collective-permute-start | bytes 1990664 | tf_op jit(solution)/shard_map/ppermute | solution.py:442
  66.4 11.9 %collective-permute-start.9 = (bf16[288,1152]{1,0:T(8,128)(2,1)}, bf16[288,1152]{1,0:T(8,128)(2,1)S(1)}, u32[]{:S(2)}, u32[]{:S(2)}) collective-permute-start(bf16[288,1152]{1,0:T(8,128)(2,1)} %collective-permute-done.4.refs_2_), channel_id=1, source_target_pairs={{0,64},{1,449},{2,66},{3,451},{4,68},{5,453},{6,70},{7,455},{8,72}... | collective-permute-start | bytes 1990664 | tf_op jit(solution)/shard_map/ppermute | solution.py:413
  69.6 15.9 %collective-permute-start.14 = (bf16[288,1152]{1,0:T(8,128)(2,1)}, bf16[288,1152]{1,0:T(8,128)(2,1)S(1)}, u32[]{:S(2)}, u32[]{:S(2)}) collective-permute-start(bf16[288,1152]{1,0:T(8,128)(2,1)} %shard_map.87.refs_0_), channel_id=1, source_target_pairs={{0,64},{1,449},{2,66},{3,451},{4,68},{5,453},{6,70},{7,455},{8,72}... | collective-permute-start | bytes 1990664 | tf_op jit(solution)/shard_map/ppermute | solution.py:413
  71.9 35.4 %copy-start.11 = (bf16[288,1152]{1,0:T(8,128)(2,1)}, bf16[288,1152]{1,0:T(8,128)(2,1)S(1)}, u32[]{:S(2)}) copy-start(bf16[288,1152]{1,0:T(8,128)(2,1)S(1)} %collective-permute-done.10.refs_5_) | copy-start | bytes 1990660
  78.4 28.9 %copy-start.4 = (bf16[288,1152]{1,0:T(8,128)(2,1)}, bf16[288,1152]{1,0:T(8,128)(2,1)S(1)}, u32[]{:S(2)}) copy-start(bf16[288,1152]{1,0:T(8,128)(2,1)S(1)} %collective-permute-done.9.refs_3_) | copy-start | bytes 1990660
  78.4 13.1 %collective-permute-start.12 = (bf16[288,1152]{1,0:T(8,128)(2,1)S(1)}, bf16[288,1152]{1,0:T(8,128)(2,1)S(1)}, u32[]{:S(2)}, u32[]{:S(2)}) collective-permute-start(bf16[288,1152]{1,0:T(8,128)(2,1)S(1)} %collective-permute-done.9.refs_3_), channel_id=1, source_target_pairs={{0,1},{1,0},{2,3},{3,2},{4,5},{5,4},{6,7},{7,6},{8,9},{9,8},{10,11... | collective-permute-start | bytes 1990664 | tf_op jit(solution)/shard_map/ppermute | solution.py:442
  82.4 9.1 %collective-permute-start.11 = (bf16[144,1152]{1,0:T(8,128)(2,1)S(1)}, bf16[144,1152]{1,0:T(8,128)(2,1)S(1)}, u32[]{:S(2)}, u32[]{:S(2)}) collective-permute-start(bf16[144,1152]{1,0:T(8,128)(2,1)S(1)} %constant_dynamic-slice_fusion.1), channel_id=1, source_target_pairs={{0,64},{1,449},{2,66},{3,451},{4,68},{5,453},{6,70},{7,455},{8,72}... | collective-permute-start | bytes 995336 | tf_op jit(solution)/shard_map/ppermute | solution.py:413
  85.5 30.4 %copy-start.13 = (bf16[288,1152]{1,0:T(8,128)(2,1)}, bf16[288,1152]{1,0:T(8,128)(2,1)S(1)}, u32[]{:S(2)}) copy-start(bf16[288,1152]{1,0:T(8,128)(2,1)S(1)} %collective-permute-done.14.refs_1_) | copy-start | bytes 1990660
  85.5 9.9 %collective-permute-start.16 = (bf16[288,1152]{1,0:T(8,128)(2,1)S(1)}, bf16[288,1152]{1,0:T(8,128)(2,1)S(1)}, u32[]{:S(2)}, u32[]{:S(2)}) collective-permute-start(bf16[288,1152]{1,0:T(8,128)(2,1)S(1)} %collective-permute-done.14.refs_1_), channel_id=1, source_target_pairs={{0,1},{1,0},{2,3},{3,2},{4,5},{5,4},{6,7},{7,6},{8,9},{9,8},{10,11... | collective-permute-start | bytes 1990664 | tf_op jit(solution)/shard_map/ppermute | solution.py:442
  89.4 11.8 %collective-permute-start.15 = (bf16[288,1152]{1,0:T(8,128)(2,1)S(1)}, bf16[288,1152]{1,0:T(8,128)(2,1)}, u32[]{:S(2)}, u32[]{:S(2)}) collective-permute-start(bf16[288,1152]{1,0:T(8,128)(2,1)S(1)} %collective-permute-done.14.refs_1_), channel_id=1, source_target_pairs={{0,64},{1,449},{2,66},{3,451},{4,68},{5,453},{6,70},{7,455},{8,72}... | collective-permute-start | bytes 1990664 | tf_op jit(solution)/shard_map/ppermute | solution.py:413
  91.5 9.8 %copy-start.16 = (bf16[144,1152]{1,0:T(8,128)(2,1)}, bf16[144,1152]{1,0:T(8,128)(2,1)S(1)}, u32[]{:S(2)}) copy-start(bf16[144,1152]{1,0:T(8,128)(2,1)S(1)} %collective-permute-done.11.refs_7_) | copy-start | bytes 995332
  92.4 8.9 %collective-permute-start.13 = (bf16[144,1152]{1,0:T(8,128)(2,1)S(1)}, bf16[144,1152]{1,0:T(8,128)(2,1)S(1)}, u32[]{:S(2)}, u32[]{:S(2)}) collective-permute-start(bf16[144,1152]{1,0:T(8,128)(2,1)S(1)} %collective-permute-done.11.refs_7_), channel_id=1, source_target_pairs={{0,1},{1,0},{2,3},{3,2},{4,5},{5,4},{6,7},{7,6},{8,9},{9,8},{10,11... | collective-permute-start | bytes 995336 | tf_op jit(solution)/shard_map/ppermute | solution.py:442
  95.4 5.8 %copy-start.14 = (bf16[288,1152]{1,0:T(8,128)(2,1)}, bf16[288,1152]{1,0:T(8,128)(2,1)S(1)}, u32[]{:S(2)}) copy-start(bf16[288,1152]{1,0:T(8,128)(2,1)S(1)} %collective-permute-done.16.refs_4_) | copy-start | bytes 1990660
  101.3 4.0 %copy-start.17 = (bf16[144,1152]{1,0:T(8,128)(2,1)}, bf16[144,1152]{1,0:T(8,128)(2,1)S(1)}, u32[]{:S(2)}) copy-start(bf16[144,1152]{1,0:T(8,128)(2,1)S(1)} %collective-permute-done.13.refs_8_) | copy-start | bytes 995332
  101.3 19.0 %collective-permute-start.18 = (bf16[288,1152]{1,0:T(8,128)(2,1)}, bf16[288,1152]{1,0:T(8,128)(2,1)}, u32[]{:S(2)}, u32[]{:S(2)}) collective-permute-start(bf16[288,1152]{1,0:T(8,128)(2,1)} %collective-permute-done.15.refs_2_), channel_id=1, source_target_pairs={{0,1},{1,0},{2,3},{3,2},{4,5},{5,4},{6,7},{7,6},{8,9},{9,8},{10,11... | collective-permute-start | bytes 1990664 | tf_op jit(solution)/shard_map/ppermute | solution.py:442
  105.3 15.0 %collective-permute-start.17 = (bf16[288,1152]{1,0:T(8,128)(2,1)}, bf16[288,1152]{1,0:T(8,128)(2,1)}, u32[]{:S(2)}, u32[]{:S(2)}) collective-permute-start(bf16[288,1152]{1,0:T(8,128)(2,1)} %collective-permute-done.15.refs_2_), channel_id=1, source_target_pairs={{0,64},{1,449},{2,66},{3,451},{4,68},{5,453},{6,70},{7,455},{8,72}... | collective-permute-start | bytes 1990664 | tf_op jit(solution)/shard_map/ppermute | solution.py:413
  115.8 20.2 %all-to-all-start = ((bf16[16,8,2304]{2,1,0:T(8,128)(2,1)}), bf16[16,8,2304]{2,1,0:T(8,128)(2,1)S(1)}, u32[]{:S(2)}, u32[]{:S(2)}) async-start(bf16[16,8,2304]{2,1,0:T(8,128)(2,1)} %bitcast.19), calls=%async_computation | async-start | bytes 1179648 | tf_op jit(solution)/shard_map/all_to_all | solution.py:430
  120.3 11.8 %collective-permute-start.20 = (bf16[288,1152]{1,0:T(8,128)(2,1)}, bf16[288,1152]{1,0:T(8,128)(2,1)S(1)}, u32[]{:S(2)}, u32[]{:S(2)}) collective-permute-start(bf16[288,1152]{1,0:T(8,128)(2,1)} %collective-permute-done.17.refs_3_), channel_id=1, source_target_pairs={{0,1},{1,0},{2,3},{3,2},{4,5},{5,4},{6,7},{7,6},{8,9},{9,8},{10,11... | collective-permute-start | bytes 1990664 | tf_op jit(solution)/shard_map/ppermute | solution.py:442
  123.3 8.8 %collective-permute-start.19 = (bf16[144,1152]{1,0:T(8,128)(2,1)S(1)}, bf16[144,1152]{1,0:T(8,128)(2,1)S(1)}, u32[]{:S(2)}, u32[]{:S(2)}) collective-permute-start(bf16[144,1152]{1,0:T(8,128)(2,1)S(1)} %constant_dynamic-slice_fusion), channel_id=1, source_target_pairs={{0,64},{1,449},{2,66},{3,451},{4,68},{5,453},{6,70},{7,455},{8,72}... | collective-permute-start | bytes 995336 | tf_op jit(solution)/shard_map/ppermute | solution.py:413
  132.1 5.0 %copy-start.18 = (bf16[144,1152]{1,0:T(8,128)(2,1)}, bf16[144,1152]{1,0:T(8,128)(2,1)S(1)}, u32[]{:S(2)}) copy-start(bf16[144,1152]{1,0:T(8,128)(2,1)S(1)} %collective-permute-done.19.refs_7_) | copy-start | bytes 995332
  132.1 5.0 %copy-start.15 = (bf16[288,1152]{1,0:T(8,128)(2,1)}, bf16[288,1152]{1,0:T(8,128)(2,1)S(1)}, u32[]{:S(2)}) copy-start(bf16[288,1152]{1,0:T(8,128)(2,1)S(1)} %collective-permute-done.20.refs_6_) | copy-start | bytes 1990660
  132.1 5.0 %collective-permute-start.21 = (bf16[144,1152]{1,0:T(8,128)(2,1)S(1)}, bf16[144,1152]{1,0:T(8,128)(2,1)S(1)}, u32[]{:S(2)}, u32[]{:S(2)}) collective-permute-start(bf16[144,1152]{1,0:T(8,128)(2,1)S(1)} %collective-permute-done.19.refs_7_), channel_id=1, source_target_pairs={{0,1},{1,0},{2,3},{3,2},{4,5},{5,4},{6,7},{7,6},{8,9},{9,8},{10,11... | collective-permute-start | bytes 995336 | tf_op jit(solution)/shard_map/ppermute | solution.py:442
  136.1 1.1 copy-start.3
  150.0 8.0 %copy-start.2 = (bf16[288,1152]{1,0:T(8,128)(2,1)S(1)}, bf16[288,1152]{1,0:T(8,128)(2,1)}, u32[]{:S(2)}) copy-start(bf16[288,1152]{1,0:T(8,128)(2,1)} %get-tuple-element.66) | copy-start | bytes 1990660
  150.1 8.0 %collective-permute-start.22 = (bf16[288,1152]{1,0:T(8,128)(2,1)}, bf16[288,1152]{1,0:T(8,128)(2,1)S(1)}, u32[]{:S(2)}, u32[]{:S(2)}) collective-permute-start(bf16[288,1152]{1,0:T(8,128)(2,1)} %get-tuple-element.67), channel_id=1, source_target_pairs={{0,1},{1,0},{2,3},{3,2},{4,5},{5,4},{6,7},{7,6},{8,9},{9,8},{10,11... | collective-permute-start | bytes 1990664 | tf_op jit(solution)/shard_map/ppermute | solution.py:442
  152.5 16.1 %all-to-all-start.1 = ((bf16[16,8,2304]{2,1,0:T(8,128)(2,1)}), bf16[16,8,2304]{2,1,0:T(8,128)(2,1)S(1)}, u32[]{:S(2)}, u32[]{:S(2)}) async-start(bf16[16,8,2304]{2,1,0:T(8,128)(2,1)} %bitcast.18), calls=%async_computation.1 | async-start | bytes 1179648 | tf_op jit(solution)/shard_map/all_to_all | solution.py:430
  158.2 8.2 %collective-permute-start.23 = (bf16[144,1152]{1,0:T(8,128)(2,1)S(1)}, bf16[144,1152]{1,0:T(8,128)(2,1)S(1)}, u32[]{:S(2)}, u32[]{:S(2)}) collective-permute-start(bf16[144,1152]{1,0:T(8,128)(2,1)S(1)} %slice.14), channel_id=1, source_target_pairs={{0,64},{1,449},{2,66},{3,451},{4,68},{5,453},{6,70},{7,455},{8,72}... | collective-permute-start | bytes 995336 | tf_op jit(solution)/shard_map/ppermute | solution.py:413
  168.5 9.5 %copy-start = (bf16[16,8,2304]{2,1,0:T(8,128)(2,1)}, bf16[16,8,2304]{2,1,0:T(8,128)(2,1)S(1)}, u32[]{:S(2)}) copy-start(bf16[16,8,2304]{2,1,0:T(8,128)(2,1)S(1)} %all-to-all-done.1) | copy-start | bytes 1769476
  168.5 32.0 %all-to-all-start.2 = ((bf16[16,9,1152]{2,1,0:T(8,128)(2,1)}), bf16[16,9,1152]{2,1,0:T(8,128)(2,1)S(1)}, u32[]{:S(2)}, u32[]{:S(2)}) async-start(bf16[16,9,1152]{2,1,0:T(8,128)(2,1)} %reshape.130), calls=%async_computation.2 | async-start | bytes 1179648 | tf_op jit(solution)/shard_map/all_to_all | solution.py:518
  200.7 6.4 %copy-start.1 = (bf16[16,8,2304]{2,1,0:T(8,128)(2,1)S(1)}, bf16[16,8,2304]{2,1,0:T(8,128)(2,1)}, u32[]{:S(2)}) copy-start(bf16[16,8,2304]{2,1,0:T(8,128)(2,1)} %copy-done) | copy-start | bytes 1769476
  201.6 16.1 %all-to-all-start.3 = ((bf16[16,9,1152]{2,1,0:T(8,128)(2,1)}), bf16[16,9,1152]{2,1,0:T(8,128)(2,1)S(1)}, u32[]{:S(2)}, u32[]{:S(2)}) async-start(bf16[16,9,1152]{2,1,0:T(8,128)(2,1)} %broadcast_in_dim.30), calls=%async_computation.3 | async-start | bytes 1179648 | tf_op jit(solution)/shard_map/all_to_all | solution.py:383
  (4 other events, 3.0 us)

commit v6 on v5

--- a/solution.py
+++ b/solution.py
@@ -472,10 +472,11 @@
     ring_t = [block_t, move(block_t, UP)]
     theirs.append(onward(ring))
     last, other = final(ring)
-    theirs_t = [onward(ring_t)]
+    ring_t.append(move(ring_t[-1], UP))
     last_other, ring_t[2] = lax.optimization_barrier((swap(last), ring_t[2]))
     blocks = [*ring, *theirs, other, last, last_other]
-    theirs_t.append(onward(ring_t))
+    ring_t.append(move(ring_t[-1], UP))
+    theirs_t = [swap(ring_t[1]), swap(ring_t[2])]
     last_t, other = final(ring_t)
     blocks_t = [*ring_t, *theirs_t, other, last_t, swap(last_t)]
 

time: 221 us -> 216 us (0.977)
  waiting for transfers between devices: 60.8 us -> 53.3 us
    ppermute x13, waiting for transfers between devices: 31.1 us -> 24.6 us  [move(): return lax.ppermute(a, ('dp', 'seq'), pairs)]
    ppermute x13, starting transfers between devices: 51.7 us -> 56.5 us  [move(): return lax.ppermute(a, ('dp', 'seq'), pairs)]
    ppermute x11, starting transfers between devices: 33.8 us -> 30.6 us  [swap(): return lax.ppermute(a, 'seq', SWAP)]
where the time goes in v6:
time: 216 us; the launch traced here: 215 us
  starting transfers between devices  113 us (52%)
  waiting for transfers between devices  53.3 us (25%)
  Pallas kernels  36.2 us (17%)
  local copies, waits for them, and re-layouts  9.48 us (4%)
  other arithmetic  2.48 us (1%)
    ppermute x13, starting transfers between devices, move(): return lax.ppermute(a, ('dp', 'seq'), pairs)  56.5 us
    pallas_call x6, Pallas kernels, call(): pl.pallas_call(kernel, out_shape=[jax.ShapeDtypeStruct(s, t) for s, t in...  36.2 us
    ppermute x11, starting transfers between devices, swap(): return lax.ppermute(a, 'seq', SWAP)  30.6 us
    ppermute x13, waiting for transfers between devices, move(): return lax.ppermute(a, ('dp', 'seq'), pairs)  24.6 us
    all_to_all x1, waiting for transfers between devices, per_device(): lax.all_to_all(total.reshape(16, 9, D), 'dp', 0, 0, axis_index_groups=GRO...  14.6 us
    all_to_all x2, starting transfers between devices, turn(): return lax.all_to_all(parts, 'seq', 0, 0, tiled=True).reshape(TOKENS, 2 * D)  11 us
    all_to_all x1, waiting for transfers between devices, spread(): lax.all_to_all(jnp.broadcast_to(block[None], (count,) + block.shape), axi...  9.88 us
    all_to_all x1, starting transfers between devices, per_device(): lax.all_to_all(total.reshape(16, 9, D), 'dp', 0, 0, axis_index_groups=GRO...  9.54 us
  transfers between devices with their start and end apart: 28, of which 13 were waited for; matrix products, arithmetic and copies ran while one was open for 2% of the time, Pallas kernels for 9%

profile of v6, /device:TPU:1, one launch (start us, length us, event | category | flops | bytes accessed | tf_op | source)
XLA Modules:
  0.0 215.1 jit_solution(8395540239084590403)
XLA Ops:
  1.2 2.9 %shard_map.85 = (bf16[72,1152]{1,0:T(8,128)(2,1)}, bf16[36,1152]{1,0:T(8,128)(2,1)}, bf16[72,1152]{1,0:T(8,128)(2,1)}, bf16[36,1152]{1,0:T(8,128)(2,1)}) custom-call(s32[4]{0:T(128)} %pad_add_fusion.at_ref, bf16[3,36,576]{2,1,0:T(8,128)(2,1)} %refs_0_.1, bf16[18,1152]{1,0:T(8,128)(2,1)} %refs_1_.1, bf16[3,36,576]{2,1,0:T(8,128)(2,1)} %refs_2_.1, ...), custom_call_target="tpu_custom_call" | custom-call | flops 2200000000 | bytes 3000000 | tf_op jit(solution)/shard_map/pallas_call | solution.py:351
  4.2 11.5 %collective-permute-start = (bf16[72,1152]{1,0:T(8,128)(2,1)}, bf16[72,1152]{1,0:T(8,128)(2,1)S(1)}, u32[]{:S(2)}, u32[]{:S(2)}) collective-permute-start(bf16[72,1152]{1,0:T(8,128)(2,1)} %get-tuple-element.34.own_ref), channel_id=1, source_target_pairs={{0,16},{1,49},{2,18},{3,51},{4,20},{5,53},{6,22},{7,55},{8,24},{9,... | collective-permute-start | bytes 497672 | tf_op jit(solution)/shard_map/ppermute | solution.py:413
  15.7 1.9 collective-permute-start.1
  17.6 8.0 %collective-permute-done.1.far_ref = bf16[36,1152]{1,0:T(8,128)(2,1)S(1)} collective-permute-done((bf16[36,1152]{1,0:T(8,128)(2,1)}, bf16[36,1152]{1,0:T(8,128)(2,1)S(1)}, u32[]{:S(2)}, u32[]{:S(2)}) %collective-permute-start.1) | collective-permute-done | bytes 82976 | tf_op jit(solution)/shard_map/ppermute | solution.py:413
  25.6 2.1 collective-permute-start.2
  27.7 1.5 collective-permute-done.2.other_ref
  29.9 2.4 %shard_map.86.refs_0_ = bf16[288,1152]{1,0:T(8,128)(2,1)} custom-call(s32[4]{0:T(128)} %pad_add_fusion.at_ref, bf16[72,1152]{1,0:T(8,128)(2,1)} %get-tuple-element.34.own_ref, bf16[72,1152]{1,0:T(8,128)(2,1)} %copy-done.6, bf16[36,1152]{1,0:T(8,128)(2,1)} %copy-done.8, bf16[108,1152]{1,0:T(8,128)(2,1)} %copy-done.20), custom_call_target="tpu_custom_call" | custom-call | flops 2200000000 | bytes 3000000 | tf_op jit(solution)/shard_map/pallas_call | solution.py:351
  32.3 7.2 %collective-permute-start.3 = (bf16[288,1152]{1,0:T(8,128)(2,1)}, bf16[288,1152]{1,0:T(8,128)(2,1)S(1)}, u32[]{:S(2)}, u32[]{:S(2)}) collective-permute-start(bf16[288,1152]{1,0:T(8,128)(2,1)} %shard_map.86.refs_0_), channel_id=1, source_target_pairs={{0,64},{1,449},{2,66},{3,451},{4,68},{5,453},{6,70},{7,455},{8,72}... | collective-permute-start | bytes 1990664 | tf_op jit(solution)/shard_map/ppermute | solution.py:413
  39.5 3.3 %collective-permute-start.7 = (bf16[36,1152]{1,0:T(8,128)(2,1)S(1)}, bf16[36,1152]{1,0:T(8,128)(2,1)S(1)}, u32[]{:S(2)}, u32[]{:S(2)}) collective-permute-start(bf16[36,1152]{1,0:T(8,128)(2,1)S(1)} %copy-done.23), channel_id=1, source_target_pairs={{0,32},{1,33},{2,34},{3,35},{4,36},{5,37},{6,38},{7,39},{8,40},{9,... | collective-permute-start | bytes 248840 | tf_op jit(solution)/shard_map/ppermute | solution.py:413
  42.8 4.1 %collective-permute-start.6 = (bf16[72,1152]{1,0:T(8,128)(2,1)S(1)}, bf16[72,1152]{1,0:T(8,128)(2,1)S(1)}, u32[]{:S(2)}, u32[]{:S(2)}) collective-permute-start(bf16[72,1152]{1,0:T(8,128)(2,1)S(1)} %copy-done.22), channel_id=1, source_target_pairs={{0,16},{1,49},{2,18},{3,51},{4,20},{5,53},{6,22},{7,55},{8,24},{9,... | collective-permute-start | bytes 497672 | tf_op jit(solution)/shard_map/ppermute | solution.py:413
  47.0 1.1 fusion.order_hbm
  48.1 2.5 %collective-permute-start.5 = (bf16[288,1152]{1,0:T(8,128)(2,1)S(1)}, bf16[288,1152]{1,0:T(8,128)(2,1)S(1)}, u32[]{:S(2)}, u32[]{:S(2)}) collective-permute-start(bf16[288,1152]{1,0:T(8,128)(2,1)S(1)} %collective-permute-done.3.refs_1_), channel_id=1, source_target_pairs={{0,1},{1,0},{2,3},{3,2},{4,5},{5,4},{6,7},{7,6},{8,9},{9,8},{10,11... | collective-permute-start | bytes 1990664 | tf_op jit(solution)/shard_map/ppermute | solution.py:442
  50.6 3.9 %collective-permute-start.4 = (bf16[288,1152]{1,0:T(8,128)(2,1)S(1)}, bf16[288,1152]{1,0:T(8,128)(2,1)}, u32[]{:S(2)}, u32[]{:S(2)}) collective-permute-start(bf16[288,1152]{1,0:T(8,128)(2,1)S(1)} %collective-permute-done.3.refs_1_), channel_id=1, source_target_pairs={{0,64},{1,449},{2,66},{3,451},{4,68},{5,453},{6,70},{7,455},{8,72}... | collective-permute-start | bytes 1990664 | tf_op jit(solution)/shard_map/ppermute | solution.py:413
  54.6 1.9 collective-permute-start.8
  56.5 1.5 collective-permute-done.8.other_ref
  58.7 2.4 %shard_map.87.refs_0_ = bf16[288,1152]{1,0:T(8,128)(2,1)} custom-call(s32[4]{0:T(128)} %pad_add_fusion.at_ref, bf16[72,1152]{1,0:T(8,128)(2,1)} %get-tuple-element.42.own_ref, bf16[72,1152]{1,0:T(8,128)(2,1)} %copy-done.5, bf16[36,1152]{1,0:T(8,128)(2,1)} %copy-done.7, bf16[108,1152]{1,0:T(8,128)(2,1)} %copy-done.21), custom_call_target="tpu_custom_call" | custom-call | flops 2200000000 | bytes 3000000 | tf_op jit(solution)/shard_map/pallas_call | solution.py:351
  61.1 1.3 collective-permute-done.4.refs_2_
  62.4 4.0 %collective-permute-start.10 = (bf16[288,1152]{1,0:T(8,128)(2,1)}, bf16[288,1152]{1,0:T(8,128)(2,1)S(1)}, u32[]{:S(2)}, u32[]{:S(2)}) collective-permute-start(bf16[288,1152]{1,0:T(8,128)(2,1)} %collective-permute-done.4.refs_2_), channel_id=1, source_target_pairs={{0,1},{1,0},{2,3},{3,2},{4,5},{5,4},{6,7},{7,6},{8,9},{9,8},{10,11... | collective-permute-start | bytes 1990664 | tf_op jit(solution)/shard_map/ppermute | solution.py:442
  66.4 3.1 %collective-permute-start.9 = (bf16[288,1152]{1,0:T(8,128)(2,1)}, bf16[288,1152]{1,0:T(8,128)(2,1)S(1)}, u32[]{:S(2)}, u32[]{:S(2)}) collective-permute-start(bf16[288,1152]{1,0:T(8,128)(2,1)} %collective-permute-done.4.refs_2_), channel_id=1, source_target_pairs={{0,64},{1,449},{2,66},{3,451},{4,68},{5,453},{6,70},{7,455},{8,72}... | collective-permute-start | bytes 1990664 | tf_op jit(solution)/shard_map/ppermute | solution.py:413
  69.6 2.3 %collective-permute-start.14 = (bf16[288,1152]{1,0:T(8,128)(2,1)}, bf16[288,1152]{1,0:T(8,128)(2,1)S(1)}, u32[]{:S(2)}, u32[]{:S(2)}) collective-permute-start(bf16[288,1152]{1,0:T(8,128)(2,1)} %shard_map.87.refs_0_), channel_id=1, source_target_pairs={{0,64},{1,449},{2,66},{3,451},{4,68},{5,453},{6,70},{7,455},{8,72}... | collective-permute-start | bytes 1990664 | tf_op jit(solution)/shard_map/ppermute | solution.py:413
  71.9 6.5 %collective-permute-done.9.refs_3_ = bf16[288,1152]{1,0:T(8,128)(2,1)S(1)} collective-permute-done((bf16[288,1152]{1,0:T(8,128)(2,1)}, bf16[288,1152]{1,0:T(8,128)(2,1)S(1)}, u32[]{:S(2)}, u32[]{:S(2)}) %collective-permute-start.9) | collective-permute-done | bytes 663584 | tf_op jit(solution)/shard_map/ppermute | solution.py:413
  78.4 4.0 %collective-permute-start.12 = (bf16[288,1152]{1,0:T(8,128)(2,1)S(1)}, bf16[288,1152]{1,0:T(8,128)(2,1)S(1)}, u32[]{:S(2)}, u32[]{:S(2)}) collective-permute-start(bf16[288,1152]{1,0:T(8,128)(2,1)S(1)} %collective-permute-done.9.refs_3_), channel_id=1, source_target_pairs={{0,1},{1,0},{2,3},{3,2},{4,5},{5,4},{6,7},{7,6},{8,9},{9,8},{10,11... | collective-permute-start | bytes 1990664 | tf_op jit(solution)/shard_map/ppermute | solution.py:442
  82.4 2.0 collective-permute-start.11
  84.4 1.1 collective-permute-done.14.refs_1_
  85.5 4.1 %collective-permute-start.15 = (bf16[288,1152]{1,0:T(8,128)(2,1)S(1)}, bf16[288,1152]{1,0:T(8,128)(2,1)}, u32[]{:S(2)}, u32[]{:S(2)}) collective-permute-start(bf16[288,1152]{1,0:T(8,128)(2,1)S(1)} %collective-permute-done.14.refs_1_), channel_id=1, source_target_pairs={{0,64},{1,449},{2,66},{3,451},{4,68},{5,453},{6,70},{7,455},{8,72}... | collective-permute-start | bytes 1990664 | tf_op jit(solution)/shard_map/ppermute | solution.py:413
  89.5 1.0 collective-permute-done.11.refs_7_
  91.4 4.0 %collective-permute-start.13 = (bf16[144,1152]{1,0:T(8,128)(2,1)S(1)}, bf16[144,1152]{1,0:T(8,128)(2,1)S(1)}, u32[]{:S(2)}, u32[]{:S(2)}) collective-permute-start(bf16[144,1152]{1,0:T(8,128)(2,1)S(1)} %collective-permute-done.11.refs_7_), channel_id=1, source_target_pairs={{0,1},{1,0},{2,3},{3,2},{4,5},{5,4},{6,7},{7,6},{8,9},{9,8},{10,11... | collective-permute-start | bytes 995336 | tf_op jit(solution)/shard_map/ppermute | solution.py:442
  95.4 2.3 %collective-permute-done.15.refs_2_ = bf16[288,1152]{1,0:T(8,128)(2,1)} collective-permute-done((bf16[288,1152]{1,0:T(8,128)(2,1)S(1)}, bf16[288,1152]{1,0:T(8,128)(2,1)}, u32[]{:S(2)}, u32[]{:S(2)}) %collective-permute-start.15) | collective-permute-done | bytes 663584 | tf_op jit(solution)/shard_map/ppermute | solution.py:413
  98.5 4.5 %collective-permute-start.16 = (bf16[288,1152]{1,0:T(8,128)(2,1)}, bf16[288,1152]{1,0:T(8,128)(2,1)}, u32[]{:S(2)}, u32[]{:S(2)}) collective-permute-start(bf16[288,1152]{1,0:T(8,128)(2,1)} %collective-permute-done.15.refs_2_), channel_id=1, source_target_pairs={{0,64},{1,449},{2,66},{3,451},{4,68},{5,453},{6,70},{7,455},{8,72}... | collective-permute-start | bytes 1990664 | tf_op jit(solution)/shard_map/ppermute | solution.py:413
  103.0 8.6 %shard_map.88 = (bf16[128,2304]{1,0:T(8,128)(2,1)}, bf16[3,128,640]{2,1,0:T(8,128)(2,1)}, f32[8,128,128]{2,1,0:T(8,128)}, bf16[128,640]{1,0:T(8,128)(2,1)}) custom-call(s32[4]{0:T(128)} %pad_add_fusion.at_ref, bf16[128,1152]{1,0:T(8,128)(2,1)} %bitcast.21, bf16[128,1152]{1,0:T(8,128)(2,1)} %bitcast.20, bf16[288,1152]{1,0:T(8,128)(2,1)} %shard_map.86.refs_0_, ...), custom_call_target="tpu_custom_call" | custom-call | flops 8800000000 | bytes 3000000 | tf_op jit(solution)/shard_map/pallas_call | solution.py:351
  111.6 5.4 %all-to-all-start = ((bf16[16,8,2304]{2,1,0:T(8,128)(2,1)}), bf16[16,8,2304]{2,1,0:T(8,128)(2,1)S(1)}, u32[]{:S(2)}, u32[]{:S(2)}) async-start(bf16[16,8,2304]{2,1,0:T(8,128)(2,1)} %bitcast.18), calls=%async_computation | async-start | bytes 1179648 | tf_op jit(solution)/shard_map/all_to_all | solution.py:430
  117.0 2.0 collective-permute-start.20
  119.0 1.0 constant_dynamic-slice_fusion
  120.0 4.9 %collective-permute-start.19 = (bf16[144,1152]{1,0:T(8,128)(2,1)S(1)}, bf16[144,1152]{1,0:T(8,128)(2,1)S(1)}, u32[]{:S(2)}, u32[]{:S(2)}) collective-permute-start(bf16[144,1152]{1,0:T(8,128)(2,1)S(1)} %constant_dynamic-slice_fusion), channel_id=1, source_target_pairs={{0,64},{1,449},{2,66},{3,451},{4,68},{5,453},{6,70},{7,455},{8,72}... | collective-permute-start | bytes 995336 | tf_op jit(solution)/shard_map/ppermute | solution.py:413
  124.9 1.9 collective-permute-start.17
  126.8 2.4 %collective-permute-start.18 = (bf16[288,1152]{1,0:T(8,128)(2,1)}, bf16[288,1152]{1,0:T(8,128)(2,1)}, u32[]{:S(2)}, u32[]{:S(2)}) collective-permute-start(bf16[288,1152]{1,0:T(8,128)(2,1)} %collective-permute-done.15.refs_2_), channel_id=1, source_target_pairs={{0,1},{1,0},{2,3},{3,2},{4,5},{5,4},{6,7},{7,6},{8,9},{9,8},{10,11... | collective-permute-start | bytes 1990664 | tf_op jit(solution)/shard_map/ppermute | solution.py:442
  129.3 3.5 %collective-permute-start.21 = (bf16[144,1152]{1,0:T(8,128)(2,1)S(1)}, bf16[144,1152]{1,0:T(8,128)(2,1)S(1)}, u32[]{:S(2)}, u32[]{:S(2)}) collective-permute-start(bf16[144,1152]{1,0:T(8,128)(2,1)S(1)} %collective-permute-done.19.refs_7_), channel_id=1, source_target_pairs={{0,1},{1,0},{2,3},{3,2},{4,5},{5,4},{6,7},{7,6},{8,9},{9,8},{10,11... | collective-permute-start | bytes 995336 | tf_op jit(solution)/shard_map/ppermute | solution.py:442
  134.7 12.2 %shard_map.89 = (bf16[128,2304]{1,0:T(8,128)(2,1)}, bf16[288,1152]{1,0:T(8,128)(2,1)}, bf16[288,1152]{1,0:T(8,128)(2,1)}) custom-call(s32[4]{0:T(128)} %pad_add_fusion.at_ref, bf16[128,2304]{1,0:T(8,128)(2,1)} %bitcast.17, bf16[640,640]{1,0:T(8,128)(2,1)} %fusion.order_hbm, bf16[288,1152]{1,0:T(8,128)(2,1)} %shard_map.87.refs_0_, ...), custom_call_target="tpu_custom_call" | custom-call | flops 13200000000 | bytes 3000000 | tf_op jit(solution)/shard_map/pallas_call | solution.py:351
  146.8 2.3 %collective-permute-start.22 = (bf16[288,1152]{1,0:T(8,128)(2,1)}, bf16[288,1152]{1,0:T(8,128)(2,1)S(1)}, u32[]{:S(2)}, u32[]{:S(2)}) collective-permute-start(bf16[288,1152]{1,0:T(8,128)(2,1)} %get-tuple-element.59), channel_id=1, source_target_pairs={{0,1},{1,0},{2,3},{3,2},{4,5},{5,4},{6,7},{7,6},{8,9},{9,8},{10,11... | collective-permute-start | bytes 1990664 | tf_op jit(solution)/shard_map/ppermute | solution.py:442
  149.2 5.6 %all-to-all-start.1 = ((bf16[16,8,2304]{2,1,0:T(8,128)(2,1)}), bf16[16,8,2304]{2,1,0:T(8,128)(2,1)S(1)}, u32[]{:S(2)}, u32[]{:S(2)}) async-start(bf16[16,8,2304]{2,1,0:T(8,128)(2,1)} %bitcast.19), calls=%async_computation.1 | async-start | bytes 1179648 | tf_op jit(solution)/shard_map/all_to_all | solution.py:430
  155.0 3.9 %collective-permute-start.23 = (bf16[144,1152]{1,0:T(8,128)(2,1)S(1)}, bf16[144,1152]{1,0:T(8,128)(2,1)S(1)}, u32[]{:S(2)}, u32[]{:S(2)}) collective-permute-start(bf16[144,1152]{1,0:T(8,128)(2,1)S(1)} %slice.14), channel_id=1, source_target_pairs={{0,64},{1,449},{2,66},{3,451},{4,68},{5,453},{6,70},{7,455},{8,72}... | collective-permute-start | bytes 995336 | tf_op jit(solution)/shard_map/ppermute | solution.py:413
  158.9 4.3 %collective-permute-done.23 = bf16[144,1152]{1,0:T(8,128)(2,1)S(1)} collective-permute-done((bf16[144,1152]{1,0:T(8,128)(2,1)S(1)}, bf16[144,1152]{1,0:T(8,128)(2,1)S(1)}, u32[]{:S(2)}, u32[]{:S(2)}) %collective-permute-start.23) | collective-permute-done | bytes 331808 | tf_op jit(solution)/shard_map/ppermute | solution.py:413
  164.2 1.1 all-to-all-done.1
  165.3 9.5 %all-to-all-start.2 = ((bf16[16,9,1152]{2,1,0:T(8,128)(2,1)}), bf16[16,9,1152]{2,1,0:T(8,128)(2,1)S(1)}, u32[]{:S(2)}, u32[]{:S(2)}) async-start(bf16[16,9,1152]{2,1,0:T(8,128)(2,1)} %reshape.130), calls=%async_computation.2 | async-start | bytes 1179648 | tf_op jit(solution)/shard_map/all_to_all | solution.py:519
  174.9 7.8 %shard_map.90 = bf16[128,1152]{1,0:T(8,128)(2,1)} custom-call(s32[4]{0:T(128)} %pad_add_fusion.at_ref, bf16[128,1152]{1,0:T(8,128)(2,1)} %bitcast.22, bf16[128,2304]{1,0:T(8,128)(2,1)} %bitcast.15, bf16[3,128,640]{2,1,0:T(8,128)(2,1)} %get-tuple-element.60.qkv_hbm, f32[8,128,128]{2,1,0:T(8,128)} %get-tuple-element.61.probs_hbm, ...), custom_call_target="tpu_custom_call" | custom-call | flops 9900000256 | bytes 3000000 | tf_op jit(solution)/shard_map/pallas_call | solution.py:351
  182.7 14.6 %all-to-all-done.2 = bf16[16,9,1152]{2,1,0:T(8,128)(2,1)S(1)} async-done(((bf16[16,9,1152]{2,1,0:T(8,128)(2,1)}), bf16[16,9,1152]{2,1,0:T(8,128)(2,1)S(1)}, u32[]{:S(2)}, u32[]{:S(2)}) %all-to-all-start.2) | async-done | bytes 331808 | tf_op jit(solution)/shard_map/all_to_all | solution.py:519
  198.2 4.8 %all-to-all-start.3 = ((bf16[16,9,1152]{2,1,0:T(8,128)(2,1)}), bf16[16,9,1152]{2,1,0:T(8,128)(2,1)S(1)}, u32[]{:S(2)}, u32[]{:S(2)}) async-start(bf16[16,9,1152]{2,1,0:T(8,128)(2,1)} %broadcast_in_dim.30), calls=%async_computation.3 | async-start | bytes 1179648 | tf_op jit(solution)/shard_map/all_to_all | solution.py:383
  203.8 9.9 %all-to-all-done.3 = bf16[16,9,1152]{2,1,0:T(8,128)(2,1)S(1)} async-done(((bf16[16,9,1152]{2,1,0:T(8,128)(2,1)}), bf16[16,9,1152]{2,1,0:T(8,128)(2,1)S(1)}, u32[]{:S(2)}, u32[]{:S(2)}) %all-to-all-start.3) | async-done | bytes 331808 | tf_op jit(solution)/shard_map/all_to_all | solution.py:383
  (81 shorter events, 10.0 us)
Async XLA Ops:
  4.2 21.4 %collective-permute-start = (bf16[72,1152]{1,0:T(8,128)(2,1)}, bf16[72,1152]{1,0:T(8,128)(2,1)S(1)}, u32[]{:S(2)}, u32[]{:S(2)}) collective-permute-start(bf16[72,1152]{1,0:T(8,128)(2,1)} %get-tuple-element.34.own_ref), channel_id=1, source_target_pairs={{0,16},{1,49},{2,18},{3,51},{4,20},{5,53},{6,22},{7,55},{8,24},{9,... | collective-permute-start | bytes 497672 | tf_op jit(solution)/shard_map/ppermute | solution.py:413
  15.7 9.9 %collective-permute-start.1 = (bf16[36,1152]{1,0:T(8,128)(2,1)}, bf16[36,1152]{1,0:T(8,128)(2,1)S(1)}, u32[]{:S(2)}, u32[]{:S(2)}) collective-permute-start(bf16[36,1152]{1,0:T(8,128)(2,1)} %get-tuple-element.35), channel_id=1, source_target_pairs={{0,32},{1,33},{2,34},{3,35},{4,36},{5,37},{6,38},{7,39},{8,40},{9,... | collective-permute-start | bytes 248840 | tf_op jit(solution)/shard_map/ppermute | solution.py:413
  25.6 3.6 %copy-start.8 = (bf16[36,1152]{1,0:T(8,128)(2,1)}, bf16[36,1152]{1,0:T(8,128)(2,1)S(1)}, u32[]{:S(2)}) copy-start(bf16[36,1152]{1,0:T(8,128)(2,1)S(1)} %collective-permute-done.1.far_ref) | copy-start | bytes 248836
  25.6 3.6 %copy-start.6 = (bf16[72,1152]{1,0:T(8,128)(2,1)}, bf16[72,1152]{1,0:T(8,128)(2,1)S(1)}, u32[]{:S(2)}) copy-start(bf16[72,1152]{1,0:T(8,128)(2,1)S(1)} %collective-permute-done.next_ref) | copy-start | bytes 497668
  25.6 13.9 %copy-start.23 = (bf16[36,1152]{1,0:T(8,128)(2,1)S(1)}, bf16[36,1152]{1,0:T(8,128)(2,1)}, u32[]{:S(2)}) copy-start(bf16[36,1152]{1,0:T(8,128)(2,1)} %get-tuple-element.43) | copy-start | bytes 248836
  25.6 17.2 %copy-start.22 = (bf16[72,1152]{1,0:T(8,128)(2,1)S(1)}, bf16[72,1152]{1,0:T(8,128)(2,1)}, u32[]{:S(2)}) copy-start(bf16[72,1152]{1,0:T(8,128)(2,1)} %get-tuple-element.42.own_ref) | copy-start | bytes 497668
  25.6 3.6 %collective-permute-start.2 = (bf16[108,1152]{1,0:T(8,128)(2,1)S(1)}, bf16[108,1152]{1,0:T(8,128)(2,1)S(1)}, u32[]{:S(2)}, u32[]{:S(2)}) collective-permute-start(bf16[108,1152]{1,0:T(8,128)(2,1)S(1)} %pad_maximum_fusion), channel_id=1, source_target_pairs={{0,1},{1,0},{2,3},{3,2},{4,5},{5,4},{6,7},{7,6},{8,9},{9,8},{10,11... | collective-permute-start | bytes 746504 | tf_op jit(solution)/shard_map/ppermute | solution.py:442
  32.3 15.8 %collective-permute-start.3 = (bf16[288,1152]{1,0:T(8,128)(2,1)}, bf16[288,1152]{1,0:T(8,128)(2,1)S(1)}, u32[]{:S(2)}, u32[]{:S(2)}) collective-permute-start(bf16[288,1152]{1,0:T(8,128)(2,1)} %shard_map.86.refs_0_), channel_id=1, source_target_pairs={{0,64},{1,449},{2,66},{3,451},{4,68},{5,453},{6,70},{7,455},{8,72}... | collective-permute-start | bytes 1990664 | tf_op jit(solution)/shard_map/ppermute | solution.py:413
  39.5 15.0 %collective-permute-start.7 = (bf16[36,1152]{1,0:T(8,128)(2,1)S(1)}, bf16[36,1152]{1,0:T(8,128)(2,1)S(1)}, u32[]{:S(2)}, u32[]{:S(2)}) collective-permute-start(bf16[36,1152]{1,0:T(8,128)(2,1)S(1)} %copy-done.23), channel_id=1, source_target_pairs={{0,32},{1,33},{2,34},{3,35},{4,36},{5,37},{6,38},{7,39},{8,40},{9,... | collective-permute-start | bytes 248840 | tf_op jit(solution)/shard_map/ppermute | solution.py:413
  42.8 11.7 %collective-permute-start.6 = (bf16[72,1152]{1,0:T(8,128)(2,1)S(1)}, bf16[72,1152]{1,0:T(8,128)(2,1)S(1)}, u32[]{:S(2)}, u32[]{:S(2)}) collective-permute-start(bf16[72,1152]{1,0:T(8,128)(2,1)S(1)} %copy-done.22), channel_id=1, source_target_pairs={{0,16},{1,49},{2,18},{3,51},{4,20},{5,53},{6,22},{7,55},{8,24},{9,... | collective-permute-start | bytes 497672 | tf_op jit(solution)/shard_map/ppermute | solution.py:413
  48.1 13.0 %copy-start.9 = (bf16[288,1152]{1,0:T(8,128)(2,1)}, bf16[288,1152]{1,0:T(8,128)(2,1)S(1)}, u32[]{:S(2)}) copy-start(bf16[288,1152]{1,0:T(8,128)(2,1)S(1)} %collective-permute-done.3.refs_1_) | copy-start | bytes 1990660
  48.1 13.0 %collective-permute-start.5 = (bf16[288,1152]{1,0:T(8,128)(2,1)S(1)}, bf16[288,1152]{1,0:T(8,128)(2,1)S(1)}, u32[]{:S(2)}, u32[]{:S(2)}) collective-permute-start(bf16[288,1152]{1,0:T(8,128)(2,1)S(1)} %collective-permute-done.3.refs_1_), channel_id=1, source_target_pairs={{0,1},{1,0},{2,3},{3,2},{4,5},{5,4},{6,7},{7,6},{8,9},{9,8},{10,11... | collective-permute-start | bytes 1990664 | tf_op jit(solution)/shard_map/ppermute | solution.py:442
  50.6 11.8 %collective-permute-start.4 = (bf16[288,1152]{1,0:T(8,128)(2,1)S(1)}, bf16[288,1152]{1,0:T(8,128)(2,1)}, u32[]{:S(2)}, u32[]{:S(2)}) collective-permute-start(bf16[288,1152]{1,0:T(8,128)(2,1)S(1)} %collective-permute-done.3.refs_1_), channel_id=1, source_target_pairs={{0,64},{1,449},{2,66},{3,451},{4,68},{5,453},{6,70},{7,455},{8,72}... | collective-permute-start | bytes 1990664 | tf_op jit(solution)/shard_map/ppermute | solution.py:413
  54.5 3.5 %copy-start.7 = (bf16[36,1152]{1,0:T(8,128)(2,1)}, bf16[36,1152]{1,0:T(8,128)(2,1)S(1)}, u32[]{:S(2)}) copy-start(bf16[36,1152]{1,0:T(8,128)(2,1)S(1)} %collective-permute-done.7.far_ref) | copy-start | bytes 248836
  54.5 3.5 %copy-start.5 = (bf16[72,1152]{1,0:T(8,128)(2,1)}, bf16[72,1152]{1,0:T(8,128)(2,1)S(1)}, u32[]{:S(2)}) copy-start(bf16[72,1152]{1,0:T(8,128)(2,1)S(1)} %collective-permute-done.6.next_ref) | copy-start | bytes 497668
  54.6 3.4 %collective-permute-start.8 = (bf16[108,1152]{1,0:T(8,128)(2,1)S(1)}, bf16[108,1152]{1,0:T(8,128)(2,1)S(1)}, u32[]{:S(2)}, u32[]{:S(2)}) collective-permute-start(bf16[108,1152]{1,0:T(8,128)(2,1)S(1)} %pad_maximum_fusion.1), channel_id=1, source_target_pairs={{0,1},{1,0},{2,3},{3,2},{4,5},{5,4},{6,7},{7,6},{8,9},{9,8},{10,11... | collective-permute-start | bytes 746504 | tf_op jit(solution)/shard_map/ppermute | solution.py:442
  61.1 1.4 copy-start.10
  62.4 9.4 %collective-permute-start.10 = (bf16[288,1152]{1,0:T(8,128)(2,1)}, bf16[288,1152]{1,0:T(8,128)(2,1)S(1)}, u32[]{:S(2)}, u32[]{:S(2)}) collective-permute-start(bf16[288,1152]{1,0:T(8,128)(2,1)} %collective-permute-done.4.refs_2_), channel_id=1, source_target_pairs={{0,1},{1,0},{2,3},{3,2},{4,5},{5,4},{6,7},{7,6},{8,9},{9,8},{10,11... | collective-permute-start | bytes 1990664 | tf_op jit(solution)/shard_map/ppermute | solution.py:442
  66.4 11.9 %collective-permute-start.9 = (bf16[288,1152]{1,0:T(8,128)(2,1)}, bf16[288,1152]{1,0:T(8,128)(2,1)S(1)}, u32[]{:S(2)}, u32[]{:S(2)}) collective-permute-start(bf16[288,1152]{1,0:T(8,128)(2,1)} %collective-permute-done.4.refs_2_), channel_id=1, source_target_pairs={{0,64},{1,449},{2,66},{3,451},{4,68},{5,453},{6,70},{7,455},{8,72}... | collective-permute-start | bytes 1990664 | tf_op jit(solution)/shard_map/ppermute | solution.py:413
  69.6 15.9 %collective-permute-start.14 = (bf16[288,1152]{1,0:T(8,128)(2,1)}, bf16[288,1152]{1,0:T(8,128)(2,1)S(1)}, u32[]{:S(2)}, u32[]{:S(2)}) collective-permute-start(bf16[288,1152]{1,0:T(8,128)(2,1)} %shard_map.87.refs_0_), channel_id=1, source_target_pairs={{0,64},{1,449},{2,66},{3,451},{4,68},{5,453},{6,70},{7,455},{8,72}... | collective-permute-start | bytes 1990664 | tf_op jit(solution)/shard_map/ppermute | solution.py:413
  71.9 31.1 %copy-start.11 = (bf16[288,1152]{1,0:T(8,128)(2,1)}, bf16[288,1152]{1,0:T(8,128)(2,1)S(1)}, u32[]{:S(2)}) copy-start(bf16[288,1152]{1,0:T(8,128)(2,1)S(1)} %collective-permute-done.10.refs_5_) | copy-start | bytes 1990660
  78.4 24.6 %copy-start.4 = (bf16[288,1152]{1,0:T(8,128)(2,1)}, bf16[288,1152]{1,0:T(8,128)(2,1)S(1)}, u32[]{:S(2)}) copy-start(bf16[288,1152]{1,0:T(8,128)(2,1)S(1)} %collective-permute-done.9.refs_3_) | copy-start | bytes 1990660
  78.4 12.2 %collective-permute-start.12 = (bf16[288,1152]{1,0:T(8,128)(2,1)S(1)}, bf16[288,1152]{1,0:T(8,128)(2,1)S(1)}, u32[]{:S(2)}, u32[]{:S(2)}) collective-permute-start(bf16[288,1152]{1,0:T(8,128)(2,1)S(1)} %collective-permute-done.9.refs_3_), channel_id=1, source_target_pairs={{0,1},{1,0},{2,3},{3,2},{4,5},{5,4},{6,7},{7,6},{8,9},{9,8},{10,11... | collective-permute-start | bytes 1990664 | tf_op jit(solution)/shard_map/ppermute | solution.py:442
  82.4 8.2 %collective-permute-start.11 = (bf16[144,1152]{1,0:T(8,128)(2,1)S(1)}, bf16[144,1152]{1,0:T(8,128)(2,1)S(1)}, u32[]{:S(2)}, u32[]{:S(2)}) collective-permute-start(bf16[144,1152]{1,0:T(8,128)(2,1)S(1)} %constant_dynamic-slice_fusion.1), channel_id=1, source_target_pairs={{0,64},{1,449},{2,66},{3,451},{4,68},{5,453},{6,70},{7,455},{8,72}... | collective-permute-start | bytes 995336 | tf_op jit(solution)/shard_map/ppermute | solution.py:413
  85.5 39.4 %copy-start.13 = (bf16[288,1152]{1,0:T(8,128)(2,1)}, bf16[288,1152]{1,0:T(8,128)(2,1)S(1)}, u32[]{:S(2)}) copy-start(bf16[288,1152]{1,0:T(8,128)(2,1)S(1)} %collective-permute-done.14.refs_1_) | copy-start | bytes 1990660
  85.5 12.3 %collective-permute-start.15 = (bf16[288,1152]{1,0:T(8,128)(2,1)S(1)}, bf16[288,1152]{1,0:T(8,128)(2,1)}, u32[]{:S(2)}, u32[]{:S(2)}) collective-permute-start(bf16[288,1152]{1,0:T(8,128)(2,1)S(1)} %collective-permute-done.14.refs_1_), channel_id=1, source_target_pairs={{0,64},{1,449},{2,66},{3,451},{4,68},{5,453},{6,70},{7,455},{8,72}... | collective-permute-start | bytes 1990664 | tf_op jit(solution)/shard_map/ppermute | solution.py:413
  90.5 7.2 %copy-start.16 = (bf16[144,1152]{1,0:T(8,128)(2,1)}, bf16[144,1152]{1,0:T(8,128)(2,1)S(1)}, u32[]{:S(2)}) copy-start(bf16[144,1152]{1,0:T(8,128)(2,1)S(1)} %collective-permute-done.11.refs_7_) | copy-start | bytes 995332
  90.6 0.9 copy-start.12
  91.4 6.3 %collective-permute-start.13 = (bf16[144,1152]{1,0:T(8,128)(2,1)S(1)}, bf16[144,1152]{1,0:T(8,128)(2,1)S(1)}, u32[]{:S(2)}, u32[]{:S(2)}) collective-permute-start(bf16[144,1152]{1,0:T(8,128)(2,1)S(1)} %collective-permute-done.11.refs_7_), channel_id=1, source_target_pairs={{0,1},{1,0},{2,3},{3,2},{4,5},{5,4},{6,7},{7,6},{8,9},{9,8},{10,11... | collective-permute-start | bytes 995336 | tf_op jit(solution)/shard_map/ppermute | solution.py:442
  98.5 18.5 %collective-permute-start.16 = (bf16[288,1152]{1,0:T(8,128)(2,1)}, bf16[288,1152]{1,0:T(8,128)(2,1)}, u32[]{:S(2)}, u32[]{:S(2)}) collective-permute-start(bf16[288,1152]{1,0:T(8,128)(2,1)} %collective-permute-done.15.refs_2_), channel_id=1, source_target_pairs={{0,64},{1,449},{2,66},{3,451},{4,68},{5,453},{6,70},{7,455},{8,72}... | collective-permute-start | bytes 1990664 | tf_op jit(solution)/shard_map/ppermute | solution.py:413
  111.6 22.1 %all-to-all-start = ((bf16[16,8,2304]{2,1,0:T(8,128)(2,1)}), bf16[16,8,2304]{2,1,0:T(8,128)(2,1)S(1)}, u32[]{:S(2)}, u32[]{:S(2)}) async-start(bf16[16,8,2304]{2,1,0:T(8,128)(2,1)} %bitcast.18), calls=%async_computation | async-start | bytes 1179648 | tf_op jit(solution)/shard_map/all_to_all | solution.py:430
  117.0 12.3 %collective-permute-start.20 = (bf16[288,1152]{1,0:T(8,128)(2,1)}, bf16[288,1152]{1,0:T(8,128)(2,1)S(1)}, u32[]{:S(2)}, u32[]{:S(2)}) collective-permute-start(bf16[288,1152]{1,0:T(8,128)(2,1)} %collective-permute-done.16.refs_3_), channel_id=1, source_target_pairs={{0,1},{1,0},{2,3},{3,2},{4,5},{5,4},{6,7},{7,6},{8,9},{9,8},{10,11... | collective-permute-start | bytes 1990664 | tf_op jit(solution)/shard_map/ppermute | solution.py:442
  120.0 9.2 %collective-permute-start.19 = (bf16[144,1152]{1,0:T(8,128)(2,1)S(1)}, bf16[144,1152]{1,0:T(8,128)(2,1)S(1)}, u32[]{:S(2)}, u32[]{:S(2)}) collective-permute-start(bf16[144,1152]{1,0:T(8,128)(2,1)S(1)} %constant_dynamic-slice_fusion), channel_id=1, source_target_pairs={{0,64},{1,449},{2,66},{3,451},{4,68},{5,453},{6,70},{7,455},{8,72}... | collective-permute-start | bytes 995336 | tf_op jit(solution)/shard_map/ppermute | solution.py:413
  124.9 7.9 %collective-permute-start.17 = (bf16[288,1152]{1,0:T(8,128)(2,1)S(1)}, bf16[288,1152]{1,0:T(8,128)(2,1)S(1)}, u32[]{:S(2)}, u32[]{:S(2)}) collective-permute-start(bf16[288,1152]{1,0:T(8,128)(2,1)S(1)} %collective-permute-done.14.refs_1_), channel_id=1, source_target_pairs={{0,1},{1,0},{2,3},{3,2},{4,5},{5,4},{6,7},{7,6},{8,9},{9,8},{10,11... | collective-permute-start | bytes 1990664 | tf_op jit(solution)/shard_map/ppermute | solution.py:442
  126.8 6.8 %collective-permute-start.18 = (bf16[288,1152]{1,0:T(8,128)(2,1)}, bf16[288,1152]{1,0:T(8,128)(2,1)}, u32[]{:S(2)}, u32[]{:S(2)}) collective-permute-start(bf16[288,1152]{1,0:T(8,128)(2,1)} %collective-permute-done.15.refs_2_), channel_id=1, source_target_pairs={{0,1},{1,0},{2,3},{3,2},{4,5},{5,4},{6,7},{7,6},{8,9},{9,8},{10,11... | collective-permute-start | bytes 1990664 | tf_op jit(solution)/shard_map/ppermute | solution.py:442
  129.3 4.4 %copy-start.18 = (bf16[144,1152]{1,0:T(8,128)(2,1)}, bf16[144,1152]{1,0:T(8,128)(2,1)S(1)}, u32[]{:S(2)}) copy-start(bf16[144,1152]{1,0:T(8,128)(2,1)S(1)} %collective-permute-done.19.refs_7_) | copy-start | bytes 995332
  129.3 5.4 %copy-start.14 = (bf16[288,1152]{1,0:T(8,128)(2,1)}, bf16[288,1152]{1,0:T(8,128)(2,1)S(1)}, u32[]{:S(2)}) copy-start(bf16[288,1152]{1,0:T(8,128)(2,1)S(1)} %collective-permute-done.20.refs_6_) | copy-start | bytes 1990660
  129.3 4.5 %collective-permute-start.21 = (bf16[144,1152]{1,0:T(8,128)(2,1)S(1)}, bf16[144,1152]{1,0:T(8,128)(2,1)S(1)}, u32[]{:S(2)}, u32[]{:S(2)}) collective-permute-start(bf16[144,1152]{1,0:T(8,128)(2,1)S(1)} %collective-permute-done.19.refs_7_), channel_id=1, source_target_pairs={{0,1},{1,0},{2,3},{3,2},{4,5},{5,4},{6,7},{7,6},{8,9},{9,8},{10,11... | collective-permute-start | bytes 995336 | tf_op jit(solution)/shard_map/ppermute | solution.py:442
  132.8 0.9 copy-start.15
  133.7 1.0 copy-start.3
  146.8 8.0 %copy-start.2 = (bf16[288,1152]{1,0:T(8,128)(2,1)S(1)}, bf16[288,1152]{1,0:T(8,128)(2,1)}, u32[]{:S(2)}) copy-start(bf16[288,1152]{1,0:T(8,128)(2,1)} %get-tuple-element.58) | copy-start | bytes 1990660
  146.8 7.9 %collective-permute-start.22 = (bf16[288,1152]{1,0:T(8,128)(2,1)}, bf16[288,1152]{1,0:T(8,128)(2,1)S(1)}, u32[]{:S(2)}, u32[]{:S(2)}) collective-permute-start(bf16[288,1152]{1,0:T(8,128)(2,1)} %get-tuple-element.59), channel_id=1, source_target_pairs={{0,1},{1,0},{2,3},{3,2},{4,5},{5,4},{6,7},{7,6},{8,9},{9,8},{10,11... | collective-permute-start | bytes 1990664 | tf_op jit(solution)/shard_map/ppermute | solution.py:442
  149.2 16.1 %all-to-all-start.1 = ((bf16[16,8,2304]{2,1,0:T(8,128)(2,1)}), bf16[16,8,2304]{2,1,0:T(8,128)(2,1)S(1)}, u32[]{:S(2)}, u32[]{:S(2)}) async-start(bf16[16,8,2304]{2,1,0:T(8,128)(2,1)} %bitcast.19), calls=%async_computation.1 | async-start | bytes 1179648 | tf_op jit(solution)/shard_map/all_to_all | solution.py:430
  155.0 8.2 %collective-permute-start.23 = (bf16[144,1152]{1,0:T(8,128)(2,1)S(1)}, bf16[144,1152]{1,0:T(8,128)(2,1)S(1)}, u32[]{:S(2)}, u32[]{:S(2)}) collective-permute-start(bf16[144,1152]{1,0:T(8,128)(2,1)S(1)} %slice.14), channel_id=1, source_target_pairs={{0,64},{1,449},{2,66},{3,451},{4,68},{5,453},{6,70},{7,455},{8,72}... | collective-permute-start | bytes 995336 | tf_op jit(solution)/shard_map/ppermute | solution.py:413
  165.3 9.6 %copy-start = (bf16[16,8,2304]{2,1,0:T(8,128)(2,1)}, bf16[16,8,2304]{2,1,0:T(8,128)(2,1)S(1)}, u32[]{:S(2)}) copy-start(bf16[16,8,2304]{2,1,0:T(8,128)(2,1)S(1)} %all-to-all-done.1) | copy-start | bytes 1769476
  165.3 31.9 %all-to-all-start.2 = ((bf16[16,9,1152]{2,1,0:T(8,128)(2,1)}), bf16[16,9,1152]{2,1,0:T(8,128)(2,1)S(1)}, u32[]{:S(2)}, u32[]{:S(2)}) async-start(bf16[16,9,1152]{2,1,0:T(8,128)(2,1)} %reshape.130), calls=%async_computation.2 | async-start | bytes 1179648 | tf_op jit(solution)/shard_map/all_to_all | solution.py:519
  197.3 5.7 %copy-start.1 = (bf16[16,8,2304]{2,1,0:T(8,128)(2,1)S(1)}, bf16[16,8,2304]{2,1,0:T(8,128)(2,1)}, u32[]{:S(2)}) copy-start(bf16[16,8,2304]{2,1,0:T(8,128)(2,1)} %copy-done) | copy-start | bytes 1769476
  198.2 15.5 %all-to-all-start.3 = ((bf16[16,9,1152]{2,1,0:T(8,128)(2,1)}), bf16[16,9,1152]{2,1,0:T(8,128)(2,1)S(1)}, u32[]{:S(2)}, u32[]{:S(2)}) async-start(bf16[16,9,1152]{2,1,0:T(8,128)(2,1)} %broadcast_in_dim.30), calls=%async_computation.3 | async-start | bytes 1179648 | tf_op jit(solution)/shard_map/all_to_all | solution.py:383
  (4 other events, 2.9 us)

commit v7 on v6

--- a/solution.py
+++ b/solution.py
@@ -476,9 +476,10 @@
     last_other, ring_t[2] = lax.optimization_barrier((swap(last), ring_t[2]))
     blocks = [*ring, *theirs, other, last, last_other]
     ring_t.append(move(ring_t[-1], UP))
-    theirs_t = [swap(ring_t[1]), swap(ring_t[2])]
-    last_t, other = final(ring_t)
-    blocks_t = [*ring_t, *theirs_t, other, last_t, swap(last_t)]
+    piece = lax.dynamic_slice_in_dim(ring_t[3], core * BLOCK, BLOCK, axis=0)
+    piece, *ring_t[1:] = lax.optimization_barrier((piece, *ring_t[1:]))
+    last_t = move(piece, UP)
+    blocks_t = [*ring_t, *map(swap, ring_t[1:]), last_t, swap(last_t)]
 
     more = pltpu.SemaphoreType.DMA((5,))
     weights = pltpu.VMEM((2 * D, D), BF)

time: 216 us -> 217 us (level)
    unnamed x49 -> x47, local copies, waits for them, and re-layouts: 4.77 us -> 4.08 us
where the time goes in v7:
time: 217 us; the launch traced here: 215 us
  starting transfers between devices  112 us (52%)
  waiting for transfers between devices  54.8 us (25%)
  Pallas kernels  36.2 us (17%)
  local copies, waits for them, and re-layouts  8.78 us (4%)
  other arithmetic  2.47 us (1%)
    ppermute x13, starting transfers between devices, move(): return lax.ppermute(a, ('dp', 'seq'), pairs)  55.3 us
    pallas_call x6, Pallas kernels, call(): pl.pallas_call(kernel, out_shape=[jax.ShapeDtypeStruct(s, t) for s, t in...  36.2 us
    ppermute x11, starting transfers between devices, swap(): return lax.ppermute(a, 'seq', SWAP)  29.7 us
    ppermute x13, waiting for transfers between devices, move(): return lax.ppermute(a, ('dp', 'seq'), pairs)  25.8 us
    all_to_all x1, waiting for transfers between devices, per_device(): lax.all_to_all(total.reshape(16, 9, D), 'dp', 0, 0, axis_index_groups=GRO...  14.1 us
    all_to_all x2, starting transfers between devices, turn(): return lax.all_to_all(parts, 'seq', 0, 0, tiled=True).reshape(TOKENS, 2 * D)  10.9 us
    all_to_all x1, waiting for transfers between devices, spread(): lax.all_to_all(jnp.broadcast_to(block[None], (count,) + block.shape), axi...  9.8 us
    all_to_all x1, starting transfers between devices, per_device(): lax.all_to_all(total.reshape(16, 9, D), 'dp', 0, 0, axis_index_groups=GRO...  9.54 us
  transfers between devices with their start and end apart: 28, of which 13 were waited for; matrix products, arithmetic and copies ran while one was open for 2% of the time, Pallas kernels for 9%

profile of v7, /device:TPU:1, one launch (start us, length us, event | category | flops | bytes accessed | tf_op | source)
XLA Modules:
  0.0 215.5 jit_solution(15153888198803224176)
XLA Ops:
  1.2 2.9 %shard_map.85 = (bf16[72,1152]{1,0:T(8,128)(2,1)}, bf16[36,1152]{1,0:T(8,128)(2,1)}, bf16[72,1152]{1,0:T(8,128)(2,1)}, bf16[36,1152]{1,0:T(8,128)(2,1)}) custom-call(s32[4]{0:T(128)} %pad_add_fusion.at_ref, bf16[3,36,576]{2,1,0:T(8,128)(2,1)} %refs_0_.1, bf16[18,1152]{1,0:T(8,128)(2,1)} %refs_1_.1, bf16[3,36,576]{2,1,0:T(8,128)(2,1)} %refs_2_.1, ...), custom_call_target="tpu_custom_call" | custom-call | flops 2200000000 | bytes 3000000 | tf_op jit(solution)/shard_map/pallas_call | solution.py:351
  4.2 11.5 %collective-permute-start = (bf16[72,1152]{1,0:T(8,128)(2,1)}, bf16[72,1152]{1,0:T(8,128)(2,1)S(1)}, u32[]{:S(2)}, u32[]{:S(2)}) collective-permute-start(bf16[72,1152]{1,0:T(8,128)(2,1)} %get-tuple-element.36.own_ref), channel_id=1, source_target_pairs={{0,16},{1,49},{2,18},{3,51},{4,20},{5,53},{6,22},{7,55},{8,24},{9,... | collective-permute-start | bytes 497672 | tf_op jit(solution)/shard_map/ppermute | solution.py:413
  15.7 1.9 collective-permute-start.1
  17.6 8.0 %collective-permute-done.1.far_ref = bf16[36,1152]{1,0:T(8,128)(2,1)S(1)} collective-permute-done((bf16[36,1152]{1,0:T(8,128)(2,1)}, bf16[36,1152]{1,0:T(8,128)(2,1)S(1)}, u32[]{:S(2)}, u32[]{:S(2)}) %collective-permute-start.1) | collective-permute-done | bytes 82976 | tf_op jit(solution)/shard_map/ppermute | solution.py:413
  25.6 2.1 collective-permute-start.2
  27.7 1.5 collective-permute-done.2.other_ref
  29.9 2.4 %shard_map.86.refs_0_ = bf16[288,1152]{1,0:T(8,128)(2,1)} custom-call(s32[4]{0:T(128)} %pad_add_fusion.at_ref, bf16[72,1152]{1,0:T(8,128)(2,1)} %get-tuple-element.36.own_ref, bf16[72,1152]{1,0:T(8,128)(2,1)} %copy-done.6, bf16[36,1152]{1,0:T(8,128)(2,1)} %copy-done.8, bf16[108,1152]{1,0:T(8,128)(2,1)} %copy-done.19), custom_call_target="tpu_custom_call" | custom-call | flops 2200000000 | bytes 3000000 | tf_op jit(solution)/shard_map/pallas_call | solution.py:351
  32.3 7.2 %collective-permute-start.3 = (bf16[288,1152]{1,0:T(8,128)(2,1)}, bf16[288,1152]{1,0:T(8,128)(2,1)S(1)}, u32[]{:S(2)}, u32[]{:S(2)}) collective-permute-start(bf16[288,1152]{1,0:T(8,128)(2,1)} %shard_map.86.refs_0_), channel_id=1, source_target_pairs={{0,64},{1,449},{2,66},{3,451},{4,68},{5,453},{6,70},{7,455},{8,72}... | collective-permute-start | bytes 1990664 | tf_op jit(solution)/shard_map/ppermute | solution.py:413
  39.5 3.3 %collective-permute-start.7 = (bf16[36,1152]{1,0:T(8,128)(2,1)S(1)}, bf16[36,1152]{1,0:T(8,128)(2,1)S(1)}, u32[]{:S(2)}, u32[]{:S(2)}) collective-permute-start(bf16[36,1152]{1,0:T(8,128)(2,1)S(1)} %copy-done.22), channel_id=1, source_target_pairs={{0,32},{1,33},{2,34},{3,35},{4,36},{5,37},{6,38},{7,39},{8,40},{9,... | collective-permute-start | bytes 248840 | tf_op jit(solution)/shard_map/ppermute | solution.py:413
  42.8 4.1 %collective-permute-start.6 = (bf16[72,1152]{1,0:T(8,128)(2,1)S(1)}, bf16[72,1152]{1,0:T(8,128)(2,1)S(1)}, u32[]{:S(2)}, u32[]{:S(2)}) collective-permute-start(bf16[72,1152]{1,0:T(8,128)(2,1)S(1)} %copy-done.21), channel_id=1, source_target_pairs={{0,16},{1,49},{2,18},{3,51},{4,20},{5,53},{6,22},{7,55},{8,24},{9,... | collective-permute-start | bytes 497672 | tf_op jit(solution)/shard_map/ppermute | solution.py:413
  46.9 1.1 fusion.order_hbm
  48.1 2.5 %collective-permute-start.5 = (bf16[288,1152]{1,0:T(8,128)(2,1)S(1)}, bf16[288,1152]{1,0:T(8,128)(2,1)S(1)}, u32[]{:S(2)}, u32[]{:S(2)}) collective-permute-start(bf16[288,1152]{1,0:T(8,128)(2,1)S(1)} %collective-permute-done.3.refs_1_), channel_id=1, source_target_pairs={{0,1},{1,0},{2,3},{3,2},{4,5},{5,4},{6,7},{7,6},{8,9},{9,8},{10,11... | collective-permute-start | bytes 1990664 | tf_op jit(solution)/shard_map/ppermute | solution.py:442
  50.6 3.9 %collective-permute-start.4 = (bf16[288,1152]{1,0:T(8,128)(2,1)S(1)}, bf16[288,1152]{1,0:T(8,128)(2,1)}, u32[]{:S(2)}, u32[]{:S(2)}) collective-permute-start(bf16[288,1152]{1,0:T(8,128)(2,1)S(1)} %collective-permute-done.3.refs_1_), channel_id=1, source_target_pairs={{0,64},{1,449},{2,66},{3,451},{4,68},{5,453},{6,70},{7,455},{8,72}... | collective-permute-start | bytes 1990664 | tf_op jit(solution)/shard_map/ppermute | solution.py:413
  54.6 1.9 collective-permute-start.8
  56.5 1.5 collective-permute-done.8.other_ref
  58.7 2.4 %shard_map.87.refs_0_ = bf16[288,1152]{1,0:T(8,128)(2,1)} custom-call(s32[4]{0:T(128)} %pad_add_fusion.at_ref, bf16[72,1152]{1,0:T(8,128)(2,1)} %get-tuple-element.44.own_ref, bf16[72,1152]{1,0:T(8,128)(2,1)} %copy-done.5, bf16[36,1152]{1,0:T(8,128)(2,1)} %copy-done.7, bf16[108,1152]{1,0:T(8,128)(2,1)} %copy-done.20), custom_call_target="tpu_custom_call" | custom-call | flops 2200000000 | bytes 3000000 | tf_op jit(solution)/shard_map/pallas_call | solution.py:351
  61.1 1.4 collective-permute-done.4.refs_2_
  62.4 4.0 %collective-permute-start.10 = (bf16[288,1152]{1,0:T(8,128)(2,1)}, bf16[288,1152]{1,0:T(8,128)(2,1)S(1)}, u32[]{:S(2)}, u32[]{:S(2)}) collective-permute-start(bf16[288,1152]{1,0:T(8,128)(2,1)} %collective-permute-done.4.refs_2_), channel_id=1, source_target_pairs={{0,1},{1,0},{2,3},{3,2},{4,5},{5,4},{6,7},{7,6},{8,9},{9,8},{10,11... | collective-permute-start | bytes 1990664 | tf_op jit(solution)/shard_map/ppermute | solution.py:442
  66.4 3.1 %collective-permute-start.9 = (bf16[288,1152]{1,0:T(8,128)(2,1)}, bf16[288,1152]{1,0:T(8,128)(2,1)S(1)}, u32[]{:S(2)}, u32[]{:S(2)}) collective-permute-start(bf16[288,1152]{1,0:T(8,128)(2,1)} %collective-permute-done.4.refs_2_), channel_id=1, source_target_pairs={{0,64},{1,449},{2,66},{3,451},{4,68},{5,453},{6,70},{7,455},{8,72}... | collective-permute-start | bytes 1990664 | tf_op jit(solution)/shard_map/ppermute | solution.py:413
  69.6 2.3 %collective-permute-start.14 = (bf16[288,1152]{1,0:T(8,128)(2,1)}, bf16[288,1152]{1,0:T(8,128)(2,1)S(1)}, u32[]{:S(2)}, u32[]{:S(2)}) collective-permute-start(bf16[288,1152]{1,0:T(8,128)(2,1)} %shard_map.87.refs_0_), channel_id=1, source_target_pairs={{0,64},{1,449},{2,66},{3,451},{4,68},{5,453},{6,70},{7,455},{8,72}... | collective-permute-start | bytes 1990664 | tf_op jit(solution)/shard_map/ppermute | solution.py:413
  71.8 6.5 %collective-permute-done.9.refs_3_ = bf16[288,1152]{1,0:T(8,128)(2,1)S(1)} collective-permute-done((bf16[288,1152]{1,0:T(8,128)(2,1)}, bf16[288,1152]{1,0:T(8,128)(2,1)S(1)}, u32[]{:S(2)}, u32[]{:S(2)}) %collective-permute-start.9) | collective-permute-done | bytes 663584 | tf_op jit(solution)/shard_map/ppermute | solution.py:413
  78.3 4.0 %collective-permute-start.12 = (bf16[288,1152]{1,0:T(8,128)(2,1)S(1)}, bf16[288,1152]{1,0:T(8,128)(2,1)S(1)}, u32[]{:S(2)}, u32[]{:S(2)}) collective-permute-start(bf16[288,1152]{1,0:T(8,128)(2,1)S(1)} %collective-permute-done.9.refs_3_), channel_id=1, source_target_pairs={{0,1},{1,0},{2,3},{3,2},{4,5},{5,4},{6,7},{7,6},{8,9},{9,8},{10,11... | collective-permute-start | bytes 1990664 | tf_op jit(solution)/shard_map/ppermute | solution.py:442
  82.4 2.0 collective-permute-start.11
  84.4 1.1 collective-permute-done.14.refs_1_
  85.4 4.1 %collective-permute-start.15 = (bf16[288,1152]{1,0:T(8,128)(2,1)S(1)}, bf16[288,1152]{1,0:T(8,128)(2,1)}, u32[]{:S(2)}, u32[]{:S(2)}) collective-permute-start(bf16[288,1152]{1,0:T(8,128)(2,1)S(1)} %collective-permute-done.14.refs_1_), channel_id=1, source_target_pairs={{0,64},{1,449},{2,66},{3,451},{4,68},{5,453},{6,70},{7,455},{8,72}... | collective-permute-start | bytes 1990664 | tf_op jit(solution)/shard_map/ppermute | solution.py:413
  89.5 1.0 collective-permute-done.11.refs_7_
  91.4 4.0 %collective-permute-start.13 = (bf16[144,1152]{1,0:T(8,128)(2,1)S(1)}, bf16[144,1152]{1,0:T(8,128)(2,1)S(1)}, u32[]{:S(2)}, u32[]{:S(2)}) collective-permute-start(bf16[144,1152]{1,0:T(8,128)(2,1)S(1)} %collective-permute-done.11.refs_7_), channel_id=1, source_target_pairs={{0,1},{1,0},{2,3},{3,2},{4,5},{5,4},{6,7},{7,6},{8,9},{9,8},{10,11... | collective-permute-start | bytes 995336 | tf_op jit(solution)/shard_map/ppermute | solution.py:442
  95.4 2.3 %collective-permute-done.15.refs_2_ = bf16[288,1152]{1,0:T(8,128)(2,1)} collective-permute-done((bf16[288,1152]{1,0:T(8,128)(2,1)S(1)}, bf16[288,1152]{1,0:T(8,128)(2,1)}, u32[]{:S(2)}, u32[]{:S(2)}) %collective-permute-start.15) | collective-permute-done | bytes 663584 | tf_op jit(solution)/shard_map/ppermute | solution.py:413
  98.5 4.5 %collective-permute-start.16 = (bf16[288,1152]{1,0:T(8,128)(2,1)}, bf16[288,1152]{1,0:T(8,128)(2,1)}, u32[]{:S(2)}, u32[]{:S(2)}) collective-permute-start(bf16[288,1152]{1,0:T(8,128)(2,1)} %collective-permute-done.15.refs_2_), channel_id=1, source_target_pairs={{0,64},{1,449},{2,66},{3,451},{4,68},{5,453},{6,70},{7,455},{8,72}... | collective-permute-start | bytes 1990664 | tf_op jit(solution)/shard_map/ppermute | solution.py:413
  103.0 8.6 %shard_map.88 = (bf16[128,2304]{1,0:T(8,128)(2,1)}, bf16[3,128,640]{2,1,0:T(8,128)(2,1)}, f32[8,128,128]{2,1,0:T(8,128)}, bf16[128,640]{1,0:T(8,128)(2,1)}) custom-call(s32[4]{0:T(128)} %pad_add_fusion.at_ref, bf16[128,1152]{1,0:T(8,128)(2,1)} %bitcast.21, bf16[128,1152]{1,0:T(8,128)(2,1)} %bitcast.20, bf16[288,1152]{1,0:T(8,128)(2,1)} %shard_map.86.refs_0_, ...), custom_call_target="tpu_custom_call" | custom-call | flops 8800000000 | bytes 3000000 | tf_op jit(solution)/shard_map/pallas_call | solution.py:351
  111.6 5.4 %all-to-all-start = ((bf16[16,8,2304]{2,1,0:T(8,128)(2,1)}), bf16[16,8,2304]{2,1,0:T(8,128)(2,1)S(1)}, u32[]{:S(2)}, u32[]{:S(2)}) async-start(bf16[16,8,2304]{2,1,0:T(8,128)(2,1)} %bitcast.19), calls=%async_computation | async-start | bytes 1179648 | tf_op jit(solution)/shard_map/all_to_all | solution.py:430
  118.0 4.9 %collective-permute-start.20 = (bf16[144,1152]{1,0:T(8,128)(2,1)S(1)}, bf16[144,1152]{1,0:T(8,128)(2,1)S(1)}, u32[]{:S(2)}, u32[]{:S(2)}) collective-permute-start(bf16[144,1152]{1,0:T(8,128)(2,1)S(1)} %constant_dynamic-slice_fusion), channel_id=1, source_target_pairs={{0,64},{1,449},{2,66},{3,451},{4,68},{5,453},{6,70},{7,455},{8,72}... | collective-permute-start | bytes 995336 | tf_op jit(solution)/shard_map/ppermute | solution.py:413
  122.9 1.9 collective-permute-start.17
  124.8 2.4 %collective-permute-start.18 = (bf16[288,1152]{1,0:T(8,128)(2,1)}, bf16[288,1152]{1,0:T(8,128)(2,1)}, u32[]{:S(2)}, u32[]{:S(2)}) collective-permute-start(bf16[288,1152]{1,0:T(8,128)(2,1)} %collective-permute-done.15.refs_2_), channel_id=1, source_target_pairs={{0,1},{1,0},{2,3},{3,2},{4,5},{5,4},{6,7},{7,6},{8,9},{9,8},{10,11... | collective-permute-start | bytes 1990664 | tf_op jit(solution)/shard_map/ppermute | solution.py:442
  127.2 1.9 collective-permute-start.19
  129.2 2.6 %collective-permute-start.21 = (bf16[144,1152]{1,0:T(8,128)(2,1)S(1)}, bf16[144,1152]{1,0:T(8,128)(2,1)S(1)}, u32[]{:S(2)}, u32[]{:S(2)}) collective-permute-start(bf16[144,1152]{1,0:T(8,128)(2,1)S(1)} %collective-permute-done.20.refs_7_), channel_id=1, source_target_pairs={{0,1},{1,0},{2,3},{3,2},{4,5},{5,4},{6,7},{7,6},{8,9},{9,8},{10,11... | collective-permute-start | bytes 995336 | tf_op jit(solution)/shard_map/ppermute | solution.py:442
  131.8 1.0 collective-permute-done.21.refs_8_
  133.8 12.2 %shard_map.89 = (bf16[128,2304]{1,0:T(8,128)(2,1)}, bf16[288,1152]{1,0:T(8,128)(2,1)}, bf16[288,1152]{1,0:T(8,128)(2,1)}) custom-call(s32[4]{0:T(128)} %pad_add_fusion.at_ref, bf16[128,2304]{1,0:T(8,128)(2,1)} %bitcast.17, bf16[640,640]{1,0:T(8,128)(2,1)} %fusion.order_hbm, bf16[288,1152]{1,0:T(8,128)(2,1)} %shard_map.87.refs_0_, ...), custom_call_target="tpu_custom_call" | custom-call | flops 13200000000 | bytes 3000000 | tf_op jit(solution)/shard_map/pallas_call | solution.py:351
  146.0 2.4 %collective-permute-start.22 = (bf16[288,1152]{1,0:T(8,128)(2,1)}, bf16[288,1152]{1,0:T(8,128)(2,1)S(1)}, u32[]{:S(2)}, u32[]{:S(2)}) collective-permute-start(bf16[288,1152]{1,0:T(8,128)(2,1)} %get-tuple-element.63), channel_id=1, source_target_pairs={{0,1},{1,0},{2,3},{3,2},{4,5},{5,4},{6,7},{7,6},{8,9},{9,8},{10,11... | collective-permute-start | bytes 1990664 | tf_op jit(solution)/shard_map/ppermute | solution.py:442
  148.4 5.5 %all-to-all-start.1 = ((bf16[16,8,2304]{2,1,0:T(8,128)(2,1)}), bf16[16,8,2304]{2,1,0:T(8,128)(2,1)S(1)}, u32[]{:S(2)}, u32[]{:S(2)}) async-start(bf16[16,8,2304]{2,1,0:T(8,128)(2,1)} %bitcast.18), calls=%async_computation.1 | async-start | bytes 1179648 | tf_op jit(solution)/shard_map/all_to_all | solution.py:430
  154.2 2.6 %collective-permute-start.23 = (bf16[144,1152]{1,0:T(8,128)(2,1)S(1)}, bf16[144,1152]{1,0:T(8,128)(2,1)S(1)}, u32[]{:S(2)}, u32[]{:S(2)}) collective-permute-start(bf16[144,1152]{1,0:T(8,128)(2,1)S(1)} %slice.14), channel_id=1, source_target_pairs={{0,64},{1,449},{2,66},{3,451},{4,68},{5,453},{6,70},{7,455},{8,72}... | collective-permute-start | bytes 995336 | tf_op jit(solution)/shard_map/ppermute | solution.py:413
  156.8 5.5 %collective-permute-done.23 = bf16[144,1152]{1,0:T(8,128)(2,1)S(1)} collective-permute-done((bf16[144,1152]{1,0:T(8,128)(2,1)S(1)}, bf16[144,1152]{1,0:T(8,128)(2,1)S(1)}, u32[]{:S(2)}, u32[]{:S(2)}) %collective-permute-start.23) | collective-permute-done | bytes 331808 | tf_op jit(solution)/shard_map/ppermute | solution.py:413
  163.4 1.1 all-to-all-done.1
  164.5 9.5 %all-to-all-start.2 = ((bf16[16,9,1152]{2,1,0:T(8,128)(2,1)}), bf16[16,9,1152]{2,1,0:T(8,128)(2,1)S(1)}, u32[]{:S(2)}, u32[]{:S(2)}) async-start(bf16[16,9,1152]{2,1,0:T(8,128)(2,1)} %reshape.130), calls=%async_computation.2 | async-start | bytes 1179648 | tf_op jit(solution)/shard_map/all_to_all | solution.py:520
  174.1 7.8 %shard_map.90 = bf16[128,1152]{1,0:T(8,128)(2,1)} custom-call(s32[4]{0:T(128)} %pad_add_fusion.at_ref, bf16[128,1152]{1,0:T(8,128)(2,1)} %bitcast.22, bf16[128,2304]{1,0:T(8,128)(2,1)} %bitcast.15, bf16[3,128,640]{2,1,0:T(8,128)(2,1)} %get-tuple-element.64.qkv_hbm, f32[8,128,128]{2,1,0:T(8,128)} %get-tuple-element.65.probs_hbm, ...), custom_call_target="tpu_custom_call" | custom-call | flops 9900000256 | bytes 3000000 | tf_op jit(solution)/shard_map/pallas_call | solution.py:351
  181.9 14.1 %all-to-all-done.2 = bf16[16,9,1152]{2,1,0:T(8,128)(2,1)S(1)} async-done(((bf16[16,9,1152]{2,1,0:T(8,128)(2,1)}), bf16[16,9,1152]{2,1,0:T(8,128)(2,1)S(1)}, u32[]{:S(2)}, u32[]{:S(2)}) %all-to-all-start.2) | async-done | bytes 331808 | tf_op jit(solution)/shard_map/all_to_all | solution.py:520
  196.9 6.6 %all-to-all-start.3 = ((bf16[16,9,1152]{2,1,0:T(8,128)(2,1)}), bf16[16,9,1152]{2,1,0:T(8,128)(2,1)S(1)}, u32[]{:S(2)}, u32[]{:S(2)}) async-start(bf16[16,9,1152]{2,1,0:T(8,128)(2,1)} %broadcast_in_dim.30), calls=%async_computation.3 | async-start | bytes 1179648 | tf_op jit(solution)/shard_map/all_to_all | solution.py:383
  204.3 9.8 %all-to-all-done.3 = bf16[16,9,1152]{2,1,0:T(8,128)(2,1)S(1)} async-done(((bf16[16,9,1152]{2,1,0:T(8,128)(2,1)}), bf16[16,9,1152]{2,1,0:T(8,128)(2,1)S(1)}, u32[]{:S(2)}, u32[]{:S(2)}) %all-to-all-start.3) | async-done | bytes 331808 | tf_op jit(solution)/shard_map/all_to_all | solution.py:383
  (79 shorter events, 10.2 us)
Async XLA Ops:
  4.2 21.4 %collective-permute-start = (bf16[72,1152]{1,0:T(8,128)(2,1)}, bf16[72,1152]{1,0:T(8,128)(2,1)S(1)}, u32[]{:S(2)}, u32[]{:S(2)}) collective-permute-start(bf16[72,1152]{1,0:T(8,128)(2,1)} %get-tuple-element.36.own_ref), channel_id=1, source_target_pairs={{0,16},{1,49},{2,18},{3,51},{4,20},{5,53},{6,22},{7,55},{8,24},{9,... | collective-permute-start | bytes 497672 | tf_op jit(solution)/shard_map/ppermute | solution.py:413
  15.7 9.9 %collective-permute-start.1 = (bf16[36,1152]{1,0:T(8,128)(2,1)}, bf16[36,1152]{1,0:T(8,128)(2,1)S(1)}, u32[]{:S(2)}, u32[]{:S(2)}) collective-permute-start(bf16[36,1152]{1,0:T(8,128)(2,1)} %get-tuple-element.37), channel_id=1, source_target_pairs={{0,32},{1,33},{2,34},{3,35},{4,36},{5,37},{6,38},{7,39},{8,40},{9,... | collective-permute-start | bytes 248840 | tf_op jit(solution)/shard_map/ppermute | solution.py:413
  25.6 3.6 %copy-start.8 = (bf16[36,1152]{1,0:T(8,128)(2,1)}, bf16[36,1152]{1,0:T(8,128)(2,1)S(1)}, u32[]{:S(2)}) copy-start(bf16[36,1152]{1,0:T(8,128)(2,1)S(1)} %collective-permute-done.1.far_ref) | copy-start | bytes 248836
  25.6 3.6 %copy-start.6 = (bf16[72,1152]{1,0:T(8,128)(2,1)}, bf16[72,1152]{1,0:T(8,128)(2,1)S(1)}, u32[]{:S(2)}) copy-start(bf16[72,1152]{1,0:T(8,128)(2,1)S(1)} %collective-permute-done.next_ref) | copy-start | bytes 497668
  25.6 13.8 %copy-start.22 = (bf16[36,1152]{1,0:T(8,128)(2,1)S(1)}, bf16[36,1152]{1,0:T(8,128)(2,1)}, u32[]{:S(2)}) copy-start(bf16[36,1152]{1,0:T(8,128)(2,1)} %get-tuple-element.45) | copy-start | bytes 248836
  25.6 17.2 %copy-start.21 = (bf16[72,1152]{1,0:T(8,128)(2,1)S(1)}, bf16[72,1152]{1,0:T(8,128)(2,1)}, u32[]{:S(2)}) copy-start(bf16[72,1152]{1,0:T(8,128)(2,1)} %get-tuple-element.44.own_ref) | copy-start | bytes 497668
  25.6 3.6 %collective-permute-start.2 = (bf16[108,1152]{1,0:T(8,128)(2,1)S(1)}, bf16[108,1152]{1,0:T(8,128)(2,1)S(1)}, u32[]{:S(2)}, u32[]{:S(2)}) collective-permute-start(bf16[108,1152]{1,0:T(8,128)(2,1)S(1)} %pad_maximum_fusion), channel_id=1, source_target_pairs={{0,1},{1,0},{2,3},{3,2},{4,5},{5,4},{6,7},{7,6},{8,9},{9,8},{10,11... | collective-permute-start | bytes 746504 | tf_op jit(solution)/shard_map/ppermute | solution.py:442
  32.3 15.8 %collective-permute-start.3 = (bf16[288,1152]{1,0:T(8,128)(2,1)}, bf16[288,1152]{1,0:T(8,128)(2,1)S(1)}, u32[]{:S(2)}, u32[]{:S(2)}) collective-permute-start(bf16[288,1152]{1,0:T(8,128)(2,1)} %shard_map.86.refs_0_), channel_id=1, source_target_pairs={{0,64},{1,449},{2,66},{3,451},{4,68},{5,453},{6,70},{7,455},{8,72}... | collective-permute-start | bytes 1990664 | tf_op jit(solution)/shard_map/ppermute | solution.py:413
  39.5 15.0 %collective-permute-start.7 = (bf16[36,1152]{1,0:T(8,128)(2,1)S(1)}, bf16[36,1152]{1,0:T(8,128)(2,1)S(1)}, u32[]{:S(2)}, u32[]{:S(2)}) collective-permute-start(bf16[36,1152]{1,0:T(8,128)(2,1)S(1)} %copy-done.22), channel_id=1, source_target_pairs={{0,32},{1,33},{2,34},{3,35},{4,36},{5,37},{6,38},{7,39},{8,40},{9,... | collective-permute-start | bytes 248840 | tf_op jit(solution)/shard_map/ppermute | solution.py:413
  42.8 11.7 %collective-permute-start.6 = (bf16[72,1152]{1,0:T(8,128)(2,1)S(1)}, bf16[72,1152]{1,0:T(8,128)(2,1)S(1)}, u32[]{:S(2)}, u32[]{:S(2)}) collective-permute-start(bf16[72,1152]{1,0:T(8,128)(2,1)S(1)} %copy-done.21), channel_id=1, source_target_pairs={{0,16},{1,49},{2,18},{3,51},{4,20},{5,53},{6,22},{7,55},{8,24},{9,... | collective-permute-start | bytes 497672 | tf_op jit(solution)/shard_map/ppermute | solution.py:413
  48.1 13.0 %copy-start.9 = (bf16[288,1152]{1,0:T(8,128)(2,1)}, bf16[288,1152]{1,0:T(8,128)(2,1)S(1)}, u32[]{:S(2)}) copy-start(bf16[288,1152]{1,0:T(8,128)(2,1)S(1)} %collective-permute-done.3.refs_1_) | copy-start | bytes 1990660
  48.1 13.0 %collective-permute-start.5 = (bf16[288,1152]{1,0:T(8,128)(2,1)S(1)}, bf16[288,1152]{1,0:T(8,128)(2,1)S(1)}, u32[]{:S(2)}, u32[]{:S(2)}) collective-permute-start(bf16[288,1152]{1,0:T(8,128)(2,1)S(1)} %collective-permute-done.3.refs_1_), channel_id=1, source_target_pairs={{0,1},{1,0},{2,3},{3,2},{4,5},{5,4},{6,7},{7,6},{8,9},{9,8},{10,11... | collective-permute-start | bytes 1990664 | tf_op jit(solution)/shard_map/ppermute | solution.py:442
  50.6 11.8 %collective-permute-start.4 = (bf16[288,1152]{1,0:T(8,128)(2,1)S(1)}, bf16[288,1152]{1,0:T(8,128)(2,1)}, u32[]{:S(2)}, u32[]{:S(2)}) collective-permute-start(bf16[288,1152]{1,0:T(8,128)(2,1)S(1)} %collective-permute-done.3.refs_1_), channel_id=1, source_target_pairs={{0,64},{1,449},{2,66},{3,451},{4,68},{5,453},{6,70},{7,455},{8,72}... | collective-permute-start | bytes 1990664 | tf_op jit(solution)/shard_map/ppermute | solution.py:413
  54.5 3.5 %copy-start.7 = (bf16[36,1152]{1,0:T(8,128)(2,1)}, bf16[36,1152]{1,0:T(8,128)(2,1)S(1)}, u32[]{:S(2)}) copy-start(bf16[36,1152]{1,0:T(8,128)(2,1)S(1)} %collective-permute-done.7.far_ref) | copy-start | bytes 248836
  54.5 3.5 %copy-start.5 = (bf16[72,1152]{1,0:T(8,128)(2,1)}, bf16[72,1152]{1,0:T(8,128)(2,1)S(1)}, u32[]{:S(2)}) copy-start(bf16[72,1152]{1,0:T(8,128)(2,1)S(1)} %collective-permute-done.6.next_ref) | copy-start | bytes 497668
  54.6 3.4 %collective-permute-start.8 = (bf16[108,1152]{1,0:T(8,128)(2,1)S(1)}, bf16[108,1152]{1,0:T(8,128)(2,1)S(1)}, u32[]{:S(2)}, u32[]{:S(2)}) collective-permute-start(bf16[108,1152]{1,0:T(8,128)(2,1)S(1)} %pad_maximum_fusion.1), channel_id=1, source_target_pairs={{0,1},{1,0},{2,3},{3,2},{4,5},{5,4},{6,7},{7,6},{8,9},{9,8},{10,11... | collective-permute-start | bytes 746504 | tf_op jit(solution)/shard_map/ppermute | solution.py:442
  61.1 1.4 copy-start.10
  62.4 9.4 %collective-permute-start.10 = (bf16[288,1152]{1,0:T(8,128)(2,1)}, bf16[288,1152]{1,0:T(8,128)(2,1)S(1)}, u32[]{:S(2)}, u32[]{:S(2)}) collective-permute-start(bf16[288,1152]{1,0:T(8,128)(2,1)} %collective-permute-done.4.refs_2_), channel_id=1, source_target_pairs={{0,1},{1,0},{2,3},{3,2},{4,5},{5,4},{6,7},{7,6},{8,9},{9,8},{10,11... | collective-permute-start | bytes 1990664 | tf_op jit(solution)/shard_map/ppermute | solution.py:442
  66.4 11.9 %collective-permute-start.9 = (bf16[288,1152]{1,0:T(8,128)(2,1)}, bf16[288,1152]{1,0:T(8,128)(2,1)S(1)}, u32[]{:S(2)}, u32[]{:S(2)}) collective-permute-start(bf16[288,1152]{1,0:T(8,128)(2,1)} %collective-permute-done.4.refs_2_), channel_id=1, source_target_pairs={{0,64},{1,449},{2,66},{3,451},{4,68},{5,453},{6,70},{7,455},{8,72}... | collective-permute-start | bytes 1990664 | tf_op jit(solution)/shard_map/ppermute | solution.py:413
  69.6 15.9 %collective-permute-start.14 = (bf16[288,1152]{1,0:T(8,128)(2,1)}, bf16[288,1152]{1,0:T(8,128)(2,1)S(1)}, u32[]{:S(2)}, u32[]{:S(2)}) collective-permute-start(bf16[288,1152]{1,0:T(8,128)(2,1)} %shard_map.87.refs_0_), channel_id=1, source_target_pairs={{0,64},{1,449},{2,66},{3,451},{4,68},{5,453},{6,70},{7,455},{8,72}... | collective-permute-start | bytes 1990664 | tf_op jit(solution)/shard_map/ppermute | solution.py:413
  71.8 31.1 %copy-start.11 = (bf16[288,1152]{1,0:T(8,128)(2,1)}, bf16[288,1152]{1,0:T(8,128)(2,1)S(1)}, u32[]{:S(2)}) copy-start(bf16[288,1152]{1,0:T(8,128)(2,1)S(1)} %collective-permute-done.10.refs_5_) | copy-start | bytes 1990660
  78.3 24.6 %copy-start.4 = (bf16[288,1152]{1,0:T(8,128)(2,1)}, bf16[288,1152]{1,0:T(8,128)(2,1)S(1)}, u32[]{:S(2)}) copy-start(bf16[288,1152]{1,0:T(8,128)(2,1)S(1)} %collective-permute-done.9.refs_3_) | copy-start | bytes 1990660
  78.3 12.2 %collective-permute-start.12 = (bf16[288,1152]{1,0:T(8,128)(2,1)S(1)}, bf16[288,1152]{1,0:T(8,128)(2,1)S(1)}, u32[]{:S(2)}, u32[]{:S(2)}) collective-permute-start(bf16[288,1152]{1,0:T(8,128)(2,1)S(1)} %collective-permute-done.9.refs_3_), channel_id=1, source_target_pairs={{0,1},{1,0},{2,3},{3,2},{4,5},{5,4},{6,7},{7,6},{8,9},{9,8},{10,11... | collective-permute-start | bytes 1990664 | tf_op jit(solution)/shard_map/ppermute | solution.py:442
  82.4 8.2 %collective-permute-start.11 = (bf16[144,1152]{1,0:T(8,128)(2,1)S(1)}, bf16[144,1152]{1,0:T(8,128)(2,1)S(1)}, u32[]{:S(2)}, u32[]{:S(2)}) collective-permute-start(bf16[144,1152]{1,0:T(8,128)(2,1)S(1)} %constant_dynamic-slice_fusion.1), channel_id=1, source_target_pairs={{0,64},{1,449},{2,66},{3,451},{4,68},{5,453},{6,70},{7,455},{8,72}... | collective-permute-start | bytes 995336 | tf_op jit(solution)/shard_map/ppermute | solution.py:413
  85.4 37.4 %copy-start.13 = (bf16[288,1152]{1,0:T(8,128)(2,1)}, bf16[288,1152]{1,0:T(8,128)(2,1)S(1)}, u32[]{:S(2)}) copy-start(bf16[288,1152]{1,0:T(8,128)(2,1)S(1)} %collective-permute-done.14.refs_1_) | copy-start | bytes 1990660
  85.4 12.3 %collective-permute-start.15 = (bf16[288,1152]{1,0:T(8,128)(2,1)S(1)}, bf16[288,1152]{1,0:T(8,128)(2,1)}, u32[]{:S(2)}, u32[]{:S(2)}) collective-permute-start(bf16[288,1152]{1,0:T(8,128)(2,1)S(1)} %collective-permute-done.14.refs_1_), channel_id=1, source_target_pairs={{0,64},{1,449},{2,66},{3,451},{4,68},{5,453},{6,70},{7,455},{8,72}... | collective-permute-start | bytes 1990664 | tf_op jit(solution)/shard_map/ppermute | solution.py:413
  90.5 7.2 %copy-start.15 = (bf16[144,1152]{1,0:T(8,128)(2,1)}, bf16[144,1152]{1,0:T(8,128)(2,1)S(1)}, u32[]{:S(2)}) copy-start(bf16[144,1152]{1,0:T(8,128)(2,1)S(1)} %collective-permute-done.11.refs_7_) | copy-start | bytes 995332
  90.5 0.9 copy-start.12
  91.4 6.3 %collective-permute-start.13 = (bf16[144,1152]{1,0:T(8,128)(2,1)S(1)}, bf16[144,1152]{1,0:T(8,128)(2,1)S(1)}, u32[]{:S(2)}, u32[]{:S(2)}) collective-permute-start(bf16[144,1152]{1,0:T(8,128)(2,1)S(1)} %collective-permute-done.11.refs_7_), channel_id=1, source_target_pairs={{0,1},{1,0},{2,3},{3,2},{4,5},{5,4},{6,7},{7,6},{8,9},{9,8},{10,11... | collective-permute-start | bytes 995336 | tf_op jit(solution)/shard_map/ppermute | solution.py:442
  98.5 18.5 %collective-permute-start.16 = (bf16[288,1152]{1,0:T(8,128)(2,1)}, bf16[288,1152]{1,0:T(8,128)(2,1)}, u32[]{:S(2)}, u32[]{:S(2)}) collective-permute-start(bf16[288,1152]{1,0:T(8,128)(2,1)} %collective-permute-done.15.refs_2_), channel_id=1, source_target_pairs={{0,64},{1,449},{2,66},{3,451},{4,68},{5,453},{6,70},{7,455},{8,72}... | collective-permute-start | bytes 1990664 | tf_op jit(solution)/shard_map/ppermute | solution.py:413
  111.6 20.2 %all-to-all-start = ((bf16[16,8,2304]{2,1,0:T(8,128)(2,1)}), bf16[16,8,2304]{2,1,0:T(8,128)(2,1)S(1)}, u32[]{:S(2)}, u32[]{:S(2)}) async-start(bf16[16,8,2304]{2,1,0:T(8,128)(2,1)} %bitcast.19), calls=%async_computation | async-start | bytes 1179648 | tf_op jit(solution)/shard_map/all_to_all | solution.py:430
  118.0 11.2 %collective-permute-start.20 = (bf16[144,1152]{1,0:T(8,128)(2,1)S(1)}, bf16[144,1152]{1,0:T(8,128)(2,1)S(1)}, u32[]{:S(2)}, u32[]{:S(2)}) collective-permute-start(bf16[144,1152]{1,0:T(8,128)(2,1)S(1)} %constant_dynamic-slice_fusion), channel_id=1, source_target_pairs={{0,64},{1,449},{2,66},{3,451},{4,68},{5,453},{6,70},{7,455},{8,72}... | collective-permute-start | bytes 995336 | tf_op jit(solution)/shard_map/ppermute | solution.py:413
  122.9 10.0 %collective-permute-start.17 = (bf16[288,1152]{1,0:T(8,128)(2,1)S(1)}, bf16[288,1152]{1,0:T(8,128)(2,1)S(1)}, u32[]{:S(2)}, u32[]{:S(2)}) collective-permute-start(bf16[288,1152]{1,0:T(8,128)(2,1)S(1)} %collective-permute-done.14.refs_1_), channel_id=1, source_target_pairs={{0,1},{1,0},{2,3},{3,2},{4,5},{5,4},{6,7},{7,6},{8,9},{9,8},{10,11... | collective-permute-start | bytes 1990664 | tf_op jit(solution)/shard_map/ppermute | solution.py:442
  124.8 8.0 %collective-permute-start.18 = (bf16[288,1152]{1,0:T(8,128)(2,1)}, bf16[288,1152]{1,0:T(8,128)(2,1)}, u32[]{:S(2)}, u32[]{:S(2)}) collective-permute-start(bf16[288,1152]{1,0:T(8,128)(2,1)} %collective-permute-done.15.refs_2_), channel_id=1, source_target_pairs={{0,1},{1,0},{2,3},{3,2},{4,5},{5,4},{6,7},{7,6},{8,9},{9,8},{10,11... | collective-permute-start | bytes 1990664 | tf_op jit(solution)/shard_map/ppermute | solution.py:442
  127.2 6.3 %collective-permute-start.19 = (bf16[288,1152]{1,0:T(8,128)(2,1)}, bf16[288,1152]{1,0:T(8,128)(2,1)}, u32[]{:S(2)}, u32[]{:S(2)}) collective-permute-start(bf16[288,1152]{1,0:T(8,128)(2,1)} %collective-permute-done.16.refs_3_), channel_id=1, source_target_pairs={{0,1},{1,0},{2,3},{3,2},{4,5},{5,4},{6,7},{7,6},{8,9},{9,8},{10,11... | collective-permute-start | bytes 1990664 | tf_op jit(solution)/shard_map/ppermute | solution.py:442
  129.2 3.7 %copy-start.17 = (bf16[144,1152]{1,0:T(8,128)(2,1)}, bf16[144,1152]{1,0:T(8,128)(2,1)S(1)}, u32[]{:S(2)}) copy-start(bf16[144,1152]{1,0:T(8,128)(2,1)S(1)} %collective-permute-done.20.refs_7_) | copy-start | bytes 995332
  129.2 3.7 %collective-permute-start.21 = (bf16[144,1152]{1,0:T(8,128)(2,1)S(1)}, bf16[144,1152]{1,0:T(8,128)(2,1)S(1)}, u32[]{:S(2)}, u32[]{:S(2)}) collective-permute-start(bf16[144,1152]{1,0:T(8,128)(2,1)S(1)} %collective-permute-done.20.refs_7_), channel_id=1, source_target_pairs={{0,1},{1,0},{2,3},{3,2},{4,5},{5,4},{6,7},{7,6},{8,9},{9,8},{10,11... | collective-permute-start | bytes 995336 | tf_op jit(solution)/shard_map/ppermute | solution.py:442
  131.8 1.8 copy-start.3
  132.8 0.7 copy-start.18
  132.8 1.0 copy-start.14
  146.0 8.0 %copy-start.2 = (bf16[288,1152]{1,0:T(8,128)(2,1)S(1)}, bf16[288,1152]{1,0:T(8,128)(2,1)}, u32[]{:S(2)}) copy-start(bf16[288,1152]{1,0:T(8,128)(2,1)} %get-tuple-element.62) | copy-start | bytes 1990660
  146.0 7.9 %collective-permute-start.22 = (bf16[288,1152]{1,0:T(8,128)(2,1)}, bf16[288,1152]{1,0:T(8,128)(2,1)S(1)}, u32[]{:S(2)}, u32[]{:S(2)}) collective-permute-start(bf16[288,1152]{1,0:T(8,128)(2,1)} %get-tuple-element.63), channel_id=1, source_target_pairs={{0,1},{1,0},{2,3},{3,2},{4,5},{5,4},{6,7},{7,6},{8,9},{9,8},{10,11... | collective-permute-start | bytes 1990664 | tf_op jit(solution)/shard_map/ppermute | solution.py:442
  148.4 16.1 %all-to-all-start.1 = ((bf16[16,8,2304]{2,1,0:T(8,128)(2,1)}), bf16[16,8,2304]{2,1,0:T(8,128)(2,1)S(1)}, u32[]{:S(2)}, u32[]{:S(2)}) async-start(bf16[16,8,2304]{2,1,0:T(8,128)(2,1)} %bitcast.18), calls=%async_computation.1 | async-start | bytes 1179648 | tf_op jit(solution)/shard_map/all_to_all | solution.py:430
  154.2 8.2 %collective-permute-start.23 = (bf16[144,1152]{1,0:T(8,128)(2,1)S(1)}, bf16[144,1152]{1,0:T(8,128)(2,1)S(1)}, u32[]{:S(2)}, u32[]{:S(2)}) collective-permute-start(bf16[144,1152]{1,0:T(8,128)(2,1)S(1)} %slice.14), channel_id=1, source_target_pairs={{0,64},{1,449},{2,66},{3,451},{4,68},{5,453},{6,70},{7,455},{8,72}... | collective-permute-start | bytes 995336 | tf_op jit(solution)/shard_map/ppermute | solution.py:413
  164.5 9.6 %copy-start = (bf16[16,8,2304]{2,1,0:T(8,128)(2,1)}, bf16[16,8,2304]{2,1,0:T(8,128)(2,1)S(1)}, u32[]{:S(2)}) copy-start(bf16[16,8,2304]{2,1,0:T(8,128)(2,1)S(1)} %all-to-all-done.1) | copy-start | bytes 1769476
  164.5 31.4 %all-to-all-start.2 = ((bf16[16,9,1152]{2,1,0:T(8,128)(2,1)}), bf16[16,9,1152]{2,1,0:T(8,128)(2,1)S(1)}, u32[]{:S(2)}, u32[]{:S(2)}) async-start(bf16[16,9,1152]{2,1,0:T(8,128)(2,1)} %reshape.130), calls=%async_computation.2 | async-start | bytes 1179648 | tf_op jit(solution)/shard_map/all_to_all | solution.py:520
  196.0 7.5 %copy-start.1 = (bf16[16,8,2304]{2,1,0:T(8,128)(2,1)S(1)}, bf16[16,8,2304]{2,1,0:T(8,128)(2,1)}, u32[]{:S(2)}) copy-start(bf16[16,8,2304]{2,1,0:T(8,128)(2,1)} %copy-done) | copy-start | bytes 1769476
  196.9 17.1 %all-to-all-start.3 = ((bf16[16,9,1152]{2,1,0:T(8,128)(2,1)}), bf16[16,9,1152]{2,1,0:T(8,128)(2,1)S(1)}, u32[]{:S(2)}, u32[]{:S(2)}) async-start(bf16[16,9,1152]{2,1,0:T(8,128)(2,1)} %broadcast_in_dim.30), calls=%async_computation.3 | async-start | bytes 1179648 | tf_op jit(solution)/shard_map/all_to_all | solution.py:383
  (3 other events, 2.1 us)
